TPU v7x, 256 devices: a whole 4x4x8 slice. The times are simulated.
256 devices in a mesh: row: 8 (over z_lo, y), col: 32 (over x, z_hi, core).
Axes of the slice: x: 4, y: 4, z: 8 (z_hi: 4, z_lo: 2; z = z_hi * 2 + z_lo), core: 2. Of those that a mesh axis runs over, the one named last changes fastest.
Arguments:
- codes: int32 [2, 2048, 2048], P(None, 'row', 'col'), may hold values from 0 to 255
- codebooks: bfloat16 [2, 256, 8], replicated, may hold values from -3 to 3
- row_scale: float32 [2048], P('row'), may hold values from 0.5 to 2
- initial: bfloat16 [2048, 16384], P('row', 'col'), may hold values from -6 to 6
- hessian: bfloat16 [16384, 16384], P('row', 'col'), as said below
Outputs:
- hessian_product: float32 [2048, 16384], P('row', 'col')
- scale_grad: float32 [2048], P('row')
- codebook_grad: float32 [2, 256, 8], replicated
Inputs may be any that keep to these rules, and one draw needn't show every extreme that they name: hessian is exactly symmetric.
All inputs are finite; a program needn't handle non-finite values.
Results may differ from a plain program's by a relative error of at most 0.0029.
Values may be sent and summed in bfloat16 or wider, within the bound.
No kernel may reach another device: no remote copies, remote signals or barrier semaphores. Data moves between devices by JAX's collectives and lax.ppermute only.
A program may use at most 128 MiB of HBM per device.

v0:
```python
import jax
import jax.numpy as jnp
from jax import lax
from jax.sharding import PartitionSpec as P


def body(codes, codebooks, row_scale, initial, hessian):
    rows, width = initial.shape
    groups = width // 8
    words = codebooks.shape[1]
    row_count = lax.axis_size("row")
    col_count = lax.axis_size("col")
    labels = lax.broadcasted_iota(jnp.int32, (1, 1, words), 2)
    picks = [(codes[m][:, :, None] == labels).astype(jnp.bfloat16) for m in range(2)]
    unscaled = jnp.einsum("rgk,kt->rgt", picks[0], codebooks[0], preferred_element_type=jnp.float32)
    unscaled = unscaled + jnp.einsum(
        "rgk,kt->rgt", picks[1], codebooks[1], preferred_element_type=jnp.float32
    )
    unscaled = unscaled.reshape(rows, width)
    error = (row_scale[:, None] * unscaled - initial.astype(jnp.float32)).astype(jnp.bfloat16)
    partial_terms = lax.dot_general(
        error,
        lax.all_gather(hessian, "row", axis=0, tiled=True),
        (((1,), (1,)), ((), ())),
        preferred_element_type=jnp.float32,
    )
    summed = lax.psum_scatter(partial_terms, "col", scatter_dimension=1, tiled=True)
    product = 2.0 * summed
    local_scale = jnp.sum(product * unscaled, axis=1)
    weighted = (row_scale[:, None] * product).reshape(rows, groups, 8)
    local_books = jnp.stack(
        [
            jnp.einsum(
                "rgk,rgt->kt",
                picks[m].astype(jnp.float32),
                weighted,
                precision=lax.Precision.HIGHEST,
            )
            for m in range(2)
        ]
    )
    scale_total = lax.psum(local_scale, "col")
    book_total = lax.psum(local_books, ("row", "col"))
    full_width = width * col_count
    all_groups = rows * row_count * (full_width // 8)
    scale_grad = scale_total / full_width
    codebook_grad = book_total * (words / all_groups)
    return (product, scale_grad, codebook_grad)


def solution(mesh):
    in_specs = (P(None, "row", "col"), P(), P("row"), P("row", "col"), P("row", "col"))
    out_specs = (P("row", "col"), P("row"), P())
    return jax.shard_map(body, mesh=mesh, in_specs=in_specs, out_specs=out_specs, check_vma=False)
```

profile of v0, /device:TPU:8, one launch (start us, length us, event | category | flops | bytes accessed | tf_op | source)
XLA Modules:
  0.0 529.6 jit_solution(12379621464132215888)
XLA Ops:
  7.2 0.0 all-gather.2.cloned.1.call-start
  7.2 0.7 all-gather.2.cloned.1.call-update
  7.9 0.0 reduce-scatter.2.cloned.1.call-start
  7.9 0.9 slice_bitcast_fusion.1
  8.8 3.5 fusion.1
  12.3 3.5 fusion.9
  15.9 0.2 copy.12
  16.1 167.6 %all-gather.2.cloned.1.call-done = bf16[16384,512]{1,0:T(8,128)(2,1)} async-done(((bf16[2048,512]{1,0:T(8,128)(2,1)}), bf16[16384,512]{1,0:T(8,128)(2,1)}) %all-gather.2.cloned.1.call-update) | async-done | bytes 16777232 | tf_op jit(solution)/shard_map/all_gather | solution.py:23
  183.6 11.5 %fusion.14 = f32[256,16384]{1,0:T(8,128)} fusion(bf16[16384,512]{1,0:T(8,128)(2,1)} %all-gather.2.cloned.1.call-done, bf16[256,512]{1,0:T(8,128)(2,1)} %param.8, f32[256,512]{1,0:T(8,128)S(1)} %copy.12, f32[256]{0:T(256)} %param.7), kind=kOutput, calls=%fused_computation.18 | convolution fusion | flops 4295491584 | bytes 34341888 | tf_op jit(solution)/shard_map/dot_general | solution.py:21
  195.1 0.0 copy-start
  195.1 0.0 reduce-scatter.2.cloned.1.call-update
  195.2 0.7 copy-done
  195.8 167.6 %reduce-scatter.2.cloned.1.call-done = f32[256,512]{1,0:T(8,128)} async-done(((f32[256,16384]{1,0:T(8,128)}), f32[256,512]{1,0:T(8,128)}) %reduce-scatter.2.cloned.1.call-update) | async-done | bytes 524304 | tf_op jit(solution)/shard_map/reduce_scatter | solution.py:27
  363.4 1.9 multiply_reduce_fusion
  365.3 0.2 copy.14
  365.5 5.1 fusion.10
  370.6 5.1 fusion.11
  375.7 74.2 %psum.15 = f32[2,256,8]{1,2,0:T(8,128)S(1)} all-reduce(f32[2,256,8]{1,2,0:T(8,128)S(1)} %pad_maximum_fusion), channel_id=1, replica_groups=mesh['row'=8,'col'=32] {'row','col'}, use_global_device_ids=true, to_apply=%region_3.0 | all-reduce | flops 4096 | bytes 32768 | tf_op jit(solution)/shard_map/psum | solution.py:43
  449.9 0.6 broadcast_multiply_fusion.2
  450.5 71.7 %psum.14 = f32[256]{0:T(256)S(1)} all-reduce(f32[256]{0:T(256)S(1)} %get-tuple-element.3), channel_id=1, replica_groups=mesh['row'=8,'col'=32] {'col'}, use_global_device_ids=true, to_apply=%region_2.0 | all-reduce | flops 256 | bytes 2048 | tf_op jit(solution)/shard_map/psum | solution.py:42
  522.2 0.6 broadcast_multiply_fusion.4
  (2 shorter events, 0.0 us)
Async XLA Ops:
  7.2 176.5 %all-gather.2.cloned.1.call-start = ((), (), s32[]{:S(2)}) async-start(), calls=%async_computation.1 | async-start | bytes 18874368 | tf_op jit(solution)/shard_map/all_gather | solution.py:23
  7.9 355.5 %reduce-scatter.2.cloned.1.call-start = ((), (), s32[]{:S(2)}) async-start(), calls=%async_computation.2 | async-start | bytes 17301504 | tf_op jit(solution)/shard_map/reduce_scatter | solution.py:27
  195.1 0.7 copy-start
Sparse Core Ops, SparseCore 0:
  9.8 173.7 all-gather.1
  195.3 168.0 reduce-scatter.1
where the time goes:
time: 531 us; the launch traced here: 530 us
  waiting for transfers between devices  336 us (63%)
  blocking collectives  146 us (27%)
  matrix products  28.7 us (5%)
  between operations  14.1 us (3%)
    reduce_scatter x1, waiting for transfers between devices, body(): lax.psum_scatter(partial_terms, 'col', scatter_dimension=1, tiled=True)  168 us
    all_gather x1, waiting for transfers between devices, body(): lax.all_gather(hessian, 'row', axis=0, tiled=True)  168 us
    psum x1, blocking collectives, body(): book_total = lax.psum(local_books, ('row', 'col'))  74.2 us
    psum x1, blocking collectives, body(): scale_total = lax.psum(local_scale, 'col')  71.7 us
    dot_general x1, matrix products, body(): lax.dot_general(error, lax.all_gather(hessian, 'row', axis=0, tiled=True)...  11.5 us
  transfers between devices with their start and end apart: 2, of which 2 were waited for; matrix products, arithmetic and copies ran while one was open for 2% of the time, Pallas kernels for 0%

commit v1 on v0

v1 whole, which is shorter than its diff:
```python
import functools

import jax
import jax.numpy as jnp
import numpy as np
from jax import lax
from jax.experimental import pallas as pl
from jax.experimental.pallas import tpu as pltpu
from jax.sharding import Mesh
from jax.sharding import PartitionSpec as P

AXES = ("z_lo", "y", "x", "z_hi", "core")
SIZES = (2, 4, 4, 4, 2)
ROW = ("z_lo", "y")
COL = ("x", "z_hi", "core")
PLACES = np.arange(256).reshape(SIZES)


def route(target):
    pairs = []
    for place in np.ndindex(*SIZES):
        to = tuple(t % n for t, n in zip(target(*place), SIZES))
        pairs.append((int(PLACES[place]), int(PLACES[to])))
    assert len({d for _, d in pairs}) == PLACES.size
    return pairs


def send(a, target):
    return lax.ppermute(a, AXES, route(target))


def to_plane(z_lo, y, x, z_hi, core):
    return (
        z_lo,
        (x % 2) * 2 + z_hi // 2,
        x + y % 2,
        z_hi if y < 2 else 3 - z_hi,
        core,
    )


def ring_x(a):
    return send(a, lambda zl, y, x, zh, c: (zl, y, x + (1 - 2 * c), zh, c))


def ring_z(a):
    return send(a, lambda zl, y, x, zh, c: (zl, y, x, zh + (1 - 2 * c), c))


def swap_core(a):
    return send(a, lambda zl, y, x, zh, c: (zl, y, x, zh, 1 - c))


def matmul_kernel(slots, *refs):
    blocks, (own, across), out, held, h_own, h_across, sem = (
        refs[:4],
        refs[4:6],
        refs[6],
        refs[7],
        refs[8],
        refs[9],
        refs[10],
    )
    copies = [
        pltpu.make_async_copy(own, h_own, sem.at[0]),
        pltpu.make_async_copy(across, h_across, sem.at[1]),
    ]
    n = 0
    for group in blocks:
        for place in range(group.shape[0]):
            for half in range(2):
                slot = slots[n]
                copies.append(
                    pltpu.make_async_copy(
                        group.at[place, half], held.at[slot], sem.at[2 + n]
                    )
                )
                n += 1
    for copy in copies:
        copy.start()
    for copy in copies:
        copy.wait()
    for row in range(4):
        lhs = [held[part * 4 + row] for part in range(8)]
        for side, h in enumerate((h_own, h_across)):
            total = jnp.zeros((128, 512), jnp.float32)
            for part in range(8):
                total += jnp.dot(
                    lhs[part],
                    h[part // 4, pl.ds((part % 4) * 512, 512), :],
                    preferred_element_type=jnp.float32,
                )
            out[row, :, side * 512 : (side + 1) * 512] = total.astype(out.dtype)


def body(codes, codebooks, row_scale, initial, hessian):
    rows, width = initial.shape
    groups = width // 8
    words = codebooks.shape[1]
    z_lo, y, x, z_hi, core = (lax.axis_index(a) for a in AXES)

    hess_far = send(hessian, lambda zl, y, x, zh, c: (1 - zl, y, x, zh, c))
    hess_own = jnp.stack([hessian, hess_far])
    hess_across = swap_core(hess_own)

    labels = lax.broadcasted_iota(jnp.int32, (1, 1, words), 2)
    picks = [(codes[m][:, :, None] == labels).astype(jnp.bfloat16) for m in range(2)]
    unscaled = jnp.einsum("rgk,kt->rgt", picks[0], codebooks[0], preferred_element_type=jnp.float32)
    unscaled = unscaled + jnp.einsum(
        "rgk,kt->rgt", picks[1], codebooks[1], preferred_element_type=jnp.float32
    )
    unscaled = unscaled.reshape(rows, width)
    error = (row_scale[:, None] * unscaled - initial.astype(jnp.float32)).astype(jnp.bfloat16)

    half = rows // 2
    mine = lax.dynamic_slice_in_dim(error, core * half, half, 0)
    other = lax.dynamic_slice_in_dim(error, (1 - core) * half, half, 0)
    same = send(mine, to_plane)
    cross = send(other, lambda zl, y, x, zh, c: to_plane(zl, y, x, zh, c)[:4] + (1 - c,))
    block = jnp.stack([same, cross])

    z1 = ring_z(block)
    z2 = ring_z(z1)
    z3 = ring_z(z2)
    first = jnp.stack([block, z1])
    second = jnp.stack([z2, z3])
    f1 = ring_x(first)
    f2 = ring_x(f1)
    f3 = ring_x(f2)
    s1 = ring_x(second)
    s2 = ring_x(s1)
    s3 = ring_x(s2)
    gathered = [
        jnp.concatenate([first, f1]),
        jnp.concatenate([f2, f3]),
        jnp.concatenate([second, s1]),
        jnp.concatenate([s2, s3]),
    ]
    step = 1 - 2 * core
    slots = []
    for which in range(2):
        for dx in range(4):
            for dz in (2 * which, 2 * which + 1):
                from_x = (x - step * dx) % 4
                from_z = (z_hi - step * dz) % 4
                d = (from_x - y // 2) % 4
                q = (d // 2) ^ z_lo
                upper = (from_z // 2) ^ (y % 2)
                b = (from_z % 2) ^ upper
                source_y = upper * 2 + d % 2
                for side in range(2):
                    part = q * 4 + b * 2 + (core ^ side)
                    slots.append(part * 4 + source_y)
    slots = jnp.stack(slots).astype(jnp.int32)

    partial = pl.pallas_call(
        matmul_kernel,
        out_shape=jax.ShapeDtypeStruct((4, half, 2 * width), jnp.bfloat16),
        in_specs=[pl.BlockSpec(memory_space=pltpu.SMEM)]
        + [pl.BlockSpec(memory_space=pl.ANY)] * 6,
        out_specs=pl.BlockSpec(memory_space=pltpu.VMEM),
        scratch_shapes=[
            pltpu.VMEM((32, half, width), jnp.bfloat16),
            pltpu.VMEM((2, 2048, 512), jnp.bfloat16),
            pltpu.VMEM((2, 2048, 512), jnp.bfloat16),
            pltpu.SemaphoreType.DMA((34,)),
        ],
        compiler_params=pltpu.CompilerParams(vmem_limit_bytes=40 * 2**20),
        cost_estimate=pl.CostEstimate(
            flops=2 * 512 * 4096 * 1024, bytes_accessed=13 * 2**20, transcendentals=0
        ),
        name="matmul",
    )(slots, *gathered, hess_own, hess_across)

    parts = lax.all_to_all(partial, "y", 0, 0, tiled=True)
    summed = jnp.sum(parts.astype(jnp.float32), axis=0)
    kept, given = summed[:, :width], summed[:, width:]
    got = swap_core(given)
    product = 2.0 * jnp.where(
        core == 0, jnp.concatenate([kept, got]), jnp.concatenate([got, kept])
    )

    local_scale = jnp.sum(product * unscaled, axis=1)
    weighted = (row_scale[:, None] * product).reshape(rows, groups, 8)
    local_books = jnp.stack(
        [
            jnp.einsum(
                "rgk,rgt->kt",
                picks[m].astype(jnp.float32),
                weighted,
                precision=lax.Precision.HIGHEST,
            )
            for m in range(2)
        ]
    )
    total = jnp.concatenate([local_books.reshape(-1, 128), local_scale.reshape(-1, 128)])
    total = total + swap_core(total)
    for axis in (2, 3):

        def shifted(by):
            return lambda *place: place[:axis] + (place[axis] + by,) + place[axis + 1 :]

        total = total + send(total, shifted(1)) + send(total, shifted(2)) + send(total, shifted(3))
    scale_total = total[-(rows // 128) :].reshape(rows)
    books = total[: -(rows // 128)]
    books = books + send(books, lambda zl, y, x, zh, c: (1 - zl, y, x, zh, c))
    books = (
        books
        + send(books, lambda zl, y, x, zh, c: (zl, y + 1, x, zh, c))
        + send(books, lambda zl, y, x, zh, c: (zl, y + 2, x, zh, c))
        + send(books, lambda zl, y, x, zh, c: (zl, y + 3, x, zh, c))
    )
    full_width = width * 32
    all_groups = rows * 8 * (full_width // 8)
    scale_grad = scale_total / full_width
    codebook_grad = books.reshape(local_books.shape) * (words / all_groups)
    return (product, scale_grad, codebook_grad)


def solution(mesh):
    grid = Mesh(mesh.devices.reshape(SIZES), AXES)
    in_specs = (P(None, ROW, COL), P(), P(ROW), P(ROW, COL), P(ROW, COL))
    out_specs = (P(ROW, COL), P(ROW), P())
    return jax.shard_map(body, mesh=grid, in_specs=in_specs, out_specs=out_specs, check_vma=False)
```

time: 531 us -> 217 us (0.41)
  waiting for transfers between devices: 336 us -> 117 us
  blocking collectives: 146 us -> 20.6 us
  starting transfers between devices: 0.08 us -> 39.9 us
  between operations: 14.1 us -> 0.88 us
  matrix products: 28.7 us -> 16.3 us
  Pallas kernels: 0 us -> 11.4 us
  other arithmetic: 3.07 us -> 8.64 us
    reduce_scatter x1 -> x0, waiting for transfers between devices: 168 us -> none  [body(): lax.psum_scatter(partial_terms, 'col', scatter_dimension=1, tiled=True)]
    all_gather x1 -> x0, waiting for transfers between devices: 168 us -> none  [body(): lax.all_gather(hessian, 'row', axis=0, tiled=True)]
    psum x2 -> x0, blocking collectives: 146 us -> none  [the longest x1 74.2 us: body(): book_total = lax.psum(local_books, ('row', 'col'))]
    ppermute x0 -> x25, waiting for transfers between devices: none -> 117 us  [send(): return lax.ppermute(a, AXES, route(target))]
    ppermute x0 -> x25, starting transfers between devices: none -> 39.9 us  [send(): return lax.ppermute(a, AXES, route(target))]
    all_to_all x0 -> x1, blocking collectives: none -> 20.6 us  [body(): parts = lax.all_to_all(partial, 'y', 0, 0, tiled=True)]
    dot_general x1 -> x0, matrix products: 11.5 us -> none  [body(): lax.dot_general(error, lax.all_gather(hessian, 'row', axis=0, tiled=True)...]
    pallas_call x0 -> x1, Pallas kernels: none -> 11.4 us  [body(): pl.pallas_call(matmul_kernel, out_shape=jax.ShapeDtypeStruct((4, half, 2...]
  transfers between devices with their start and end apart: 2 -> 25, of which waited for: 2 -> 22; matrix products, arithmetic and copies ran while one was open for 2% -> 5% of each run, Pallas kernels for 0% -> 0%
where the time goes in v1:
time: 217 us
  waiting for transfers between devices  117 us (54%)
  starting transfers between devices  39.9 us (18%)
  blocking collectives  20.6 us (9%)
  matrix products  16.3 us (8%)
  Pallas kernels  11.4 us (5%)
  other arithmetic  8.64 us (4%)
    ppermute x25, waiting for transfers between devices, send(): return lax.ppermute(a, AXES, route(target))  117 us
    ppermute x25, starting transfers between devices, send(): return lax.ppermute(a, AXES, route(target))  39.9 us
    all_to_all x1, blocking collectives, body(): parts = lax.all_to_all(partial, 'y', 0, 0, tiled=True)  20.6 us
    pallas_call x1, Pallas kernels, body(): pl.pallas_call(matmul_kernel, out_shape=jax.ShapeDtypeStruct((4, half, 2...  11.4 us
    dot_general x2, matrix products, body(): jnp.einsum('rgk,rgt->kt', picks[m].astype(jnp.float32), weighted, precisi...  10.7 us
  transfers between devices with their start and end apart: 25, of which 22 were waited for; matrix products, arithmetic and copies ran while one was open for 5% of the time, Pallas kernels for 0%

profile of v1, /device:TPU:8, one launch (start us, length us, event | category | flops | bytes accessed | tf_op | source)
XLA Modules:
  0.0 216.8 jit_solution(15021362613387877993)
XLA Ops:
  0.6 2.0 collective-permute-start.11
  2.6 45.8 %collective-permute-done.11 = bf16[2048,512]{1,0:T(8,128)(2,1)S(1)} collective-permute-done((bf16[2048,512]{1,0:T(8,128)(2,1)}, bf16[2048,512]{1,0:T(8,128)(2,1)S(1)}, u32[]{:S(2)}, u32[]{:S(2)}) %collective-permute-start.11) | collective-permute-done | bytes 2097184 | tf_op jit(solution)/shard_map/ppermute | solution.py:29
  48.5 4.0 %pad_maximum_fusion.refs_4_ = bf16[2,2048,512]{2,1,0:T(8,128)(2,1)} fusion(bf16[1,2048,512]{2,1,0:T(8,128)(2,1)S(1)} %bitcast.67, bf16[1,2048,512]{2,1,0:T(8,128)(2,1)} %bitcast.66), kind=kLoop, calls=%fused_computation.10 | loop fusion | flops 2097152 | bytes 8388608 | tf_op jit(solution)/shard_map/stack | solution.py:103
  52.5 2.8 %fusion.1 = f32[256,64,8]{0,2,1:T(8,128)S(1)} fusion(s32[256,64]{0,1:T(8,128)S(1)} %get-tuple-element.13, bf16[2,256,8]{1,2,0:T(8,128)(2,1)S(1)} %copy-done.3), kind=kOutput, calls=%fused_computation.2 | convolution fusion | flops 71303168 | bytes 593920 | tf_op jit(solution)/shard_map/rgk,kt->rgt/dot_general | solution.py:109
  55.3 2.8 %fusion.8 = f32[256,64,8]{0,2,1:T(8,128)S(1)} fusion(f32[256,64,8]{0,2,1:T(8,128)S(1)} %fusion.1, s32[256,64]{0,1:T(8,128)S(1)} %get-tuple-element.12, bf16[2,256,8]{1,2,0:T(8,128)(2,1)S(1)} %copy-done.3), kind=kOutput, calls=%fused_computation.12 | convolution fusion | flops 71434240 | bytes 1118208 | tf_op jit(solution)/shard_map/rgk,kt->rgt/dot_general | solution.py:108
  58.5 3.3 %collective-permute-start = (bf16[128,512]{1,0:T(8,128)(2,1)S(1)}, bf16[128,512]{1,0:T(8,128)(2,1)S(1)}, u32[]{:S(2)}, u32[]{:S(2)}) collective-permute-start(bf16[128,512]{1,0:T(8,128)(2,1)S(1)} %get-tuple-element.10), channel_id=1, source_target_pairs={{0,0},{1,1},{2,2},{3,3},{4,36},{5,37},{6,38},{7,39},{8,72},{9,73},... | collective-permute-start | bytes 393224 | tf_op jit(solution)/shard_map/ppermute | solution.py:29
  61.8 3.1 %collective-permute-start.1 = (bf16[128,512]{1,0:T(8,128)(2,1)S(1)}, bf16[128,512]{1,0:T(8,128)(2,1)S(1)}, u32[]{:S(2)}, u32[]{:S(2)}) collective-permute-start(bf16[128,512]{1,0:T(8,128)(2,1)S(1)} %get-tuple-element.11), channel_id=1, source_target_pairs={{0,1},{1,0},{2,3},{3,2},{4,37},{5,36},{6,39},{7,38},{8,73},{9,72},... | collective-permute-start | bytes 393224 | tf_op jit(solution)/shard_map/ppermute | solution.py:29
  64.9 7.1 %collective-permute-done = bf16[128,512]{1,0:T(8,128)(2,1)S(1)} collective-permute-done((bf16[128,512]{1,0:T(8,128)(2,1)S(1)}, bf16[128,512]{1,0:T(8,128)(2,1)S(1)}, u32[]{:S(2)}, u32[]{:S(2)}) %collective-permute-start) | collective-permute-done | bytes 131104 | tf_op jit(solution)/shard_map/ppermute | solution.py:29
  72.0 2.4 %collective-permute-done.1 = bf16[128,512]{1,0:T(8,128)(2,1)S(1)} collective-permute-done((bf16[128,512]{1,0:T(8,128)(2,1)S(1)}, bf16[128,512]{1,0:T(8,128)(2,1)S(1)}, u32[]{:S(2)}, u32[]{:S(2)}) %collective-permute-start.1) | collective-permute-done | bytes 131104 | tf_op jit(solution)/shard_map/ppermute | solution.py:29
  74.5 7.0 %collective-permute-start.2 = (bf16[2,128,512]{2,1,0:T(8,128)(2,1)S(1)}, bf16[2,128,512]{2,1,0:T(8,128)(2,1)S(1)}, u32[]{:S(2)}, u32[]{:S(2)}) collective-permute-start(bf16[2,128,512]{2,1,0:T(8,128)(2,1)S(1)} %get-tuple-element.9), channel_id=1, source_target_pairs={{0,2},{1,7},{2,4},{3,1},{4,6},{5,3},{6,0},{7,5},{8,10},{9,15},{10,... | collective-permute-start | bytes 786440 | tf_op jit(solution)/shard_map/ppermute | solution.py:29
  81.5 6.7 %collective-permute-done.2 = bf16[2,128,512]{2,1,0:T(8,128)(2,1)S(1)} collective-permute-done((bf16[2,128,512]{2,1,0:T(8,128)(2,1)S(1)}, bf16[2,128,512]{2,1,0:T(8,128)(2,1)S(1)}, u32[]{:S(2)}, u32[]{:S(2)}) %collective-permute-start.2) | collective-permute-done | bytes 262176 | tf_op jit(solution)/shard_map/ppermute | solution.py:29
  88.3 3.4 %collective-permute-start.6 = (bf16[2,128,512]{2,1,0:T(8,128)(2,1)S(1)}, bf16[2,128,512]{2,1,0:T(8,128)(2,1)S(1)}, u32[]{:S(2)}, u32[]{:S(2)}) collective-permute-start(bf16[2,128,512]{2,1,0:T(8,128)(2,1)S(1)} %collective-permute-done.2), channel_id=1, source_target_pairs={{0,2},{1,7},{2,4},{3,1},{4,6},{5,3},{6,0},{7,5},{8,10},{9,15},{10,... | collective-permute-start | bytes 786440 | tf_op jit(solution)/shard_map/ppermute | solution.py:29
  91.7 5.7 %collective-permute-done.6 = bf16[2,128,512]{2,1,0:T(8,128)(2,1)S(1)} collective-permute-done((bf16[2,128,512]{2,1,0:T(8,128)(2,1)S(1)}, bf16[2,128,512]{2,1,0:T(8,128)(2,1)S(1)}, u32[]{:S(2)}, u32[]{:S(2)}) %collective-permute-start.6) | collective-permute-done | bytes 262176 | tf_op jit(solution)/shard_map/ppermute | solution.py:29
  97.4 2.2 %collective-permute-start.7 = (bf16[2,128,512]{2,1,0:T(8,128)(2,1)S(1)}, bf16[2,128,512]{2,1,0:T(8,128)(2,1)S(1)}, u32[]{:S(2)}, u32[]{:S(2)}) collective-permute-start(bf16[2,128,512]{2,1,0:T(8,128)(2,1)S(1)} %collective-permute-done.6), channel_id=1, source_target_pairs={{0,2},{1,7},{2,4},{3,1},{4,6},{5,3},{6,0},{7,5},{8,10},{9,15},{10,... | collective-permute-start | bytes 786440 | tf_op jit(solution)/shard_map/ppermute | solution.py:29
  99.6 2.8 %collective-permute-start.3 = (bf16[2,2,128,512]{3,2,1,0:T(8,128)(2,1)S(1)}, bf16[2,2,128,512]{3,2,1,0:T(8,128)(2,1)S(1)}, u32[]{:S(2)}, u32[]{:S(2)}) collective-permute-start(bf16[2,2,128,512]{3,2,1,0:T(8,128)(2,1)S(1)} %pad_maximum_fusion.5), channel_id=1, source_target_pairs={{0,8},{1,25},{2,10},{3,27},{4,12},{5,29},{6,14},{7,31},{8,16},{9,1... | collective-permute-start | bytes 1572872 | tf_op jit(solution)/shard_map/ppermute | solution.py:29
  102.4 5.3 %collective-permute-done.7 = bf16[2,128,512]{2,1,0:T(8,128)(2,1)S(1)} collective-permute-done((bf16[2,128,512]{2,1,0:T(8,128)(2,1)S(1)}, bf16[2,128,512]{2,1,0:T(8,128)(2,1)S(1)}, u32[]{:S(2)}, u32[]{:S(2)}) %collective-permute-start.7) | collective-permute-done | bytes 262176 | tf_op jit(solution)/shard_map/ppermute | solution.py:29
  108.9 2.0 collective-permute-done.3
  111.6 6.7 %collective-permute-done.8 = bf16[2,2,128,512]{3,2,1,0:T(8,128)(2,1)S(1)} collective-permute-done((bf16[2,2,128,512]{3,2,1,0:T(8,128)(2,1)S(1)}, bf16[2,2,128,512]{3,2,1,0:T(8,128)(2,1)S(1)}, u32[]{:S(2)}, u32[]{:S(2)}) %collective-permute-start.8) | collective-permute-done | bytes 524320 | tf_op jit(solution)/shard_map/ppermute | solution.py:29
  118.3 5.6 %collective-permute-done.4 = bf16[2,2,128,512]{3,2,1,0:T(8,128)(2,1)S(1)} collective-permute-done((bf16[2,2,128,512]{3,2,1,0:T(8,128)(2,1)S(1)}, bf16[2,2,128,512]{3,2,1,0:T(8,128)(2,1)S(1)}, u32[]{:S(2)}, u32[]{:S(2)}) %collective-permute-start.4) | collective-permute-done | bytes 524320 | tf_op jit(solution)/shard_map/ppermute | solution.py:29
  123.9 5.7 %collective-permute-done.9 = bf16[2,2,128,512]{3,2,1,0:T(8,128)(2,1)} collective-permute-done((bf16[2,2,128,512]{3,2,1,0:T(8,128)(2,1)S(1)}, bf16[2,2,128,512]{3,2,1,0:T(8,128)(2,1)}, u32[]{:S(2)}, u32[]{:S(2)}) %collective-permute-start.9) | collective-permute-done | bytes 524320 | tf_op jit(solution)/shard_map/ppermute | solution.py:29
  130.0 5.3 %collective-permute-done.5 = bf16[2,2,128,512]{3,2,1,0:T(8,128)(2,1)} collective-permute-done((bf16[2,2,128,512]{3,2,1,0:T(8,128)(2,1)S(1)}, bf16[2,2,128,512]{3,2,1,0:T(8,128)(2,1)}, u32[]{:S(2)}, u32[]{:S(2)}) %collective-permute-start.5) | collective-permute-done | bytes 524320 | tf_op jit(solution)/shard_map/ppermute | solution.py:29
  136.4 4.5 %collective-permute-done.10 = bf16[2,2,128,512]{3,2,1,0:T(8,128)(2,1)} collective-permute-done((bf16[2,2,128,512]{3,2,1,0:T(8,128)(2,1)}, bf16[2,2,128,512]{3,2,1,0:T(8,128)(2,1)}, u32[]{:S(2)}, u32[]{:S(2)}) %collective-permute-start.10) | collective-permute-done | bytes 524320 | tf_op jit(solution)/shard_map/ppermute | solution.py:29
  142.2 11.4 %matmul.1 = bf16[4,128,1024]{2,1,0:T(8,128)(2,1)S(1)} custom-call(s32[32]{0:T(128)S(1)} %stack.176.slots, bf16[4,2,128,512]{3,2,1,0:T(8,128)(2,1)S(1)} %pad_maximum_fusion.1.refs_0_, bf16[4,2,128,512]{3,2,1,0:T(8,128)(2,1)S(1)} %pad_maximum_fusion.2.refs_1_, bf16[4,2,128,512]{3,2,1,0:T(8,128)(2,1)S(1)} %pad_maximum_fusion.3.refs_2_, ...), custom_call_target="tpu_custom_call" | custom-call | flops 4294967296 | bytes 13631488 | tf_op jit(solution)/shard_map/matmul/pallas_call | solution.py:156
  153.6 20.6 %all_to_all.5 = bf16[4,128,1024]{2,1,0:T(8,128)(2,1)S(1)} all-to-all(bf16[4,128,1024]{2,1,0:T(8,128)(2,1)S(1)} %matmul.1), channel_id=1, replica_groups=mesh['z_lo'=2,'y'=4,'x'=4,'z_hi'=4,'core'=2] {'y'}, dimensions={0} | all-to-all | bytes 2097152 | tf_op jit(solution)/shard_map/all_to_all | solution.py:175
  176.2 5.3 %fusion.9 = f32[1,256,8]{1,2,0:T(8,128)S(1)} fusion(s32[256,64]{0,1:T(8,128)S(1)} %get-tuple-element.12, f32[256]{0:T(256)S(1)} %broadcast_multiply_fusion, f32[128,64,8]{0,2,1:T(8,128)S(1)} %bitcast.71, f32[128,64,8]{0,2,1:T(8,128)S(1)} %bitcast.68, pred[]{:T(512)S(6)} %eq.130), kind=kOutput, calls=%fused_computation.13 | convolution fusion | flops 407371776 | bytes 599041 | tf_op jit(solution)/shard_map/rgk,rgt->kt/dot_general | solution.py:187
  181.6 5.3 %fusion.10 = f32[1,256,8]{1,2,0:T(8,128)S(1)} fusion(s32[256,64]{0,1:T(8,128)S(1)} %get-tuple-element.13, f32[256]{0:T(256)S(1)} %broadcast_multiply_fusion, f32[128,64,8]{0,2,1:T(8,128)S(1)} %bitcast.72, f32[128,64,8]{0,2,1:T(8,128)S(1)} %bitcast.69, pred[]{:T(512)S(6)} %eq.130), kind=kOutput, calls=%fused_computation.14 | convolution fusion | flops 407371776 | bytes 599041 | tf_op jit(solution)/shard_map/rgk,rgt->kt/dot_general | solution.py:187
  189.6 2.2 %collective-permute-start.17 = (f32[34,128]{1,0:T(8,128)S(1)}, f32[34,128]{1,0:T(8,128)S(1)}, u32[]{:S(2)}, u32[]{:S(2)}) collective-permute-start(f32[34,128]{1,0:T(8,128)S(1)} %fusion.23), channel_id=1, source_target_pairs={{0,24},{1,25},{2,26},{3,27},{4,28},{5,29},{6,30},{7,31},{8,0},{9,1... | collective-permute-start | bytes 52232 | tf_op jit(solution)/shard_map/ppermute | solution.py:29
  194.8 5.4 %collective-permute-start.19 = (f32[34,128]{1,0:T(8,128)S(1)}, f32[34,128]{1,0:T(8,128)S(1)}, u32[]{:S(2)}, u32[]{:S(2)}) collective-permute-start(f32[34,128]{1,0:T(8,128)S(1)} %add_add_fusion.1), channel_id=1, source_target_pairs={{0,4},{1,5},{2,6},{3,7},{4,0},{5,1},{6,2},{7,3},{8,12},{9,13},{10,... | collective-permute-start | bytes 52232 | tf_op jit(solution)/shard_map/ppermute | solution.py:29
  202.6 2.3 %collective-permute-done.20 = f32[34,128]{1,0:T(8,128)S(1)} collective-permute-done((f32[34,128]{1,0:T(8,128)S(1)}, f32[34,128]{1,0:T(8,128)S(1)}, u32[]{:S(2)}, u32[]{:S(2)}) %collective-permute-start.20) | collective-permute-done | bytes 17440 | tf_op jit(solution)/shard_map/ppermute | solution.py:29
  206.1 2.6 %collective-permute-done.21 = f32[32,128]{1,0:T(8,128)S(1)} collective-permute-done((f32[32,128]{1,0:T(8,128)S(1)}, f32[32,128]{1,0:T(8,128)S(1)}, u32[]{:S(2)}, u32[]{:S(2)}) %collective-permute-start.21) | collective-permute-done | bytes 16416 | tf_op jit(solution)/shard_map/ppermute | solution.py:29
  208.9 3.3 %collective-permute-start.23 = (f32[32,128]{1,0:T(8,128)S(1)}, f32[32,128]{1,0:T(8,128)S(1)}, u32[]{:S(2)}, u32[]{:S(2)}) collective-permute-start(f32[32,128]{1,0:T(8,128)S(1)} %slice_add_fusion), channel_id=1, source_target_pairs={{0,64},{1,65},{2,66},{3,67},{4,68},{5,69},{6,70},{7,71},{8,72},{9,... | collective-permute-start | bytes 49160 | tf_op jit(solution)/shard_map/ppermute | solution.py:29
  214.1 1.8 collective-permute-done.24
  (65 shorter events, 19.4 us)
Async XLA Ops:
  0.6 47.8 %collective-permute-start.11 = (bf16[2048,512]{1,0:T(8,128)(2,1)}, bf16[2048,512]{1,0:T(8,128)(2,1)S(1)}, u32[]{:S(2)}, u32[]{:S(2)}) collective-permute-start(bf16[2048,512]{1,0:T(8,128)(2,1)} %param.9), channel_id=1, source_target_pairs={{0,128},{1,129},{2,130},{3,131},{4,132},{5,133},{6,134},{7,135},{8... | collective-permute-start | bytes 6291464 | tf_op jit(solution)/shard_map/ppermute | solution.py:29
  48.5 4.0 %copy-start.1 = (s32[2,256,64]{1,2,0:T(8,128)S(1)}, s32[2,256,64]{1,2,0:T(8,128)}, u32[]{:S(2)}) copy-start(s32[2,256,64]{1,2,0:T(8,128)} %param.5) | copy-start | bytes 393220
  48.5 4.0 %copy-start.3 = (bf16[2,256,8]{1,2,0:T(8,128)(2,1)S(1)}, bf16[2,256,8]{1,2,0:T(8,128)(2,1)}, u32[]{:S(2)}) copy-start(bf16[2,256,8]{1,2,0:T(8,128)(2,1)} %param.6) | copy-start | bytes 24580
  52.4 89.7 %collective-permute-start.12 = (bf16[2,2048,512]{2,1,0:T(8,128)(2,1)}, bf16[2,2048,512]{2,1,0:T(8,128)(2,1)}, u32[]{:S(2)}, u32[]{:S(2)}) collective-permute-start(bf16[2,2048,512]{2,1,0:T(8,128)(2,1)} %pad_maximum_fusion.refs_4_), channel_id=1, source_target_pairs={{0,1},{1,0},{2,3},{3,2},{4,5},{5,4},{6,7},{7,6},{8,9},{9,8},{10,11... | collective-permute-start | bytes 12582920 | tf_op jit(solution)/shard_map/ppermute | solution.py:29
  55.3 3.1 %copy-start = (bf16[256,512]{1,0:T(8,128)(2,1)S(1)}, bf16[256,512]{1,0:T(8,128)(2,1)}, u32[]{:S(2)}) copy-start(bf16[256,512]{1,0:T(8,128)(2,1)} %param.8) | copy-start | bytes 786436
  55.3 3.1 %copy-start.2 = (f32[256]{0:T(256)S(1)}, f32[256]{0:T(256)}, u32[]{:S(2)}) copy-start(f32[256]{0:T(256)} %param.7) | copy-start | bytes 3076
  58.5 13.5 %collective-permute-start = (bf16[128,512]{1,0:T(8,128)(2,1)S(1)}, bf16[128,512]{1,0:T(8,128)(2,1)S(1)}, u32[]{:S(2)}, u32[]{:S(2)}) collective-permute-start(bf16[128,512]{1,0:T(8,128)(2,1)S(1)} %get-tuple-element.10), channel_id=1, source_target_pairs={{0,0},{1,1},{2,2},{3,3},{4,36},{5,37},{6,38},{7,39},{8,72},{9,73},... | collective-permute-start | bytes 393224 | tf_op jit(solution)/shard_map/ppermute | solution.py:29
  61.8 12.6 %collective-permute-start.1 = (bf16[128,512]{1,0:T(8,128)(2,1)S(1)}, bf16[128,512]{1,0:T(8,128)(2,1)S(1)}, u32[]{:S(2)}, u32[]{:S(2)}) collective-permute-start(bf16[128,512]{1,0:T(8,128)(2,1)S(1)} %get-tuple-element.11), channel_id=1, source_target_pairs={{0,1},{1,0},{2,3},{3,2},{4,37},{5,36},{6,39},{7,38},{8,73},{9,72},... | collective-permute-start | bytes 393224 | tf_op jit(solution)/shard_map/ppermute | solution.py:29
  74.5 13.8 %collective-permute-start.2 = (bf16[2,128,512]{2,1,0:T(8,128)(2,1)S(1)}, bf16[2,128,512]{2,1,0:T(8,128)(2,1)S(1)}, u32[]{:S(2)}, u32[]{:S(2)}) collective-permute-start(bf16[2,128,512]{2,1,0:T(8,128)(2,1)S(1)} %get-tuple-element.9), channel_id=1, source_target_pairs={{0,2},{1,7},{2,4},{3,1},{4,6},{5,3},{6,0},{7,5},{8,10},{9,15},{10,... | collective-permute-start | bytes 786440 | tf_op jit(solution)/shard_map/ppermute | solution.py:29
  88.3 9.1 %collective-permute-start.6 = (bf16[2,128,512]{2,1,0:T(8,128)(2,1)S(1)}, bf16[2,128,512]{2,1,0:T(8,128)(2,1)S(1)}, u32[]{:S(2)}, u32[]{:S(2)}) collective-permute-start(bf16[2,128,512]{2,1,0:T(8,128)(2,1)S(1)} %collective-permute-done.2), channel_id=1, source_target_pairs={{0,2},{1,7},{2,4},{3,1},{4,6},{5,3},{6,0},{7,5},{8,10},{9,15},{10,... | collective-permute-start | bytes 786440 | tf_op jit(solution)/shard_map/ppermute | solution.py:29
  97.4 10.4 %collective-permute-start.7 = (bf16[2,128,512]{2,1,0:T(8,128)(2,1)S(1)}, bf16[2,128,512]{2,1,0:T(8,128)(2,1)S(1)}, u32[]{:S(2)}, u32[]{:S(2)}) collective-permute-start(bf16[2,128,512]{2,1,0:T(8,128)(2,1)S(1)} %collective-permute-done.6), channel_id=1, source_target_pairs={{0,2},{1,7},{2,4},{3,1},{4,6},{5,3},{6,0},{7,5},{8,10},{9,15},{10,... | collective-permute-start | bytes 786440 | tf_op jit(solution)/shard_map/ppermute | solution.py:29
  99.6 11.3 %collective-permute-start.3 = (bf16[2,2,128,512]{3,2,1,0:T(8,128)(2,1)S(1)}, bf16[2,2,128,512]{3,2,1,0:T(8,128)(2,1)S(1)}, u32[]{:S(2)}, u32[]{:S(2)}) collective-permute-start(bf16[2,2,128,512]{3,2,1,0:T(8,128)(2,1)S(1)} %pad_maximum_fusion.5), channel_id=1, source_target_pairs={{0,8},{1,25},{2,10},{3,27},{4,12},{5,29},{6,14},{7,31},{8,16},{9,1... | collective-permute-start | bytes 1572872 | tf_op jit(solution)/shard_map/ppermute | solution.py:29
  107.8 10.5 %collective-permute-start.8 = (bf16[2,2,128,512]{3,2,1,0:T(8,128)(2,1)S(1)}, bf16[2,2,128,512]{3,2,1,0:T(8,128)(2,1)S(1)}, u32[]{:S(2)}, u32[]{:S(2)}) collective-permute-start(bf16[2,2,128,512]{3,2,1,0:T(8,128)(2,1)S(1)} %pad_maximum_fusion.6), channel_id=1, source_target_pairs={{0,8},{1,25},{2,10},{3,27},{4,12},{5,29},{6,14},{7,31},{8,16},{9,1... | collective-permute-start | bytes 1572872 | tf_op jit(solution)/shard_map/ppermute | solution.py:29
  110.9 13.0 %collective-permute-start.4 = (bf16[2,2,128,512]{3,2,1,0:T(8,128)(2,1)S(1)}, bf16[2,2,128,512]{3,2,1,0:T(8,128)(2,1)S(1)}, u32[]{:S(2)}, u32[]{:S(2)}) collective-permute-start(bf16[2,2,128,512]{3,2,1,0:T(8,128)(2,1)S(1)} %collective-permute-done.3), channel_id=1, source_target_pairs={{0,8},{1,25},{2,10},{3,27},{4,12},{5,29},{6,14},{7,31},{8,16},{9,1... | collective-permute-start | bytes 1572872 | tf_op jit(solution)/shard_map/ppermute | solution.py:29
  118.3 11.3 %collective-permute-start.9 = (bf16[2,2,128,512]{3,2,1,0:T(8,128)(2,1)S(1)}, bf16[2,2,128,512]{3,2,1,0:T(8,128)(2,1)}, u32[]{:S(2)}, u32[]{:S(2)}) collective-permute-start(bf16[2,2,128,512]{3,2,1,0:T(8,128)(2,1)S(1)} %collective-permute-done.8), channel_id=1, source_target_pairs={{0,8},{1,25},{2,10},{3,27},{4,12},{5,29},{6,14},{7,31},{8,16},{9,1... | collective-permute-start | bytes 1572872 | tf_op jit(solution)/shard_map/ppermute | solution.py:29
  123.9 11.3 %collective-permute-start.5 = (bf16[2,2,128,512]{3,2,1,0:T(8,128)(2,1)S(1)}, bf16[2,2,128,512]{3,2,1,0:T(8,128)(2,1)}, u32[]{:S(2)}, u32[]{:S(2)}) collective-permute-start(bf16[2,2,128,512]{3,2,1,0:T(8,128)(2,1)S(1)} %collective-permute-done.4), channel_id=1, source_target_pairs={{0,8},{1,25},{2,10},{3,27},{4,12},{5,29},{6,14},{7,31},{8,16},{9,1... | collective-permute-start | bytes 1572872 | tf_op jit(solution)/shard_map/ppermute | solution.py:29
  129.6 11.2 %collective-permute-start.10 = (bf16[2,2,128,512]{3,2,1,0:T(8,128)(2,1)}, bf16[2,2,128,512]{3,2,1,0:T(8,128)(2,1)}, u32[]{:S(2)}, u32[]{:S(2)}) collective-permute-start(bf16[2,2,128,512]{3,2,1,0:T(8,128)(2,1)} %collective-permute-done.9), channel_id=1, source_target_pairs={{0,8},{1,25},{2,10},{3,27},{4,12},{5,29},{6,14},{7,31},{8,16},{9,1... | collective-permute-start | bytes 1572872 | tf_op jit(solution)/shard_map/ppermute | solution.py:29
  174.5 1.6 collective-permute-start.13
  187.3 1.3 collective-permute-start.14
  188.6 5.0 %collective-permute-start.15 = (f32[34,128]{1,0:T(8,128)S(1)}, f32[34,128]{1,0:T(8,128)S(1)}, u32[]{:S(2)}, u32[]{:S(2)}) collective-permute-start(f32[34,128]{1,0:T(8,128)S(1)} %fusion.23), channel_id=1, source_target_pairs={{0,8},{1,9},{2,10},{3,11},{4,12},{5,13},{6,14},{7,15},{8,16},{9,17... | collective-permute-start | bytes 52232 | tf_op jit(solution)/shard_map/ppermute | solution.py:29
  188.6 5.4 %collective-permute-start.16 = (f32[34,128]{1,0:T(8,128)S(1)}, f32[34,128]{1,0:T(8,128)S(1)}, u32[]{:S(2)}, u32[]{:S(2)}) collective-permute-start(f32[34,128]{1,0:T(8,128)S(1)} %fusion.23), channel_id=1, source_target_pairs={{0,16},{1,17},{2,18},{3,19},{4,20},{5,21},{6,22},{7,23},{8,24},{9,... | collective-permute-start | bytes 52232 | tf_op jit(solution)/shard_map/ppermute | solution.py:29
  189.6 5.1 %collective-permute-start.17 = (f32[34,128]{1,0:T(8,128)S(1)}, f32[34,128]{1,0:T(8,128)S(1)}, u32[]{:S(2)}, u32[]{:S(2)}) collective-permute-start(f32[34,128]{1,0:T(8,128)S(1)} %fusion.23), channel_id=1, source_target_pairs={{0,24},{1,25},{2,26},{3,27},{4,28},{5,29},{6,30},{7,31},{8,0},{9,1... | collective-permute-start | bytes 52232 | tf_op jit(solution)/shard_map/ppermute | solution.py:29
  194.7 6.2 %collective-permute-start.18 = (f32[34,128]{1,0:T(8,128)S(1)}, f32[34,128]{1,0:T(8,128)S(1)}, u32[]{:S(2)}, u32[]{:S(2)}) collective-permute-start(f32[34,128]{1,0:T(8,128)S(1)} %add_add_fusion.1), channel_id=1, source_target_pairs={{0,2},{1,3},{2,4},{3,5},{4,6},{5,7},{6,0},{7,1},{8,10},{9,11},{10,... | collective-permute-start | bytes 52232 | tf_op jit(solution)/shard_map/ppermute | solution.py:29
  194.8 7.8 %collective-permute-start.19 = (f32[34,128]{1,0:T(8,128)S(1)}, f32[34,128]{1,0:T(8,128)S(1)}, u32[]{:S(2)}, u32[]{:S(2)}) collective-permute-start(f32[34,128]{1,0:T(8,128)S(1)} %add_add_fusion.1), channel_id=1, source_target_pairs={{0,4},{1,5},{2,6},{3,7},{4,0},{5,1},{6,2},{7,3},{8,12},{9,13},{10,... | collective-permute-start | bytes 52232 | tf_op jit(solution)/shard_map/ppermute | solution.py:29
  200.1 4.7 %collective-permute-start.20 = (f32[34,128]{1,0:T(8,128)S(1)}, f32[34,128]{1,0:T(8,128)S(1)}, u32[]{:S(2)}, u32[]{:S(2)}) collective-permute-start(f32[34,128]{1,0:T(8,128)S(1)} %add_add_fusion.1), channel_id=1, source_target_pairs={{0,6},{1,7},{2,0},{3,1},{4,2},{5,3},{6,4},{7,5},{8,14},{9,15},{10,... | collective-permute-start | bytes 52232 | tf_op jit(solution)/shard_map/ppermute | solution.py:29
  204.9 3.8 %collective-permute-start.21 = (f32[32,128]{1,0:T(8,128)S(1)}, f32[32,128]{1,0:T(8,128)S(1)}, u32[]{:S(2)}, u32[]{:S(2)}) collective-permute-start(f32[32,128]{1,0:T(8,128)S(1)} %slice.35), channel_id=1, source_target_pairs={{0,128},{1,129},{2,130},{3,131},{4,132},{5,133},{6,134},{7,135},{8... | collective-permute-start | bytes 49160 | tf_op jit(solution)/shard_map/ppermute | solution.py:29
  208.7 4.7 %collective-permute-start.22 = (f32[32,128]{1,0:T(8,128)S(1)}, f32[32,128]{1,0:T(8,128)S(1)}, u32[]{:S(2)}, u32[]{:S(2)}) collective-permute-start(f32[32,128]{1,0:T(8,128)S(1)} %slice_add_fusion), channel_id=1, source_target_pairs={{0,32},{1,33},{2,34},{3,35},{4,36},{5,37},{6,38},{7,39},{8,40},{9,... | collective-permute-start | bytes 49160 | tf_op jit(solution)/shard_map/ppermute | solution.py:29
  208.9 5.2 %collective-permute-start.23 = (f32[32,128]{1,0:T(8,128)S(1)}, f32[32,128]{1,0:T(8,128)S(1)}, u32[]{:S(2)}, u32[]{:S(2)}) collective-permute-start(f32[32,128]{1,0:T(8,128)S(1)} %slice_add_fusion), channel_id=1, source_target_pairs={{0,64},{1,65},{2,66},{3,67},{4,68},{5,69},{6,70},{7,71},{8,72},{9,... | collective-permute-start | bytes 49160 | tf_op jit(solution)/shard_map/ppermute | solution.py:29
  212.2 3.7 %collective-permute-start.24 = (f32[32,128]{1,0:T(8,128)S(1)}, f32[32,128]{1,0:T(8,128)S(1)}, u32[]{:S(2)}, u32[]{:S(2)}) collective-permute-start(f32[32,128]{1,0:T(8,128)S(1)} %slice_add_fusion), channel_id=1, source_target_pairs={{0,96},{1,97},{2,98},{3,99},{4,100},{5,101},{6,102},{7,103},{8,104... | collective-permute-start | bytes 49160 | tf_op jit(solution)/shard_map/ppermute | solution.py:29

commit v2 on v0

v2 whole, which is shorter than its diff:
```python
import jax
import jax.numpy as jnp
import numpy as np
from jax import lax
from jax.experimental import pallas as pl
from jax.experimental.pallas import tpu as pltpu
from jax.sharding import Mesh
from jax.sharding import PartitionSpec as P

AXES = ("z_lo", "y_hi", "y_lo", "x", "z_hi", "core")
SIZES = (2, 2, 2, 4, 4, 2)
ROW = ("z_lo", "y_hi", "y_lo")
COL = ("x", "z_hi", "core")
PLACES = np.arange(256).reshape(SIZES)


def send(a, target):
    pairs = []
    for place in np.ndindex(*SIZES):
        to = tuple(t % n for t, n in zip(target(*place), SIZES))
        pairs.append((int(PLACES[place]), int(PLACES[to])))
    assert len({d for _, d in pairs}) == PLACES.size
    return lax.ppermute(a, AXES, pairs)


def shift(a, axis, by):
    at = AXES.index(axis)
    return send(a, lambda *p: p[:at] + (p[at] + by,) + p[at + 1 :])


def turn(a, axis, by):
    at = AXES.index(axis)
    return send(a, lambda *p: p[:at] + (p[at] + by * (1 - 2 * p[-1]),) + p[at + 1 :])


def to_plane(z_lo, y_hi, y_lo, x, z_hi, core):
    return (x // 2, x % 2, y_lo, x + 2 * z_lo + y_hi, z_hi, core)


def decode_kernel(codes, books, scale, initial, decoded, error):
    picks = [codes[m].T for m in range(2)]
    rows = initial.shape[0]
    for g in range(picks[0].shape[0]):
        for lane in range(0, rows, 128):
            total = None
            for m in range(2):
                word = jnp.broadcast_to(picks[m][g : g + 1, lane : lane + 128], (8, 128))
                low = word & 127
                found = jnp.where(
                    word < 128,
                    jnp.take_along_axis(books[m, :, :128], low, axis=1, mode="promise_in_bounds"),
                    jnp.take_along_axis(books[m, :, 128:], low, axis=1, mode="promise_in_bounds"),
                )
                total = found if total is None else total + found
            decoded[8 * g : 8 * g + 8, lane : lane + 128] = total
    error[...] = (scale[...] * decoded[...].T - initial[...].astype(jnp.float32)).astype(error.dtype)

def decode(codes, codebooks, row_scale, initial):
    rows, width = initial.shape
    return pl.pallas_call(
        decode_kernel,
        out_shape=(jax.ShapeDtypeStruct((width, rows), jnp.float32), jax.ShapeDtypeStruct((rows, width), jnp.bfloat16)),
        in_specs=[pl.BlockSpec(memory_space=pltpu.VMEM)] * 4,
        out_specs=(pl.BlockSpec(memory_space=pltpu.VMEM),) * 2,
        compiler_params=pltpu.CompilerParams(vmem_limit_bytes=16 * 2**20),
        cost_estimate=pl.CostEstimate(flops=2**21, bytes_accessed=2**20, transcendentals=0),
        name="decode",
    )(codes, jnp.swapaxes(codebooks, 1, 2).astype(jnp.float32), row_scale.reshape(rows, 1), initial)

def finish_kernel(core, codes, scale, decoded, kept, got, product, totals):
    half = kept.shape[0]
    first = core[0] == 0
    product[:half] = 2.0 * jnp.where(first, kept[...], got[...])
    product[half:] = 2.0 * jnp.where(first, got[...], kept[...])
    totals[16:17, :] = jnp.sum(product[...].T * decoded[...], axis=0, keepdims=True)
    picks = [codes[m].T.astype(jnp.bfloat16) for m in range(2)]
    rows = product.shape[0]
    words = lax.broadcasted_iota(jnp.int32, (256, rows), 0).astype(jnp.bfloat16)
    group = lax.rem(lax.broadcasted_iota(jnp.int32, (rows, 256), 1), 128) // 8
    sums = jnp.zeros((512, 256), jnp.float32)
    for block in range(product.shape[1] // 128):
        weighted = scale[...] * product[:, block * 128 : (block + 1) * 128]
        high = weighted.astype(jnp.bfloat16)
        low = (weighted - high.astype(jnp.float32)).astype(jnp.bfloat16)
        both = jnp.concatenate([high, low], axis=1)
        for part in range(0, 16, 4):
            lhs = []
            rhs = []
            for g in range(part, part + 4):
                at = block * 16 + g
                lhs.append(jnp.concatenate(
                    [(words == picks[m][at : at + 1, :]).astype(jnp.bfloat16) for m in range(2)], axis=0))
                rhs.append(jnp.where(group == g, both, jnp.zeros_like(both)))
            sums += jnp.dot(jnp.concatenate(lhs, axis=1), jnp.concatenate(rhs, axis=0), preferred_element_type=jnp.float32)
    sums = (sums[:, :128] + sums[:, 128:]).T
    folded = jnp.sum(sums.reshape(16, 8, 512), axis=0)
    totals[0:8, :] = folded[:, :256]
    totals[8:16, :] = folded[:, 256:]

def finish(core, codes, row_scale, decoded, kept, got):
    half, width = kept.shape
    rows = 2 * half
    return pl.pallas_call(
        finish_kernel,
        out_shape=(jax.ShapeDtypeStruct((rows, width), jnp.float32), jax.ShapeDtypeStruct((17, 256), jnp.float32)),
        in_specs=[pl.BlockSpec(memory_space=pltpu.SMEM)] + [pl.BlockSpec(memory_space=pltpu.VMEM)] * 5,
        out_specs=(pl.BlockSpec(memory_space=pltpu.VMEM),) * 2,
        compiler_params=pltpu.CompilerParams(vmem_limit_bytes=24 * 2**20),
        cost_estimate=pl.CostEstimate(flops=2**32, bytes_accessed=2**21, transcendentals=0),
        name="finish",
    )(core.reshape(1), codes, row_scale.reshape(rows, 1), decoded, kept, got)

def matmul_kernel(slots, *refs):
    blocks, tiles = refs[:-9], refs[-9:-5]
    out, held, h_own, h_across, sem = refs[-5:]
    copies = [
        pltpu.make_async_copy(tiles[0], h_own.at[0:2048], sem.at[0]),
        pltpu.make_async_copy(tiles[1], h_own.at[2048:4096], sem.at[1]),
        pltpu.make_async_copy(tiles[2], h_across.at[0:2048], sem.at[2]),
        pltpu.make_async_copy(tiles[3], h_across.at[2048:4096], sem.at[3]),
    ]
    n = 0
    for group in blocks:
        for place in range(group.shape[0]):
            for side in range(2):
                rows = pl.multiple_of(slots[2 * n] * 128, 128)
                columns = pl.multiple_of(slots[2 * n + 1] * 512, 512)
                copies.append(
                    pltpu.make_async_copy(
                        group.at[place, side],
                        held.at[pl.ds(rows, 128), pl.ds(columns, 512)],
                        sem.at[4 + n],
                    )
                )
                n += 1
    for copy in copies:
        copy.start()
    for copy in copies[:2] + copies[4:]:
        copy.wait()
    for side, h in enumerate((h_own, h_across)):
        if side:
            copies[2].wait()
            copies[3].wait()
        total = jnp.dot(held[...], h[...], preferred_element_type=jnp.float32)
        for s in range(4):
            out[s, :, side * 512 : (side + 1) * 512] = total[s * 128 : (s + 1) * 128].astype(
                out.dtype
            )


def body(codes, codebooks, row_scale, initial, hessian):
    rows, width = initial.shape
    words = codebooks.shape[1]
    half = rows // 2
    z_lo, y_hi, y_lo, x, z_hi, core = (lax.axis_index(a) for a in AXES)

    far = send(hessian, lambda zl, yh, yl, x, zh, c: (zl, yh, 1 - yl, x, zh, c))
    across = shift(hessian, "core", 1)

    decoded, error = decode(codes, codebooks, row_scale, initial)

    mine = lax.dynamic_slice_in_dim(error, core * half, half, 0)
    other = lax.dynamic_slice_in_dim(error, (1 - core) * half, half, 0)
    same = send(mine, to_plane)
    cross = send(other, lambda *p: to_plane(*p)[:-1] + (1 - p[-1],))
    block = jnp.stack([same, cross])

    own = block[None]
    z_back, z_on = turn(block, "z_hi", 1), turn(block, "z_hi", -1)
    own_back, own_on = turn(own, "x", 1), turn(own, "x", -1)
    near, z_back, own_back, own_on = lax.optimization_barrier(
        (jnp.stack([z_back, z_on]), z_back, own_back, own_on)
    )
    z_two, own_two = turn(z_back, "z_hi", 1), turn(own_back, "x", 1)
    near_back, near_on = turn(near, "x", 1), turn(near, "x", -1)
    last, own_two, near_back, near_on, far = lax.optimization_barrier(
        (z_two[None], own_two, near_back, near_on, far)
    )
    last_back, last_on = turn(last, "x", 1), turn(last, "x", -1)
    near_two, last_two = turn(near_back, "x", 1), turn(last_back, "x", 1)
    far_across = shift(far, "core", 1)
    wide = (
        (own, own_back, own_on, own_two),
        (near, near_back, near_on, near_two),
        (last, last_back, last_on, last_two),
    )

    step = 1 - 2 * core
    slots = []
    for dzs in ((0,), (1, 3), (2,)):
        for dx in (0, 1, 3, 2):
            for dz in dzs:
                from_x = (x - step * dx) % 4
                from_z = (z_hi - step * dz) % 4
                s = (from_x - 2 * z_lo - y_hi) % 4
                tile = (from_z // 2) ^ y_lo
                for side in range(2):
                    slots += [s, tile * 4 + (from_z % 2) * 2 + (core ^ side)]
    slots = jnp.stack(slots).astype(jnp.int32)

    blocks = [b for group in wide for b in group]
    partial = pl.pallas_call(
        matmul_kernel,
        out_shape=jax.ShapeDtypeStruct((4, half, 2 * width), jnp.bfloat16),
        in_specs=[pl.BlockSpec(memory_space=pltpu.SMEM)]
        + [pl.BlockSpec(memory_space=pl.ANY)] * (len(blocks) + 4),
        out_specs=pl.BlockSpec(memory_space=pltpu.VMEM),
        scratch_shapes=[
            pltpu.VMEM((4 * half, 8 * width), jnp.bfloat16),
            pltpu.VMEM((8 * width, width), jnp.bfloat16),
            pltpu.VMEM((8 * width, width), jnp.bfloat16),
            pltpu.SemaphoreType.DMA((36,)),
        ],
        compiler_params=pltpu.CompilerParams(vmem_limit_bytes=32 * 2**20),
        cost_estimate=pl.CostEstimate(
            flops=2 * 512 * 4096 * 1024, bytes_accessed=13 * 2**20, transcendentals=0
        ),
        name="matmul",
    )(slots, *blocks, hessian, far, across, far_across)

    parts = lax.all_to_all(partial, ("z_lo", "y_hi"), 0, 0, tiled=True)
    summed = jnp.sum(parts.astype(jnp.float32), axis=0)
    kept, given = summed[:, :width], summed[:, width:]
    got = shift(given, "core", 1)
    product, total = finish(core, codes, row_scale, decoded, kept, got)

    total = total + shift(total, "core", 1)
    for axis in ("x", "z_hi"):
        total = total + shift(total, axis, 1) + shift(total, axis, -1) + shift(total, axis, 2)
    scale_total, books = total[16], total[:16]
    books = books + shift(books, "z_lo", 1)
    books = books + shift(books, "y_lo", 1)
    books = books + shift(books, "y_hi", 1)
    full_width = width * 32
    all_groups = rows * 8 * (full_width // 8)
    scale_grad = scale_total / full_width
    codebook_grad = jnp.swapaxes(books.reshape(2, 8, words), 1, 2) * (words / all_groups)
    return (product, scale_grad, codebook_grad)


def solution(mesh):
    grid = Mesh(mesh.devices.reshape(SIZES), AXES)
    in_specs = (P(None, ROW, COL), P(), P(ROW), P(ROW, COL), P(ROW, COL))
    out_specs = (P(ROW, COL), P(ROW), P())
    return jax.shard_map(body, mesh=grid, in_specs=in_specs, out_specs=out_specs, check_vma=False)
```

time: 531 us -> 178 us (0.34)
  waiting for transfers between devices: 336 us -> 55 us
  blocking collectives: 146 us -> 19.1 us
  starting transfers between devices: 0.08 us -> 75.8 us
  matrix products: 28.7 us -> 0 us
  Pallas kernels: 0 us -> 16.2 us
  between operations: 14.1 us -> 0.83 us
  local copies, waits for them, and re-layouts: 1.93 us -> 8.21 us
    reduce_scatter x1 -> x0, waiting for transfers between devices: 168 us -> none  [body(): lax.psum_scatter(partial_terms, 'col', scatter_dimension=1, tiled=True)]
    all_gather x1 -> x0, waiting for transfers between devices: 168 us -> none  [body(): lax.all_gather(hessian, 'row', axis=0, tiled=True)]
    psum x2 -> x0, blocking collectives: 146 us -> none  [the longest x1 74.2 us: body(): book_total = lax.psum(local_books, ('row', 'col'))]
    ppermute x0 -> x28, starting transfers between devices: none -> 75.8 us  [send(): return lax.ppermute(a, AXES, pairs)]
    ppermute x0 -> x28, waiting for transfers between devices: none -> 55 us  [send(): return lax.ppermute(a, AXES, pairs)]
    dot_general x5 -> x0, matrix products: 28.7 us -> none  [the longest x1 11.5 us: body(): lax.dot_general(error, lax.all_gather(hessian, 'row', axis=0, tiled=True)...]
    all_to_all x0 -> x1, blocking collectives: none -> 19.1 us  [body(): parts = lax.all_to_all(partial, ('z_lo', 'y_hi'), 0, 0, tiled=True)]
    pallas_call x0 -> x3, Pallas kernels: none -> 16.2 us  [the longest x1 9.08 us: body(): pl.pallas_call(matmul_kernel, out_shape=jax.ShapeDtypeStruct((4, half, 2...]
  transfers between devices with their start and end apart: 2 -> 28, of which waited for: 2 -> 17; matrix products, arithmetic and copies ran while one was open for 2% -> 2% of each run, Pallas kernels for 0% -> 1%
where the time goes in v2:
time: 178 us; the launch traced here: 177 us
  starting transfers between devices  75.8 us (43%)
  waiting for transfers between devices  55 us (31%)
  blocking collectives  19.1 us (11%)
  Pallas kernels  16.2 us (9%)
  local copies, waits for them, and re-layouts  8.21 us (5%)
  other arithmetic  2.18 us (1%)
    ppermute x28, starting transfers between devices, send(): return lax.ppermute(a, AXES, pairs)  75.8 us
    ppermute x28, waiting for transfers between devices, send(): return lax.ppermute(a, AXES, pairs)  55 us
    all_to_all x1, blocking collectives, body(): parts = lax.all_to_all(partial, ('z_lo', 'y_hi'), 0, 0, tiled=True)  19.1 us
    pallas_call x1, Pallas kernels, body(): pl.pallas_call(matmul_kernel, out_shape=jax.ShapeDtypeStruct((4, half, 2...  9.08 us
    unnamed x21, local copies, waits for them, and re-layouts  7.19 us
    pallas_call x1, Pallas kernels, finish(): pl.pallas_call(finish_kernel, out_shape=(jax.ShapeDtypeStruct((rows, widt...  5.5 us
  transfers between devices with their start and end apart: 28, of which 17 were waited for; matrix products, arithmetic and copies ran while one was open for 2% of the time, Pallas kernels for 1%

profile of v2, /device:TPU:8, one launch (start us, length us, event | category | flops | bytes accessed | tf_op | source)
XLA Modules:
  0.0 177.3 jit_solution(9026617456152943564)
XLA Ops:
  0.6 2.3 %collective-permute-start.10 = (bf16[2048,512]{1,0:T(8,128)(2,1)}, bf16[2048,512]{1,0:T(8,128)(2,1)}, u32[]{:S(2)}, u32[]{:S(2)}) collective-permute-start(bf16[2048,512]{1,0:T(8,128)(2,1)} %refs_12_.1), channel_id=1, source_target_pairs={{0,32},{1,33},{2,34},{3,35},{4,36},{5,37},{6,38},{7,39},{8,40},{9,... | collective-permute-start | bytes 6291464 | tf_op jit(solution)/shard_map/ppermute | solution.py:23
  6.4 1.6 decode.1
  8.9 1.3 collective-permute-done.1
  10.2 1.6 collective-permute-start.2
  11.8 3.1 %collective-permute-start.3 = (bf16[2,128,512]{2,1,0:T(8,128)(2,1)S(1)}, bf16[2,128,512]{2,1,0:T(8,128)(2,1)S(1)}, u32[]{:S(2)}, u32[]{:S(2)}) collective-permute-start(bf16[2,128,512]{2,1,0:T(8,128)(2,1)S(1)} %get-tuple-element.31), channel_id=1, source_target_pairs={{0,6},{1,3},{2,0},{3,5},{4,2},{5,7},{6,4},{7,1},{8,14},{9,11},{10,... | collective-permute-start | bytes 786440 | tf_op jit(solution)/shard_map/ppermute | solution.py:23
  15.0 15.6 %collective-permute-start.5 = (bf16[1,2,128,512]{3,2,1,0:T(8,128)(2,1)S(1)}, bf16[1,2,128,512]{3,2,1,0:T(8,128)(2,1)S(1)}, u32[]{:S(2)}, u32[]{:S(2)}) collective-permute-start(bf16[1,2,128,512]{3,2,1,0:T(8,128)(2,1)S(1)} %get-tuple-element.32.refs_0_), channel_id=1, source_target_pairs={{0,24},{1,9},{2,26},{3,11},{4,28},{5,13},{6,30},{7,15},{8,0},{9,17... | collective-permute-start | bytes 786440 | tf_op jit(solution)/shard_map/ppermute | solution.py:23
  30.5 29.4 %collective-permute-start.4 = (bf16[1,2,128,512]{3,2,1,0:T(8,128)(2,1)S(1)}, bf16[1,2,128,512]{3,2,1,0:T(8,128)(2,1)S(1)}, u32[]{:S(2)}, u32[]{:S(2)}) collective-permute-start(bf16[1,2,128,512]{3,2,1,0:T(8,128)(2,1)S(1)} %get-tuple-element.32.refs_0_), channel_id=1, source_target_pairs={{0,8},{1,25},{2,10},{3,27},{4,12},{5,29},{6,14},{7,31},{8,16},{9,1... | collective-permute-start | bytes 786440 | tf_op jit(solution)/shard_map/ppermute | solution.py:23
  60.0 6.5 %collective-permute-done.5.refs_2_ = bf16[1,2,128,512]{3,2,1,0:T(8,128)(2,1)S(1)} collective-permute-done((bf16[1,2,128,512]{3,2,1,0:T(8,128)(2,1)S(1)}, bf16[1,2,128,512]{3,2,1,0:T(8,128)(2,1)S(1)}, u32[]{:S(2)}, u32[]{:S(2)}) %collective-permute-start.5) | collective-permute-done | bytes 262176 | tf_op jit(solution)/shard_map/ppermute | solution.py:23
  66.9 1.6 collective-permute-start.8
  68.4 1.5 collective-permute-start.6
  70.0 1.9 %collective-permute-start.7 = (bf16[1,2,128,512]{3,2,1,0:T(8,128)(2,1)S(1)}, bf16[1,2,128,512]{3,2,1,0:T(8,128)(2,1)S(1)}, u32[]{:S(2)}, u32[]{:S(2)}) collective-permute-start(bf16[1,2,128,512]{3,2,1,0:T(8,128)(2,1)S(1)} %collective-permute-done.4.refs_1_), channel_id=1, source_target_pairs={{0,8},{1,25},{2,10},{3,27},{4,12},{5,29},{6,14},{7,31},{8,16},{9,1... | collective-permute-start | bytes 786440 | tf_op jit(solution)/shard_map/ppermute | solution.py:23
  72.6 4.4 %collective-permute-done.6 = bf16[2,128,512]{2,1,0:T(8,128)(2,1)} collective-permute-done((bf16[2,128,512]{2,1,0:T(8,128)(2,1)S(1)}, bf16[2,128,512]{2,1,0:T(8,128)(2,1)}, u32[]{:S(2)}, u32[]{:S(2)}) %collective-permute-start.6) | collective-permute-done | bytes 262176 | tf_op jit(solution)/shard_map/ppermute | solution.py:23
  77.0 6.8 %collective-permute-done.7.refs_3_ = bf16[1,2,128,512]{3,2,1,0:T(8,128)(2,1)S(1)} collective-permute-done((bf16[1,2,128,512]{3,2,1,0:T(8,128)(2,1)S(1)}, bf16[1,2,128,512]{3,2,1,0:T(8,128)(2,1)S(1)}, u32[]{:S(2)}, u32[]{:S(2)}) %collective-permute-start.7) | collective-permute-done | bytes 262176 | tf_op jit(solution)/shard_map/ppermute | solution.py:23
  85.5 1.1 collective-permute-start.11
  86.6 2.2 %collective-permute-start.13 = (bf16[1,2,128,512]{3,2,1,0:T(8,128)(2,1)}, bf16[1,2,128,512]{3,2,1,0:T(8,128)(2,1)}, u32[]{:S(2)}, u32[]{:S(2)}) collective-permute-start(bf16[1,2,128,512]{3,2,1,0:T(8,128)(2,1)} %bitcast.20.refs_8_), channel_id=1, source_target_pairs={{0,24},{1,9},{2,26},{3,11},{4,28},{5,13},{6,30},{7,15},{8,0},{9,17... | collective-permute-start | bytes 786440 | tf_op jit(solution)/shard_map/ppermute | solution.py:23
  88.8 6.9 %collective-permute-done.12.refs_9_ = bf16[1,2,128,512]{3,2,1,0:T(8,128)(2,1)} collective-permute-done((bf16[1,2,128,512]{3,2,1,0:T(8,128)(2,1)}, bf16[1,2,128,512]{3,2,1,0:T(8,128)(2,1)}, u32[]{:S(2)}, u32[]{:S(2)}) %collective-permute-start.12) | collective-permute-done | bytes 262176 | tf_op jit(solution)/shard_map/ppermute | solution.py:23
  96.2 8.4 %collective-permute-done.14.refs_11_ = bf16[1,2,128,512]{3,2,1,0:T(8,128)(2,1)} collective-permute-done((bf16[1,2,128,512]{3,2,1,0:T(8,128)(2,1)}, bf16[1,2,128,512]{3,2,1,0:T(8,128)(2,1)}, u32[]{:S(2)}, u32[]{:S(2)}) %collective-permute-start.14) | collective-permute-done | bytes 262176 | tf_op jit(solution)/shard_map/ppermute | solution.py:23
  107.5 9.1 %matmul.1 = bf16[4,128,1024]{2,1,0:T(8,128)(2,1)S(1)} custom-call(s32[64]{0:T(128)S(1)} %stack.50.slots, bf16[1,2,128,512]{3,2,1,0:T(8,128)(2,1)S(1)} %get-tuple-element.32.refs_0_, bf16[1,2,128,512]{3,2,1,0:T(8,128)(2,1)S(1)} %copy-done.7, bf16[1,2,128,512]{3,2,1,0:T(8,128)(2,1)S(1)} %collective-permute-done.5.refs_2_, ...), custom_call_target="tpu_custom_call" | custom-call | flops 4294967296 | bytes 13631488 | tf_op jit(solution)/shard_map/matmul/pallas_call | solution.py:202
  116.6 19.1 %all_to_all.5 = bf16[4,128,1024]{2,1,0:T(8,128)(2,1)S(1)} all-to-all(bf16[4,128,1024]{2,1,0:T(8,128)(2,1)S(1)} %matmul.1), channel_id=1, replica_groups=mesh['z_lo'=2,'y_hi'=2,'y_lo'=2,'x'=4,'z_hi'=4,'core'=2] {'z_lo','y_hi'}, dimensions={0} | all-to-all | bytes 2097152 | tf_op jit(solution)/shard_map/all_to_all | solution.py:221
  136.1 1.5 collective-permute-done.17.got
  137.6 5.5 %finish.1 = (f32[256,512]{1,0:T(8,128)}, f32[17,256]{1,0:T(8,128)S(1)}) custom-call(s32[1]{0:T(128)} %bitcast.core, s32[2,256,64]{2,1,0:T(8,128)S(1)} %copy.12.codes, f32[256,1]{1,0:T(8,128)S(1)} %copy.13.scale, f32[512,256]{1,0:T(8,128)S(1)} %copy-done.3, f32[128,512]{1,0:T(8,128)S(1)} %get-tuple-element.30.kept, f32[128,512]{1,0:T(8,128)S(1)} %collective-permute-done.17.got), custom_call_target="tpu_custom_call" | custom-call | flops 4294967296 | bytes 2097152 | tf_op jit(solution)/shard_map/finish/pallas_call | solution.py:103
  143.3 1.1 collective-permute-done.18
  145.3 2.3 %collective-permute-start.20 = (f32[17,256]{1,0:T(8,128)S(1)}, f32[17,256]{1,0:T(8,128)S(1)}, u32[]{:S(2)}, u32[]{:S(2)}) collective-permute-start(f32[17,256]{1,0:T(8,128)S(1)} %add.271), channel_id=1, source_target_pairs={{0,24},{1,25},{2,26},{3,27},{4,28},{5,29},{6,30},{7,31},{8,0},{9,1... | collective-permute-start | bytes 52232 | tf_op jit(solution)/shard_map/ppermute | solution.py:23
  147.6 2.2 %collective-permute-done.21 = f32[17,256]{1,0:T(8,128)S(1)} collective-permute-done((f32[17,256]{1,0:T(8,128)S(1)}, f32[17,256]{1,0:T(8,128)S(1)}, u32[]{:S(2)}, u32[]{:S(2)}) %collective-permute-start.21) | collective-permute-done | bytes 17440 | tf_op jit(solution)/shard_map/ppermute | solution.py:23
  149.7 2.9 %collective-permute-done.19 = f32[17,256]{1,0:T(8,128)S(1)} collective-permute-done((f32[17,256]{1,0:T(8,128)S(1)}, f32[17,256]{1,0:T(8,128)S(1)}, u32[]{:S(2)}, u32[]{:S(2)}) %collective-permute-start.19) | collective-permute-done | bytes 17440 | tf_op jit(solution)/shard_map/ppermute | solution.py:23
  152.6 4.3 %collective-permute-start.24 = (f32[17,256]{1,0:T(8,128)S(1)}, f32[17,256]{1,0:T(8,128)S(1)}, u32[]{:S(2)}, u32[]{:S(2)}) collective-permute-start(f32[17,256]{1,0:T(8,128)S(1)} %add_add_fusion.1), channel_id=1, source_target_pairs={{0,4},{1,5},{2,6},{3,7},{4,0},{5,1},{6,2},{7,3},{8,12},{9,13},{10,... | collective-permute-start | bytes 52232 | tf_op jit(solution)/shard_map/ppermute | solution.py:23
  157.9 2.0 %collective-permute-start.22 = (f32[17,256]{1,0:T(8,128)S(1)}, f32[17,256]{1,0:T(8,128)S(1)}, u32[]{:S(2)}, u32[]{:S(2)}) collective-permute-start(f32[17,256]{1,0:T(8,128)S(1)} %add_add_fusion.1), channel_id=1, source_target_pairs={{0,2},{1,3},{2,4},{3,5},{4,6},{5,7},{6,0},{7,1},{8,10},{9,11},{10,... | collective-permute-start | bytes 52232 | tf_op jit(solution)/shard_map/ppermute | solution.py:23
  161.7 2.2 %collective-permute-done.22 = f32[17,256]{1,0:T(8,128)S(1)} collective-permute-done((f32[17,256]{1,0:T(8,128)S(1)}, f32[17,256]{1,0:T(8,128)S(1)}, u32[]{:S(2)}, u32[]{:S(2)}) %collective-permute-start.22) | collective-permute-done | bytes 17440 | tf_op jit(solution)/shard_map/ppermute | solution.py:23
  164.8 2.8 %collective-permute-done.25 = f32[16,256]{1,0:T(8,128)S(1)} collective-permute-done((f32[16,256]{1,0:T(8,128)S(1)}, f32[16,256]{1,0:T(8,128)S(1)}, u32[]{:S(2)}, u32[]{:S(2)}) %collective-permute-start.25) | collective-permute-done | bytes 16416 | tf_op jit(solution)/shard_map/ppermute | solution.py:23
  167.7 1.6 collective-permute-start.26
  169.3 2.2 %collective-permute-done.26 = f32[16,256]{1,0:T(8,128)S(1)} collective-permute-done((f32[16,256]{1,0:T(8,128)S(1)}, f32[16,256]{1,0:T(8,128)S(1)}, u32[]{:S(2)}, u32[]{:S(2)}) %collective-permute-start.26) | collective-permute-done | bytes 16416 | tf_op jit(solution)/shard_map/ppermute | solution.py:23
  172.9 3.8 %collective-permute-done.27 = f32[16,256]{1,0:T(8,128)S(1)} collective-permute-done((f32[16,256]{1,0:T(8,128)S(1)}, f32[16,256]{1,0:T(8,128)S(1)}, u32[]{:S(2)}, u32[]{:S(2)}) %collective-permute-start.27) | collective-permute-done | bytes 16416 | tf_op jit(solution)/shard_map/ppermute | solution.py:23
  (65 shorter events, 17.9 us)
Async XLA Ops:
  0.6 84.7 %collective-permute-start.10 = (bf16[2048,512]{1,0:T(8,128)(2,1)}, bf16[2048,512]{1,0:T(8,128)(2,1)}, u32[]{:S(2)}, u32[]{:S(2)}) collective-permute-start(bf16[2048,512]{1,0:T(8,128)(2,1)} %refs_12_.1), channel_id=1, source_target_pairs={{0,32},{1,33},{2,34},{3,35},{4,36},{5,37},{6,38},{7,39},{8,40},{9,... | collective-permute-start | bytes 6291464 | tf_op jit(solution)/shard_map/ppermute | solution.py:23
  6.4 70.6 %copy-start.1 = (bf16[2048,512]{1,0:T(8,128)(2,1)S(1)}, bf16[2048,512]{1,0:T(8,128)(2,1)}, u32[]{:S(2)}) copy-start(bf16[2048,512]{1,0:T(8,128)(2,1)} %refs_12_.1) | copy-start | bytes 6291460
  8.0 51.8 %copy-start.2 = (f32[512,256]{1,0:T(8,128)}, f32[512,256]{1,0:T(8,128)S(1)}, u32[]{:S(2)}) copy-start(f32[512,256]{1,0:T(8,128)S(1)} %get-tuple-element.16.decoded) | copy-start | bytes 1572868
  8.1 0.8 collective-permute-start
  8.8 1.4 collective-permute-start.1
  10.2 49.7 %collective-permute-start.2 = (bf16[2,128,512]{2,1,0:T(8,128)(2,1)S(1)}, bf16[2,128,512]{2,1,0:T(8,128)(2,1)S(1)}, u32[]{:S(2)}, u32[]{:S(2)}) collective-permute-start(bf16[2,128,512]{2,1,0:T(8,128)(2,1)S(1)} %get-tuple-element.31), channel_id=1, source_target_pairs={{0,2},{1,7},{2,4},{3,1},{4,6},{5,3},{6,0},{7,5},{8,10},{9,15},{10,... | collective-permute-start | bytes 786440 | tf_op jit(solution)/shard_map/ppermute | solution.py:23
  11.8 48.0 %collective-permute-start.3 = (bf16[2,128,512]{2,1,0:T(8,128)(2,1)S(1)}, bf16[2,128,512]{2,1,0:T(8,128)(2,1)S(1)}, u32[]{:S(2)}, u32[]{:S(2)}) collective-permute-start(bf16[2,128,512]{2,1,0:T(8,128)(2,1)S(1)} %get-tuple-element.31), channel_id=1, source_target_pairs={{0,6},{1,3},{2,0},{3,5},{4,2},{5,7},{6,4},{7,1},{8,14},{9,11},{10,... | collective-permute-start | bytes 786440 | tf_op jit(solution)/shard_map/ppermute | solution.py:23
  15.0 51.4 %collective-permute-start.5 = (bf16[1,2,128,512]{3,2,1,0:T(8,128)(2,1)S(1)}, bf16[1,2,128,512]{3,2,1,0:T(8,128)(2,1)S(1)}, u32[]{:S(2)}, u32[]{:S(2)}) collective-permute-start(bf16[1,2,128,512]{3,2,1,0:T(8,128)(2,1)S(1)} %get-tuple-element.32.refs_0_), channel_id=1, source_target_pairs={{0,24},{1,9},{2,26},{3,11},{4,28},{5,13},{6,30},{7,15},{8,0},{9,17... | collective-permute-start | bytes 786440 | tf_op jit(solution)/shard_map/ppermute | solution.py:23
  30.5 35.9 %collective-permute-start.4 = (bf16[1,2,128,512]{3,2,1,0:T(8,128)(2,1)S(1)}, bf16[1,2,128,512]{3,2,1,0:T(8,128)(2,1)S(1)}, u32[]{:S(2)}, u32[]{:S(2)}) collective-permute-start(bf16[1,2,128,512]{3,2,1,0:T(8,128)(2,1)S(1)} %get-tuple-element.32.refs_0_), channel_id=1, source_target_pairs={{0,8},{1,25},{2,10},{3,27},{4,12},{5,29},{6,14},{7,31},{8,16},{9,1... | collective-permute-start | bytes 786440 | tf_op jit(solution)/shard_map/ppermute | solution.py:23
  66.4 18.1 %collective-permute-start.9 = (bf16[2,2,128,512]{3,2,1,0:T(8,128)(2,1)S(1)}, bf16[2,2,128,512]{3,2,1,0:T(8,128)(2,1)S(1)}, u32[]{:S(2)}, u32[]{:S(2)}) collective-permute-start(bf16[2,2,128,512]{3,2,1,0:T(8,128)(2,1)S(1)} %pad_maximum_fusion.refs_4_), channel_id=1, source_target_pairs={{0,24},{1,9},{2,26},{3,11},{4,28},{5,13},{6,30},{7,15},{8,0},{9,17... | collective-permute-start | bytes 1572872 | tf_op jit(solution)/shard_map/ppermute | solution.py:23
  66.9 18.5 %collective-permute-start.8 = (bf16[2,2,128,512]{3,2,1,0:T(8,128)(2,1)S(1)}, bf16[2,2,128,512]{3,2,1,0:T(8,128)(2,1)}, u32[]{:S(2)}, u32[]{:S(2)}) collective-permute-start(bf16[2,2,128,512]{3,2,1,0:T(8,128)(2,1)S(1)} %pad_maximum_fusion.refs_4_), channel_id=1, source_target_pairs={{0,8},{1,25},{2,10},{3,27},{4,12},{5,29},{6,14},{7,31},{8,16},{9,1... | collective-permute-start | bytes 1572872 | tf_op jit(solution)/shard_map/ppermute | solution.py:23
  68.4 8.6 %collective-permute-start.6 = (bf16[2,128,512]{2,1,0:T(8,128)(2,1)S(1)}, bf16[2,128,512]{2,1,0:T(8,128)(2,1)}, u32[]{:S(2)}, u32[]{:S(2)}) collective-permute-start(bf16[2,128,512]{2,1,0:T(8,128)(2,1)S(1)} %collective-permute-done.2), channel_id=1, source_target_pairs={{0,2},{1,7},{2,4},{3,1},{4,6},{5,3},{6,0},{7,5},{8,10},{9,15},{10,... | collective-permute-start | bytes 786440 | tf_op jit(solution)/shard_map/ppermute | solution.py:23
  70.0 13.8 %collective-permute-start.7 = (bf16[1,2,128,512]{3,2,1,0:T(8,128)(2,1)S(1)}, bf16[1,2,128,512]{3,2,1,0:T(8,128)(2,1)S(1)}, u32[]{:S(2)}, u32[]{:S(2)}) collective-permute-start(bf16[1,2,128,512]{3,2,1,0:T(8,128)(2,1)S(1)} %collective-permute-done.4.refs_1_), channel_id=1, source_target_pairs={{0,8},{1,25},{2,10},{3,27},{4,12},{5,29},{6,14},{7,31},{8,16},{9,1... | collective-permute-start | bytes 786440 | tf_op jit(solution)/shard_map/ppermute | solution.py:23
  77.0 18.8 %collective-permute-start.15 = (bf16[2048,512]{1,0:T(8,128)(2,1)S(1)}, bf16[2048,512]{1,0:T(8,128)(2,1)}, u32[]{:S(2)}, u32[]{:S(2)}) collective-permute-start(bf16[2048,512]{1,0:T(8,128)(2,1)S(1)} %copy-done.1), channel_id=1, source_target_pairs={{0,1},{1,0},{2,3},{3,2},{4,5},{5,4},{6,7},{7,6},{8,9},{9,8},{10,11... | collective-permute-start | bytes 6291464 | tf_op jit(solution)/shard_map/ppermute | solution.py:23
  85.4 19.2 %collective-permute-start.16 = (bf16[2048,512]{1,0:T(8,128)(2,1)}, bf16[2048,512]{1,0:T(8,128)(2,1)}, u32[]{:S(2)}, u32[]{:S(2)}) collective-permute-start(bf16[2048,512]{1,0:T(8,128)(2,1)} %collective-permute-done.10.refs_13_), channel_id=1, source_target_pairs={{0,1},{1,0},{2,3},{3,2},{4,5},{5,4},{6,7},{7,6},{8,9},{9,8},{10,11... | collective-permute-start | bytes 6291464 | tf_op jit(solution)/shard_map/ppermute | solution.py:23
  85.4 10.3 %collective-permute-start.12 = (bf16[1,2,128,512]{3,2,1,0:T(8,128)(2,1)}, bf16[1,2,128,512]{3,2,1,0:T(8,128)(2,1)}, u32[]{:S(2)}, u32[]{:S(2)}) collective-permute-start(bf16[1,2,128,512]{3,2,1,0:T(8,128)(2,1)} %bitcast.20.refs_8_), channel_id=1, source_target_pairs={{0,8},{1,25},{2,10},{3,27},{4,12},{5,29},{6,14},{7,31},{8,16},{9,1... | collective-permute-start | bytes 786440 | tf_op jit(solution)/shard_map/ppermute | solution.py:23
  85.5 19.1 %collective-permute-start.11 = (bf16[2,2,128,512]{3,2,1,0:T(8,128)(2,1)}, bf16[2,2,128,512]{3,2,1,0:T(8,128)(2,1)}, u32[]{:S(2)}, u32[]{:S(2)}) collective-permute-start(bf16[2,2,128,512]{3,2,1,0:T(8,128)(2,1)} %collective-permute-done.8.refs_5_), channel_id=1, source_target_pairs={{0,8},{1,25},{2,10},{3,27},{4,12},{5,29},{6,14},{7,31},{8,16},{9,1... | collective-permute-start | bytes 1572872 | tf_op jit(solution)/shard_map/ppermute | solution.py:23
  86.6 9.6 %collective-permute-start.13 = (bf16[1,2,128,512]{3,2,1,0:T(8,128)(2,1)}, bf16[1,2,128,512]{3,2,1,0:T(8,128)(2,1)}, u32[]{:S(2)}, u32[]{:S(2)}) collective-permute-start(bf16[1,2,128,512]{3,2,1,0:T(8,128)(2,1)} %bitcast.20.refs_8_), channel_id=1, source_target_pairs={{0,24},{1,9},{2,26},{3,11},{4,28},{5,13},{6,30},{7,15},{8,0},{9,17... | collective-permute-start | bytes 786440 | tf_op jit(solution)/shard_map/ppermute | solution.py:23
  95.7 8.9 %collective-permute-start.14 = (bf16[1,2,128,512]{3,2,1,0:T(8,128)(2,1)}, bf16[1,2,128,512]{3,2,1,0:T(8,128)(2,1)}, u32[]{:S(2)}, u32[]{:S(2)}) collective-permute-start(bf16[1,2,128,512]{3,2,1,0:T(8,128)(2,1)} %collective-permute-done.12.refs_9_), channel_id=1, source_target_pairs={{0,8},{1,25},{2,10},{3,27},{4,12},{5,29},{6,14},{7,31},{8,16},{9,1... | collective-permute-start | bytes 786440 | tf_op jit(solution)/shard_map/ppermute | solution.py:23
  104.6 1.0 copy-start.5
  116.6 21.0 %copy-start.3 = (f32[512,256]{1,0:T(8,128)S(1)}, f32[512,256]{1,0:T(8,128)}, u32[]{:S(2)}) copy-start(f32[512,256]{1,0:T(8,128)} %copy-done.2) | copy-start | bytes 1572868
  136.0 1.6 collective-permute-start.17
  143.1 1.3 collective-permute-start.18
  144.4 5.3 %collective-permute-start.21 = (f32[17,256]{1,0:T(8,128)S(1)}, f32[17,256]{1,0:T(8,128)S(1)}, u32[]{:S(2)}, u32[]{:S(2)}) collective-permute-start(f32[17,256]{1,0:T(8,128)S(1)} %add.271), channel_id=1, source_target_pairs={{0,16},{1,17},{2,18},{3,19},{4,20},{5,21},{6,22},{7,23},{8,24},{9,... | collective-permute-start | bytes 52232 | tf_op jit(solution)/shard_map/ppermute | solution.py:23
  145.3 4.5 %collective-permute-start.20 = (f32[17,256]{1,0:T(8,128)S(1)}, f32[17,256]{1,0:T(8,128)S(1)}, u32[]{:S(2)}, u32[]{:S(2)}) collective-permute-start(f32[17,256]{1,0:T(8,128)S(1)} %add.271), channel_id=1, source_target_pairs={{0,24},{1,25},{2,26},{3,27},{4,28},{5,29},{6,30},{7,31},{8,0},{9,1... | collective-permute-start | bytes 52232 | tf_op jit(solution)/shard_map/ppermute | solution.py:23
  147.6 5.0 %collective-permute-start.19 = (f32[17,256]{1,0:T(8,128)S(1)}, f32[17,256]{1,0:T(8,128)S(1)}, u32[]{:S(2)}, u32[]{:S(2)}) collective-permute-start(f32[17,256]{1,0:T(8,128)S(1)} %add.271), channel_id=1, source_target_pairs={{0,8},{1,9},{2,10},{3,11},{4,12},{5,13},{6,14},{7,15},{8,16},{9,17... | collective-permute-start | bytes 52232 | tf_op jit(solution)/shard_map/ppermute | solution.py:23
  152.6 8.2 %collective-permute-start.24 = (f32[17,256]{1,0:T(8,128)S(1)}, f32[17,256]{1,0:T(8,128)S(1)}, u32[]{:S(2)}, u32[]{:S(2)}) collective-permute-start(f32[17,256]{1,0:T(8,128)S(1)} %add_add_fusion.1), channel_id=1, source_target_pairs={{0,4},{1,5},{2,6},{3,7},{4,0},{5,1},{6,2},{7,3},{8,12},{9,13},{10,... | collective-permute-start | bytes 52232 | tf_op jit(solution)/shard_map/ppermute | solution.py:23
  156.9 4.7 %collective-permute-start.23 = (f32[17,256]{1,0:T(8,128)S(1)}, f32[17,256]{1,0:T(8,128)S(1)}, u32[]{:S(2)}, u32[]{:S(2)}) collective-permute-start(f32[17,256]{1,0:T(8,128)S(1)} %add_add_fusion.1), channel_id=1, source_target_pairs={{0,6},{1,7},{2,0},{3,1},{4,2},{5,3},{6,4},{7,5},{8,14},{9,15},{10,... | collective-permute-start | bytes 52232 | tf_op jit(solution)/shard_map/ppermute | solution.py:23
  157.9 5.9 %collective-permute-start.22 = (f32[17,256]{1,0:T(8,128)S(1)}, f32[17,256]{1,0:T(8,128)S(1)}, u32[]{:S(2)}, u32[]{:S(2)}) collective-permute-start(f32[17,256]{1,0:T(8,128)S(1)} %add_add_fusion.1), channel_id=1, source_target_pairs={{0,2},{1,3},{2,4},{3,5},{4,6},{5,7},{6,0},{7,1},{8,10},{9,11},{10,... | collective-permute-start | bytes 52232 | tf_op jit(solution)/shard_map/ppermute | solution.py:23
  163.8 3.8 %collective-permute-start.25 = (f32[16,256]{1,0:T(8,128)S(1)}, f32[16,256]{1,0:T(8,128)S(1)}, u32[]{:S(2)}, u32[]{:S(2)}) collective-permute-start(f32[16,256]{1,0:T(8,128)S(1)} %slice.19), channel_id=1, source_target_pairs={{0,128},{1,129},{2,130},{3,131},{4,132},{5,133},{6,134},{7,135},{8... | collective-permute-start | bytes 49160 | tf_op jit(solution)/shard_map/ppermute | solution.py:23
  167.7 3.7 %collective-permute-start.26 = (f32[16,256]{1,0:T(8,128)S(1)}, f32[16,256]{1,0:T(8,128)S(1)}, u32[]{:S(2)}, u32[]{:S(2)}) collective-permute-start(f32[16,256]{1,0:T(8,128)S(1)} %slice_add_fusion), channel_id=1, source_target_pairs={{0,32},{1,33},{2,34},{3,35},{4,36},{5,37},{6,38},{7,39},{8,40},{9,... | collective-permute-start | bytes 49160 | tf_op jit(solution)/shard_map/ppermute | solution.py:23
  171.4 5.2 %collective-permute-start.27 = (f32[16,256]{1,0:T(8,128)S(1)}, f32[16,256]{1,0:T(8,128)S(1)}, u32[]{:S(2)}, u32[]{:S(2)}) collective-permute-start(f32[16,256]{1,0:T(8,128)S(1)} %add.279), channel_id=1, source_target_pairs={{0,64},{1,65},{2,66},{3,67},{4,68},{5,69},{6,70},{7,71},{8,72},{9,... | collective-permute-start | bytes 49160 | tf_op jit(solution)/shard_map/ppermute | solution.py:23
  (6 other events, 5.1 us)

commit v3 on v2

--- a/solution.py
+++ b/solution.py
@@ -37,8 +37,19 @@
     return (x // 2, x % 2, y_lo, x + 2 * z_lo + y_hi, z_hi, core)
 
 
-def decode_kernel(codes, books, scale, initial, decoded, error):
-    picks = [codes[m].T for m in range(2)]
+def decode_kernel(codes_in, books_in, scale, initial_in, decoded, error, codes, books, initial, sem):
+    copies = [
+        pltpu.make_async_copy(a, b, sem.at[i])
+        for i, (a, b) in enumerate(
+            ((codes_in, codes), (books_in, books), (initial_in, initial))
+        )
+    ]
+    for copy in copies:
+        copy.start()
+    copies[0].wait()
+    picks = [codes[m] for m in range(2)]
+    copies[1].wait()
+    tables = [books[m].astype(jnp.float32) for m in range(2)]
     rows = initial.shape[0]
     for g in range(picks[0].shape[0]):
         for lane in range(0, rows, 128):
@@ -46,26 +57,47 @@
             for m in range(2):
                 word = jnp.broadcast_to(picks[m][g : g + 1, lane : lane + 128], (8, 128))
                 low = word & 127
-                found = jnp.where(
-                    word < 128,
-                    jnp.take_along_axis(books[m, :, :128], low, axis=1, mode="promise_in_bounds"),
-                    jnp.take_along_axis(books[m, :, 128:], low, axis=1, mode="promise_in_bounds"),
-                )
+                found = [
+                    jnp.take_along_axis(
+                        tables[m][:, at : at + 128], low, axis=1, mode="promise_in_bounds"
+                    )
+                    for at in (0, 128)
+                ]
+                found = jnp.where(word < 128, *found)
                 total = found if total is None else total + found
             decoded[8 * g : 8 * g + 8, lane : lane + 128] = total
-    error[...] = (scale[...] * decoded[...].T - initial[...].astype(jnp.float32)).astype(error.dtype)
+    copies[2].wait()
+    error[...] = ((scale[...] * decoded[...]).T - initial[...].astype(jnp.float32)).astype(
+        error.dtype
+    )
+
 
 def decode(codes, codebooks, row_scale, initial):
     rows, width = initial.shape
     return pl.pallas_call(
         decode_kernel,
-        out_shape=(jax.ShapeDtypeStruct((width, rows), jnp.float32), jax.ShapeDtypeStruct((rows, width), jnp.bfloat16)),
-        in_specs=[pl.BlockSpec(memory_space=pltpu.VMEM)] * 4,
+        out_shape=(
+            jax.ShapeDtypeStruct((width, rows), jnp.float32),
+            jax.ShapeDtypeStruct((rows, width), jnp.bfloat16),
+        ),
+        in_specs=[
+            pl.BlockSpec(memory_space=pl.ANY),
+            pl.BlockSpec(memory_space=pl.ANY),
+            pl.BlockSpec(memory_space=pltpu.VMEM),
+            pl.BlockSpec(memory_space=pl.ANY),
+        ],
         out_specs=(pl.BlockSpec(memory_space=pltpu.VMEM),) * 2,
-        compiler_params=pltpu.CompilerParams(vmem_limit_bytes=16 * 2**20),
+        scratch_shapes=[
+            pltpu.VMEM(codes.shape, codes.dtype),
+            pltpu.VMEM(codebooks.shape, codebooks.dtype),
+            pltpu.VMEM(initial.shape, initial.dtype),
+            pltpu.SemaphoreType.DMA((3,)),
+        ],
+        compiler_params=pltpu.CompilerParams(vmem_limit_bytes=60 * 2**20),
         cost_estimate=pl.CostEstimate(flops=2**21, bytes_accessed=2**20, transcendentals=0),
         name="decode",
-    )(codes, jnp.swapaxes(codebooks, 1, 2).astype(jnp.float32), row_scale.reshape(rows, 1), initial)
+    )(codes, codebooks, row_scale.reshape(1, rows), initial)
+
 
 def finish_kernel(core, codes, scale, decoded, kept, got, product, totals):
     half = kept.shape[0]
@@ -73,13 +105,14 @@
     product[:half] = 2.0 * jnp.where(first, kept[...], got[...])
     product[half:] = 2.0 * jnp.where(first, got[...], kept[...])
     totals[16:17, :] = jnp.sum(product[...].T * decoded[...], axis=0, keepdims=True)
-    picks = [codes[m].T.astype(jnp.bfloat16) for m in range(2)]
+    picks = [codes[m].astype(jnp.bfloat16) for m in range(2)]
     rows = product.shape[0]
     words = lax.broadcasted_iota(jnp.int32, (256, rows), 0).astype(jnp.bfloat16)
     group = lax.rem(lax.broadcasted_iota(jnp.int32, (rows, 256), 1), 128) // 8
     sums = jnp.zeros((512, 256), jnp.float32)
+    scales = jnp.broadcast_to(scale[...], (128, rows)).T
     for block in range(product.shape[1] // 128):
-        weighted = scale[...] * product[:, block * 128 : (block + 1) * 128]
+        weighted = scales * product[:, block * 128 : (block + 1) * 128]
         high = weighted.astype(jnp.bfloat16)
         low = (weighted - high.astype(jnp.float32)).astype(jnp.bfloat16)
         both = jnp.concatenate([high, low], axis=1)
@@ -108,40 +141,39 @@
         compiler_params=pltpu.CompilerParams(vmem_limit_bytes=24 * 2**20),
         cost_estimate=pl.CostEstimate(flops=2**32, bytes_accessed=2**21, transcendentals=0),
         name="finish",
-    )(core.reshape(1), codes, row_scale.reshape(rows, 1), decoded, kept, got)
-
-def matmul_kernel(slots, *refs):
-    blocks, tiles = refs[:-9], refs[-9:-5]
-    out, held, h_own, h_across, sem = refs[-5:]
-    copies = [
-        pltpu.make_async_copy(tiles[0], h_own.at[0:2048], sem.at[0]),
-        pltpu.make_async_copy(tiles[1], h_own.at[2048:4096], sem.at[1]),
-        pltpu.make_async_copy(tiles[2], h_across.at[0:2048], sem.at[2]),
-        pltpu.make_async_copy(tiles[3], h_across.at[2048:4096], sem.at[3]),
-    ]
-    n = 0
+    )(core.reshape(1), codes, row_scale.reshape(1, rows), decoded, kept, got)
+
+def matmul_kernel(slots, own, far_a, far_b, across, across_a, across_b, *refs):
+    blocks = refs[:-3]
+    out, held, sem = refs[-3:]
+    copies = []
     for group in blocks:
         for place in range(group.shape[0]):
             for side in range(2):
+                n = len(copies)
                 rows = pl.multiple_of(slots[2 * n] * 128, 128)
                 columns = pl.multiple_of(slots[2 * n + 1] * 512, 512)
                 copies.append(
                     pltpu.make_async_copy(
                         group.at[place, side],
                         held.at[pl.ds(rows, 128), pl.ds(columns, 512)],
-                        sem.at[4 + n],
+                        sem.at[n],
                     )
                 )
-                n += 1
     for copy in copies:
         copy.start()
-    for copy in copies[:2] + copies[4:]:
+    for copy in copies:
         copy.wait()
-    for side, h in enumerate((h_own, h_across)):
-        if side:
-            copies[2].wait()
-            copies[3].wait()
-        total = jnp.dot(held[...], h[...], preferred_element_type=jnp.float32)
+    for side, tiles in enumerate(((own, far_a, far_b), (across, across_a, across_b))):
+        total = None
+        at = 0
+        for tile in tiles:
+            depth = tile.shape[0]
+            term = jnp.dot(
+                held[:, at : at + depth], tile[...], preferred_element_type=jnp.float32
+            )
+            total = term if total is None else total + term
+            at += depth
         for s in range(4):
             out[s, :, side * 512 : (side + 1) * 512] = total[s * 128 : (s + 1) * 128].astype(
                 out.dtype
@@ -151,10 +183,11 @@
 def body(codes, codebooks, row_scale, initial, hessian):
     rows, width = initial.shape
     words = codebooks.shape[1]
+    codes, codebooks = jnp.swapaxes(codes, 1, 2), jnp.swapaxes(codebooks, 1, 2)
     half = rows // 2
     z_lo, y_hi, y_lo, x, z_hi, core = (lax.axis_index(a) for a in AXES)
 
-    far = send(hessian, lambda zl, yh, yl, x, zh, c: (zl, yh, 1 - yl, x, zh, c))
+    far_a = shift(hessian[:512], "y_lo", 1)
     across = shift(hessian, "core", 1)
 
     decoded, error = decode(codes, codebooks, row_scale, initial)
@@ -164,6 +197,9 @@
     same = send(mine, to_plane)
     cross = send(other, lambda *p: to_plane(*p)[:-1] + (1 - p[-1],))
     block = jnp.stack([same, cross])
+
+    rest, block, far_a = lax.optimization_barrier((hessian[512:], block, far_a))
+    far_b = shift(rest, "y_lo", 1)
 
     own = block[None]
     z_back, z_on = turn(block, "z_hi", 1), turn(block, "z_hi", -1)
@@ -173,12 +209,11 @@
     )
     z_two, own_two = turn(z_back, "z_hi", 1), turn(own_back, "x", 1)
     near_back, near_on = turn(near, "x", 1), turn(near, "x", -1)
-    last, own_two, near_back, near_on, far = lax.optimization_barrier(
-        (z_two[None], own_two, near_back, near_on, far)
-    )
+    last = z_two[None]
     last_back, last_on = turn(last, "x", 1), turn(last, "x", -1)
     near_two, last_two = turn(near_back, "x", 1), turn(last_back, "x", 1)
-    far_across = shift(far, "core", 1)
+    far_b, *_ = lax.optimization_barrier((far_b, near_back, near_on, z_two, own_two))
+    across_a, across_b = shift(far_a, "core", 1), shift(far_b, "core", 1)
     wide = (
         (own, own_back, own_on, own_two),
         (near, near_back, near_on, near_two),
@@ -203,20 +238,19 @@
         matmul_kernel,
         out_shape=jax.ShapeDtypeStruct((4, half, 2 * width), jnp.bfloat16),
         in_specs=[pl.BlockSpec(memory_space=pltpu.SMEM)]
-        + [pl.BlockSpec(memory_space=pl.ANY)] * (len(blocks) + 4),
+        + [pl.BlockSpec(memory_space=pltpu.VMEM)] * 6
+        + [pl.BlockSpec(memory_space=pl.ANY)] * len(blocks),
         out_specs=pl.BlockSpec(memory_space=pltpu.VMEM),
         scratch_shapes=[
             pltpu.VMEM((4 * half, 8 * width), jnp.bfloat16),
-            pltpu.VMEM((8 * width, width), jnp.bfloat16),
-            pltpu.VMEM((8 * width, width), jnp.bfloat16),
-            pltpu.SemaphoreType.DMA((36,)),
+            pltpu.SemaphoreType.DMA((32,)),
         ],
         compiler_params=pltpu.CompilerParams(vmem_limit_bytes=32 * 2**20),
         cost_estimate=pl.CostEstimate(
             flops=2 * 512 * 4096 * 1024, bytes_accessed=13 * 2**20, transcendentals=0
         ),
         name="matmul",
-    )(slots, *blocks, hessian, far, across, far_across)
+    )(slots, hessian, far_a, far_b, across, across_a, across_b, *blocks)
 
     parts = lax.all_to_all(partial, ("z_lo", "y_hi"), 0, 0, tiled=True)
     summed = jnp.sum(parts.astype(jnp.float32), axis=0)

time: 178 us -> 157 us (0.88)
  starting transfers between devices: 75.8 us -> 47.4 us
  local copies, waits for them, and re-layouts: 8.21 us -> 12.6 us
  Pallas kernels: 16.2 us -> 18 us
    ppermute x28 -> x30, starting transfers between devices: 75.8 us -> 47.4 us  [send(): return lax.ppermute(a, AXES, pairs)]
    slice x0 -> x2, local copies, waits for them, and re-layouts: none -> 2.72 us  [the longest x1 1.64 us: body(): rest, block, far_a = lax.optimization_barrier((hessian[512:], block, far_a))]
    unnamed x21 -> x28, local copies, waits for them, and re-layouts: 7.19 us -> 8.66 us
    ppermute x28 -> x30, waiting for transfers between devices: 55 us -> 55.9 us  [send(): return lax.ppermute(a, AXES, pairs)]
  transfers between devices with their start and end apart: 28 -> 30, of which waited for: 17 -> 19; matrix products, arithmetic and copies ran while one was open for 2% -> 2% of each run, Pallas kernels for 1% -> 2%
where the time goes in v3:
time: 157 us; the launch traced here: 156 us
  waiting for transfers between devices  55.9 us (36%)
  starting transfers between devices  47.4 us (30%)
  blocking collectives  19.6 us (12%)
  Pallas kernels  18 us (11%)
  local copies, waits for them, and re-layouts  12.6 us (8%)
    ppermute x30, waiting for transfers between devices, send(): return lax.ppermute(a, AXES, pairs)  55.9 us
    ppermute x30, starting transfers between devices, send(): return lax.ppermute(a, AXES, pairs)  47.4 us
    all_to_all x1, blocking collectives, body(): parts = lax.all_to_all(partial, ('z_lo', 'y_hi'), 0, 0, tiled=True)  19.6 us
    pallas_call x1, Pallas kernels, body(): pl.pallas_call(matmul_kernel, out_shape=jax.ShapeDtypeStruct((4, half, 2...  9.17 us
    unnamed x28, local copies, waits for them, and re-layouts  8.66 us
    pallas_call x1, Pallas kernels, finish(): pl.pallas_call(finish_kernel, out_shape=(jax.ShapeDtypeStruct((rows, widt...  5.48 us
    pallas_call x1, Pallas kernels, decode(): pl.pallas_call(decode_kernel, out_shape=(jax.ShapeDtypeStruct((width, row...  3.31 us
  transfers between devices with their start and end apart: 30, of which 19 were waited for; matrix products, arithmetic and copies ran while one was open for 2% of the time, Pallas kernels for 2%

profile of v3, /device:TPU:8, one launch (start us, length us, event | category | flops | bytes accessed | tf_op | source)
XLA Modules:
  0.0 155.8 jit_solution(8144123321541761567)
XLA Ops:
  1.7 2.3 %collective-permute-start.2 = (bf16[512,512]{1,0:T(8,128)(2,1)S(1)}, bf16[512,512]{1,0:T(8,128)(2,1)S(1)}, u32[]{:S(2)}, u32[]{:S(2)}) collective-permute-start(bf16[512,512]{1,0:T(8,128)(2,1)S(1)} %slice.19), channel_id=1, source_target_pairs={{0,32},{1,33},{2,34},{3,35},{4,36},{5,37},{6,38},{7,39},{8,40},{9,... | collective-permute-start | bytes 1572872 | tf_op jit(solution)/shard_map/ppermute | solution.py:23
  4.0 3.3 %decode.1 = (f32[512,256]{1,0:T(8,128)}, bf16[256,512]{1,0:T(8,128)(2,1)}) custom-call(s32[2,64,256]{2,1,0:T(8,128)} %bitcast.30, bf16[2,8,256]{2,1,0:T(8,128)(2,1)} %bitcast.38, f32[1,256]{1,0:T(1,128)} %bitcast.32, bf16[256,512]{1,0:T(8,128)(2,1)} %initial_in.1), custom_call_target="tpu_custom_call" | custom-call | flops 2097152 | bytes 1048576 | tf_op jit(solution)/shard_map/decode/pallas_call | solution.py:77
  9.1 1.6 %slice.18 = bf16[1536,512]{1,0:T(8,128)(2,1)S(1)} slice(bf16[2048,512]{1,0:T(8,128)(2,1)} %own.1), slice={[512:2048], [0:512]} | slice | bytes 3145728 | tf_op jit(solution)/shard_map/slice | solution.py:201
  10.8 4.7 %collective-permute-done.2.far_a = bf16[512,512]{1,0:T(8,128)(2,1)S(1)} collective-permute-done((bf16[512,512]{1,0:T(8,128)(2,1)S(1)}, bf16[512,512]{1,0:T(8,128)(2,1)S(1)}, u32[]{:S(2)}, u32[]{:S(2)}) %collective-permute-start.2) | collective-permute-done | bytes 524320 | tf_op jit(solution)/shard_map/ppermute | solution.py:23
  15.7 6.5 %collective-permute-start.5 = (bf16[2,128,512]{2,1,0:T(8,128)(2,1)S(1)}, bf16[2,128,512]{2,1,0:T(8,128)(2,1)S(1)}, u32[]{:S(2)}, u32[]{:S(2)}) collective-permute-start(bf16[2,128,512]{2,1,0:T(8,128)(2,1)S(1)} %pad_maximum_fusion.1), channel_id=1, source_target_pairs={{0,6},{1,3},{2,0},{3,5},{4,2},{5,7},{6,4},{7,1},{8,14},{9,11},{10,... | collective-permute-start | bytes 786440 | tf_op jit(solution)/shard_map/ppermute | solution.py:23
  22.2 10.3 %collective-permute-start.7 = (bf16[1,2,128,512]{3,2,1,0:T(8,128)(2,1)S(1)}, bf16[1,2,128,512]{3,2,1,0:T(8,128)(2,1)S(1)}, u32[]{:S(2)}, u32[]{:S(2)}) collective-permute-start(bf16[1,2,128,512]{3,2,1,0:T(8,128)(2,1)S(1)} %bitcast.27), channel_id=1, source_target_pairs={{0,24},{1,9},{2,26},{3,11},{4,28},{5,13},{6,30},{7,15},{8,0},{9,17... | collective-permute-start | bytes 786440 | tf_op jit(solution)/shard_map/ppermute | solution.py:23
  32.6 3.8 %collective-permute-done.4 = bf16[2,128,512]{2,1,0:T(8,128)(2,1)S(1)} collective-permute-done((bf16[2,128,512]{2,1,0:T(8,128)(2,1)S(1)}, bf16[2,128,512]{2,1,0:T(8,128)(2,1)S(1)}, u32[]{:S(2)}, u32[]{:S(2)}) %collective-permute-start.4) | collective-permute-done | bytes 262176 | tf_op jit(solution)/shard_map/ppermute | solution.py:23
  38.0 2.2 %collective-permute-done.6.refs_1_ = bf16[1,2,128,512]{3,2,1,0:T(8,128)(2,1)S(1)} collective-permute-done((bf16[1,2,128,512]{3,2,1,0:T(8,128)(2,1)S(1)}, bf16[1,2,128,512]{3,2,1,0:T(8,128)(2,1)S(1)}, u32[]{:S(2)}, u32[]{:S(2)}) %collective-permute-start.6) | collective-permute-done | bytes 262176 | tf_op jit(solution)/shard_map/ppermute | solution.py:23
  40.1 1.9 %collective-permute-start.10 = (bf16[2,128,512]{2,1,0:T(8,128)(2,1)S(1)}, bf16[2,128,512]{2,1,0:T(8,128)(2,1)}, u32[]{:S(2)}, u32[]{:S(2)}) collective-permute-start(bf16[2,128,512]{2,1,0:T(8,128)(2,1)S(1)} %collective-permute-done.4), channel_id=1, source_target_pairs={{0,2},{1,7},{2,4},{3,1},{4,6},{5,3},{6,0},{7,5},{8,10},{9,15},{10,... | collective-permute-start | bytes 786440 | tf_op jit(solution)/shard_map/ppermute | solution.py:23
  42.0 5.7 %collective-permute-start.9 = (bf16[2,2,128,512]{3,2,1,0:T(8,128)(2,1)S(1)}, bf16[2,2,128,512]{3,2,1,0:T(8,128)(2,1)S(1)}, u32[]{:S(2)}, u32[]{:S(2)}) collective-permute-start(bf16[2,2,128,512]{3,2,1,0:T(8,128)(2,1)S(1)} %pad_maximum_fusion.refs_4_), channel_id=1, source_target_pairs={{0,24},{1,9},{2,26},{3,11},{4,28},{5,13},{6,30},{7,15},{8,0},{9,17... | collective-permute-start | bytes 1572872 | tf_op jit(solution)/shard_map/ppermute | solution.py:23
  47.8 3.8 %collective-permute-done.10 = bf16[2,128,512]{2,1,0:T(8,128)(2,1)} collective-permute-done((bf16[2,128,512]{2,1,0:T(8,128)(2,1)S(1)}, bf16[2,128,512]{2,1,0:T(8,128)(2,1)}, u32[]{:S(2)}, u32[]{:S(2)}) %collective-permute-start.10) | collective-permute-done | bytes 262176 | tf_op jit(solution)/shard_map/ppermute | solution.py:23
  51.6 2.4 %collective-permute-start.11 = (bf16[1,2,128,512]{3,2,1,0:T(8,128)(2,1)S(1)}, bf16[1,2,128,512]{3,2,1,0:T(8,128)(2,1)S(1)}, u32[]{:S(2)}, u32[]{:S(2)}) collective-permute-start(bf16[1,2,128,512]{3,2,1,0:T(8,128)(2,1)S(1)} %collective-permute-done.6.refs_1_), channel_id=1, source_target_pairs={{0,8},{1,25},{2,10},{3,27},{4,12},{5,29},{6,14},{7,31},{8,16},{9,1... | collective-permute-start | bytes 786440 | tf_op jit(solution)/shard_map/ppermute | solution.py:23
  54.7 7.3 %collective-permute-done.11.refs_3_ = bf16[1,2,128,512]{3,2,1,0:T(8,128)(2,1)S(1)} collective-permute-done((bf16[1,2,128,512]{3,2,1,0:T(8,128)(2,1)S(1)}, bf16[1,2,128,512]{3,2,1,0:T(8,128)(2,1)S(1)}, u32[]{:S(2)}, u32[]{:S(2)}) %collective-permute-start.11) | collective-permute-done | bytes 262176 | tf_op jit(solution)/shard_map/ppermute | solution.py:23
  64.0 2.2 %collective-permute-start.15 = (bf16[2,2,128,512]{3,2,1,0:T(8,128)(2,1)}, bf16[2,2,128,512]{3,2,1,0:T(8,128)(2,1)}, u32[]{:S(2)}, u32[]{:S(2)}) collective-permute-start(bf16[2,2,128,512]{3,2,1,0:T(8,128)(2,1)} %collective-permute-done.8.refs_5_), channel_id=1, source_target_pairs={{0,8},{1,25},{2,10},{3,27},{4,12},{5,29},{6,14},{7,31},{8,16},{9,1... | collective-permute-start | bytes 1572872 | tf_op jit(solution)/shard_map/ppermute | solution.py:23
  68.1 2.6 %collective-permute-start.17 = (bf16[1,2,128,512]{3,2,1,0:T(8,128)(2,1)}, bf16[1,2,128,512]{3,2,1,0:T(8,128)(2,1)}, u32[]{:S(2)}, u32[]{:S(2)}) collective-permute-start(bf16[1,2,128,512]{3,2,1,0:T(8,128)(2,1)} %bitcast.21.refs_8_), channel_id=1, source_target_pairs={{0,24},{1,9},{2,26},{3,11},{4,28},{5,13},{6,30},{7,15},{8,0},{9,17... | collective-permute-start | bytes 786440 | tf_op jit(solution)/shard_map/ppermute | solution.py:23
  72.0 5.7 %collective-permute-done.17.refs_10_ = bf16[1,2,128,512]{3,2,1,0:T(8,128)(2,1)} collective-permute-done((bf16[1,2,128,512]{3,2,1,0:T(8,128)(2,1)}, bf16[1,2,128,512]{3,2,1,0:T(8,128)(2,1)}, u32[]{:S(2)}, u32[]{:S(2)}) %collective-permute-start.17) | collective-permute-done | bytes 262176 | tf_op jit(solution)/shard_map/ppermute | solution.py:23
  77.8 5.3 %collective-permute-done.18.refs_11_ = bf16[1,2,128,512]{3,2,1,0:T(8,128)(2,1)} collective-permute-done((bf16[1,2,128,512]{3,2,1,0:T(8,128)(2,1)}, bf16[1,2,128,512]{3,2,1,0:T(8,128)(2,1)}, u32[]{:S(2)}, u32[]{:S(2)}) %collective-permute-start.18) | collective-permute-done | bytes 262176 | tf_op jit(solution)/shard_map/ppermute | solution.py:23
  88.1 9.2 %matmul.1 = bf16[4,128,1024]{2,1,0:T(8,128)(2,1)S(1)} custom-call(s32[64]{0:T(128)S(1)} %stack.50.slots, bf16[2048,512]{1,0:T(8,128)(2,1)S(1)} %copy-done, bf16[512,512]{1,0:T(8,128)(2,1)S(1)} %collective-permute-done.2.far_a, bf16[1536,512]{1,0:T(8,128)(2,1)} %collective-permute-done.3.far_b, bf16[2048,512]{1,0:T(8,128)(2,1)} %collective-permute-done.12.across, ...), custom_call_target="tpu_custom_call" | custom-call | flops 4294967296 | bytes 13631488 | tf_op jit(solution)/shard_map/matmul/pallas_call | solution.py:237
  97.3 19.6 %all_to_all.5 = bf16[4,128,1024]{2,1,0:T(8,128)(2,1)S(1)} all-to-all(bf16[4,128,1024]{2,1,0:T(8,128)(2,1)S(1)} %matmul.1), channel_id=1, replica_groups=mesh['z_lo'=2,'y_hi'=2,'y_lo'=2,'x'=4,'z_hi'=4,'core'=2] {'z_lo','y_hi'}, dimensions={0} | all-to-all | bytes 2097152 | tf_op jit(solution)/shard_map/all_to_all | solution.py:255
  117.2 1.5 collective-permute-done.19.got
  118.8 5.5 %finish.1 = (f32[256,512]{1,0:T(8,128)}, f32[17,256]{1,0:T(8,128)S(1)}) custom-call(s32[1]{0:T(128)} %bitcast.core, s32[2,64,256]{2,1,0:T(8,128)S(1)} %bitcast.31, f32[1,256]{1,0:T(1,128)S(1)} %bitcast.33, f32[512,256]{1,0:T(8,128)S(1)} %copy-done.3, f32[128,512]{1,0:T(8,128)S(1)} %get-tuple-element.28.kept, f32[128,512]{1,0:T(8,128)S(1)} %collective-permute-done.19.got), custom_call_target="tpu_custom_call" | custom-call | flops 4294967296 | bytes 2097152 | tf_op jit(solution)/shard_map/finish/pallas_call | solution.py:136
  125.5 2.2 %collective-permute-start.22 = (f32[17,256]{1,0:T(8,128)S(1)}, f32[17,256]{1,0:T(8,128)S(1)}, u32[]{:S(2)}, u32[]{:S(2)}) collective-permute-start(f32[17,256]{1,0:T(8,128)S(1)} %add.271), channel_id=1, source_target_pairs={{0,24},{1,25},{2,26},{3,27},{4,28},{5,29},{6,30},{7,31},{8,0},{9,1... | collective-permute-start | bytes 52232 | tf_op jit(solution)/shard_map/ppermute | solution.py:23
  127.8 3.1 %collective-permute-done.23 = f32[17,256]{1,0:T(8,128)S(1)} collective-permute-done((f32[17,256]{1,0:T(8,128)S(1)}, f32[17,256]{1,0:T(8,128)S(1)}, u32[]{:S(2)}, u32[]{:S(2)}) %collective-permute-start.23) | collective-permute-done | bytes 17440 | tf_op jit(solution)/shard_map/ppermute | solution.py:23
  130.9 1.9 %collective-permute-done.21 = f32[17,256]{1,0:T(8,128)S(1)} collective-permute-done((f32[17,256]{1,0:T(8,128)S(1)}, f32[17,256]{1,0:T(8,128)S(1)}, u32[]{:S(2)}, u32[]{:S(2)}) %collective-permute-start.21) | collective-permute-done | bytes 17440 | tf_op jit(solution)/shard_map/ppermute | solution.py:23
  132.8 2.3 %collective-permute-start.26 = (f32[17,256]{1,0:T(8,128)S(1)}, f32[17,256]{1,0:T(8,128)S(1)}, u32[]{:S(2)}, u32[]{:S(2)}) collective-permute-start(f32[17,256]{1,0:T(8,128)S(1)} %add_add_fusion.1), channel_id=1, source_target_pairs={{0,4},{1,5},{2,6},{3,7},{4,0},{5,1},{6,2},{7,3},{8,12},{9,13},{10,... | collective-permute-start | bytes 52232 | tf_op jit(solution)/shard_map/ppermute | solution.py:23
  136.1 1.9 %collective-permute-start.24 = (f32[17,256]{1,0:T(8,128)S(1)}, f32[17,256]{1,0:T(8,128)S(1)}, u32[]{:S(2)}, u32[]{:S(2)}) collective-permute-start(f32[17,256]{1,0:T(8,128)S(1)} %add_add_fusion.1), channel_id=1, source_target_pairs={{0,2},{1,3},{2,4},{3,5},{4,6},{5,7},{6,0},{7,1},{8,10},{9,11},{10,... | collective-permute-start | bytes 52232 | tf_op jit(solution)/shard_map/ppermute | solution.py:23
  138.0 2.7 %collective-permute-done.26 = f32[17,256]{1,0:T(8,128)S(1)} collective-permute-done((f32[17,256]{1,0:T(8,128)S(1)}, f32[17,256]{1,0:T(8,128)S(1)}, u32[]{:S(2)}, u32[]{:S(2)}) %collective-permute-start.26) | collective-permute-done | bytes 17440 | tf_op jit(solution)/shard_map/ppermute | solution.py:23
  140.7 1.3 collective-permute-done.24
  143.2 2.7 %collective-permute-done.27 = f32[16,256]{1,0:T(8,128)S(1)} collective-permute-done((f32[16,256]{1,0:T(8,128)S(1)}, f32[16,256]{1,0:T(8,128)S(1)}, u32[]{:S(2)}, u32[]{:S(2)}) %collective-permute-start.27) | collective-permute-done | bytes 16416 | tf_op jit(solution)/shard_map/ppermute | solution.py:23
  145.9 2.2 %collective-permute-start.28 = (f32[16,256]{1,0:T(8,128)S(1)}, f32[16,256]{1,0:T(8,128)S(1)}, u32[]{:S(2)}, u32[]{:S(2)}) collective-permute-start(f32[16,256]{1,0:T(8,128)S(1)} %slice_add_fusion), channel_id=1, source_target_pairs={{0,32},{1,33},{2,34},{3,35},{4,36},{5,37},{6,38},{7,39},{8,40},{9,... | collective-permute-start | bytes 49160 | tf_op jit(solution)/shard_map/ppermute | solution.py:23
  148.2 1.7 %collective-permute-done.28 = f32[16,256]{1,0:T(8,128)S(1)} collective-permute-done((f32[16,256]{1,0:T(8,128)S(1)}, f32[16,256]{1,0:T(8,128)S(1)}, u32[]{:S(2)}, u32[]{:S(2)}) %collective-permute-start.28) | collective-permute-done | bytes 16416 | tf_op jit(solution)/shard_map/ppermute | solution.py:23
  151.3 3.9 %collective-permute-done.29 = f32[16,256]{1,0:T(8,128)S(1)} collective-permute-done((f32[16,256]{1,0:T(8,128)S(1)}, f32[16,256]{1,0:T(8,128)S(1)}, u32[]{:S(2)}, u32[]{:S(2)}) %collective-permute-start.29) | collective-permute-done | bytes 16416 | tf_op jit(solution)/shard_map/ppermute | solution.py:23
  (76 shorter events, 21.5 us)
Async XLA Ops:
  1.7 13.8 %collective-permute-start.2 = (bf16[512,512]{1,0:T(8,128)(2,1)S(1)}, bf16[512,512]{1,0:T(8,128)(2,1)S(1)}, u32[]{:S(2)}, u32[]{:S(2)}) collective-permute-start(bf16[512,512]{1,0:T(8,128)(2,1)S(1)} %slice.19), channel_id=1, source_target_pairs={{0,32},{1,33},{2,34},{3,35},{4,36},{5,37},{6,38},{7,39},{8,40},{9,... | collective-permute-start | bytes 1572872 | tf_op jit(solution)/shard_map/ppermute | solution.py:23
  8.3 2.4 %collective-permute-start = (bf16[128,512]{1,0:T(8,128)(2,1)S(1)}, bf16[128,512]{1,0:T(8,128)(2,1)S(1)}, u32[]{:S(2)}, u32[]{:S(2)}) collective-permute-start(bf16[128,512]{1,0:T(8,128)(2,1)S(1)} %get-tuple-element.29), channel_id=1, source_target_pairs={{0,0},{1,1},{2,2},{3,3},{4,4},{5,5},{6,6},{7,7},{8,72},{9,73},{10,... | collective-permute-start | bytes 393224 | tf_op jit(solution)/shard_map/ppermute | solution.py:23
  9.0 38.8 %copy-start = (bf16[2048,512]{1,0:T(8,128)(2,1)S(1)}, bf16[2048,512]{1,0:T(8,128)(2,1)}, u32[]{:S(2)}) copy-start(bf16[2048,512]{1,0:T(8,128)(2,1)} %own.1) | copy-start | bytes 6291460
  9.0 1.7 %collective-permute-start.1 = (bf16[128,512]{1,0:T(8,128)(2,1)S(1)}, bf16[128,512]{1,0:T(8,128)(2,1)S(1)}, u32[]{:S(2)}, u32[]{:S(2)}) collective-permute-start(bf16[128,512]{1,0:T(8,128)(2,1)S(1)} %get-tuple-element.30), channel_id=1, source_target_pairs={{0,1},{1,0},{2,3},{3,2},{4,5},{5,4},{6,7},{7,6},{8,73},{9,72},{10,... | collective-permute-start | bytes 393224 | tf_op jit(solution)/shard_map/ppermute | solution.py:23
  15.5 48.0 %collective-permute-start.3 = (bf16[1536,512]{1,0:T(8,128)(2,1)S(1)}, bf16[1536,512]{1,0:T(8,128)(2,1)}, u32[]{:S(2)}, u32[]{:S(2)}) collective-permute-start(bf16[1536,512]{1,0:T(8,128)(2,1)S(1)} %slice.18), channel_id=1, source_target_pairs={{0,32},{1,33},{2,34},{3,35},{4,36},{5,37},{6,38},{7,39},{8,40},{9,... | collective-permute-start | bytes 4718600 | tf_op jit(solution)/shard_map/ppermute | solution.py:23
  15.7 16.8 %collective-permute-start.5 = (bf16[2,128,512]{2,1,0:T(8,128)(2,1)S(1)}, bf16[2,128,512]{2,1,0:T(8,128)(2,1)S(1)}, u32[]{:S(2)}, u32[]{:S(2)}) collective-permute-start(bf16[2,128,512]{2,1,0:T(8,128)(2,1)S(1)} %pad_maximum_fusion.1), channel_id=1, source_target_pairs={{0,6},{1,3},{2,0},{3,5},{4,2},{5,7},{6,4},{7,1},{8,14},{9,11},{10,... | collective-permute-start | bytes 786440 | tf_op jit(solution)/shard_map/ppermute | solution.py:23
  22.2 14.1 %collective-permute-start.4 = (bf16[2,128,512]{2,1,0:T(8,128)(2,1)S(1)}, bf16[2,128,512]{2,1,0:T(8,128)(2,1)S(1)}, u32[]{:S(2)}, u32[]{:S(2)}) collective-permute-start(bf16[2,128,512]{2,1,0:T(8,128)(2,1)S(1)} %pad_maximum_fusion.1), channel_id=1, source_target_pairs={{0,2},{1,7},{2,4},{3,1},{4,6},{5,3},{6,0},{7,5},{8,10},{9,15},{10,... | collective-permute-start | bytes 786440 | tf_op jit(solution)/shard_map/ppermute | solution.py:23
  22.2 15.0 %collective-permute-start.7 = (bf16[1,2,128,512]{3,2,1,0:T(8,128)(2,1)S(1)}, bf16[1,2,128,512]{3,2,1,0:T(8,128)(2,1)S(1)}, u32[]{:S(2)}, u32[]{:S(2)}) collective-permute-start(bf16[1,2,128,512]{3,2,1,0:T(8,128)(2,1)S(1)} %bitcast.27), channel_id=1, source_target_pairs={{0,24},{1,9},{2,26},{3,11},{4,28},{5,13},{6,30},{7,15},{8,0},{9,17... | collective-permute-start | bytes 786440 | tf_op jit(solution)/shard_map/ppermute | solution.py:23
  32.6 7.6 %collective-permute-start.6 = (bf16[1,2,128,512]{3,2,1,0:T(8,128)(2,1)S(1)}, bf16[1,2,128,512]{3,2,1,0:T(8,128)(2,1)S(1)}, u32[]{:S(2)}, u32[]{:S(2)}) collective-permute-start(bf16[1,2,128,512]{3,2,1,0:T(8,128)(2,1)S(1)} %bitcast.28), channel_id=1, source_target_pairs={{0,8},{1,25},{2,10},{3,27},{4,12},{5,29},{6,14},{7,31},{8,16},{9,1... | collective-permute-start | bytes 786440 | tf_op jit(solution)/shard_map/ppermute | solution.py:23
  40.1 11.4 %collective-permute-start.10 = (bf16[2,128,512]{2,1,0:T(8,128)(2,1)S(1)}, bf16[2,128,512]{2,1,0:T(8,128)(2,1)}, u32[]{:S(2)}, u32[]{:S(2)}) collective-permute-start(bf16[2,128,512]{2,1,0:T(8,128)(2,1)S(1)} %collective-permute-done.4), channel_id=1, source_target_pairs={{0,2},{1,7},{2,4},{3,1},{4,6},{5,3},{6,0},{7,5},{8,10},{9,15},{10,... | collective-permute-start | bytes 786440 | tf_op jit(solution)/shard_map/ppermute | solution.py:23
  42.0 20.6 %collective-permute-start.9 = (bf16[2,2,128,512]{3,2,1,0:T(8,128)(2,1)S(1)}, bf16[2,2,128,512]{3,2,1,0:T(8,128)(2,1)S(1)}, u32[]{:S(2)}, u32[]{:S(2)}) collective-permute-start(bf16[2,2,128,512]{3,2,1,0:T(8,128)(2,1)S(1)} %pad_maximum_fusion.refs_4_), channel_id=1, source_target_pairs={{0,24},{1,9},{2,26},{3,11},{4,28},{5,13},{6,30},{7,15},{8,0},{9,17... | collective-permute-start | bytes 1572872 | tf_op jit(solution)/shard_map/ppermute | solution.py:23
  47.8 15.7 %collective-permute-start.8 = (bf16[2,2,128,512]{3,2,1,0:T(8,128)(2,1)S(1)}, bf16[2,2,128,512]{3,2,1,0:T(8,128)(2,1)}, u32[]{:S(2)}, u32[]{:S(2)}) collective-permute-start(bf16[2,2,128,512]{3,2,1,0:T(8,128)(2,1)S(1)} %pad_maximum_fusion.refs_4_), channel_id=1, source_target_pairs={{0,8},{1,25},{2,10},{3,27},{4,12},{5,29},{6,14},{7,31},{8,16},{9,1... | collective-permute-start | bytes 1572872 | tf_op jit(solution)/shard_map/ppermute | solution.py:23
  47.8 35.4 %collective-permute-start.12 = (bf16[2048,512]{1,0:T(8,128)(2,1)S(1)}, bf16[2048,512]{1,0:T(8,128)(2,1)}, u32[]{:S(2)}, u32[]{:S(2)}) collective-permute-start(bf16[2048,512]{1,0:T(8,128)(2,1)S(1)} %copy-done), channel_id=1, source_target_pairs={{0,1},{1,0},{2,3},{3,2},{4,5},{5,4},{6,7},{7,6},{8,9},{9,8},{10,11... | collective-permute-start | bytes 6291464 | tf_op jit(solution)/shard_map/ppermute | solution.py:23
  51.6 10.4 %collective-permute-start.11 = (bf16[1,2,128,512]{3,2,1,0:T(8,128)(2,1)S(1)}, bf16[1,2,128,512]{3,2,1,0:T(8,128)(2,1)S(1)}, u32[]{:S(2)}, u32[]{:S(2)}) collective-permute-start(bf16[1,2,128,512]{3,2,1,0:T(8,128)(2,1)S(1)} %collective-permute-done.6.refs_1_), channel_id=1, source_target_pairs={{0,8},{1,25},{2,10},{3,27},{4,12},{5,29},{6,14},{7,31},{8,16},{9,1... | collective-permute-start | bytes 786440 | tf_op jit(solution)/shard_map/ppermute | solution.py:23
  63.5 19.7 %collective-permute-start.14 = (bf16[1536,512]{1,0:T(8,128)(2,1)}, bf16[1536,512]{1,0:T(8,128)(2,1)}, u32[]{:S(2)}, u32[]{:S(2)}) collective-permute-start(bf16[1536,512]{1,0:T(8,128)(2,1)} %collective-permute-done.3.far_b), channel_id=1, source_target_pairs={{0,1},{1,0},{2,3},{3,2},{4,5},{5,4},{6,7},{7,6},{8,9},{9,8},{10,11... | collective-permute-start | bytes 4718600 | tf_op jit(solution)/shard_map/ppermute | solution.py:23
  63.5 3.8 %collective-permute-start.13 = (bf16[512,512]{1,0:T(8,128)(2,1)S(1)}, bf16[512,512]{1,0:T(8,128)(2,1)S(1)}, u32[]{:S(2)}, u32[]{:S(2)}) collective-permute-start(bf16[512,512]{1,0:T(8,128)(2,1)S(1)} %collective-permute-done.2.far_a), channel_id=1, source_target_pairs={{0,1},{1,0},{2,3},{3,2},{4,5},{5,4},{6,7},{7,6},{8,9},{9,8},{10,11... | collective-permute-start | bytes 1572872 | tf_op jit(solution)/shard_map/ppermute | solution.py:23
  64.0 7.9 %collective-permute-start.16 = (bf16[1,2,128,512]{3,2,1,0:T(8,128)(2,1)}, bf16[1,2,128,512]{3,2,1,0:T(8,128)(2,1)}, u32[]{:S(2)}, u32[]{:S(2)}) collective-permute-start(bf16[1,2,128,512]{3,2,1,0:T(8,128)(2,1)} %bitcast.21.refs_8_), channel_id=1, source_target_pairs={{0,8},{1,25},{2,10},{3,27},{4,12},{5,29},{6,14},{7,31},{8,16},{9,1... | collective-permute-start | bytes 786440 | tf_op jit(solution)/shard_map/ppermute | solution.py:23
  64.0 19.1 %collective-permute-start.15 = (bf16[2,2,128,512]{3,2,1,0:T(8,128)(2,1)}, bf16[2,2,128,512]{3,2,1,0:T(8,128)(2,1)}, u32[]{:S(2)}, u32[]{:S(2)}) collective-permute-start(bf16[2,2,128,512]{3,2,1,0:T(8,128)(2,1)} %collective-permute-done.8.refs_5_), channel_id=1, source_target_pairs={{0,8},{1,25},{2,10},{3,27},{4,12},{5,29},{6,14},{7,31},{8,16},{9,1... | collective-permute-start | bytes 1572872 | tf_op jit(solution)/shard_map/ppermute | solution.py:23
  68.1 9.7 %collective-permute-start.17 = (bf16[1,2,128,512]{3,2,1,0:T(8,128)(2,1)}, bf16[1,2,128,512]{3,2,1,0:T(8,128)(2,1)}, u32[]{:S(2)}, u32[]{:S(2)}) collective-permute-start(bf16[1,2,128,512]{3,2,1,0:T(8,128)(2,1)} %bitcast.21.refs_8_), channel_id=1, source_target_pairs={{0,24},{1,9},{2,26},{3,11},{4,28},{5,13},{6,30},{7,15},{8,0},{9,17... | collective-permute-start | bytes 786440 | tf_op jit(solution)/shard_map/ppermute | solution.py:23
  71.9 11.2 %collective-permute-start.18 = (bf16[1,2,128,512]{3,2,1,0:T(8,128)(2,1)}, bf16[1,2,128,512]{3,2,1,0:T(8,128)(2,1)}, u32[]{:S(2)}, u32[]{:S(2)}) collective-permute-start(bf16[1,2,128,512]{3,2,1,0:T(8,128)(2,1)} %collective-permute-done.16.refs_9_), channel_id=1, source_target_pairs={{0,8},{1,25},{2,10},{3,27},{4,12},{5,29},{6,14},{7,31},{8,16},{9,1... | collective-permute-start | bytes 786440 | tf_op jit(solution)/shard_map/ppermute | solution.py:23
  97.3 21.5 %copy-start.1 = (s32[2,256,64]{1,2,0:T(8,128)S(1)}, s32[2,256,64]{1,2,0:T(8,128)}, u32[]{:S(2)}) copy-start(s32[2,256,64]{1,2,0:T(8,128)} %param.5) | copy-start | bytes 393220
  117.1 1.6 %collective-permute-start.19 = (f32[128,512]{1,0:T(8,128)S(1)}, f32[128,512]{1,0:T(8,128)S(1)}, u32[]{:S(2)}, u32[]{:S(2)}) collective-permute-start(f32[128,512]{1,0:T(8,128)S(1)} %get-tuple-element.27), channel_id=1, source_target_pairs={{0,1},{1,0},{2,3},{3,2},{4,5},{5,4},{6,7},{7,6},{8,9},{9,8},{10,11... | collective-permute-start | bytes 786440 | tf_op jit(solution)/shard_map/ppermute | solution.py:23
  124.2 1.3 collective-permute-start.20
  125.5 5.3 %collective-permute-start.23 = (f32[17,256]{1,0:T(8,128)S(1)}, f32[17,256]{1,0:T(8,128)S(1)}, u32[]{:S(2)}, u32[]{:S(2)}) collective-permute-start(f32[17,256]{1,0:T(8,128)S(1)} %add.271), channel_id=1, source_target_pairs={{0,16},{1,17},{2,18},{3,19},{4,20},{5,21},{6,22},{7,23},{8,24},{9,... | collective-permute-start | bytes 52232 | tf_op jit(solution)/shard_map/ppermute | solution.py:23
  125.5 5.3 %collective-permute-start.22 = (f32[17,256]{1,0:T(8,128)S(1)}, f32[17,256]{1,0:T(8,128)S(1)}, u32[]{:S(2)}, u32[]{:S(2)}) collective-permute-start(f32[17,256]{1,0:T(8,128)S(1)} %add.271), channel_id=1, source_target_pairs={{0,24},{1,25},{2,26},{3,27},{4,28},{5,29},{6,30},{7,31},{8,0},{9,1... | collective-permute-start | bytes 52232 | tf_op jit(solution)/shard_map/ppermute | solution.py:23
  127.7 5.0 %collective-permute-start.21 = (f32[17,256]{1,0:T(8,128)S(1)}, f32[17,256]{1,0:T(8,128)S(1)}, u32[]{:S(2)}, u32[]{:S(2)}) collective-permute-start(f32[17,256]{1,0:T(8,128)S(1)} %add.271), channel_id=1, source_target_pairs={{0,8},{1,9},{2,10},{3,11},{4,12},{5,13},{6,14},{7,15},{8,16},{9,17... | collective-permute-start | bytes 52232 | tf_op jit(solution)/shard_map/ppermute | solution.py:23
  132.8 7.9 %collective-permute-start.26 = (f32[17,256]{1,0:T(8,128)S(1)}, f32[17,256]{1,0:T(8,128)S(1)}, u32[]{:S(2)}, u32[]{:S(2)}) collective-permute-start(f32[17,256]{1,0:T(8,128)S(1)} %add_add_fusion.1), channel_id=1, source_target_pairs={{0,4},{1,5},{2,6},{3,7},{4,0},{5,1},{6,2},{7,3},{8,12},{9,13},{10,... | collective-permute-start | bytes 52232 | tf_op jit(solution)/shard_map/ppermute | solution.py:23
  135.1 5.6 %collective-permute-start.25 = (f32[17,256]{1,0:T(8,128)S(1)}, f32[17,256]{1,0:T(8,128)S(1)}, u32[]{:S(2)}, u32[]{:S(2)}) collective-permute-start(f32[17,256]{1,0:T(8,128)S(1)} %add_add_fusion.1), channel_id=1, source_target_pairs={{0,6},{1,7},{2,0},{3,1},{4,2},{5,3},{6,4},{7,5},{8,14},{9,15},{10,... | collective-permute-start | bytes 52232 | tf_op jit(solution)/shard_map/ppermute | solution.py:23
  136.1 5.9 %collective-permute-start.24 = (f32[17,256]{1,0:T(8,128)S(1)}, f32[17,256]{1,0:T(8,128)S(1)}, u32[]{:S(2)}, u32[]{:S(2)}) collective-permute-start(f32[17,256]{1,0:T(8,128)S(1)} %add_add_fusion.1), channel_id=1, source_target_pairs={{0,2},{1,3},{2,4},{3,5},{4,6},{5,7},{6,0},{7,1},{8,10},{9,11},{10,... | collective-permute-start | bytes 52232 | tf_op jit(solution)/shard_map/ppermute | solution.py:23
  142.1 3.8 %collective-permute-start.27 = (f32[16,256]{1,0:T(8,128)S(1)}, f32[16,256]{1,0:T(8,128)S(1)}, u32[]{:S(2)}, u32[]{:S(2)}) collective-permute-start(f32[16,256]{1,0:T(8,128)S(1)} %slice.27), channel_id=1, source_target_pairs={{0,128},{1,129},{2,130},{3,131},{4,132},{5,133},{6,134},{7,135},{8... | collective-permute-start | bytes 49160 | tf_op jit(solution)/shard_map/ppermute | solution.py:23
  145.9 4.0 %collective-permute-start.28 = (f32[16,256]{1,0:T(8,128)S(1)}, f32[16,256]{1,0:T(8,128)S(1)}, u32[]{:S(2)}, u32[]{:S(2)}) collective-permute-start(f32[16,256]{1,0:T(8,128)S(1)} %slice_add_fusion), channel_id=1, source_target_pairs={{0,32},{1,33},{2,34},{3,35},{4,36},{5,37},{6,38},{7,39},{8,40},{9,... | collective-permute-start | bytes 49160 | tf_op jit(solution)/shard_map/ppermute | solution.py:23
  149.9 5.2 %collective-permute-start.29 = (f32[16,256]{1,0:T(8,128)S(1)}, f32[16,256]{1,0:T(8,128)S(1)}, u32[]{:S(2)}, u32[]{:S(2)}) collective-permute-start(f32[16,256]{1,0:T(8,128)S(1)} %add.279), channel_id=1, source_target_pairs={{0,64},{1,65},{2,66},{3,67},{4,68},{5,69},{6,70},{7,71},{8,72},{9,... | collective-permute-start | bytes 49160 | tf_op jit(solution)/shard_map/ppermute | solution.py:23
  (12 other events, 51.6 us)

commit v4 on v3

--- a/solution.py
+++ b/solution.py
@@ -104,31 +104,37 @@
     first = core[0] == 0
     product[:half] = 2.0 * jnp.where(first, kept[...], got[...])
     product[half:] = 2.0 * jnp.where(first, got[...], kept[...])
-    totals[16:17, :] = jnp.sum(product[...].T * decoded[...], axis=0, keepdims=True)
+    rows, width = product.shape
+    turned = product[...].T
+    totals[16:17, :] = jnp.sum(turned * decoded[...], axis=0, keepdims=True)
+    weighted = (turned * scale[...]).reshape(width // 8, 8, rows)
+    high = weighted.astype(jnp.bfloat16).astype(jnp.float32)
+    both = jnp.concatenate([high, weighted - high], axis=1).astype(jnp.bfloat16)
     picks = [codes[m].astype(jnp.bfloat16) for m in range(2)]
-    rows = product.shape[0]
     words = lax.broadcasted_iota(jnp.int32, (256, rows), 0).astype(jnp.bfloat16)
-    group = lax.rem(lax.broadcasted_iota(jnp.int32, (rows, 256), 1), 128) // 8
-    sums = jnp.zeros((512, 256), jnp.float32)
-    scales = jnp.broadcast_to(scale[...], (128, rows)).T
-    for block in range(product.shape[1] // 128):
-        weighted = scales * product[:, block * 128 : (block + 1) * 128]
-        high = weighted.astype(jnp.bfloat16)
-        low = (weighted - high.astype(jnp.float32)).astype(jnp.bfloat16)
-        both = jnp.concatenate([high, low], axis=1)
-        for part in range(0, 16, 4):
-            lhs = []
-            rhs = []
-            for g in range(part, part + 4):
-                at = block * 16 + g
-                lhs.append(jnp.concatenate(
-                    [(words == picks[m][at : at + 1, :]).astype(jnp.bfloat16) for m in range(2)], axis=0))
-                rhs.append(jnp.where(group == g, both, jnp.zeros_like(both)))
-            sums += jnp.dot(jnp.concatenate(lhs, axis=1), jnp.concatenate(rhs, axis=0), preferred_element_type=jnp.float32)
-    sums = (sums[:, :128] + sums[:, 128:]).T
-    folded = jnp.sum(sums.reshape(16, 8, 512), axis=0)
-    totals[0:8, :] = folded[:, :256]
-    totals[8:16, :] = folded[:, 256:]
+    one, none = jnp.bfloat16(1), jnp.bfloat16(0)
+    sums = jnp.zeros((16, 512), jnp.float32)
+    for at in range(0, width // 8, 8):
+        chosen = [
+            jnp.concatenate(
+                [
+                    jnp.maximum(one - jnp.abs(words - picks[m][g : g + 1, :]), none)
+                    for m in range(2)
+                ],
+                axis=0,
+            )
+            for g in range(at, at + 8)
+        ]
+        sums += lax.dot_general(
+            jnp.concatenate([both[g] for g in range(at, at + 8)], axis=1),
+            jnp.concatenate(chosen, axis=1),
+            (((1,), (1,)), ((), ())),
+            preferred_element_type=jnp.float32,
+        )
+    sums = sums[:8] + sums[8:]
+    totals[0:8, :] = sums[:, :256]
+    totals[8:16, :] = sums[:, 256:]
+
 
 def finish(core, codes, row_scale, decoded, kept, got):
     half, width = kept.shape
@@ -138,14 +144,33 @@
         out_shape=(jax.ShapeDtypeStruct((rows, width), jnp.float32), jax.ShapeDtypeStruct((17, 256), jnp.float32)),
         in_specs=[pl.BlockSpec(memory_space=pltpu.SMEM)] + [pl.BlockSpec(memory_space=pltpu.VMEM)] * 5,
         out_specs=(pl.BlockSpec(memory_space=pltpu.VMEM),) * 2,
-        compiler_params=pltpu.CompilerParams(vmem_limit_bytes=24 * 2**20),
+        compiler_params=pltpu.CompilerParams(vmem_limit_bytes=16 * 2**20),
         cost_estimate=pl.CostEstimate(flops=2**32, bytes_accessed=2**21, transcendentals=0),
         name="finish",
     )(core.reshape(1), codes, row_scale.reshape(1, rows), decoded, kept, got)
 
-def matmul_kernel(slots, own, far_a, far_b, across, across_a, across_b, *refs):
-    blocks = refs[:-3]
-    out, held, sem = refs[-3:]
+def matmul_kernel(slots, own, far, across, far_across, *refs):
+    blocks = refs[:-4]
+    out, held, hess, sem = refs[-4:]
+    depth, width = 512, own.shape[1]
+
+    def fetch(part):
+        at = part * depth
+        tiles = (own, across) if at < own.shape[0] else (far, far_across)
+        copies = [
+            pltpu.make_async_copy(
+                tile.at[pl.ds(at % own.shape[0], depth)],
+                hess.at[pl.ds(at, depth), pl.ds(side * width, width)],
+                sem.at[2 * part + side],
+            )
+            for side, tile in enumerate(tiles)
+        ]
+        for copy in copies:
+            copy.start()
+        return copies
+
+    parts = hess.shape[0] // depth
+    fetched = [fetch(0)]
     copies = []
     for group in blocks:
         for place in range(group.shape[0]):
@@ -157,27 +182,24 @@
                     pltpu.make_async_copy(
                         group.at[place, side],
                         held.at[pl.ds(rows, 128), pl.ds(columns, 512)],
-                        sem.at[n],
+                        sem.at[2 * parts + n],
                     )
                 )
-    for copy in copies:
-        copy.start()
+                copies[-1].start()
+    fetched += [fetch(part) for part in range(1, parts)]
     for copy in copies:
         copy.wait()
-    for side, tiles in enumerate(((own, far_a, far_b), (across, across_a, across_b))):
-        total = None
-        at = 0
-        for tile in tiles:
-            depth = tile.shape[0]
-            term = jnp.dot(
-                held[:, at : at + depth], tile[...], preferred_element_type=jnp.float32
-            )
-            total = term if total is None else total + term
-            at += depth
-        for s in range(4):
-            out[s, :, side * 512 : (side + 1) * 512] = total[s * 128 : (s + 1) * 128].astype(
-                out.dtype
-            )
+    total = None
+    for part in range(parts):
+        for copy in fetched[part]:
+            copy.wait()
+        at = part * depth
+        term = jnp.dot(
+            held[:, at : at + depth], hess[at : at + depth], preferred_element_type=jnp.float32
+        )
+        total = term if total is None else total + term
+    for s in range(4):
+        out[s] = total[s * 128 : (s + 1) * 128].astype(out.dtype)
 
 
 def body(codes, codebooks, row_scale, initial, hessian):
@@ -187,7 +209,6 @@
     half = rows // 2
     z_lo, y_hi, y_lo, x, z_hi, core = (lax.axis_index(a) for a in AXES)
 
-    far_a = shift(hessian[:512], "y_lo", 1)
     across = shift(hessian, "core", 1)
 
     decoded, error = decode(codes, codebooks, row_scale, initial)
@@ -198,22 +219,25 @@
     cross = send(other, lambda *p: to_plane(*p)[:-1] + (1 - p[-1],))
     block = jnp.stack([same, cross])
 
-    rest, block, far_a = lax.optimization_barrier((hessian[512:], block, far_a))
-    far_b = shift(rest, "y_lo", 1)
+    mine, block, across = lax.optimization_barrier((hessian, block, across))
+    far = shift(mine, "y_lo", 1)
 
     own = block[None]
     z_back, z_on = turn(block, "z_hi", 1), turn(block, "z_hi", -1)
     own_back, own_on = turn(own, "x", 1), turn(own, "x", -1)
-    near, z_back, own_back, own_on = lax.optimization_barrier(
-        (jnp.stack([z_back, z_on]), z_back, own_back, own_on)
+    own_two = turn(own_back, "x", 1)
+    near, own_on, own_two = lax.optimization_barrier(
+        (jnp.stack([z_back, z_on]), own_on, own_two)
     )
-    z_two, own_two = turn(z_back, "z_hi", 1), turn(own_back, "x", 1)
     near_back, near_on = turn(near, "x", 1), turn(near, "x", -1)
-    last = z_two[None]
+    last = turn(z_back, "z_hi", 1)[None]
     last_back, last_on = turn(last, "x", 1), turn(last, "x", -1)
+    near_back, near_on, last_back, last_on = lax.optimization_barrier(
+        (near_back, near_on, last_back, last_on)
+    )
     near_two, last_two = turn(near_back, "x", 1), turn(last_back, "x", 1)
-    far_b, *_ = lax.optimization_barrier((far_b, near_back, near_on, z_two, own_two))
-    across_a, across_b = shift(far_a, "core", 1), shift(far_b, "core", 1)
+    far, near_two, last_two = lax.optimization_barrier((far, near_two, last_two))
+    far_across = shift(far, "core", 1)
     wide = (
         (own, own_back, own_on, own_two),
         (near, near_back, near_on, near_two),
@@ -238,19 +262,19 @@
         matmul_kernel,
         out_shape=jax.ShapeDtypeStruct((4, half, 2 * width), jnp.bfloat16),
         in_specs=[pl.BlockSpec(memory_space=pltpu.SMEM)]
-        + [pl.BlockSpec(memory_space=pltpu.VMEM)] * 6
-        + [pl.BlockSpec(memory_space=pl.ANY)] * len(blocks),
+        + [pl.BlockSpec(memory_space=pl.ANY)] * (4 + len(blocks)),
         out_specs=pl.BlockSpec(memory_space=pltpu.VMEM),
         scratch_shapes=[
             pltpu.VMEM((4 * half, 8 * width), jnp.bfloat16),
-            pltpu.SemaphoreType.DMA((32,)),
+            pltpu.VMEM((8 * width, 2 * width), jnp.bfloat16),
+            pltpu.SemaphoreType.DMA((48,)),
         ],
-        compiler_params=pltpu.CompilerParams(vmem_limit_bytes=32 * 2**20),
+        compiler_params=pltpu.CompilerParams(vmem_limit_bytes=20 * 2**20),
         cost_estimate=pl.CostEstimate(
             flops=2 * 512 * 4096 * 1024, bytes_accessed=13 * 2**20, transcendentals=0
         ),
         name="matmul",
-    )(slots, hessian, far_a, far_b, across, across_a, across_b, *blocks)
+    )(slots, hessian, far, across, far_across, *blocks)
 
     parts = lax.all_to_all(partial, ("z_lo", "y_hi"), 0, 0, tiled=True)
     summed = jnp.sum(parts.astype(jnp.float32), axis=0)
@@ -262,9 +286,8 @@
     for axis in ("x", "z_hi"):
         total = total + shift(total, axis, 1) + shift(total, axis, -1) + shift(total, axis, 2)
     scale_total, books = total[16], total[:16]
-    books = books + shift(books, "z_lo", 1)
-    books = books + shift(books, "y_lo", 1)
-    books = books + shift(books, "y_hi", 1)
+    copies = jnp.broadcast_to(books, (8, *books.shape))
+    books = jnp.sum(lax.all_to_all(copies, ROW, 0, 0, tiled=True), axis=0)
     full_width = width * 32
     all_groups = rows * 8 * (full_width // 8)
     scale_grad = scale_total / full_width

time: 157 us -> 156 us (level)
  waiting for transfers between devices: 55.9 us -> 46.7 us
  starting transfers between devices: 47.4 us -> 54.9 us
  local copies, waits for them, and re-layouts: 12.6 us -> 16.5 us
  Pallas kernels: 18 us -> 16.1 us
    ppermute x30 -> x25, waiting for transfers between devices: 55.9 us -> 42.2 us  [send(): return lax.ppermute(a, AXES, pairs)]
    unnamed x28 -> x44, local copies, waits for them, and re-layouts: 8.66 us -> 14.6 us
    all_to_all x0 -> x1, waiting for transfers between devices: none -> 4.54 us  [body(): books = jnp.sum(lax.all_to_all(copies, ROW, 0, 0, tiled=True), axis=0)]
    all_to_all x0 -> x1, starting transfers between devices: none -> 3.87 us  [body(): books = jnp.sum(lax.all_to_all(copies, ROW, 0, 0, tiled=True), axis=0)]
    ppermute x30 -> x25, starting transfers between devices: 47.4 us -> 51 us  [send(): return lax.ppermute(a, AXES, pairs)]
    slice x2 -> x0, local copies, waits for them, and re-layouts: 2.72 us -> none  [the longest x1 1.64 us: body(): rest, block, far_a = lax.optimization_barrier((hessian[512:], block, far_a))]
    pallas_call x1, Pallas kernels: 9.17 us -> 7.55 us  [body(): pl.pallas_call(matmul_kernel, out_shape=jax.ShapeDtypeStruct((4, half, 2...]
  transfers between devices with their start and end apart: 30 -> 26, of which waited for: 19 -> 14; matrix products, arithmetic and copies ran while one was open for 2% -> 1% of each run, Pallas kernels for 2% -> 2%
where the time goes in v4:
time: 156 us; the launch traced here: 155 us
  starting transfers between devices  54.9 us (35%)
  waiting for transfers between devices  46.7 us (30%)
  blocking collectives  18.8 us (12%)
  local copies, waits for them, and re-layouts  16.5 us (11%)
  Pallas kernels  16.1 us (10%)
    ppermute x25, starting transfers between devices, send(): return lax.ppermute(a, AXES, pairs)  51 us
    ppermute x25, waiting for transfers between devices, send(): return lax.ppermute(a, AXES, pairs)  42.2 us
    all_to_all x1, blocking collectives, body(): parts = lax.all_to_all(partial, ('z_lo', 'y_hi'), 0, 0, tiled=True)  18.8 us
    unnamed x44, local copies, waits for them, and re-layouts  14.6 us
    pallas_call x1, Pallas kernels, body(): pl.pallas_call(matmul_kernel, out_shape=jax.ShapeDtypeStruct((4, half, 2...  7.55 us
    pallas_call x1, Pallas kernels, finish(): pl.pallas_call(finish_kernel, out_shape=(jax.ShapeDtypeStruct((rows, widt...  5.08 us
    all_to_all x1, waiting for transfers between devices, body(): books = jnp.sum(lax.all_to_all(copies, ROW, 0, 0, tiled=True), axis=0)  4.54 us
    all_to_all x1, starting transfers between devices, body(): books = jnp.sum(lax.all_to_all(copies, ROW, 0, 0, tiled=True), axis=0)  3.87 us
  transfers between devices with their start and end apart: 26, of which 14 were waited for; matrix products, arithmetic and copies ran while one was open for 1% of the time, Pallas kernels for 2%

profile of v4, /device:TPU:8, one launch (start us, length us, event | category | flops | bytes accessed | tf_op | source)
XLA Modules:
  0.0 155.3 jit_solution(9607442185523381355)
XLA Ops:
  0.8 3.5 %decode.1 = (f32[512,256]{1,0:T(8,128)}, bf16[256,512]{1,0:T(8,128)(2,1)}) custom-call(s32[2,64,256]{2,1,0:T(8,128)} %bitcast.30, bf16[2,8,256]{2,1,0:T(8,128)(2,1)} %bitcast.41, f32[1,256]{1,0:T(1,128)} %bitcast.32, bf16[256,512]{1,0:T(8,128)(2,1)} %initial_in.1), custom_call_target="tpu_custom_call" | custom-call | flops 2097152 | bytes 1048576 | tf_op jit(solution)/shard_map/decode/pallas_call | solution.py:77
  4.2 1.0 constant_dynamic-slice_fusion.1
  6.3 1.0 collective-permute-done.1
  7.4 2.3 %collective-permute-start.3 = (bf16[2048,512]{1,0:T(8,128)(2,1)}, bf16[2048,512]{1,0:T(8,128)(2,1)}, u32[]{:S(2)}, u32[]{:S(2)}) collective-permute-start(bf16[2048,512]{1,0:T(8,128)(2,1)} %own.1), channel_id=1, source_target_pairs={{0,32},{1,33},{2,34},{3,35},{4,36},{5,37},{6,38},{7,39},{8,40},{9,... | collective-permute-start | bytes 6291464 | tf_op jit(solution)/shard_map/ppermute | solution.py:23
  9.6 10.8 %collective-permute-start.7 = (bf16[1,2,128,512]{3,2,1,0:T(8,128)(2,1)S(1)}, bf16[1,2,128,512]{3,2,1,0:T(8,128)(2,1)S(1)}, u32[]{:S(2)}, u32[]{:S(2)}) collective-permute-start(bf16[1,2,128,512]{3,2,1,0:T(8,128)(2,1)S(1)} %bitcast.27), channel_id=1, source_target_pairs={{0,8},{1,25},{2,10},{3,27},{4,12},{5,29},{6,14},{7,31},{8,16},{9,1... | collective-permute-start | bytes 786440 | tf_op jit(solution)/shard_map/ppermute | solution.py:23
  20.4 3.3 %collective-permute-start.4 = (bf16[2,128,512]{2,1,0:T(8,128)(2,1)S(1)}, bf16[2,128,512]{2,1,0:T(8,128)(2,1)S(1)}, u32[]{:S(2)}, u32[]{:S(2)}) collective-permute-start(bf16[2,128,512]{2,1,0:T(8,128)(2,1)S(1)} %pad_maximum_fusion.1), channel_id=1, source_target_pairs={{0,2},{1,7},{2,4},{3,1},{4,6},{5,3},{6,0},{7,5},{8,10},{9,15},{10,... | collective-permute-start | bytes 786440 | tf_op jit(solution)/shard_map/ppermute | solution.py:23
  23.7 3.0 %collective-permute-start.5 = (bf16[2,128,512]{2,1,0:T(8,128)(2,1)S(1)}, bf16[2,128,512]{2,1,0:T(8,128)(2,1)S(1)}, u32[]{:S(2)}, u32[]{:S(2)}) collective-permute-start(bf16[2,128,512]{2,1,0:T(8,128)(2,1)S(1)} %pad_maximum_fusion.1), channel_id=1, source_target_pairs={{0,6},{1,3},{2,0},{3,5},{4,2},{5,7},{6,4},{7,1},{8,14},{9,11},{10,... | collective-permute-start | bytes 786440 | tf_op jit(solution)/shard_map/ppermute | solution.py:23
  26.7 3.8 %collective-permute-start.6 = (bf16[1,2,128,512]{3,2,1,0:T(8,128)(2,1)S(1)}, bf16[1,2,128,512]{3,2,1,0:T(8,128)(2,1)S(1)}, u32[]{:S(2)}, u32[]{:S(2)}) collective-permute-start(bf16[1,2,128,512]{3,2,1,0:T(8,128)(2,1)S(1)} %bitcast.28), channel_id=1, source_target_pairs={{0,24},{1,9},{2,26},{3,11},{4,28},{5,13},{6,30},{7,15},{8,0},{9,17... | collective-permute-start | bytes 786440 | tf_op jit(solution)/shard_map/ppermute | solution.py:23
  31.2 8.4 %collective-permute-start.11 = (bf16[2,128,512]{2,1,0:T(8,128)(2,1)S(1)}, bf16[2,128,512]{2,1,0:T(8,128)(2,1)S(1)}, u32[]{:S(2)}, u32[]{:S(2)}) collective-permute-start(bf16[2,128,512]{2,1,0:T(8,128)(2,1)S(1)} %collective-permute-done.4), channel_id=1, source_target_pairs={{0,2},{1,7},{2,4},{3,1},{4,6},{5,3},{6,0},{7,5},{8,10},{9,15},{10,... | collective-permute-start | bytes 786440 | tf_op jit(solution)/shard_map/ppermute | solution.py:23
  41.1 4.2 %collective-permute-start.10 = (bf16[2,2,128,512]{3,2,1,0:T(8,128)(2,1)S(1)}, bf16[2,2,128,512]{3,2,1,0:T(8,128)(2,1)S(1)}, u32[]{:S(2)}, u32[]{:S(2)}) collective-permute-start(bf16[2,2,128,512]{3,2,1,0:T(8,128)(2,1)S(1)} %pad_maximum_fusion.refs_4_), channel_id=1, source_target_pairs={{0,24},{1,9},{2,26},{3,11},{4,28},{5,13},{6,30},{7,15},{8,0},{9,17... | collective-permute-start | bytes 1572872 | tf_op jit(solution)/shard_map/ppermute | solution.py:23
  45.4 7.6 %collective-permute-start.13 = (bf16[1,2,128,512]{3,2,1,0:T(8,128)(2,1)S(1)}, bf16[1,2,128,512]{3,2,1,0:T(8,128)(2,1)S(1)}, u32[]{:S(2)}, u32[]{:S(2)}) collective-permute-start(bf16[1,2,128,512]{3,2,1,0:T(8,128)(2,1)S(1)} %bitcast.34), channel_id=1, source_target_pairs={{0,24},{1,9},{2,26},{3,11},{4,28},{5,13},{6,30},{7,15},{8,0},{9,17... | collective-permute-start | bytes 786440 | tf_op jit(solution)/shard_map/ppermute | solution.py:23
  53.7 6.6 %collective-permute-done.13.refs_10_ = bf16[1,2,128,512]{3,2,1,0:T(8,128)(2,1)S(1)} collective-permute-done((bf16[1,2,128,512]{3,2,1,0:T(8,128)(2,1)S(1)}, bf16[1,2,128,512]{3,2,1,0:T(8,128)(2,1)S(1)}, u32[]{:S(2)}, u32[]{:S(2)}) %collective-permute-start.13) | collective-permute-done | bytes 262176 | tf_op jit(solution)/shard_map/ppermute | solution.py:23
  61.1 5.8 %collective-permute-done.12.refs_9_ = bf16[1,2,128,512]{3,2,1,0:T(8,128)(2,1)S(1)} collective-permute-done((bf16[1,2,128,512]{3,2,1,0:T(8,128)(2,1)S(1)}, bf16[1,2,128,512]{3,2,1,0:T(8,128)(2,1)S(1)}, u32[]{:S(2)}, u32[]{:S(2)}) %collective-permute-start.12) | collective-permute-done | bytes 262176 | tf_op jit(solution)/shard_map/ppermute | solution.py:23
  68.4 11.7 %collective-permute-done.15.refs_11_ = bf16[1,2,128,512]{3,2,1,0:T(8,128)(2,1)S(1)} collective-permute-done((bf16[1,2,128,512]{3,2,1,0:T(8,128)(2,1)S(1)}, bf16[1,2,128,512]{3,2,1,0:T(8,128)(2,1)S(1)}, u32[]{:S(2)}, u32[]{:S(2)}) %collective-permute-start.15) | collective-permute-done | bytes 262176 | tf_op jit(solution)/shard_map/ppermute | solution.py:23
  81.8 4.3 %collective-permute-done.16.far_across = bf16[2048,512]{1,0:T(8,128)(2,1)} collective-permute-done((bf16[2048,512]{1,0:T(8,128)(2,1)}, bf16[2048,512]{1,0:T(8,128)(2,1)}, u32[]{:S(2)}, u32[]{:S(2)}) %collective-permute-start.16) | collective-permute-done | bytes 2097184 | tf_op jit(solution)/shard_map/ppermute | solution.py:23
  86.1 1.0 copy-done.5
  87.2 1.0 copy-done.7
  89.2 0.9 copy-done.11
  90.1 0.9 copy-done.13
  94.9 7.6 %matmul.1 = bf16[4,128,1024]{2,1,0:T(8,128)(2,1)S(1)} custom-call(s32[64]{0:T(128)S(1)} %stack.50.slots, bf16[2048,512]{1,0:T(8,128)(2,1)S(1)} %copy-done.2, bf16[2048,512]{1,0:T(8,128)(2,1)} %collective-permute-done.3.far, bf16[2048,512]{1,0:T(8,128)(2,1)} %collective-permute-done.2.across, bf16[2048,512]{1,0:T(8,128)(2,1)} %collective-permute-done.16.far_across, ...), custom_call_target="tpu_custom_call" | custom-call | flops 4294967296 | bytes 13631488 | tf_op jit(solution)/shard_map/matmul/pallas_call | solution.py:261
  102.5 18.8 %all_to_all.10 = bf16[4,128,1024]{2,1,0:T(8,128)(2,1)S(1)} all-to-all(bf16[4,128,1024]{2,1,0:T(8,128)(2,1)S(1)} %matmul.1), channel_id=1, replica_groups=mesh['z_lo'=2,'y_hi'=2,'y_lo'=2,'x'=4,'z_hi'=4,'core'=2] {'z_lo','y_hi'}, dimensions={0} | all-to-all | bytes 2097152 | tf_op jit(solution)/shard_map/all_to_all | solution.py:279
  121.6 1.5 collective-permute-done.17.got
  123.1 5.1 %finish.1 = (f32[256,512]{1,0:T(8,128)}, f32[17,256]{1,0:T(8,128)S(1)}) custom-call(s32[1]{0:T(128)} %bitcast.core, s32[2,64,256]{2,1,0:T(8,128)S(1)} %bitcast.31, f32[1,256]{1,0:T(1,128)S(1)} %bitcast.33, f32[512,256]{1,0:T(8,128)S(1)} %copy-done.3, f32[128,512]{1,0:T(8,128)S(1)} %get-tuple-element.38.kept, f32[128,512]{1,0:T(8,128)S(1)} %collective-permute-done.17.got), custom_call_target="tpu_custom_call" | custom-call | flops 4294967296 | bytes 2097152 | tf_op jit(solution)/shard_map/finish/pallas_call | solution.py:142
  128.3 1.1 collective-permute-done.18
  129.4 1.5 collective-permute-start.20
  131.5 3.3 %collective-permute-done.21 = f32[17,256]{1,0:T(8,128)S(1)} collective-permute-done((f32[17,256]{1,0:T(8,128)S(1)}, f32[17,256]{1,0:T(8,128)S(1)}, u32[]{:S(2)}, u32[]{:S(2)}) %collective-permute-start.21) | collective-permute-done | bytes 17440 | tf_op jit(solution)/shard_map/ppermute | solution.py:23
  134.8 1.1 collective-permute-done.19
  136.8 2.3 %collective-permute-start.23 = (f32[17,256]{1,0:T(8,128)S(1)}, f32[17,256]{1,0:T(8,128)S(1)}, u32[]{:S(2)}, u32[]{:S(2)}) collective-permute-start(f32[17,256]{1,0:T(8,128)S(1)} %add_add_fusion.1), channel_id=1, source_target_pairs={{0,6},{1,7},{2,0},{3,1},{4,2},{5,3},{6,4},{7,5},{8,14},{9,15},{10,... | collective-permute-start | bytes 52232 | tf_op jit(solution)/shard_map/ppermute | solution.py:23
  139.9 3.9 %collective-permute-done.24 = f32[17,256]{1,0:T(8,128)S(1)} collective-permute-done((f32[17,256]{1,0:T(8,128)S(1)}, f32[17,256]{1,0:T(8,128)S(1)}, u32[]{:S(2)}, u32[]{:S(2)}) %collective-permute-start.24) | collective-permute-done | bytes 17440 | tf_op jit(solution)/shard_map/ppermute | solution.py:23
  143.9 1.1 collective-permute-done.22
  145.7 3.9 %all-to-all-start.1 = ((f32[8,16,256]{2,1,0:T(8,128)}), f32[8,16,256]{2,1,0:T(8,128)S(1)}, u32[]{:S(2)}, u32[]{:S(2)}) async-start(f32[8,16,256]{2,1,0:T(8,128)} %broadcast_in_dim.11), calls=%async_computation.1 | async-start | bytes 262144 | tf_op jit(solution)/shard_map/all_to_all | solution.py:290
  150.1 4.5 %all-to-all-done.1 = f32[8,16,256]{2,1,0:T(8,128)S(1)} async-done(((f32[8,16,256]{2,1,0:T(8,128)}), f32[8,16,256]{2,1,0:T(8,128)S(1)}, u32[]{:S(2)}, u32[]{:S(2)}) %all-to-all-start.1) | async-done | bytes 131104 | tf_op jit(solution)/shard_map/all_to_all | solution.py:290
  (82 shorter events, 17.5 us)
Async XLA Ops:
  0.6 85.5 %copy-start.2 = (bf16[2048,512]{1,0:T(8,128)(2,1)S(1)}, bf16[2048,512]{1,0:T(8,128)(2,1)}, u32[]{:S(2)}) copy-start(bf16[2048,512]{1,0:T(8,128)(2,1)} %own.1) | copy-start | bytes 6291460
  0.6 6.7 %collective-permute-start.2 = (bf16[2048,512]{1,0:T(8,128)(2,1)}, bf16[2048,512]{1,0:T(8,128)(2,1)}, u32[]{:S(2)}, u32[]{:S(2)}) collective-permute-start(bf16[2048,512]{1,0:T(8,128)(2,1)} %own.1), channel_id=1, source_target_pairs={{0,1},{1,0},{2,3},{3,2},{4,5},{5,4},{6,7},{7,6},{8,9},{9,8},{10,11... | collective-permute-start | bytes 6291464 | tf_op jit(solution)/shard_map/ppermute | solution.py:23
  5.2 1.1 collective-permute-start
  5.9 1.4 collective-permute-start.1
  7.4 74.3 %collective-permute-start.3 = (bf16[2048,512]{1,0:T(8,128)(2,1)}, bf16[2048,512]{1,0:T(8,128)(2,1)}, u32[]{:S(2)}, u32[]{:S(2)}) collective-permute-start(bf16[2048,512]{1,0:T(8,128)(2,1)} %own.1), channel_id=1, source_target_pairs={{0,32},{1,33},{2,34},{3,35},{4,36},{5,37},{6,38},{7,39},{8,40},{9,... | collective-permute-start | bytes 6291464 | tf_op jit(solution)/shard_map/ppermute | solution.py:23
  9.6 20.9 %collective-permute-start.7 = (bf16[1,2,128,512]{3,2,1,0:T(8,128)(2,1)S(1)}, bf16[1,2,128,512]{3,2,1,0:T(8,128)(2,1)S(1)}, u32[]{:S(2)}, u32[]{:S(2)}) collective-permute-start(bf16[1,2,128,512]{3,2,1,0:T(8,128)(2,1)S(1)} %bitcast.27), channel_id=1, source_target_pairs={{0,8},{1,25},{2,10},{3,27},{4,12},{5,29},{6,14},{7,31},{8,16},{9,1... | collective-permute-start | bytes 786440 | tf_op jit(solution)/shard_map/ppermute | solution.py:23
  20.4 10.7 %collective-permute-start.4 = (bf16[2,128,512]{2,1,0:T(8,128)(2,1)S(1)}, bf16[2,128,512]{2,1,0:T(8,128)(2,1)S(1)}, u32[]{:S(2)}, u32[]{:S(2)}) collective-permute-start(bf16[2,128,512]{2,1,0:T(8,128)(2,1)S(1)} %pad_maximum_fusion.1), channel_id=1, source_target_pairs={{0,2},{1,7},{2,4},{3,1},{4,6},{5,3},{6,0},{7,5},{8,10},{9,15},{10,... | collective-permute-start | bytes 786440 | tf_op jit(solution)/shard_map/ppermute | solution.py:23
  23.7 15.9 %collective-permute-start.5 = (bf16[2,128,512]{2,1,0:T(8,128)(2,1)S(1)}, bf16[2,128,512]{2,1,0:T(8,128)(2,1)S(1)}, u32[]{:S(2)}, u32[]{:S(2)}) collective-permute-start(bf16[2,128,512]{2,1,0:T(8,128)(2,1)S(1)} %pad_maximum_fusion.1), channel_id=1, source_target_pairs={{0,6},{1,3},{2,0},{3,5},{4,2},{5,7},{6,4},{7,1},{8,14},{9,11},{10,... | collective-permute-start | bytes 786440 | tf_op jit(solution)/shard_map/ppermute | solution.py:23
  26.7 13.0 %collective-permute-start.6 = (bf16[1,2,128,512]{3,2,1,0:T(8,128)(2,1)S(1)}, bf16[1,2,128,512]{3,2,1,0:T(8,128)(2,1)S(1)}, u32[]{:S(2)}, u32[]{:S(2)}) collective-permute-start(bf16[1,2,128,512]{3,2,1,0:T(8,128)(2,1)S(1)} %bitcast.28), channel_id=1, source_target_pairs={{0,24},{1,9},{2,26},{3,11},{4,28},{5,13},{6,30},{7,15},{8,0},{9,17... | collective-permute-start | bytes 786440 | tf_op jit(solution)/shard_map/ppermute | solution.py:23
  30.6 50.3 %copy-start.8 = (bf16[1,2,128,512]{3,2,1,0:T(8,128)(2,1)}, bf16[1,2,128,512]{3,2,1,0:T(8,128)(2,1)S(1)}, u32[]{:S(2)}) copy-start(bf16[1,2,128,512]{3,2,1,0:T(8,128)(2,1)S(1)} %collective-permute-done.7.refs_1_) | copy-start | bytes 786436
  30.6 9.8 %collective-permute-start.8 = (bf16[1,2,128,512]{3,2,1,0:T(8,128)(2,1)S(1)}, bf16[1,2,128,512]{3,2,1,0:T(8,128)(2,1)S(1)}, u32[]{:S(2)}, u32[]{:S(2)}) collective-permute-start(bf16[1,2,128,512]{3,2,1,0:T(8,128)(2,1)S(1)} %collective-permute-done.7.refs_1_), channel_id=1, source_target_pairs={{0,8},{1,25},{2,10},{3,27},{4,12},{5,29},{6,14},{7,31},{8,16},{9,1... | collective-permute-start | bytes 786440 | tf_op jit(solution)/shard_map/ppermute | solution.py:23
  31.2 14.2 %collective-permute-start.11 = (bf16[2,128,512]{2,1,0:T(8,128)(2,1)S(1)}, bf16[2,128,512]{2,1,0:T(8,128)(2,1)S(1)}, u32[]{:S(2)}, u32[]{:S(2)}) collective-permute-start(bf16[2,128,512]{2,1,0:T(8,128)(2,1)S(1)} %collective-permute-done.4), channel_id=1, source_target_pairs={{0,2},{1,7},{2,4},{3,1},{4,6},{5,3},{6,0},{7,5},{8,10},{9,15},{10,... | collective-permute-start | bytes 786440 | tf_op jit(solution)/shard_map/ppermute | solution.py:23
  41.1 25.8 %collective-permute-start.10 = (bf16[2,2,128,512]{3,2,1,0:T(8,128)(2,1)S(1)}, bf16[2,2,128,512]{3,2,1,0:T(8,128)(2,1)S(1)}, u32[]{:S(2)}, u32[]{:S(2)}) collective-permute-start(bf16[2,2,128,512]{3,2,1,0:T(8,128)(2,1)S(1)} %pad_maximum_fusion.refs_4_), channel_id=1, source_target_pairs={{0,24},{1,9},{2,26},{3,11},{4,28},{5,13},{6,30},{7,15},{8,0},{9,17... | collective-permute-start | bytes 1572872 | tf_op jit(solution)/shard_map/ppermute | solution.py:23
  45.4 21.6 %collective-permute-start.9 = (bf16[2,2,128,512]{3,2,1,0:T(8,128)(2,1)S(1)}, bf16[2,2,128,512]{3,2,1,0:T(8,128)(2,1)S(1)}, u32[]{:S(2)}, u32[]{:S(2)}) collective-permute-start(bf16[2,2,128,512]{3,2,1,0:T(8,128)(2,1)S(1)} %pad_maximum_fusion.refs_4_), channel_id=1, source_target_pairs={{0,8},{1,25},{2,10},{3,27},{4,12},{5,29},{6,14},{7,31},{8,16},{9,1... | collective-permute-start | bytes 1572872 | tf_op jit(solution)/shard_map/ppermute | solution.py:23
  45.4 15.0 %collective-permute-start.13 = (bf16[1,2,128,512]{3,2,1,0:T(8,128)(2,1)S(1)}, bf16[1,2,128,512]{3,2,1,0:T(8,128)(2,1)S(1)}, u32[]{:S(2)}, u32[]{:S(2)}) collective-permute-start(bf16[1,2,128,512]{3,2,1,0:T(8,128)(2,1)S(1)} %bitcast.34), channel_id=1, source_target_pairs={{0,24},{1,9},{2,26},{3,11},{4,28},{5,13},{6,30},{7,15},{8,0},{9,17... | collective-permute-start | bytes 786440 | tf_op jit(solution)/shard_map/ppermute | solution.py:23
  53.0 13.9 %collective-permute-start.12 = (bf16[1,2,128,512]{3,2,1,0:T(8,128)(2,1)S(1)}, bf16[1,2,128,512]{3,2,1,0:T(8,128)(2,1)S(1)}, u32[]{:S(2)}, u32[]{:S(2)}) collective-permute-start(bf16[1,2,128,512]{3,2,1,0:T(8,128)(2,1)S(1)} %bitcast.35), channel_id=1, source_target_pairs={{0,8},{1,25},{2,10},{3,27},{4,12},{5,29},{6,14},{7,31},{8,16},{9,1... | collective-permute-start | bytes 786440 | tf_op jit(solution)/shard_map/ppermute | solution.py:23
  66.9 13.9 %collective-permute-start.14 = (bf16[2,2,128,512]{3,2,1,0:T(8,128)(2,1)S(1)}, bf16[2,2,128,512]{3,2,1,0:T(8,128)(2,1)S(1)}, u32[]{:S(2)}, u32[]{:S(2)}) collective-permute-start(bf16[2,2,128,512]{3,2,1,0:T(8,128)(2,1)S(1)} %collective-permute-done.9.refs_5_), channel_id=1, source_target_pairs={{0,8},{1,25},{2,10},{3,27},{4,12},{5,29},{6,14},{7,31},{8,16},{9,1... | collective-permute-start | bytes 1572872 | tf_op jit(solution)/shard_map/ppermute | solution.py:23
  67.7 12.4 %collective-permute-start.15 = (bf16[1,2,128,512]{3,2,1,0:T(8,128)(2,1)S(1)}, bf16[1,2,128,512]{3,2,1,0:T(8,128)(2,1)S(1)}, u32[]{:S(2)}, u32[]{:S(2)}) collective-permute-start(bf16[1,2,128,512]{3,2,1,0:T(8,128)(2,1)S(1)} %collective-permute-done.12.refs_9_), channel_id=1, source_target_pairs={{0,8},{1,25},{2,10},{3,27},{4,12},{5,29},{6,14},{7,31},{8,16},{9,1... | collective-permute-start | bytes 786440 | tf_op jit(solution)/shard_map/ppermute | solution.py:23
  81.6 4.5 %collective-permute-start.16 = (bf16[2048,512]{1,0:T(8,128)(2,1)}, bf16[2048,512]{1,0:T(8,128)(2,1)}, u32[]{:S(2)}, u32[]{:S(2)}) collective-permute-start(bf16[2048,512]{1,0:T(8,128)(2,1)} %collective-permute-done.3.far), channel_id=1, source_target_pairs={{0,1},{1,0},{2,3},{3,2},{4,5},{5,4},{6,7},{7,6},{8,9},{9,8},{10,11... | collective-permute-start | bytes 6291464 | tf_op jit(solution)/shard_map/ppermute | solution.py:23
  86.1 1.0 copy-start.5
  102.4 20.7 %copy-start = (s32[2,256,64]{1,2,0:T(8,128)S(1)}, s32[2,256,64]{1,2,0:T(8,128)}, u32[]{:S(2)}) copy-start(s32[2,256,64]{1,2,0:T(8,128)} %param.5) | copy-start | bytes 393220
  102.5 20.7 %copy-start.1 = (f32[256]{0:T(256)S(1)}, f32[256]{0:T(256)}, u32[]{:S(2)}) copy-start(f32[256]{0:T(256)} %param.7) | copy-start | bytes 3076
  102.5 20.7 %copy-start.3 = (f32[512,256]{1,0:T(8,128)S(1)}, f32[512,256]{1,0:T(8,128)}, u32[]{:S(2)}) copy-start(f32[512,256]{1,0:T(8,128)} %get-tuple-element.20.decoded) | copy-start | bytes 1572868
  121.5 1.6 %collective-permute-start.17 = (f32[128,512]{1,0:T(8,128)S(1)}, f32[128,512]{1,0:T(8,128)S(1)}, u32[]{:S(2)}, u32[]{:S(2)}) collective-permute-start(f32[128,512]{1,0:T(8,128)S(1)} %get-tuple-element.37), channel_id=1, source_target_pairs={{0,1},{1,0},{2,3},{3,2},{4,5},{5,4},{6,7},{7,6},{8,9},{9,8},{10,11... | collective-permute-start | bytes 786440 | tf_op jit(solution)/shard_map/ppermute | solution.py:23
  128.2 1.2 collective-permute-start.18
  129.4 5.4 %collective-permute-start.21 = (f32[17,256]{1,0:T(8,128)S(1)}, f32[17,256]{1,0:T(8,128)S(1)}, u32[]{:S(2)}, u32[]{:S(2)}) collective-permute-start(f32[17,256]{1,0:T(8,128)S(1)} %add.262), channel_id=1, source_target_pairs={{0,16},{1,17},{2,18},{3,19},{4,20},{5,21},{6,22},{7,23},{8,24},{9,... | collective-permute-start | bytes 52232 | tf_op jit(solution)/shard_map/ppermute | solution.py:23
  129.4 5.4 %collective-permute-start.20 = (f32[17,256]{1,0:T(8,128)S(1)}, f32[17,256]{1,0:T(8,128)S(1)}, u32[]{:S(2)}, u32[]{:S(2)}) collective-permute-start(f32[17,256]{1,0:T(8,128)S(1)} %add.262), channel_id=1, source_target_pairs={{0,24},{1,25},{2,26},{3,27},{4,28},{5,29},{6,30},{7,31},{8,0},{9,1... | collective-permute-start | bytes 52232 | tf_op jit(solution)/shard_map/ppermute | solution.py:23
  130.9 5.0 %collective-permute-start.19 = (f32[17,256]{1,0:T(8,128)S(1)}, f32[17,256]{1,0:T(8,128)S(1)}, u32[]{:S(2)}, u32[]{:S(2)}) collective-permute-start(f32[17,256]{1,0:T(8,128)S(1)} %add.262), channel_id=1, source_target_pairs={{0,8},{1,9},{2,10},{3,11},{4,12},{5,13},{6,14},{7,15},{8,16},{9,17... | collective-permute-start | bytes 52232 | tf_op jit(solution)/shard_map/ppermute | solution.py:23
  135.9 7.9 %collective-permute-start.24 = (f32[17,256]{1,0:T(8,128)S(1)}, f32[17,256]{1,0:T(8,128)S(1)}, u32[]{:S(2)}, u32[]{:S(2)}) collective-permute-start(f32[17,256]{1,0:T(8,128)S(1)} %add_add_fusion.1), channel_id=1, source_target_pairs={{0,4},{1,5},{2,6},{3,7},{4,0},{5,1},{6,2},{7,3},{8,12},{9,13},{10,... | collective-permute-start | bytes 52232 | tf_op jit(solution)/shard_map/ppermute | solution.py:23
  136.8 7.0 %collective-permute-start.23 = (f32[17,256]{1,0:T(8,128)S(1)}, f32[17,256]{1,0:T(8,128)S(1)}, u32[]{:S(2)}, u32[]{:S(2)}) collective-permute-start(f32[17,256]{1,0:T(8,128)S(1)} %add_add_fusion.1), channel_id=1, source_target_pairs={{0,6},{1,7},{2,0},{3,1},{4,2},{5,3},{6,4},{7,5},{8,14},{9,15},{10,... | collective-permute-start | bytes 52232 | tf_op jit(solution)/shard_map/ppermute | solution.py:23
  139.1 5.9 %collective-permute-start.22 = (f32[17,256]{1,0:T(8,128)S(1)}, f32[17,256]{1,0:T(8,128)S(1)}, u32[]{:S(2)}, u32[]{:S(2)}) collective-permute-start(f32[17,256]{1,0:T(8,128)S(1)} %add_add_fusion.1), channel_id=1, source_target_pairs={{0,2},{1,3},{2,4},{3,5},{4,6},{5,7},{6,0},{7,1},{8,10},{9,11},{10,... | collective-permute-start | bytes 52232 | tf_op jit(solution)/shard_map/ppermute | solution.py:23
  145.7 9.0 %all-to-all-start.1 = ((f32[8,16,256]{2,1,0:T(8,128)}), f32[8,16,256]{2,1,0:T(8,128)S(1)}, u32[]{:S(2)}, u32[]{:S(2)}) async-start(f32[8,16,256]{2,1,0:T(8,128)} %broadcast_in_dim.11), calls=%async_computation.1 | async-start | bytes 262144 | tf_op jit(solution)/shard_map/all_to_all | solution.py:290
  (16 other events, 13.6 us)

commit v5 on v4

--- a/solution.py
+++ b/solution.py
@@ -37,7 +37,9 @@
     return (x // 2, x % 2, y_lo, x + 2 * z_lo + y_hi, z_hi, core)
 
 
-def decode_kernel(codes_in, books_in, scale, initial_in, decoded, error, codes, books, initial, sem):
+def decode_kernel(
+    codes_in, books_in, scale, initial_in, decoded, mine, other, codes, books, initial, error, sem
+):
     copies = [
         pltpu.make_async_copy(a, b, sem.at[i])
         for i, (a, b) in enumerate(
@@ -67,9 +69,11 @@
                 total = found if total is None else total + found
             decoded[8 * g : 8 * g + 8, lane : lane + 128] = total
     copies[2].wait()
-    error[...] = ((scale[...] * decoded[...]).T - initial[...].astype(jnp.float32)).astype(
-        error.dtype
-    )
+    error[...] = (scale[...] * decoded[...]).T - initial[...].astype(jnp.float32)
+    half = rows // 2
+    core = lax.axis_index("core")
+    mine[...] = error[pl.ds(pl.multiple_of(core * half, half), half)].astype(mine.dtype)
+    other[...] = error[pl.ds(pl.multiple_of((1 - core) * half, half), half)].astype(mine.dtype)
 
 
 def decode(codes, codebooks, row_scale, initial):
@@ -78,7 +82,8 @@
         decode_kernel,
         out_shape=(
             jax.ShapeDtypeStruct((width, rows), jnp.float32),
-            jax.ShapeDtypeStruct((rows, width), jnp.bfloat16),
+            jax.ShapeDtypeStruct((rows // 2, width), jnp.bfloat16),
+            jax.ShapeDtypeStruct((rows // 2, width), jnp.bfloat16),
         ),
         in_specs=[
             pl.BlockSpec(memory_space=pl.ANY),
@@ -86,11 +91,12 @@
             pl.BlockSpec(memory_space=pltpu.VMEM),
             pl.BlockSpec(memory_space=pl.ANY),
         ],
-        out_specs=(pl.BlockSpec(memory_space=pltpu.VMEM),) * 2,
+        out_specs=(pl.BlockSpec(memory_space=pltpu.VMEM),) * 3,
         scratch_shapes=[
             pltpu.VMEM(codes.shape, codes.dtype),
             pltpu.VMEM(codebooks.shape, codebooks.dtype),
             pltpu.VMEM(initial.shape, initial.dtype),
+            pltpu.VMEM(initial.shape, jnp.float32),
             pltpu.SemaphoreType.DMA((3,)),
         ],
         compiler_params=pltpu.CompilerParams(vmem_limit_bytes=60 * 2**20),
@@ -99,9 +105,9 @@
     )(codes, codebooks, row_scale.reshape(1, rows), initial)
 
 
-def finish_kernel(core, codes, scale, decoded, kept, got, product, totals):
+def finish_kernel(codes, scale, decoded, kept, got, product, totals):
     half = kept.shape[0]
-    first = core[0] == 0
+    first = lax.axis_index("core") == 0
     product[:half] = 2.0 * jnp.where(first, kept[...], got[...])
     product[half:] = 2.0 * jnp.where(first, got[...], kept[...])
     rows, width = product.shape
@@ -136,20 +142,20 @@
     totals[8:16, :] = sums[:, 256:]
 
 
-def finish(core, codes, row_scale, decoded, kept, got):
+def finish(codes, row_scale, decoded, kept, got):
     half, width = kept.shape
     rows = 2 * half
     return pl.pallas_call(
         finish_kernel,
         out_shape=(jax.ShapeDtypeStruct((rows, width), jnp.float32), jax.ShapeDtypeStruct((17, 256), jnp.float32)),
-        in_specs=[pl.BlockSpec(memory_space=pltpu.SMEM)] + [pl.BlockSpec(memory_space=pltpu.VMEM)] * 5,
+        in_specs=[pl.BlockSpec(memory_space=pltpu.VMEM)] * 5,
         out_specs=(pl.BlockSpec(memory_space=pltpu.VMEM),) * 2,
         compiler_params=pltpu.CompilerParams(vmem_limit_bytes=16 * 2**20),
         cost_estimate=pl.CostEstimate(flops=2**32, bytes_accessed=2**21, transcendentals=0),
         name="finish",
-    )(core.reshape(1), codes, row_scale.reshape(1, rows), decoded, kept, got)
-
-def matmul_kernel(slots, own, far, across, far_across, *refs):
+    )(codes, row_scale.reshape(1, rows), decoded, kept, got)
+
+def matmul_kernel(own, far, across, far_across, *refs):
     blocks = refs[:-4]
     out, held, hess, sem = refs[-4:]
     depth, width = 512, own.shape[1]
@@ -171,17 +177,24 @@
 
     parts = hess.shape[0] // depth
     fetched = [fetch(0)]
+    z_lo, y_hi, y_lo, x, z_hi, core = (lax.axis_index(a) for a in AXES)
+    step = 1 - 2 * core
     copies = []
-    for group in blocks:
-        for place in range(group.shape[0]):
+    for at, (dx, dzs) in enumerate((dx, dzs) for dzs in ((0,), (1, 3), (2,)) for dx in (0, 1, 3, 2)):
+        for place, dz in enumerate(dzs):
+            from_x = (x + 8 - step * dx) % 4
+            from_z = (z_hi + 8 - step * dz) % 4
+            s = (from_x + 8 - 2 * z_lo - y_hi) % 4
+            tile = (from_z // 2 + y_lo) % 2
             for side in range(2):
                 n = len(copies)
-                rows = pl.multiple_of(slots[2 * n] * 128, 128)
-                columns = pl.multiple_of(slots[2 * n + 1] * 512, 512)
+                part = tile * 4 + (from_z % 2) * 2 + (core + side) % 2
+                rows = pl.multiple_of(s * 128, 128)
+                columns = pl.multiple_of(part * width, width)
                 copies.append(
                     pltpu.make_async_copy(
-                        group.at[place, side],
-                        held.at[pl.ds(rows, 128), pl.ds(columns, 512)],
+                        blocks[at].at[place, side],
+                        held.at[pl.ds(rows, 128), pl.ds(columns, width)],
                         sem.at[2 * parts + n],
                     )
                 )
@@ -207,20 +220,16 @@
     words = codebooks.shape[1]
     codes, codebooks = jnp.swapaxes(codes, 1, 2), jnp.swapaxes(codebooks, 1, 2)
     half = rows // 2
-    z_lo, y_hi, y_lo, x, z_hi, core = (lax.axis_index(a) for a in AXES)
 
     across = shift(hessian, "core", 1)
 
-    decoded, error = decode(codes, codebooks, row_scale, initial)
-
-    mine = lax.dynamic_slice_in_dim(error, core * half, half, 0)
-    other = lax.dynamic_slice_in_dim(error, (1 - core) * half, half, 0)
+    decoded, mine, other = decode(codes, codebooks, row_scale, initial)
     same = send(mine, to_plane)
     cross = send(other, lambda *p: to_plane(*p)[:-1] + (1 - p[-1],))
     block = jnp.stack([same, cross])
 
-    mine, block, across = lax.optimization_barrier((hessian, block, across))
-    far = shift(mine, "y_lo", 1)
+    tile, block, across = lax.optimization_barrier((hessian, block, across))
+    far = shift(tile, "y_lo", 1)
 
     own = block[None]
     z_back, z_on = turn(block, "z_hi", 1), turn(block, "z_hi", -1)
@@ -244,25 +253,11 @@
         (last, last_back, last_on, last_two),
     )
 
-    step = 1 - 2 * core
-    slots = []
-    for dzs in ((0,), (1, 3), (2,)):
-        for dx in (0, 1, 3, 2):
-            for dz in dzs:
-                from_x = (x - step * dx) % 4
-                from_z = (z_hi - step * dz) % 4
-                s = (from_x - 2 * z_lo - y_hi) % 4
-                tile = (from_z // 2) ^ y_lo
-                for side in range(2):
-                    slots += [s, tile * 4 + (from_z % 2) * 2 + (core ^ side)]
-    slots = jnp.stack(slots).astype(jnp.int32)
-
     blocks = [b for group in wide for b in group]
     partial = pl.pallas_call(
         matmul_kernel,
         out_shape=jax.ShapeDtypeStruct((4, half, 2 * width), jnp.bfloat16),
-        in_specs=[pl.BlockSpec(memory_space=pltpu.SMEM)]
-        + [pl.BlockSpec(memory_space=pl.ANY)] * (4 + len(blocks)),
+        in_specs=[pl.BlockSpec(memory_space=pl.ANY)] * (4 + len(blocks)),
         out_specs=pl.BlockSpec(memory_space=pltpu.VMEM),
         scratch_shapes=[
             pltpu.VMEM((4 * half, 8 * width), jnp.bfloat16),
@@ -274,13 +269,13 @@
             flops=2 * 512 * 4096 * 1024, bytes_accessed=13 * 2**20, transcendentals=0
         ),
         name="matmul",
-    )(slots, hessian, far, across, far_across, *blocks)
+    )(hessian, far, across, far_across, *blocks)
 
     parts = lax.all_to_all(partial, ("z_lo", "y_hi"), 0, 0, tiled=True)
     summed = jnp.sum(parts.astype(jnp.float32), axis=0)
     kept, given = summed[:, :width], summed[:, width:]
     got = shift(given, "core", 1)
-    product, total = finish(core, codes, row_scale, decoded, kept, got)
+    product, total = finish(codes, row_scale, decoded, kept, got)
 
     total = total + shift(total, "core", 1)
     for axis in ("x", "z_hi"):

time: 156 us -> 144 us (0.923)
  local copies, waits for them, and re-layouts: 16.5 us -> 2.32 us
  starting transfers between devices: 54.9 us -> 56.9 us
    unnamed x44 -> x8, local copies, waits for them, and re-layouts: 14.6 us -> 1.61 us
  transfers between devices with their start and end apart: 26 -> 26, of which waited for: 14 -> 15; matrix products, arithmetic and copies ran while one was open for 1% -> 0% of each run, Pallas kernels for 2% -> 2%
where the time goes in v5:
time: 144 us
  starting transfers between devices  56.9 us (40%)
  waiting for transfers between devices  48 us (33%)
  blocking collectives  18.8 us (13%)
  Pallas kernels  15.7 us (11%)
  local copies, waits for them, and re-layouts  2.32 us (2%)
  other arithmetic  1.47 us (1%)
    ppermute x25, starting transfers between devices, send(): return lax.ppermute(a, AXES, pairs)  52.1 us
    ppermute x25, waiting for transfers between devices, send(): return lax.ppermute(a, AXES, pairs)  43.4 us
    all_to_all x1, blocking collectives, body(): parts = lax.all_to_all(partial, ('z_lo', 'y_hi'), 0, 0, tiled=True)  18.8 us
    pallas_call x1, Pallas kernels, body(): pl.pallas_call(matmul_kernel, out_shape=jax.ShapeDtypeStruct((4, half, 2...  7.25 us
    pallas_call x1, Pallas kernels, finish(): pl.pallas_call(finish_kernel, out_shape=(jax.ShapeDtypeStruct((rows, widt...  5.08 us
    all_to_all x1, starting transfers between devices, body(): books = jnp.sum(lax.all_to_all(copies, ROW, 0, 0, tiled=True), axis=0)  4.8 us
    all_to_all x1, waiting for transfers between devices, body(): books = jnp.sum(lax.all_to_all(copies, ROW, 0, 0, tiled=True), axis=0)  4.54 us
    pallas_call x1, Pallas kernels, decode(): pl.pallas_call(decode_kernel, out_shape=(jax.ShapeDtypeStruct((width, row...  3.36 us
  transfers between devices with their start and end apart: 26, of which 15 were waited for; matrix products, arithmetic and copies ran while one was open for 0% of the time, Pallas kernels for 2%

profile of v5, /device:TPU:8, one launch (start us, length us, event | category | flops | bytes accessed | tf_op | source)
XLA Modules:
  0.0 143.9 jit_solution(16221181802596639203)
XLA Ops:
  0.7 3.4 %decode.1 = (f32[512,256]{1,0:T(8,128)}, bf16[128,512]{1,0:T(8,128)(2,1)}, bf16[128,512]{1,0:T(8,128)(2,1)}) custom-call(s32[2,64,256]{2,1,0:T(8,128)} %bitcast.17, bf16[2,8,256]{2,1,0:T(8,128)(2,1)} %bitcast.28, f32[1,256]{1,0:T(1,128)} %bitcast.19, bf16[256,512]{1,0:T(8,128)(2,1)} %initial_in.1), custom_call_target="tpu_custom_call" | custom-call | flops 2097152 | bytes 1048576 | tf_op jit(solution)/shard_map/decode/pallas_call | solution.py:81
  4.1 1.6 %collective-permute-start = (bf16[128,512]{1,0:T(8,128)(2,1)}, bf16[128,512]{1,0:T(8,128)(2,1)S(1)}, u32[]{:S(2)}, u32[]{:S(2)}) collective-permute-start(bf16[128,512]{1,0:T(8,128)(2,1)} %get-tuple-element.22), channel_id=1, source_target_pairs={{0,0},{1,1},{2,2},{3,3},{4,4},{5,5},{6,6},{7,7},{8,72},{9,73},{10,... | collective-permute-start | bytes 393224 | tf_op jit(solution)/shard_map/ppermute | solution.py:23
  6.2 1.2 collective-permute-done.1
  7.4 2.3 %collective-permute-start.3 = (bf16[2048,512]{1,0:T(8,128)(2,1)}, bf16[2048,512]{1,0:T(8,128)(2,1)S(1)}, u32[]{:S(2)}, u32[]{:S(2)}) collective-permute-start(bf16[2048,512]{1,0:T(8,128)(2,1)} %own.1), channel_id=1, source_target_pairs={{0,32},{1,33},{2,34},{3,35},{4,36},{5,37},{6,38},{7,39},{8,40},{9,... | collective-permute-start | bytes 6291464 | tf_op jit(solution)/shard_map/ppermute | solution.py:23
  9.7 9.8 %collective-permute-start.7 = (bf16[1,2,128,512]{3,2,1,0:T(8,128)(2,1)S(1)}, bf16[1,2,128,512]{3,2,1,0:T(8,128)(2,1)S(1)}, u32[]{:S(2)}, u32[]{:S(2)}) collective-permute-start(bf16[1,2,128,512]{3,2,1,0:T(8,128)(2,1)S(1)} %bitcast.14), channel_id=1, source_target_pairs={{0,8},{1,25},{2,10},{3,27},{4,12},{5,29},{6,14},{7,31},{8,16},{9,1... | collective-permute-start | bytes 786440 | tf_op jit(solution)/shard_map/ppermute | solution.py:23
  19.5 3.3 %collective-permute-start.4 = (bf16[2,128,512]{2,1,0:T(8,128)(2,1)S(1)}, bf16[2,128,512]{2,1,0:T(8,128)(2,1)S(1)}, u32[]{:S(2)}, u32[]{:S(2)}) collective-permute-start(bf16[2,128,512]{2,1,0:T(8,128)(2,1)S(1)} %pad_maximum_fusion.1), channel_id=1, source_target_pairs={{0,2},{1,7},{2,4},{3,1},{4,6},{5,3},{6,0},{7,5},{8,10},{9,15},{10,... | collective-permute-start | bytes 786440 | tf_op jit(solution)/shard_map/ppermute | solution.py:23
  22.7 3.0 %collective-permute-start.5 = (bf16[2,128,512]{2,1,0:T(8,128)(2,1)S(1)}, bf16[2,128,512]{2,1,0:T(8,128)(2,1)S(1)}, u32[]{:S(2)}, u32[]{:S(2)}) collective-permute-start(bf16[2,128,512]{2,1,0:T(8,128)(2,1)S(1)} %pad_maximum_fusion.1), channel_id=1, source_target_pairs={{0,6},{1,3},{2,0},{3,5},{4,2},{5,7},{6,4},{7,1},{8,14},{9,11},{10,... | collective-permute-start | bytes 786440 | tf_op jit(solution)/shard_map/ppermute | solution.py:23
  25.8 3.8 %collective-permute-start.6 = (bf16[1,2,128,512]{3,2,1,0:T(8,128)(2,1)S(1)}, bf16[1,2,128,512]{3,2,1,0:T(8,128)(2,1)S(1)}, u32[]{:S(2)}, u32[]{:S(2)}) collective-permute-start(bf16[1,2,128,512]{3,2,1,0:T(8,128)(2,1)S(1)} %bitcast.15), channel_id=1, source_target_pairs={{0,24},{1,9},{2,26},{3,11},{4,28},{5,13},{6,30},{7,15},{8,0},{9,17... | collective-permute-start | bytes 786440 | tf_op jit(solution)/shard_map/ppermute | solution.py:23
  30.2 8.4 %collective-permute-start.11 = (bf16[2,128,512]{2,1,0:T(8,128)(2,1)S(1)}, bf16[2,128,512]{2,1,0:T(8,128)(2,1)S(1)}, u32[]{:S(2)}, u32[]{:S(2)}) collective-permute-start(bf16[2,128,512]{2,1,0:T(8,128)(2,1)S(1)} %collective-permute-done.4), channel_id=1, source_target_pairs={{0,2},{1,7},{2,4},{3,1},{4,6},{5,3},{6,0},{7,5},{8,10},{9,15},{10,... | collective-permute-start | bytes 786440 | tf_op jit(solution)/shard_map/ppermute | solution.py:23
  38.7 4.3 %collective-permute-start.10 = (bf16[2,2,128,512]{3,2,1,0:T(8,128)(2,1)S(1)}, bf16[2,2,128,512]{3,2,1,0:T(8,128)(2,1)S(1)}, u32[]{:S(2)}, u32[]{:S(2)}) collective-permute-start(bf16[2,2,128,512]{3,2,1,0:T(8,128)(2,1)S(1)} %pad_maximum_fusion.refs_4_), channel_id=1, source_target_pairs={{0,24},{1,9},{2,26},{3,11},{4,28},{5,13},{6,30},{7,15},{8,0},{9,17... | collective-permute-start | bytes 1572872 | tf_op jit(solution)/shard_map/ppermute | solution.py:23
  43.1 0.8 collective-permute-done.11
  43.8 8.2 %collective-permute-start.13 = (bf16[1,2,128,512]{3,2,1,0:T(8,128)(2,1)S(1)}, bf16[1,2,128,512]{3,2,1,0:T(8,128)(2,1)S(1)}, u32[]{:S(2)}, u32[]{:S(2)}) collective-permute-start(bf16[1,2,128,512]{3,2,1,0:T(8,128)(2,1)S(1)} %bitcast.21), channel_id=1, source_target_pairs={{0,24},{1,9},{2,26},{3,11},{4,28},{5,13},{6,30},{7,15},{8,0},{9,17... | collective-permute-start | bytes 786440 | tf_op jit(solution)/shard_map/ppermute | solution.py:23
  52.1 6.8 %collective-permute-done.13.refs_10_ = bf16[1,2,128,512]{3,2,1,0:T(8,128)(2,1)S(1)} collective-permute-done((bf16[1,2,128,512]{3,2,1,0:T(8,128)(2,1)S(1)}, bf16[1,2,128,512]{3,2,1,0:T(8,128)(2,1)S(1)}, u32[]{:S(2)}, u32[]{:S(2)}) %collective-permute-start.13) | collective-permute-done | bytes 262176 | tf_op jit(solution)/shard_map/ppermute | solution.py:23
  58.8 5.8 %collective-permute-done.12.refs_9_ = bf16[1,2,128,512]{3,2,1,0:T(8,128)(2,1)S(1)} collective-permute-done((bf16[1,2,128,512]{3,2,1,0:T(8,128)(2,1)S(1)}, bf16[1,2,128,512]{3,2,1,0:T(8,128)(2,1)S(1)}, u32[]{:S(2)}, u32[]{:S(2)}) %collective-permute-start.12) | collective-permute-done | bytes 262176 | tf_op jit(solution)/shard_map/ppermute | solution.py:23
  64.7 13.1 %collective-permute-done.15.refs_11_ = bf16[1,2,128,512]{3,2,1,0:T(8,128)(2,1)S(1)} collective-permute-done((bf16[1,2,128,512]{3,2,1,0:T(8,128)(2,1)S(1)}, bf16[1,2,128,512]{3,2,1,0:T(8,128)(2,1)S(1)}, u32[]{:S(2)}, u32[]{:S(2)}) %collective-permute-start.15) | collective-permute-done | bytes 262176 | tf_op jit(solution)/shard_map/ppermute | solution.py:23
  77.8 4.2 %collective-permute-done.16.far_across = bf16[2048,512]{1,0:T(8,128)(2,1)S(1)} collective-permute-done((bf16[2048,512]{1,0:T(8,128)(2,1)S(1)}, bf16[2048,512]{1,0:T(8,128)(2,1)S(1)}, u32[]{:S(2)}, u32[]{:S(2)}) %collective-permute-start.16) | collective-permute-done | bytes 2097184 | tf_op jit(solution)/shard_map/ppermute | solution.py:23
  82.0 1.6 %copy-done.2 = bf16[2048,512]{1,0:T(8,128)(2,1)S(1)} copy-done((bf16[2048,512]{1,0:T(8,128)(2,1)S(1)}, bf16[2048,512]{1,0:T(8,128)(2,1)}, u32[]{:S(2)}) %copy-start.2) | copy-done | bytes 2097176
  83.6 7.2 %matmul.1 = bf16[4,128,1024]{2,1,0:T(8,128)(2,1)S(1)} custom-call(bf16[2048,512]{1,0:T(8,128)(2,1)S(1)} %copy-done.2, bf16[2048,512]{1,0:T(8,128)(2,1)S(1)} %collective-permute-done.3.far, bf16[2048,512]{1,0:T(8,128)(2,1)S(1)} %collective-permute-done.2.across, bf16[2048,512]{1,0:T(8,128)(2,1)S(1)} %collective-permute-done.16.far_across, ...), custom_call_target="tpu_custom_call" | custom-call | flops 4294967296 | bytes 13631488 | tf_op jit(solution)/shard_map/matmul/pallas_call | solution.py:257
  90.9 18.8 %all_to_all.10 = bf16[4,128,1024]{2,1,0:T(8,128)(2,1)S(1)} all-to-all(bf16[4,128,1024]{2,1,0:T(8,128)(2,1)S(1)} %matmul.1), channel_id=1, replica_groups=mesh['z_lo'=2,'y_hi'=2,'y_lo'=2,'x'=4,'z_hi'=4,'core'=2] {'z_lo','y_hi'}, dimensions={0} | all-to-all | bytes 2097152 | tf_op jit(solution)/shard_map/all_to_all | solution.py:274
  110.0 1.5 %collective-permute-done.17.got = f32[128,512]{1,0:T(8,128)S(1)} collective-permute-done((f32[128,512]{1,0:T(8,128)S(1)}, f32[128,512]{1,0:T(8,128)S(1)}, u32[]{:S(2)}, u32[]{:S(2)}) %collective-permute-start.17) | collective-permute-done | bytes 262176 | tf_op jit(solution)/shard_map/ppermute | solution.py:23
  111.5 5.1 %finish.1 = (f32[256,512]{1,0:T(8,128)}, f32[17,256]{1,0:T(8,128)S(1)}) custom-call(s32[2,64,256]{2,1,0:T(8,128)S(1)} %bitcast.18, f32[1,256]{1,0:T(1,128)S(1)} %bitcast.20, f32[512,256]{1,0:T(8,128)S(1)} %copy-done.3, f32[128,512]{1,0:T(8,128)S(1)} %get-tuple-element.40.kept, f32[128,512]{1,0:T(8,128)S(1)} %collective-permute-done.17.got), custom_call_target="tpu_custom_call" | custom-call | flops 4294967296 | bytes 2097152 | tf_op jit(solution)/shard_map/finish/pallas_call | solution.py:148
  116.7 1.1 collective-permute-done.18
  117.8 1.5 %collective-permute-start.20 = (f32[17,256]{1,0:T(8,128)S(1)}, f32[17,256]{1,0:T(8,128)S(1)}, u32[]{:S(2)}, u32[]{:S(2)}) collective-permute-start(f32[17,256]{1,0:T(8,128)S(1)} %add.21), channel_id=1, source_target_pairs={{0,24},{1,25},{2,26},{3,27},{4,28},{5,29},{6,30},{7,31},{8,0},{9,1... | collective-permute-start | bytes 52232 | tf_op jit(solution)/shard_map/ppermute | solution.py:23
  119.3 0.6 collective-permute-start.19
  119.9 3.3 %collective-permute-done.21 = f32[17,256]{1,0:T(8,128)S(1)} collective-permute-done((f32[17,256]{1,0:T(8,128)S(1)}, f32[17,256]{1,0:T(8,128)S(1)}, u32[]{:S(2)}, u32[]{:S(2)}) %collective-permute-start.21) | collective-permute-done | bytes 17440 | tf_op jit(solution)/shard_map/ppermute | solution.py:23
  123.2 1.1 collective-permute-done.19
  124.6 2.0 %collective-permute-start.23 = (f32[17,256]{1,0:T(8,128)S(1)}, f32[17,256]{1,0:T(8,128)S(1)}, u32[]{:S(2)}, u32[]{:S(2)}) collective-permute-start(f32[17,256]{1,0:T(8,128)S(1)} %add_add_fusion.1), channel_id=1, source_target_pairs={{0,6},{1,7},{2,0},{3,1},{4,2},{5,3},{6,4},{7,5},{8,14},{9,15},{10,... | collective-permute-start | bytes 52232 | tf_op jit(solution)/shard_map/ppermute | solution.py:23
  126.6 2.1 %collective-permute-start.22 = (f32[17,256]{1,0:T(8,128)S(1)}, f32[17,256]{1,0:T(8,128)S(1)}, u32[]{:S(2)}, u32[]{:S(2)}) collective-permute-start(f32[17,256]{1,0:T(8,128)S(1)} %add_add_fusion.1), channel_id=1, source_target_pairs={{0,2},{1,3},{2,4},{3,5},{4,6},{5,7},{6,0},{7,1},{8,10},{9,11},{10,... | collective-permute-start | bytes 52232 | tf_op jit(solution)/shard_map/ppermute | solution.py:23
  128.7 3.6 %collective-permute-done.24 = f32[17,256]{1,0:T(8,128)S(1)} collective-permute-done((f32[17,256]{1,0:T(8,128)S(1)}, f32[17,256]{1,0:T(8,128)S(1)}, u32[]{:S(2)}, u32[]{:S(2)}) %collective-permute-start.24) | collective-permute-done | bytes 17440 | tf_op jit(solution)/shard_map/ppermute | solution.py:23
  132.7 0.7 broadcast_in_dim.11
  133.4 4.8 %all-to-all-start.1 = ((f32[8,16,256]{2,1,0:T(8,128)}), f32[8,16,256]{2,1,0:T(8,128)S(1)}, u32[]{:S(2)}, u32[]{:S(2)}) async-start(f32[8,16,256]{2,1,0:T(8,128)} %broadcast_in_dim.11), calls=%async_computation.1 | async-start | bytes 262144 | tf_op jit(solution)/shard_map/all_to_all | solution.py:285
  138.8 4.5 %all-to-all-done.1 = f32[8,16,256]{2,1,0:T(8,128)S(1)} async-done(((f32[8,16,256]{2,1,0:T(8,128)}), f32[8,16,256]{2,1,0:T(8,128)S(1)}, u32[]{:S(2)}, u32[]{:S(2)}) %all-to-all-start.1) | async-done | bytes 131104 | tf_op jit(solution)/shard_map/all_to_all | solution.py:285
  (44 shorter events, 3.8 us)
Async XLA Ops:
  0.6 6.8 %collective-permute-start.2 = (bf16[2048,512]{1,0:T(8,128)(2,1)}, bf16[2048,512]{1,0:T(8,128)(2,1)S(1)}, u32[]{:S(2)}, u32[]{:S(2)}) collective-permute-start(bf16[2048,512]{1,0:T(8,128)(2,1)} %own.1), channel_id=1, source_target_pairs={{0,1},{1,0},{2,3},{3,2},{4,5},{5,4},{6,7},{7,6},{8,9},{9,8},{10,11... | collective-permute-start | bytes 6291464 | tf_op jit(solution)/shard_map/ppermute | solution.py:23
  4.1 2.1 %collective-permute-start = (bf16[128,512]{1,0:T(8,128)(2,1)}, bf16[128,512]{1,0:T(8,128)(2,1)S(1)}, u32[]{:S(2)}, u32[]{:S(2)}) collective-permute-start(bf16[128,512]{1,0:T(8,128)(2,1)} %get-tuple-element.22), channel_id=1, source_target_pairs={{0,0},{1,1},{2,2},{3,3},{4,4},{5,5},{6,6},{7,7},{8,72},{9,73},{10,... | collective-permute-start | bytes 393224 | tf_op jit(solution)/shard_map/ppermute | solution.py:23
  5.7 1.7 %collective-permute-start.1 = (bf16[128,512]{1,0:T(8,128)(2,1)}, bf16[128,512]{1,0:T(8,128)(2,1)S(1)}, u32[]{:S(2)}, u32[]{:S(2)}) collective-permute-start(bf16[128,512]{1,0:T(8,128)(2,1)} %get-tuple-element.23), channel_id=1, source_target_pairs={{0,1},{1,0},{2,3},{3,2},{4,5},{5,4},{6,7},{7,6},{8,73},{9,72},{10,... | collective-permute-start | bytes 393224 | tf_op jit(solution)/shard_map/ppermute | solution.py:23
  7.4 70.4 %collective-permute-start.3 = (bf16[2048,512]{1,0:T(8,128)(2,1)}, bf16[2048,512]{1,0:T(8,128)(2,1)S(1)}, u32[]{:S(2)}, u32[]{:S(2)}) collective-permute-start(bf16[2048,512]{1,0:T(8,128)(2,1)} %own.1), channel_id=1, source_target_pairs={{0,32},{1,33},{2,34},{3,35},{4,36},{5,37},{6,38},{7,39},{8,40},{9,... | collective-permute-start | bytes 6291464 | tf_op jit(solution)/shard_map/ppermute | solution.py:23
  9.7 19.9 %collective-permute-start.7 = (bf16[1,2,128,512]{3,2,1,0:T(8,128)(2,1)S(1)}, bf16[1,2,128,512]{3,2,1,0:T(8,128)(2,1)S(1)}, u32[]{:S(2)}, u32[]{:S(2)}) collective-permute-start(bf16[1,2,128,512]{3,2,1,0:T(8,128)(2,1)S(1)} %bitcast.14), channel_id=1, source_target_pairs={{0,8},{1,25},{2,10},{3,27},{4,12},{5,29},{6,14},{7,31},{8,16},{9,1... | collective-permute-start | bytes 786440 | tf_op jit(solution)/shard_map/ppermute | solution.py:23
  19.5 10.7 %collective-permute-start.4 = (bf16[2,128,512]{2,1,0:T(8,128)(2,1)S(1)}, bf16[2,128,512]{2,1,0:T(8,128)(2,1)S(1)}, u32[]{:S(2)}, u32[]{:S(2)}) collective-permute-start(bf16[2,128,512]{2,1,0:T(8,128)(2,1)S(1)} %pad_maximum_fusion.1), channel_id=1, source_target_pairs={{0,2},{1,7},{2,4},{3,1},{4,6},{5,3},{6,0},{7,5},{8,10},{9,15},{10,... | collective-permute-start | bytes 786440 | tf_op jit(solution)/shard_map/ppermute | solution.py:23
  22.7 15.9 %collective-permute-start.5 = (bf16[2,128,512]{2,1,0:T(8,128)(2,1)S(1)}, bf16[2,128,512]{2,1,0:T(8,128)(2,1)S(1)}, u32[]{:S(2)}, u32[]{:S(2)}) collective-permute-start(bf16[2,128,512]{2,1,0:T(8,128)(2,1)S(1)} %pad_maximum_fusion.1), channel_id=1, source_target_pairs={{0,6},{1,3},{2,0},{3,5},{4,2},{5,7},{6,4},{7,1},{8,14},{9,11},{10,... | collective-permute-start | bytes 786440 | tf_op jit(solution)/shard_map/ppermute | solution.py:23
  25.8 13.0 %collective-permute-start.6 = (bf16[1,2,128,512]{3,2,1,0:T(8,128)(2,1)S(1)}, bf16[1,2,128,512]{3,2,1,0:T(8,128)(2,1)S(1)}, u32[]{:S(2)}, u32[]{:S(2)}) collective-permute-start(bf16[1,2,128,512]{3,2,1,0:T(8,128)(2,1)S(1)} %bitcast.15), channel_id=1, source_target_pairs={{0,24},{1,9},{2,26},{3,11},{4,28},{5,13},{6,30},{7,15},{8,0},{9,17... | collective-permute-start | bytes 786440 | tf_op jit(solution)/shard_map/ppermute | solution.py:23
  29.6 9.1 %collective-permute-start.8 = (bf16[1,2,128,512]{3,2,1,0:T(8,128)(2,1)S(1)}, bf16[1,2,128,512]{3,2,1,0:T(8,128)(2,1)S(1)}, u32[]{:S(2)}, u32[]{:S(2)}) collective-permute-start(bf16[1,2,128,512]{3,2,1,0:T(8,128)(2,1)S(1)} %collective-permute-done.7.refs_1_), channel_id=1, source_target_pairs={{0,8},{1,25},{2,10},{3,27},{4,12},{5,29},{6,14},{7,31},{8,16},{9,1... | collective-permute-start | bytes 786440 | tf_op jit(solution)/shard_map/ppermute | solution.py:23
  30.2 13.6 %collective-permute-start.11 = (bf16[2,128,512]{2,1,0:T(8,128)(2,1)S(1)}, bf16[2,128,512]{2,1,0:T(8,128)(2,1)S(1)}, u32[]{:S(2)}, u32[]{:S(2)}) collective-permute-start(bf16[2,128,512]{2,1,0:T(8,128)(2,1)S(1)} %collective-permute-done.4), channel_id=1, source_target_pairs={{0,2},{1,7},{2,4},{3,1},{4,6},{5,3},{6,0},{7,5},{8,10},{9,15},{10,... | collective-permute-start | bytes 786440 | tf_op jit(solution)/shard_map/ppermute | solution.py:23
  38.7 25.9 %collective-permute-start.10 = (bf16[2,2,128,512]{3,2,1,0:T(8,128)(2,1)S(1)}, bf16[2,2,128,512]{3,2,1,0:T(8,128)(2,1)S(1)}, u32[]{:S(2)}, u32[]{:S(2)}) collective-permute-start(bf16[2,2,128,512]{3,2,1,0:T(8,128)(2,1)S(1)} %pad_maximum_fusion.refs_4_), channel_id=1, source_target_pairs={{0,24},{1,9},{2,26},{3,11},{4,28},{5,13},{6,30},{7,15},{8,0},{9,17... | collective-permute-start | bytes 1572872 | tf_op jit(solution)/shard_map/ppermute | solution.py:23
  43.1 21.5 %collective-permute-start.9 = (bf16[2,2,128,512]{3,2,1,0:T(8,128)(2,1)S(1)}, bf16[2,2,128,512]{3,2,1,0:T(8,128)(2,1)S(1)}, u32[]{:S(2)}, u32[]{:S(2)}) collective-permute-start(bf16[2,2,128,512]{3,2,1,0:T(8,128)(2,1)S(1)} %pad_maximum_fusion.refs_4_), channel_id=1, source_target_pairs={{0,8},{1,25},{2,10},{3,27},{4,12},{5,29},{6,14},{7,31},{8,16},{9,1... | collective-permute-start | bytes 1572872 | tf_op jit(solution)/shard_map/ppermute | solution.py:23
  43.8 15.0 %collective-permute-start.13 = (bf16[1,2,128,512]{3,2,1,0:T(8,128)(2,1)S(1)}, bf16[1,2,128,512]{3,2,1,0:T(8,128)(2,1)S(1)}, u32[]{:S(2)}, u32[]{:S(2)}) collective-permute-start(bf16[1,2,128,512]{3,2,1,0:T(8,128)(2,1)S(1)} %bitcast.21), channel_id=1, source_target_pairs={{0,24},{1,9},{2,26},{3,11},{4,28},{5,13},{6,30},{7,15},{8,0},{9,17... | collective-permute-start | bytes 786440 | tf_op jit(solution)/shard_map/ppermute | solution.py:23
  52.1 12.6 %collective-permute-start.12 = (bf16[1,2,128,512]{3,2,1,0:T(8,128)(2,1)S(1)}, bf16[1,2,128,512]{3,2,1,0:T(8,128)(2,1)S(1)}, u32[]{:S(2)}, u32[]{:S(2)}) collective-permute-start(bf16[1,2,128,512]{3,2,1,0:T(8,128)(2,1)S(1)} %bitcast.22), channel_id=1, source_target_pairs={{0,8},{1,25},{2,10},{3,27},{4,12},{5,29},{6,14},{7,31},{8,16},{9,1... | collective-permute-start | bytes 786440 | tf_op jit(solution)/shard_map/ppermute | solution.py:23
  64.6 13.2 %collective-permute-start.14 = (bf16[2,2,128,512]{3,2,1,0:T(8,128)(2,1)S(1)}, bf16[2,2,128,512]{3,2,1,0:T(8,128)(2,1)S(1)}, u32[]{:S(2)}, u32[]{:S(2)}) collective-permute-start(bf16[2,2,128,512]{3,2,1,0:T(8,128)(2,1)S(1)} %collective-permute-done.9.refs_5_), channel_id=1, source_target_pairs={{0,8},{1,25},{2,10},{3,27},{4,12},{5,29},{6,14},{7,31},{8,16},{9,1... | collective-permute-start | bytes 1572872 | tf_op jit(solution)/shard_map/ppermute | solution.py:23
  64.6 13.2 %collective-permute-start.15 = (bf16[1,2,128,512]{3,2,1,0:T(8,128)(2,1)S(1)}, bf16[1,2,128,512]{3,2,1,0:T(8,128)(2,1)S(1)}, u32[]{:S(2)}, u32[]{:S(2)}) collective-permute-start(bf16[1,2,128,512]{3,2,1,0:T(8,128)(2,1)S(1)} %collective-permute-done.12.refs_9_), channel_id=1, source_target_pairs={{0,8},{1,25},{2,10},{3,27},{4,12},{5,29},{6,14},{7,31},{8,16},{9,1... | collective-permute-start | bytes 786440 | tf_op jit(solution)/shard_map/ppermute | solution.py:23
  77.8 4.2 %collective-permute-start.16 = (bf16[2048,512]{1,0:T(8,128)(2,1)S(1)}, bf16[2048,512]{1,0:T(8,128)(2,1)S(1)}, u32[]{:S(2)}, u32[]{:S(2)}) collective-permute-start(bf16[2048,512]{1,0:T(8,128)(2,1)S(1)} %collective-permute-done.3.far), channel_id=1, source_target_pairs={{0,1},{1,0},{2,3},{3,2},{4,5},{5,4},{6,7},{7,6},{8,9},{9,8},{10,11... | collective-permute-start | bytes 6291464 | tf_op jit(solution)/shard_map/ppermute | solution.py:23
  82.0 1.6 %copy-start.2 = (bf16[2048,512]{1,0:T(8,128)(2,1)S(1)}, bf16[2048,512]{1,0:T(8,128)(2,1)}, u32[]{:S(2)}) copy-start(bf16[2048,512]{1,0:T(8,128)(2,1)} %own.1) | copy-start | bytes 6291460
  90.8 20.7 %copy-start = (s32[2,256,64]{1,2,0:T(8,128)S(1)}, s32[2,256,64]{1,2,0:T(8,128)}, u32[]{:S(2)}) copy-start(s32[2,256,64]{1,2,0:T(8,128)} %param.5) | copy-start | bytes 393220
  90.8 20.7 %copy-start.1 = (f32[256]{0:T(256)S(1)}, f32[256]{0:T(256)}, u32[]{:S(2)}) copy-start(f32[256]{0:T(256)} %param.7) | copy-start | bytes 3076
  90.9 20.7 %copy-start.3 = (f32[512,256]{1,0:T(8,128)S(1)}, f32[512,256]{1,0:T(8,128)}, u32[]{:S(2)}) copy-start(f32[512,256]{1,0:T(8,128)} %get-tuple-element.21.decoded) | copy-start | bytes 1572868
  109.9 1.6 %collective-permute-start.17 = (f32[128,512]{1,0:T(8,128)S(1)}, f32[128,512]{1,0:T(8,128)S(1)}, u32[]{:S(2)}, u32[]{:S(2)}) collective-permute-start(f32[128,512]{1,0:T(8,128)S(1)} %get-tuple-element.39), channel_id=1, source_target_pairs={{0,1},{1,0},{2,3},{3,2},{4,5},{5,4},{6,7},{7,6},{8,9},{9,8},{10,11... | collective-permute-start | bytes 786440 | tf_op jit(solution)/shard_map/ppermute | solution.py:23
  116.6 1.2 collective-permute-start.18
  117.8 5.4 %collective-permute-start.21 = (f32[17,256]{1,0:T(8,128)S(1)}, f32[17,256]{1,0:T(8,128)S(1)}, u32[]{:S(2)}, u32[]{:S(2)}) collective-permute-start(f32[17,256]{1,0:T(8,128)S(1)} %add.21), channel_id=1, source_target_pairs={{0,16},{1,17},{2,18},{3,19},{4,20},{5,21},{6,22},{7,23},{8,24},{9,... | collective-permute-start | bytes 52232 | tf_op jit(solution)/shard_map/ppermute | solution.py:23
  117.8 5.4 %collective-permute-start.20 = (f32[17,256]{1,0:T(8,128)S(1)}, f32[17,256]{1,0:T(8,128)S(1)}, u32[]{:S(2)}, u32[]{:S(2)}) collective-permute-start(f32[17,256]{1,0:T(8,128)S(1)} %add.21), channel_id=1, source_target_pairs={{0,24},{1,25},{2,26},{3,27},{4,28},{5,29},{6,30},{7,31},{8,0},{9,1... | collective-permute-start | bytes 52232 | tf_op jit(solution)/shard_map/ppermute | solution.py:23
  119.3 5.0 %collective-permute-start.19 = (f32[17,256]{1,0:T(8,128)S(1)}, f32[17,256]{1,0:T(8,128)S(1)}, u32[]{:S(2)}, u32[]{:S(2)}) collective-permute-start(f32[17,256]{1,0:T(8,128)S(1)} %add.21), channel_id=1, source_target_pairs={{0,8},{1,9},{2,10},{3,11},{4,12},{5,13},{6,14},{7,15},{8,16},{9,17... | collective-permute-start | bytes 52232 | tf_op jit(solution)/shard_map/ppermute | solution.py:23
  124.3 7.9 %collective-permute-start.24 = (f32[17,256]{1,0:T(8,128)S(1)}, f32[17,256]{1,0:T(8,128)S(1)}, u32[]{:S(2)}, u32[]{:S(2)}) collective-permute-start(f32[17,256]{1,0:T(8,128)S(1)} %add_add_fusion.1), channel_id=1, source_target_pairs={{0,4},{1,5},{2,6},{3,7},{4,0},{5,1},{6,2},{7,3},{8,12},{9,13},{10,... | collective-permute-start | bytes 52232 | tf_op jit(solution)/shard_map/ppermute | solution.py:23
  124.6 7.7 %collective-permute-start.23 = (f32[17,256]{1,0:T(8,128)S(1)}, f32[17,256]{1,0:T(8,128)S(1)}, u32[]{:S(2)}, u32[]{:S(2)}) collective-permute-start(f32[17,256]{1,0:T(8,128)S(1)} %add_add_fusion.1), channel_id=1, source_target_pairs={{0,6},{1,7},{2,0},{3,1},{4,2},{5,3},{6,4},{7,5},{8,14},{9,15},{10,... | collective-permute-start | bytes 52232 | tf_op jit(solution)/shard_map/ppermute | solution.py:23
  126.6 6.1 %collective-permute-start.22 = (f32[17,256]{1,0:T(8,128)S(1)}, f32[17,256]{1,0:T(8,128)S(1)}, u32[]{:S(2)}, u32[]{:S(2)}) collective-permute-start(f32[17,256]{1,0:T(8,128)S(1)} %add_add_fusion.1), channel_id=1, source_target_pairs={{0,2},{1,3},{2,4},{3,5},{4,6},{5,7},{6,0},{7,1},{8,10},{9,11},{10,... | collective-permute-start | bytes 52232 | tf_op jit(solution)/shard_map/ppermute | solution.py:23
  133.4 9.9 %all-to-all-start.1 = ((f32[8,16,256]{2,1,0:T(8,128)}), f32[8,16,256]{2,1,0:T(8,128)S(1)}, u32[]{:S(2)}, u32[]{:S(2)}) async-start(f32[8,16,256]{2,1,0:T(8,128)} %broadcast_in_dim.11), calls=%async_computation.1 | async-start | bytes 262144 | tf_op jit(solution)/shard_map/all_to_all | solution.py:285

commit v6 on v5

--- a/solution.py
+++ b/solution.py
@@ -234,18 +234,17 @@
     own = block[None]
     z_back, z_on = turn(block, "z_hi", 1), turn(block, "z_hi", -1)
     own_back, own_on = turn(own, "x", 1), turn(own, "x", -1)
+    near, own_back, own_on = lax.optimization_barrier(
+        (jnp.stack([z_back, z_on]), own_back, own_on)
+    )
     own_two = turn(own_back, "x", 1)
-    near, own_on, own_two = lax.optimization_barrier(
-        (jnp.stack([z_back, z_on]), own_on, own_two)
-    )
     near_back, near_on = turn(near, "x", 1), turn(near, "x", -1)
     last = turn(z_back, "z_hi", 1)[None]
     last_back, last_on = turn(last, "x", 1), turn(last, "x", -1)
-    near_back, near_on, last_back, last_on = lax.optimization_barrier(
-        (near_back, near_on, last_back, last_on)
+    near_back, near_on, last_back, last_on, own_two, far = lax.optimization_barrier(
+        (near_back, near_on, last_back, last_on, own_two, far)
     )
     near_two, last_two = turn(near_back, "x", 1), turn(last_back, "x", 1)
-    far, near_two, last_two = lax.optimization_barrier((far, near_two, last_two))
     far_across = shift(far, "core", 1)
     wide = (
         (own, own_back, own_on, own_two),
@@ -257,7 +256,8 @@
     partial = pl.pallas_call(
         matmul_kernel,
         out_shape=jax.ShapeDtypeStruct((4, half, 2 * width), jnp.bfloat16),
-        in_specs=[pl.BlockSpec(memory_space=pl.ANY)] * (4 + len(blocks)),
+        in_specs=[pl.BlockSpec(memory_space=pl.ANY)] * 4
+        + [pl.BlockSpec(memory_space=pl.ANY)] * len(blocks),
         out_specs=pl.BlockSpec(memory_space=pltpu.VMEM),
         scratch_shapes=[
             pltpu.VMEM((4 * half, 8 * width), jnp.bfloat16),

time: 144 us -> 150 us (1.042)
  starting transfers between devices: 56.9 us -> 71.1 us
  waiting for transfers between devices: 48 us -> 40.4 us
    ppermute x25, starting transfers between devices: 52.1 us -> 67.4 us  [send(): return lax.ppermute(a, AXES, pairs)]
    ppermute x25, waiting for transfers between devices: 43.4 us -> 35.9 us  [send(): return lax.ppermute(a, AXES, pairs)]
  transfers between devices with their start and end apart: 26 -> 26, of which waited for: 15 -> 13; matrix products, arithmetic and copies ran while one was open for 0% -> 0% of each run, Pallas kernels for 2% -> 2%
where the time goes in v6:
time: 150 us
  starting transfers between devices  71.1 us (47%)
  waiting for transfers between devices  40.4 us (27%)
  blocking collectives  18.2 us (12%)
  Pallas kernels  15.7 us (10%)
  local copies, waits for them, and re-layouts  2.32 us (2%)
    ppermute x25, starting transfers between devices, send(): return lax.ppermute(a, AXES, pairs)  67.4 us
    ppermute x25, waiting for transfers between devices, send(): return lax.ppermute(a, AXES, pairs)  35.9 us
    all_to_all x1, blocking collectives, body(): parts = lax.all_to_all(partial, ('z_lo', 'y_hi'), 0, 0, tiled=True)  18.2 us
    pallas_call x1, Pallas kernels, body(): pl.pallas_call(matmul_kernel, out_shape=jax.ShapeDtypeStruct((4, half, 2...  7.25 us
    pallas_call x1, Pallas kernels, finish(): pl.pallas_call(finish_kernel, out_shape=(jax.ShapeDtypeStruct((rows, widt...  5.08 us
    all_to_all x1, waiting for transfers between devices, body(): books = jnp.sum(lax.all_to_all(copies, ROW, 0, 0, tiled=True), axis=0)  4.51 us
    all_to_all x1, starting transfers between devices, body(): books = jnp.sum(lax.all_to_all(copies, ROW, 0, 0, tiled=True), axis=0)  3.74 us
    pallas_call x1, Pallas kernels, decode(): pl.pallas_call(decode_kernel, out_shape=(jax.ShapeDtypeStruct((width, row...  3.36 us
  transfers between devices with their start and end apart: 26, of which 13 were waited for; matrix products, arithmetic and copies ran while one was open for 0% of the time, Pallas kernels for 2%

profile of v6, /device:TPU:8, one launch (start us, length us, event | category | flops | bytes accessed | tf_op | source)
XLA Modules:
  0.0 150.0 jit_solution(12836258133560044599)
XLA Ops:
  0.7 3.4 %decode.1 = (f32[512,256]{1,0:T(8,128)}, bf16[128,512]{1,0:T(8,128)(2,1)}, bf16[128,512]{1,0:T(8,128)(2,1)}) custom-call(s32[2,64,256]{2,1,0:T(8,128)} %bitcast.17, bf16[2,8,256]{2,1,0:T(8,128)(2,1)} %bitcast.28, f32[1,256]{1,0:T(1,128)} %bitcast.19, bf16[256,512]{1,0:T(8,128)(2,1)} %initial_in.1), custom_call_target="tpu_custom_call" | custom-call | flops 2097152 | bytes 1048576 | tf_op jit(solution)/shard_map/decode/pallas_call | solution.py:81
  4.1 1.6 %collective-permute-start = (bf16[128,512]{1,0:T(8,128)(2,1)}, bf16[128,512]{1,0:T(8,128)(2,1)S(1)}, u32[]{:S(2)}, u32[]{:S(2)}) collective-permute-start(bf16[128,512]{1,0:T(8,128)(2,1)} %get-tuple-element.21), channel_id=1, source_target_pairs={{0,0},{1,1},{2,2},{3,3},{4,4},{5,5},{6,6},{7,7},{8,72},{9,73},{10,... | collective-permute-start | bytes 393224 | tf_op jit(solution)/shard_map/ppermute | solution.py:23
  7.4 2.3 %collective-permute-start.13 = (bf16[2048,512]{1,0:T(8,128)(2,1)}, bf16[2048,512]{1,0:T(8,128)(2,1)S(1)}, u32[]{:S(2)}, u32[]{:S(2)}) collective-permute-start(bf16[2048,512]{1,0:T(8,128)(2,1)} %own.1), channel_id=1, source_target_pairs={{0,32},{1,33},{2,34},{3,35},{4,36},{5,37},{6,38},{7,39},{8,40},{9,... | collective-permute-start | bytes 6291464 | tf_op jit(solution)/shard_map/ppermute | solution.py:23
  9.7 1.5 %collective-permute-start.3 = (bf16[2,128,512]{2,1,0:T(8,128)(2,1)S(1)}, bf16[2,128,512]{2,1,0:T(8,128)(2,1)S(1)}, u32[]{:S(2)}, u32[]{:S(2)}) collective-permute-start(bf16[2,128,512]{2,1,0:T(8,128)(2,1)S(1)} %pad_maximum_fusion.1), channel_id=1, source_target_pairs={{0,2},{1,7},{2,4},{3,1},{4,6},{5,3},{6,0},{7,5},{8,10},{9,15},{10,... | collective-permute-start | bytes 786440 | tf_op jit(solution)/shard_map/ppermute | solution.py:23
  11.2 3.0 %collective-permute-start.4 = (bf16[2,128,512]{2,1,0:T(8,128)(2,1)S(1)}, bf16[2,128,512]{2,1,0:T(8,128)(2,1)S(1)}, u32[]{:S(2)}, u32[]{:S(2)}) collective-permute-start(bf16[2,128,512]{2,1,0:T(8,128)(2,1)S(1)} %pad_maximum_fusion.1), channel_id=1, source_target_pairs={{0,6},{1,3},{2,0},{3,5},{4,2},{5,7},{6,4},{7,1},{8,14},{9,11},{10,... | collective-permute-start | bytes 786440 | tf_op jit(solution)/shard_map/ppermute | solution.py:23
  14.2 15.4 %collective-permute-start.6 = (bf16[1,2,128,512]{3,2,1,0:T(8,128)(2,1)S(1)}, bf16[1,2,128,512]{3,2,1,0:T(8,128)(2,1)S(1)}, u32[]{:S(2)}, u32[]{:S(2)}) collective-permute-start(bf16[1,2,128,512]{3,2,1,0:T(8,128)(2,1)S(1)} %bitcast.14), channel_id=1, source_target_pairs={{0,24},{1,9},{2,26},{3,11},{4,28},{5,13},{6,30},{7,15},{8,0},{9,17... | collective-permute-start | bytes 786440 | tf_op jit(solution)/shard_map/ppermute | solution.py:23
  29.6 1.5 collective-permute-start.9
  31.1 3.8 %collective-permute-done.6.refs_2_ = bf16[1,2,128,512]{3,2,1,0:T(8,128)(2,1)S(1)} collective-permute-done((bf16[1,2,128,512]{3,2,1,0:T(8,128)(2,1)S(1)}, bf16[1,2,128,512]{3,2,1,0:T(8,128)(2,1)S(1)}, u32[]{:S(2)}, u32[]{:S(2)}) %collective-permute-start.6) | collective-permute-done | bytes 262176 | tf_op jit(solution)/shard_map/ppermute | solution.py:23
  34.9 2.4 %collective-permute-done.5.refs_1_ = bf16[1,2,128,512]{3,2,1,0:T(8,128)(2,1)S(1)} collective-permute-done((bf16[1,2,128,512]{3,2,1,0:T(8,128)(2,1)S(1)}, bf16[1,2,128,512]{3,2,1,0:T(8,128)(2,1)S(1)}, u32[]{:S(2)}, u32[]{:S(2)}) %collective-permute-start.5) | collective-permute-done | bytes 262176 | tf_op jit(solution)/shard_map/ppermute | solution.py:23
  37.3 1.8 %collective-permute-start.12 = (bf16[1,2,128,512]{3,2,1,0:T(8,128)(2,1)S(1)}, bf16[1,2,128,512]{3,2,1,0:T(8,128)(2,1)S(1)}, u32[]{:S(2)}, u32[]{:S(2)}) collective-permute-start(bf16[1,2,128,512]{3,2,1,0:T(8,128)(2,1)S(1)} %collective-permute-done.5.refs_1_), channel_id=1, source_target_pairs={{0,8},{1,25},{2,10},{3,27},{4,12},{5,29},{6,14},{7,31},{8,16},{9,1... | collective-permute-start | bytes 786440 | tf_op jit(solution)/shard_map/ppermute | solution.py:23
  39.2 4.0 %collective-permute-start.8 = (bf16[2,2,128,512]{3,2,1,0:T(8,128)(2,1)S(1)}, bf16[2,2,128,512]{3,2,1,0:T(8,128)(2,1)S(1)}, u32[]{:S(2)}, u32[]{:S(2)}) collective-permute-start(bf16[2,2,128,512]{3,2,1,0:T(8,128)(2,1)S(1)} %pad_maximum_fusion.refs_4_), channel_id=1, source_target_pairs={{0,24},{1,9},{2,26},{3,11},{4,28},{5,13},{6,30},{7,15},{8,0},{9,17... | collective-permute-start | bytes 1572872 | tf_op jit(solution)/shard_map/ppermute | solution.py:23
  43.2 8.9 %collective-permute-start.11 = (bf16[1,2,128,512]{3,2,1,0:T(8,128)(2,1)S(1)}, bf16[1,2,128,512]{3,2,1,0:T(8,128)(2,1)S(1)}, u32[]{:S(2)}, u32[]{:S(2)}) collective-permute-start(bf16[1,2,128,512]{3,2,1,0:T(8,128)(2,1)S(1)} %bitcast.21), channel_id=1, source_target_pairs={{0,24},{1,9},{2,26},{3,11},{4,28},{5,13},{6,30},{7,15},{8,0},{9,17... | collective-permute-start | bytes 786440 | tf_op jit(solution)/shard_map/ppermute | solution.py:23
  52.1 9.1 %collective-permute-done.11.refs_10_ = bf16[1,2,128,512]{3,2,1,0:T(8,128)(2,1)S(1)} collective-permute-done((bf16[1,2,128,512]{3,2,1,0:T(8,128)(2,1)S(1)}, bf16[1,2,128,512]{3,2,1,0:T(8,128)(2,1)S(1)}, u32[]{:S(2)}, u32[]{:S(2)}) %collective-permute-start.11) | collective-permute-done | bytes 262176 | tf_op jit(solution)/shard_map/ppermute | solution.py:23
  61.1 3.1 %collective-permute-done.10.refs_9_ = bf16[1,2,128,512]{3,2,1,0:T(8,128)(2,1)S(1)} collective-permute-done((bf16[1,2,128,512]{3,2,1,0:T(8,128)(2,1)S(1)}, bf16[1,2,128,512]{3,2,1,0:T(8,128)(2,1)S(1)}, u32[]{:S(2)}, u32[]{:S(2)}) %collective-permute-start.10) | collective-permute-done | bytes 262176 | tf_op jit(solution)/shard_map/ppermute | solution.py:23
  64.4 2.1 %collective-permute-start.15 = (bf16[2,2,128,512]{3,2,1,0:T(8,128)(2,1)S(1)}, bf16[2,2,128,512]{3,2,1,0:T(8,128)(2,1)S(1)}, u32[]{:S(2)}, u32[]{:S(2)}) collective-permute-start(bf16[2,2,128,512]{3,2,1,0:T(8,128)(2,1)S(1)} %collective-permute-done.7.refs_5_), channel_id=1, source_target_pairs={{0,8},{1,25},{2,10},{3,27},{4,12},{5,29},{6,14},{7,31},{8,16},{9,1... | collective-permute-start | bytes 1572872 | tf_op jit(solution)/shard_map/ppermute | solution.py:23
  66.5 7.1 %collective-permute-start.16 = (bf16[1,2,128,512]{3,2,1,0:T(8,128)(2,1)S(1)}, bf16[1,2,128,512]{3,2,1,0:T(8,128)(2,1)S(1)}, u32[]{:S(2)}, u32[]{:S(2)}) collective-permute-start(bf16[1,2,128,512]{3,2,1,0:T(8,128)(2,1)S(1)} %collective-permute-done.10.refs_9_), channel_id=1, source_target_pairs={{0,8},{1,25},{2,10},{3,27},{4,12},{5,29},{6,14},{7,31},{8,16},{9,1... | collective-permute-start | bytes 786440 | tf_op jit(solution)/shard_map/ppermute | solution.py:23
  73.6 7.1 %collective-permute-done.16.refs_11_ = bf16[1,2,128,512]{3,2,1,0:T(8,128)(2,1)S(1)} collective-permute-done((bf16[1,2,128,512]{3,2,1,0:T(8,128)(2,1)S(1)}, bf16[1,2,128,512]{3,2,1,0:T(8,128)(2,1)S(1)}, u32[]{:S(2)}, u32[]{:S(2)}) %collective-permute-start.16) | collective-permute-done | bytes 262176 | tf_op jit(solution)/shard_map/ppermute | solution.py:23
  80.7 1.6 %copy-done.2 = bf16[2048,512]{1,0:T(8,128)(2,1)S(1)} copy-done((bf16[2048,512]{1,0:T(8,128)(2,1)S(1)}, bf16[2048,512]{1,0:T(8,128)(2,1)}, u32[]{:S(2)}) %copy-start.2) | copy-done | bytes 2097176
  82.3 7.2 %matmul.1 = bf16[4,128,1024]{2,1,0:T(8,128)(2,1)S(1)} custom-call(bf16[2048,512]{1,0:T(8,128)(2,1)S(1)} %copy-done.2, bf16[2048,512]{1,0:T(8,128)(2,1)S(1)} %collective-permute-done.13.far, bf16[2048,512]{1,0:T(8,128)(2,1)S(1)} %collective-permute-done.2.across, bf16[2048,512]{1,0:T(8,128)(2,1)S(1)} %collective-permute-done.14.far_across, ...), custom_call_target="tpu_custom_call" | custom-call | flops 4294967296 | bytes 13631488 | tf_op jit(solution)/shard_map/matmul/pallas_call | solution.py:256
  89.6 18.2 %all_to_all.10 = bf16[4,128,1024]{2,1,0:T(8,128)(2,1)S(1)} all-to-all(bf16[4,128,1024]{2,1,0:T(8,128)(2,1)S(1)} %matmul.1), channel_id=1, replica_groups=mesh['z_lo'=2,'y_hi'=2,'y_lo'=2,'x'=4,'z_hi'=4,'core'=2] {'z_lo','y_hi'}, dimensions={0} | all-to-all | bytes 2097152 | tf_op jit(solution)/shard_map/all_to_all | solution.py:274
  108.1 1.5 %collective-permute-done.17.got = f32[128,512]{1,0:T(8,128)S(1)} collective-permute-done((f32[128,512]{1,0:T(8,128)S(1)}, f32[128,512]{1,0:T(8,128)S(1)}, u32[]{:S(2)}, u32[]{:S(2)}) %collective-permute-start.17) | collective-permute-done | bytes 262176 | tf_op jit(solution)/shard_map/ppermute | solution.py:23
  109.6 5.1 %finish.1 = (f32[256,512]{1,0:T(8,128)}, f32[17,256]{1,0:T(8,128)S(1)}) custom-call(s32[2,64,256]{2,1,0:T(8,128)S(1)} %bitcast.18, f32[1,256]{1,0:T(1,128)S(1)} %bitcast.20, f32[512,256]{1,0:T(8,128)S(1)} %copy-done.3, f32[128,512]{1,0:T(8,128)S(1)} %get-tuple-element.38.kept, f32[128,512]{1,0:T(8,128)S(1)} %collective-permute-done.17.got), custom_call_target="tpu_custom_call" | custom-call | flops 4294967296 | bytes 2097152 | tf_op jit(solution)/shard_map/finish/pallas_call | solution.py:148
  115.9 5.1 %collective-permute-start.21 = (f32[17,256]{1,0:T(8,128)S(1)}, f32[17,256]{1,0:T(8,128)S(1)}, u32[]{:S(2)}, u32[]{:S(2)}) collective-permute-start(f32[17,256]{1,0:T(8,128)S(1)} %add.21), channel_id=1, source_target_pairs={{0,16},{1,17},{2,18},{3,19},{4,20},{5,21},{6,22},{7,23},{8,24},{9,... | collective-permute-start | bytes 52232 | tf_op jit(solution)/shard_map/ppermute | solution.py:23
  121.6 1.4 collective-permute-start.19
  123.0 1.8 %collective-permute-done.20 = f32[17,256]{1,0:T(8,128)S(1)} collective-permute-done((f32[17,256]{1,0:T(8,128)S(1)}, f32[17,256]{1,0:T(8,128)S(1)}, u32[]{:S(2)}, u32[]{:S(2)}) %collective-permute-start.20) | collective-permute-done | bytes 17440 | tf_op jit(solution)/shard_map/ppermute | solution.py:23
  124.8 1.8 %collective-permute-done.19 = f32[17,256]{1,0:T(8,128)S(1)} collective-permute-done((f32[17,256]{1,0:T(8,128)S(1)}, f32[17,256]{1,0:T(8,128)S(1)}, u32[]{:S(2)}, u32[]{:S(2)}) %collective-permute-start.19) | collective-permute-done | bytes 17440 | tf_op jit(solution)/shard_map/ppermute | solution.py:23
  126.6 7.3 %collective-permute-start.24 = (f32[17,256]{1,0:T(8,128)S(1)}, f32[17,256]{1,0:T(8,128)S(1)}, u32[]{:S(2)}, u32[]{:S(2)}) collective-permute-start(f32[17,256]{1,0:T(8,128)S(1)} %add_add_fusion.1), channel_id=1, source_target_pairs={{0,4},{1,5},{2,6},{3,7},{4,0},{5,1},{6,2},{7,3},{8,12},{9,13},{10,... | collective-permute-start | bytes 52232 | tf_op jit(solution)/shard_map/ppermute | solution.py:23
  133.9 2.9 %collective-permute-start.22 = (f32[17,256]{1,0:T(8,128)S(1)}, f32[17,256]{1,0:T(8,128)S(1)}, u32[]{:S(2)}, u32[]{:S(2)}) collective-permute-start(f32[17,256]{1,0:T(8,128)S(1)} %add_add_fusion.1), channel_id=1, source_target_pairs={{0,2},{1,3},{2,4},{3,5},{4,6},{5,7},{6,0},{7,1},{8,10},{9,11},{10,... | collective-permute-start | bytes 52232 | tf_op jit(solution)/shard_map/ppermute | solution.py:23
  136.8 1.8 %collective-permute-done.23 = f32[17,256]{1,0:T(8,128)S(1)} collective-permute-done((f32[17,256]{1,0:T(8,128)S(1)}, f32[17,256]{1,0:T(8,128)S(1)}, u32[]{:S(2)}, u32[]{:S(2)}) %collective-permute-start.23) | collective-permute-done | bytes 17440 | tf_op jit(solution)/shard_map/ppermute | solution.py:23
  138.6 1.2 collective-permute-done.22
  140.5 3.7 %all-to-all-start.1 = ((f32[8,16,256]{2,1,0:T(8,128)}), f32[8,16,256]{2,1,0:T(8,128)S(1)}, u32[]{:S(2)}, u32[]{:S(2)}) async-start(f32[8,16,256]{2,1,0:T(8,128)} %broadcast_in_dim.11), calls=%async_computation.1 | async-start | bytes 262144 | tf_op jit(solution)/shard_map/all_to_all | solution.py:285
  144.9 4.5 %all-to-all-done.1 = f32[8,16,256]{2,1,0:T(8,128)S(1)} async-done(((f32[8,16,256]{2,1,0:T(8,128)}), f32[8,16,256]{2,1,0:T(8,128)S(1)}, u32[]{:S(2)}, u32[]{:S(2)}) %all-to-all-start.1) | async-done | bytes 131104 | tf_op jit(solution)/shard_map/all_to_all | solution.py:285
  (44 shorter events, 6.0 us)
Async XLA Ops:
  0.6 6.8 %collective-permute-start.2 = (bf16[2048,512]{1,0:T(8,128)(2,1)}, bf16[2048,512]{1,0:T(8,128)(2,1)S(1)}, u32[]{:S(2)}, u32[]{:S(2)}) collective-permute-start(bf16[2048,512]{1,0:T(8,128)(2,1)} %own.1), channel_id=1, source_target_pairs={{0,1},{1,0},{2,3},{3,2},{4,5},{5,4},{6,7},{7,6},{8,9},{9,8},{10,11... | collective-permute-start | bytes 6291464 | tf_op jit(solution)/shard_map/ppermute | solution.py:23
  4.1 2.1 %collective-permute-start = (bf16[128,512]{1,0:T(8,128)(2,1)}, bf16[128,512]{1,0:T(8,128)(2,1)S(1)}, u32[]{:S(2)}, u32[]{:S(2)}) collective-permute-start(bf16[128,512]{1,0:T(8,128)(2,1)} %get-tuple-element.21), channel_id=1, source_target_pairs={{0,0},{1,1},{2,2},{3,3},{4,4},{5,5},{6,6},{7,7},{8,72},{9,73},{10,... | collective-permute-start | bytes 393224 | tf_op jit(solution)/shard_map/ppermute | solution.py:23
  5.7 1.7 %collective-permute-start.1 = (bf16[128,512]{1,0:T(8,128)(2,1)}, bf16[128,512]{1,0:T(8,128)(2,1)S(1)}, u32[]{:S(2)}, u32[]{:S(2)}) collective-permute-start(bf16[128,512]{1,0:T(8,128)(2,1)} %get-tuple-element.22), channel_id=1, source_target_pairs={{0,1},{1,0},{2,3},{3,2},{4,5},{5,4},{6,7},{7,6},{8,73},{9,72},{10,... | collective-permute-start | bytes 393224 | tf_op jit(solution)/shard_map/ppermute | solution.py:23
  7.4 56.9 %collective-permute-start.13 = (bf16[2048,512]{1,0:T(8,128)(2,1)}, bf16[2048,512]{1,0:T(8,128)(2,1)S(1)}, u32[]{:S(2)}, u32[]{:S(2)}) collective-permute-start(bf16[2048,512]{1,0:T(8,128)(2,1)} %own.1), channel_id=1, source_target_pairs={{0,32},{1,33},{2,34},{3,35},{4,36},{5,37},{6,38},{7,39},{8,40},{9,... | collective-permute-start | bytes 6291464 | tf_op jit(solution)/shard_map/ppermute | solution.py:23
  9.7 19.9 %collective-permute-start.3 = (bf16[2,128,512]{2,1,0:T(8,128)(2,1)S(1)}, bf16[2,128,512]{2,1,0:T(8,128)(2,1)S(1)}, u32[]{:S(2)}, u32[]{:S(2)}) collective-permute-start(bf16[2,128,512]{2,1,0:T(8,128)(2,1)S(1)} %pad_maximum_fusion.1), channel_id=1, source_target_pairs={{0,2},{1,7},{2,4},{3,1},{4,6},{5,3},{6,0},{7,5},{8,10},{9,15},{10,... | collective-permute-start | bytes 786440 | tf_op jit(solution)/shard_map/ppermute | solution.py:23
  11.2 19.9 %collective-permute-start.4 = (bf16[2,128,512]{2,1,0:T(8,128)(2,1)S(1)}, bf16[2,128,512]{2,1,0:T(8,128)(2,1)S(1)}, u32[]{:S(2)}, u32[]{:S(2)}) collective-permute-start(bf16[2,128,512]{2,1,0:T(8,128)(2,1)S(1)} %pad_maximum_fusion.1), channel_id=1, source_target_pairs={{0,6},{1,3},{2,0},{3,5},{4,2},{5,7},{6,4},{7,1},{8,14},{9,11},{10,... | collective-permute-start | bytes 786440 | tf_op jit(solution)/shard_map/ppermute | solution.py:23
  14.2 20.7 %collective-permute-start.6 = (bf16[1,2,128,512]{3,2,1,0:T(8,128)(2,1)S(1)}, bf16[1,2,128,512]{3,2,1,0:T(8,128)(2,1)S(1)}, u32[]{:S(2)}, u32[]{:S(2)}) collective-permute-start(bf16[1,2,128,512]{3,2,1,0:T(8,128)(2,1)S(1)} %bitcast.14), channel_id=1, source_target_pairs={{0,24},{1,9},{2,26},{3,11},{4,28},{5,13},{6,30},{7,15},{8,0},{9,17... | collective-permute-start | bytes 786440 | tf_op jit(solution)/shard_map/ppermute | solution.py:23
  29.6 7.7 %collective-permute-start.5 = (bf16[1,2,128,512]{3,2,1,0:T(8,128)(2,1)S(1)}, bf16[1,2,128,512]{3,2,1,0:T(8,128)(2,1)S(1)}, u32[]{:S(2)}, u32[]{:S(2)}) collective-permute-start(bf16[1,2,128,512]{3,2,1,0:T(8,128)(2,1)S(1)} %bitcast.15), channel_id=1, source_target_pairs={{0,8},{1,25},{2,10},{3,27},{4,12},{5,29},{6,14},{7,31},{8,16},{9,1... | collective-permute-start | bytes 786440 | tf_op jit(solution)/shard_map/ppermute | solution.py:23
  29.6 13.6 %collective-permute-start.9 = (bf16[2,128,512]{2,1,0:T(8,128)(2,1)S(1)}, bf16[2,128,512]{2,1,0:T(8,128)(2,1)S(1)}, u32[]{:S(2)}, u32[]{:S(2)}) collective-permute-start(bf16[2,128,512]{2,1,0:T(8,128)(2,1)S(1)} %collective-permute-done.3), channel_id=1, source_target_pairs={{0,2},{1,7},{2,4},{3,1},{4,6},{5,3},{6,0},{7,5},{8,10},{9,15},{10,... | collective-permute-start | bytes 786440 | tf_op jit(solution)/shard_map/ppermute | solution.py:23
  37.3 14.7 %collective-permute-start.12 = (bf16[1,2,128,512]{3,2,1,0:T(8,128)(2,1)S(1)}, bf16[1,2,128,512]{3,2,1,0:T(8,128)(2,1)S(1)}, u32[]{:S(2)}, u32[]{:S(2)}) collective-permute-start(bf16[1,2,128,512]{3,2,1,0:T(8,128)(2,1)S(1)} %collective-permute-done.5.refs_1_), channel_id=1, source_target_pairs={{0,8},{1,25},{2,10},{3,27},{4,12},{5,29},{6,14},{7,31},{8,16},{9,1... | collective-permute-start | bytes 786440 | tf_op jit(solution)/shard_map/ppermute | solution.py:23
  39.2 25.1 %collective-permute-start.8 = (bf16[2,2,128,512]{3,2,1,0:T(8,128)(2,1)S(1)}, bf16[2,2,128,512]{3,2,1,0:T(8,128)(2,1)S(1)}, u32[]{:S(2)}, u32[]{:S(2)}) collective-permute-start(bf16[2,2,128,512]{3,2,1,0:T(8,128)(2,1)S(1)} %pad_maximum_fusion.refs_4_), channel_id=1, source_target_pairs={{0,24},{1,9},{2,26},{3,11},{4,28},{5,13},{6,30},{7,15},{8,0},{9,17... | collective-permute-start | bytes 1572872 | tf_op jit(solution)/shard_map/ppermute | solution.py:23
  43.1 21.1 %collective-permute-start.7 = (bf16[2,2,128,512]{3,2,1,0:T(8,128)(2,1)S(1)}, bf16[2,2,128,512]{3,2,1,0:T(8,128)(2,1)S(1)}, u32[]{:S(2)}, u32[]{:S(2)}) collective-permute-start(bf16[2,2,128,512]{3,2,1,0:T(8,128)(2,1)S(1)} %pad_maximum_fusion.refs_4_), channel_id=1, source_target_pairs={{0,8},{1,25},{2,10},{3,27},{4,12},{5,29},{6,14},{7,31},{8,16},{9,1... | collective-permute-start | bytes 1572872 | tf_op jit(solution)/shard_map/ppermute | solution.py:23
  43.2 18.0 %collective-permute-start.11 = (bf16[1,2,128,512]{3,2,1,0:T(8,128)(2,1)S(1)}, bf16[1,2,128,512]{3,2,1,0:T(8,128)(2,1)S(1)}, u32[]{:S(2)}, u32[]{:S(2)}) collective-permute-start(bf16[1,2,128,512]{3,2,1,0:T(8,128)(2,1)S(1)} %bitcast.21), channel_id=1, source_target_pairs={{0,24},{1,9},{2,26},{3,11},{4,28},{5,13},{6,30},{7,15},{8,0},{9,17... | collective-permute-start | bytes 786440 | tf_op jit(solution)/shard_map/ppermute | solution.py:23
  52.1 12.2 %collective-permute-start.10 = (bf16[1,2,128,512]{3,2,1,0:T(8,128)(2,1)S(1)}, bf16[1,2,128,512]{3,2,1,0:T(8,128)(2,1)S(1)}, u32[]{:S(2)}, u32[]{:S(2)}) collective-permute-start(bf16[1,2,128,512]{3,2,1,0:T(8,128)(2,1)S(1)} %bitcast.22), channel_id=1, source_target_pairs={{0,8},{1,25},{2,10},{3,27},{4,12},{5,29},{6,14},{7,31},{8,16},{9,1... | collective-permute-start | bytes 786440 | tf_op jit(solution)/shard_map/ppermute | solution.py:23
  64.3 16.4 %collective-permute-start.14 = (bf16[2048,512]{1,0:T(8,128)(2,1)S(1)}, bf16[2048,512]{1,0:T(8,128)(2,1)S(1)}, u32[]{:S(2)}, u32[]{:S(2)}) collective-permute-start(bf16[2048,512]{1,0:T(8,128)(2,1)S(1)} %collective-permute-done.13.far), channel_id=1, source_target_pairs={{0,1},{1,0},{2,3},{3,2},{4,5},{5,4},{6,7},{7,6},{8,9},{9,8},{10,11... | collective-permute-start | bytes 6291464 | tf_op jit(solution)/shard_map/ppermute | solution.py:23
  64.4 16.3 %collective-permute-start.15 = (bf16[2,2,128,512]{3,2,1,0:T(8,128)(2,1)S(1)}, bf16[2,2,128,512]{3,2,1,0:T(8,128)(2,1)S(1)}, u32[]{:S(2)}, u32[]{:S(2)}) collective-permute-start(bf16[2,2,128,512]{3,2,1,0:T(8,128)(2,1)S(1)} %collective-permute-done.7.refs_5_), channel_id=1, source_target_pairs={{0,8},{1,25},{2,10},{3,27},{4,12},{5,29},{6,14},{7,31},{8,16},{9,1... | collective-permute-start | bytes 1572872 | tf_op jit(solution)/shard_map/ppermute | solution.py:23
  66.5 14.2 %collective-permute-start.16 = (bf16[1,2,128,512]{3,2,1,0:T(8,128)(2,1)S(1)}, bf16[1,2,128,512]{3,2,1,0:T(8,128)(2,1)S(1)}, u32[]{:S(2)}, u32[]{:S(2)}) collective-permute-start(bf16[1,2,128,512]{3,2,1,0:T(8,128)(2,1)S(1)} %collective-permute-done.10.refs_9_), channel_id=1, source_target_pairs={{0,8},{1,25},{2,10},{3,27},{4,12},{5,29},{6,14},{7,31},{8,16},{9,1... | collective-permute-start | bytes 786440 | tf_op jit(solution)/shard_map/ppermute | solution.py:23
  80.7 1.6 %copy-start.2 = (bf16[2048,512]{1,0:T(8,128)(2,1)S(1)}, bf16[2048,512]{1,0:T(8,128)(2,1)}, u32[]{:S(2)}) copy-start(bf16[2048,512]{1,0:T(8,128)(2,1)} %own.1) | copy-start | bytes 6291460
  89.5 20.1 %copy-start = (s32[2,256,64]{1,2,0:T(8,128)S(1)}, s32[2,256,64]{1,2,0:T(8,128)}, u32[]{:S(2)}) copy-start(s32[2,256,64]{1,2,0:T(8,128)} %param.5) | copy-start | bytes 393220
  89.6 20.1 %copy-start.1 = (f32[256]{0:T(256)S(1)}, f32[256]{0:T(256)}, u32[]{:S(2)}) copy-start(f32[256]{0:T(256)} %param.7) | copy-start | bytes 3076
  89.6 20.1 %copy-start.3 = (f32[512,256]{1,0:T(8,128)S(1)}, f32[512,256]{1,0:T(8,128)}, u32[]{:S(2)}) copy-start(f32[512,256]{1,0:T(8,128)} %get-tuple-element.20.decoded) | copy-start | bytes 1572868
  108.0 1.6 %collective-permute-start.17 = (f32[128,512]{1,0:T(8,128)S(1)}, f32[128,512]{1,0:T(8,128)S(1)}, u32[]{:S(2)}, u32[]{:S(2)}) collective-permute-start(f32[128,512]{1,0:T(8,128)S(1)} %get-tuple-element.37), channel_id=1, source_target_pairs={{0,1},{1,0},{2,3},{3,2},{4,5},{5,4},{6,7},{7,6},{8,9},{9,8},{10,11... | collective-permute-start | bytes 786440 | tf_op jit(solution)/shard_map/ppermute | solution.py:23
  114.7 1.2 collective-permute-start.18
  115.9 7.1 %collective-permute-start.21 = (f32[17,256]{1,0:T(8,128)S(1)}, f32[17,256]{1,0:T(8,128)S(1)}, u32[]{:S(2)}, u32[]{:S(2)}) collective-permute-start(f32[17,256]{1,0:T(8,128)S(1)} %add.21), channel_id=1, source_target_pairs={{0,16},{1,17},{2,18},{3,19},{4,20},{5,21},{6,22},{7,23},{8,24},{9,... | collective-permute-start | bytes 52232 | tf_op jit(solution)/shard_map/ppermute | solution.py:23
  121.0 3.8 %collective-permute-start.20 = (f32[17,256]{1,0:T(8,128)S(1)}, f32[17,256]{1,0:T(8,128)S(1)}, u32[]{:S(2)}, u32[]{:S(2)}) collective-permute-start(f32[17,256]{1,0:T(8,128)S(1)} %add.21), channel_id=1, source_target_pairs={{0,24},{1,25},{2,26},{3,27},{4,28},{5,29},{6,30},{7,31},{8,0},{9,1... | collective-permute-start | bytes 52232 | tf_op jit(solution)/shard_map/ppermute | solution.py:23
  121.6 5.0 %collective-permute-start.19 = (f32[17,256]{1,0:T(8,128)S(1)}, f32[17,256]{1,0:T(8,128)S(1)}, u32[]{:S(2)}, u32[]{:S(2)}) collective-permute-start(f32[17,256]{1,0:T(8,128)S(1)} %add.21), channel_id=1, source_target_pairs={{0,8},{1,9},{2,10},{3,11},{4,12},{5,13},{6,14},{7,15},{8,16},{9,17... | collective-permute-start | bytes 52232 | tf_op jit(solution)/shard_map/ppermute | solution.py:23
  126.6 10.2 %collective-permute-start.24 = (f32[17,256]{1,0:T(8,128)S(1)}, f32[17,256]{1,0:T(8,128)S(1)}, u32[]{:S(2)}, u32[]{:S(2)}) collective-permute-start(f32[17,256]{1,0:T(8,128)S(1)} %add_add_fusion.1), channel_id=1, source_target_pairs={{0,4},{1,5},{2,6},{3,7},{4,0},{5,1},{6,2},{7,3},{8,12},{9,13},{10,... | collective-permute-start | bytes 52232 | tf_op jit(solution)/shard_map/ppermute | solution.py:23
  133.9 4.7 %collective-permute-start.23 = (f32[17,256]{1,0:T(8,128)S(1)}, f32[17,256]{1,0:T(8,128)S(1)}, u32[]{:S(2)}, u32[]{:S(2)}) collective-permute-start(f32[17,256]{1,0:T(8,128)S(1)} %add_add_fusion.1), channel_id=1, source_target_pairs={{0,6},{1,7},{2,0},{3,1},{4,2},{5,3},{6,4},{7,5},{8,14},{9,15},{10,... | collective-permute-start | bytes 52232 | tf_op jit(solution)/shard_map/ppermute | solution.py:23
  133.9 5.9 %collective-permute-start.22 = (f32[17,256]{1,0:T(8,128)S(1)}, f32[17,256]{1,0:T(8,128)S(1)}, u32[]{:S(2)}, u32[]{:S(2)}) collective-permute-start(f32[17,256]{1,0:T(8,128)S(1)} %add_add_fusion.1), channel_id=1, source_target_pairs={{0,2},{1,3},{2,4},{3,5},{4,6},{5,7},{6,0},{7,1},{8,10},{9,11},{10,... | collective-permute-start | bytes 52232 | tf_op jit(solution)/shard_map/ppermute | solution.py:23
  140.5 8.8 %all-to-all-start.1 = ((f32[8,16,256]{2,1,0:T(8,128)}), f32[8,16,256]{2,1,0:T(8,128)S(1)}, u32[]{:S(2)}, u32[]{:S(2)}) async-start(f32[8,16,256]{2,1,0:T(8,128)} %broadcast_in_dim.11), calls=%async_computation.1 | async-start | bytes 262144 | tf_op jit(solution)/shard_map/all_to_all | solution.py:285

commit v7 on v5

--- a/solution.py
+++ b/solution.py
@@ -155,28 +155,39 @@
         name="finish",
     )(codes, row_scale.reshape(1, rows), decoded, kept, got)
 
-def matmul_kernel(own, far, across, far_across, *refs):
+DEPTH = 512
+
+
+def tile_copies(tiles, hess, sem):
+    copies = []
+    for tile in tiles:
+        for at in range(0, tile.shape[0], DEPTH):
+            n = len(copies)
+            copies.append(
+                pltpu.make_async_copy(
+                    tile.at[pl.ds(at, DEPTH)], hess.at[pl.ds(n * DEPTH, DEPTH)], sem.at[n]
+                )
+            )
+    return copies
+
+
+def multiply(held, hess, copies, out):
+    total = None
+    for n, copy in enumerate(copies):
+        copy.wait()
+        rows = slice(n * DEPTH, (n + 1) * DEPTH)
+        term = jnp.dot(held[:, rows], hess[rows], preferred_element_type=jnp.float32)
+        total = term if total is None else total + term
+    for s in range(4):
+        out[s] = total[s * 128 : (s + 1) * 128].astype(out.dtype)
+
+
+def first_kernel(own, far, *refs):
     blocks = refs[:-4]
     out, held, hess, sem = refs[-4:]
-    depth, width = 512, own.shape[1]
-
-    def fetch(part):
-        at = part * depth
-        tiles = (own, across) if at < own.shape[0] else (far, far_across)
-        copies = [
-            pltpu.make_async_copy(
-                tile.at[pl.ds(at % own.shape[0], depth)],
-                hess.at[pl.ds(at, depth), pl.ds(side * width, width)],
-                sem.at[2 * part + side],
-            )
-            for side, tile in enumerate(tiles)
-        ]
-        for copy in copies:
-            copy.start()
-        return copies
-
-    parts = hess.shape[0] // depth
-    fetched = [fetch(0)]
+    width = own.shape[1]
+    fetched = tile_copies((own, far), hess, sem)
+    fetched[0].start()
     z_lo, y_hi, y_lo, x, z_hi, core = (lax.axis_index(a) for a in AXES)
     step = 1 - 2 * core
     copies = []
@@ -195,24 +206,22 @@
                     pltpu.make_async_copy(
                         blocks[at].at[place, side],
                         held.at[pl.ds(rows, 128), pl.ds(columns, width)],
-                        sem.at[2 * parts + n],
+                        sem.at[len(fetched) + n],
                     )
                 )
                 copies[-1].start()
-    fetched += [fetch(part) for part in range(1, parts)]
+    for copy in fetched[1:]:
+        copy.start()
     for copy in copies:
         copy.wait()
-    total = None
-    for part in range(parts):
-        for copy in fetched[part]:
-            copy.wait()
-        at = part * depth
-        term = jnp.dot(
-            held[:, at : at + depth], hess[at : at + depth], preferred_element_type=jnp.float32
-        )
-        total = term if total is None else total + term
-    for s in range(4):
-        out[s] = total[s * 128 : (s + 1) * 128].astype(out.dtype)
+    multiply(held, hess, fetched, out)
+
+
+def second_kernel(held, across, far_across, out, hess, sem):
+    fetched = tile_copies((across, far_across), hess, sem)
+    for copy in fetched:
+        copy.start()
+    multiply(held, hess, fetched, out)
 
 
 def body(codes, codebooks, row_scale, initial, hessian):
@@ -254,26 +263,44 @@
     )
 
     blocks = [b for group in wide for b in group]
-    partial = pl.pallas_call(
-        matmul_kernel,
-        out_shape=jax.ShapeDtypeStruct((4, half, 2 * width), jnp.bfloat16),
-        in_specs=[pl.BlockSpec(memory_space=pl.ANY)] * (4 + len(blocks)),
-        out_specs=pl.BlockSpec(memory_space=pltpu.VMEM),
-        scratch_shapes=[
-            pltpu.VMEM((4 * half, 8 * width), jnp.bfloat16),
-            pltpu.VMEM((8 * width, 2 * width), jnp.bfloat16),
-            pltpu.SemaphoreType.DMA((48,)),
-        ],
+    hbm, vmem = pl.BlockSpec(memory_space=pl.ANY), pl.BlockSpec(memory_space=pltpu.VMEM)
+    settings = dict(
         compiler_params=pltpu.CompilerParams(vmem_limit_bytes=20 * 2**20),
         cost_estimate=pl.CostEstimate(
-            flops=2 * 512 * 4096 * 1024, bytes_accessed=13 * 2**20, transcendentals=0
+            flops=2 * 512 * 4096 * 512, bytes_accessed=8 * 2**20, transcendentals=0
         ),
-        name="matmul",
-    )(hessian, far, across, far_across, *blocks)
-
-    parts = lax.all_to_all(partial, ("z_lo", "y_hi"), 0, 0, tiled=True)
-    summed = jnp.sum(parts.astype(jnp.float32), axis=0)
-    kept, given = summed[:, :width], summed[:, width:]
+    )
+    sums = jax.ShapeDtypeStruct((4, half, width), jnp.bfloat16)
+    kept, held = pl.pallas_call(
+        first_kernel,
+        out_shape=(sums, jax.ShapeDtypeStruct((4 * half, 8 * width), jnp.bfloat16)),
+        in_specs=[hbm] * (2 + len(blocks)),
+        out_specs=(vmem, vmem),
+        scratch_shapes=[
+            pltpu.VMEM((8 * width, width), jnp.bfloat16),
+            pltpu.SemaphoreType.DMA((40,)),
+        ],
+        name="first",
+        **settings,
+    )(hessian, far, *blocks)
+    given = pl.pallas_call(
+        second_kernel,
+        out_shape=sums,
+        in_specs=[vmem, hbm, hbm],
+        out_specs=vmem,
+        scratch_shapes=[
+            pltpu.VMEM((8 * width, width), jnp.bfloat16),
+            pltpu.SemaphoreType.DMA((8,)),
+        ],
+        name="second",
+        **settings,
+    )(held, across, far_across)
+
+    def owned(partial):
+        parts = lax.all_to_all(partial, ("z_lo", "y_hi"), 0, 0, tiled=True)
+        return jnp.sum(parts.astype(jnp.float32), axis=0)
+
+    kept, given = lax.optimization_barrier((owned(kept), owned(given)))
     got = shift(given, "core", 1)
     product, total = finish(codes, row_scale, decoded, kept, got)
 

time: 144 us -> 147 us (1.021)
  blocking collectives: 18.8 us -> 0 us
  waiting for transfers between devices: 48 us -> 59.1 us
  starting transfers between devices: 56.9 us -> 62.1 us
  local copies, waits for them, and re-layouts: 2.32 us -> 6.41 us
    all_to_all x1 -> x0, blocking collectives: 18.8 us -> none  [body(): parts = lax.all_to_all(partial, ('z_lo', 'y_hi'), 0, 0, tiled=True)]
    all_to_all x0 -> x2, waiting for transfers between devices: none -> 13.9 us  [owned(): parts = lax.all_to_all(partial, ('z_lo', 'y_hi'), 0, 0, tiled=True)]
    all_to_all x0 -> x2, starting transfers between devices: none -> 6.94 us  [owned(): parts = lax.all_to_all(partial, ('z_lo', 'y_hi'), 0, 0, tiled=True)]
    unnamed x8 -> x12, local copies, waits for them, and re-layouts: 1.61 us -> 5.75 us
    ppermute x25, waiting for transfers between devices: 43.4 us -> 40.7 us  [send(): return lax.ppermute(a, AXES, pairs)]
    pallas_call x1 -> x2, Pallas kernels: 7.25 us -> 8.48 us  [the longest x1 4.73 us: body(): pl.pallas_call(first_kernel, out_shape=(sums, jax.ShapeDtypeStruct((4 * h...]
  transfers between devices with their start and end apart: 26 -> 28, of which waited for: 15 -> 16; matrix products, arithmetic and copies ran while one was open for 0% -> 0% of each run, Pallas kernels for 2% -> 8%
where the time goes in v7:
time: 147 us
  starting transfers between devices  62.1 us (42%)
  waiting for transfers between devices  59.1 us (40%)
  Pallas kernels  16.9 us (11%)
  local copies, waits for them, and re-layouts  6.41 us (4%)
    ppermute x25, starting transfers between devices, send(): return lax.ppermute(a, AXES, pairs)  51 us
    ppermute x25, waiting for transfers between devices, send(): return lax.ppermute(a, AXES, pairs)  40.7 us
    all_to_all x2, waiting for transfers between devices, owned(): parts = lax.all_to_all(partial, ('z_lo', 'y_hi'), 0, 0, tiled=True)  13.9 us
    all_to_all x2, starting transfers between devices, owned(): parts = lax.all_to_all(partial, ('z_lo', 'y_hi'), 0, 0, tiled=True)  6.94 us
    unnamed x12, local copies, waits for them, and re-layouts  5.75 us
    pallas_call x1, Pallas kernels, finish(): pl.pallas_call(finish_kernel, out_shape=(jax.ShapeDtypeStruct((rows, widt...  5.08 us
    pallas_call x1, Pallas kernels, body(): pl.pallas_call(first_kernel, out_shape=(sums, jax.ShapeDtypeStruct((4 * h...  4.73 us
    all_to_all x1, waiting for transfers between devices, body(): books = jnp.sum(lax.all_to_all(copies, ROW, 0, 0, tiled=True), axis=0)  4.5 us
  transfers between devices with their start and end apart: 28, of which 16 were waited for; matrix products, arithmetic and copies ran while one was open for 0% of the time, Pallas kernels for 8%

profile of v7, /device:TPU:8, one launch (start us, length us, event | category | flops | bytes accessed | tf_op | source)
XLA Modules:
  0.0 146.8 jit_solution(12038222065573438973)
XLA Ops:
  0.7 3.3 %decode.1 = (f32[512,256]{1,0:T(8,128)}, bf16[128,512]{1,0:T(8,128)(2,1)}, bf16[128,512]{1,0:T(8,128)(2,1)}) custom-call(s32[2,64,256]{2,1,0:T(8,128)} %bitcast.20, bf16[2,8,256]{2,1,0:T(8,128)(2,1)} %bitcast.28, f32[1,256]{1,0:T(1,128)} %bitcast.22, bf16[256,512]{1,0:T(8,128)(2,1)} %initial_in.1), custom_call_target="tpu_custom_call" | custom-call | flops 2097152 | bytes 1048576 | tf_op jit(solution)/shard_map/decode/pallas_call | solution.py:81
  4.1 1.6 %collective-permute-start = (bf16[128,512]{1,0:T(8,128)(2,1)}, bf16[128,512]{1,0:T(8,128)(2,1)S(1)}, u32[]{:S(2)}, u32[]{:S(2)}) collective-permute-start(bf16[128,512]{1,0:T(8,128)(2,1)} %get-tuple-element.26), channel_id=1, source_target_pairs={{0,0},{1,1},{2,2},{3,3},{4,4},{5,5},{6,6},{7,7},{8,72},{9,73},{10,... | collective-permute-start | bytes 393224 | tf_op jit(solution)/shard_map/ppermute | solution.py:23
  6.1 1.2 collective-permute-done.1
  7.4 2.3 %collective-permute-start.3 = (bf16[2048,512]{1,0:T(8,128)(2,1)}, bf16[2048,512]{1,0:T(8,128)(2,1)}, u32[]{:S(2)}, u32[]{:S(2)}) collective-permute-start(bf16[2048,512]{1,0:T(8,128)(2,1)} %own.1), channel_id=1, source_target_pairs={{0,32},{1,33},{2,34},{3,35},{4,36},{5,37},{6,38},{7,39},{8,40},{9,... | collective-permute-start | bytes 6291464 | tf_op jit(solution)/shard_map/ppermute | solution.py:23
  9.7 9.8 %collective-permute-start.7 = (bf16[1,2,128,512]{3,2,1,0:T(8,128)(2,1)S(1)}, bf16[1,2,128,512]{3,2,1,0:T(8,128)(2,1)S(1)}, u32[]{:S(2)}, u32[]{:S(2)}) collective-permute-start(bf16[1,2,128,512]{3,2,1,0:T(8,128)(2,1)S(1)} %bitcast.14), channel_id=1, source_target_pairs={{0,8},{1,25},{2,10},{3,27},{4,12},{5,29},{6,14},{7,31},{8,16},{9,1... | collective-permute-start | bytes 786440 | tf_op jit(solution)/shard_map/ppermute | solution.py:23
  19.5 3.3 %collective-permute-start.4 = (bf16[2,128,512]{2,1,0:T(8,128)(2,1)S(1)}, bf16[2,128,512]{2,1,0:T(8,128)(2,1)S(1)}, u32[]{:S(2)}, u32[]{:S(2)}) collective-permute-start(bf16[2,128,512]{2,1,0:T(8,128)(2,1)S(1)} %pad_maximum_fusion.1), channel_id=1, source_target_pairs={{0,2},{1,7},{2,4},{3,1},{4,6},{5,3},{6,0},{7,5},{8,10},{9,15},{10,... | collective-permute-start | bytes 786440 | tf_op jit(solution)/shard_map/ppermute | solution.py:23
  22.7 3.0 %collective-permute-start.5 = (bf16[2,128,512]{2,1,0:T(8,128)(2,1)S(1)}, bf16[2,128,512]{2,1,0:T(8,128)(2,1)S(1)}, u32[]{:S(2)}, u32[]{:S(2)}) collective-permute-start(bf16[2,128,512]{2,1,0:T(8,128)(2,1)S(1)} %pad_maximum_fusion.1), channel_id=1, source_target_pairs={{0,6},{1,3},{2,0},{3,5},{4,2},{5,7},{6,4},{7,1},{8,14},{9,11},{10,... | collective-permute-start | bytes 786440 | tf_op jit(solution)/shard_map/ppermute | solution.py:23
  25.8 3.8 %collective-permute-start.6 = (bf16[1,2,128,512]{3,2,1,0:T(8,128)(2,1)S(1)}, bf16[1,2,128,512]{3,2,1,0:T(8,128)(2,1)S(1)}, u32[]{:S(2)}, u32[]{:S(2)}) collective-permute-start(bf16[1,2,128,512]{3,2,1,0:T(8,128)(2,1)S(1)} %bitcast.15), channel_id=1, source_target_pairs={{0,24},{1,9},{2,26},{3,11},{4,28},{5,13},{6,30},{7,15},{8,0},{9,17... | collective-permute-start | bytes 786440 | tf_op jit(solution)/shard_map/ppermute | solution.py:23
  30.2 8.4 %collective-permute-start.11 = (bf16[2,128,512]{2,1,0:T(8,128)(2,1)S(1)}, bf16[2,128,512]{2,1,0:T(8,128)(2,1)S(1)}, u32[]{:S(2)}, u32[]{:S(2)}) collective-permute-start(bf16[2,128,512]{2,1,0:T(8,128)(2,1)S(1)} %collective-permute-done.4), channel_id=1, source_target_pairs={{0,2},{1,7},{2,4},{3,1},{4,6},{5,3},{6,0},{7,5},{8,10},{9,15},{10,... | collective-permute-start | bytes 786440 | tf_op jit(solution)/shard_map/ppermute | solution.py:23
  38.7 4.3 %collective-permute-start.10 = (bf16[2,2,128,512]{3,2,1,0:T(8,128)(2,1)S(1)}, bf16[2,2,128,512]{3,2,1,0:T(8,128)(2,1)S(1)}, u32[]{:S(2)}, u32[]{:S(2)}) collective-permute-start(bf16[2,2,128,512]{3,2,1,0:T(8,128)(2,1)S(1)} %pad_maximum_fusion.refs_4_), channel_id=1, source_target_pairs={{0,24},{1,9},{2,26},{3,11},{4,28},{5,13},{6,30},{7,15},{8,0},{9,17... | collective-permute-start | bytes 1572872 | tf_op jit(solution)/shard_map/ppermute | solution.py:23
  43.8 8.2 %collective-permute-start.13 = (bf16[1,2,128,512]{3,2,1,0:T(8,128)(2,1)S(1)}, bf16[1,2,128,512]{3,2,1,0:T(8,128)(2,1)S(1)}, u32[]{:S(2)}, u32[]{:S(2)}) collective-permute-start(bf16[1,2,128,512]{3,2,1,0:T(8,128)(2,1)S(1)} %bitcast.17), channel_id=1, source_target_pairs={{0,24},{1,9},{2,26},{3,11},{4,28},{5,13},{6,30},{7,15},{8,0},{9,17... | collective-permute-start | bytes 786440 | tf_op jit(solution)/shard_map/ppermute | solution.py:23
  52.0 6.8 %collective-permute-done.13.refs_10_ = bf16[1,2,128,512]{3,2,1,0:T(8,128)(2,1)S(1)} collective-permute-done((bf16[1,2,128,512]{3,2,1,0:T(8,128)(2,1)S(1)}, bf16[1,2,128,512]{3,2,1,0:T(8,128)(2,1)S(1)}, u32[]{:S(2)}, u32[]{:S(2)}) %collective-permute-start.13) | collective-permute-done | bytes 262176 | tf_op jit(solution)/shard_map/ppermute | solution.py:23
  58.8 5.8 %collective-permute-done.12.refs_9_ = bf16[1,2,128,512]{3,2,1,0:T(8,128)(2,1)S(1)} collective-permute-done((bf16[1,2,128,512]{3,2,1,0:T(8,128)(2,1)S(1)}, bf16[1,2,128,512]{3,2,1,0:T(8,128)(2,1)S(1)}, u32[]{:S(2)}, u32[]{:S(2)}) %collective-permute-start.12) | collective-permute-done | bytes 262176 | tf_op jit(solution)/shard_map/ppermute | solution.py:23
  64.7 13.1 %collective-permute-done.15.refs_11_ = bf16[1,2,128,512]{3,2,1,0:T(8,128)(2,1)S(1)} collective-permute-done((bf16[1,2,128,512]{3,2,1,0:T(8,128)(2,1)S(1)}, bf16[1,2,128,512]{3,2,1,0:T(8,128)(2,1)S(1)}, u32[]{:S(2)}, u32[]{:S(2)}) %collective-permute-start.15) | collective-permute-done | bytes 262176 | tf_op jit(solution)/shard_map/ppermute | solution.py:23
  77.8 1.6 %copy-done.2 = bf16[2048,512]{1,0:T(8,128)(2,1)S(1)} copy-done((bf16[2048,512]{1,0:T(8,128)(2,1)S(1)}, bf16[2048,512]{1,0:T(8,128)(2,1)}, u32[]{:S(2)}) %copy-start.2) | copy-done | bytes 2097176
  79.4 4.7 %first.1 = (bf16[4,128,512]{2,1,0:T(8,128)(2,1)}, bf16[512,4096]{1,0:T(8,128)(2,1)S(1)}) custom-call(bf16[2048,512]{1,0:T(8,128)(2,1)S(1)} %copy-done.2, bf16[2048,512]{1,0:T(8,128)(2,1)} %collective-permute-done.3.far, bf16[1,2,128,512]{3,2,1,0:T(8,128)(2,1)S(1)} %bitcast.16, bf16[1,2,128,512]{3,2,1,0:T(8,128)(2,1)S(1)} %collective-permute-done.7.refs_1_, ...), custom_call_target="tpu_custom_call" | custom-call | flops 2147483648 | bytes 8388608 | tf_op jit(solution)/shard_map/first/pallas_call | solution.py:274
  84.2 2.0 %copy-done = bf16[512,4096]{1,0:T(8,128)(2,1)} copy-done((bf16[512,4096]{1,0:T(8,128)(2,1)}, bf16[512,4096]{1,0:T(8,128)(2,1)S(1)}, u32[]{:S(2)}) %copy-start) | copy-done | bytes 4194328
  86.1 3.5 %all-to-all-start = ((bf16[4,128,512]{2,1,0:T(8,128)(2,1)}), bf16[4,128,512]{2,1,0:T(8,128)(2,1)S(1)}, u32[]{:S(2)}, u32[]{:S(2)}) async-start(bf16[4,128,512]{2,1,0:T(8,128)(2,1)} %get-tuple-element.40), calls=%async_computation | async-start | bytes 1048576 | tf_op jit(solution)/shard_map/all_to_all | solution.py:300
  89.6 2.2 %copy-done.1 = bf16[512,4096]{1,0:T(8,128)(2,1)S(1)} copy-done((bf16[512,4096]{1,0:T(8,128)(2,1)S(1)}, bf16[512,4096]{1,0:T(8,128)(2,1)}, u32[]{:S(2)}) %copy-start.1) | copy-done | bytes 4194328
  91.8 3.8 %second.1 = bf16[4,128,512]{2,1,0:T(8,128)(2,1)} custom-call(bf16[512,4096]{1,0:T(8,128)(2,1)S(1)} %copy-done.1, bf16[2048,512]{1,0:T(8,128)(2,1)S(1)} %collective-permute-done.2.across, bf16[2048,512]{1,0:T(8,128)(2,1)} %collective-permute-done.16.far_across), custom_call_target="tpu_custom_call" | custom-call | flops 2147483648 | bytes 8388608 | tf_op jit(solution)/shard_map/second/pallas_call | solution.py:286
  95.6 4.4 %all-to-all-done = bf16[4,128,512]{2,1,0:T(8,128)(2,1)S(1)} async-done(((bf16[4,128,512]{2,1,0:T(8,128)(2,1)}), bf16[4,128,512]{2,1,0:T(8,128)(2,1)S(1)}, u32[]{:S(2)}, u32[]{:S(2)}) %all-to-all-start) | async-done | bytes 524320 | tf_op jit(solution)/shard_map/all_to_all | solution.py:300
  100.0 3.5 %all-to-all-start.1 = ((bf16[4,128,512]{2,1,0:T(8,128)(2,1)}), bf16[4,128,512]{2,1,0:T(8,128)(2,1)S(1)}, u32[]{:S(2)}, u32[]{:S(2)}) async-start(bf16[4,128,512]{2,1,0:T(8,128)(2,1)} %second.1), calls=%async_computation.1 | async-start | bytes 1048576 | tf_op jit(solution)/shard_map/all_to_all | solution.py:300
  103.5 9.5 %all-to-all-done.1 = bf16[4,128,512]{2,1,0:T(8,128)(2,1)S(1)} async-done(((bf16[4,128,512]{2,1,0:T(8,128)(2,1)}), bf16[4,128,512]{2,1,0:T(8,128)(2,1)S(1)}, u32[]{:S(2)}, u32[]{:S(2)}) %all-to-all-start.1) | async-done | bytes 524320 | tf_op jit(solution)/shard_map/all_to_all | solution.py:300
  113.2 1.5 %collective-permute-done.17.got = f32[128,512]{1,0:T(8,128)S(1)} collective-permute-done((f32[128,512]{1,0:T(8,128)S(1)}, f32[128,512]{1,0:T(8,128)S(1)}, u32[]{:S(2)}, u32[]{:S(2)}) %collective-permute-start.17) | collective-permute-done | bytes 262176 | tf_op jit(solution)/shard_map/ppermute | solution.py:23
  114.8 5.1 %finish.1 = (f32[256,512]{1,0:T(8,128)}, f32[17,256]{1,0:T(8,128)S(1)}) custom-call(s32[2,64,256]{2,1,0:T(8,128)S(1)} %bitcast.21, f32[1,256]{1,0:T(1,128)S(1)} %bitcast.23, f32[512,256]{1,0:T(8,128)S(1)} %copy-done.5, f32[128,512]{1,0:T(8,128)S(1)} %convert_reduce_fusion.1.kept, f32[128,512]{1,0:T(8,128)S(1)} %collective-permute-done.17.got), custom_call_target="tpu_custom_call" | custom-call | flops 4294967296 | bytes 2097152 | tf_op jit(solution)/shard_map/finish/pallas_call | solution.py:148
  121.1 1.4 collective-permute-start.20
  123.2 3.3 %collective-permute-done.21 = f32[17,256]{1,0:T(8,128)S(1)} collective-permute-done((f32[17,256]{1,0:T(8,128)S(1)}, f32[17,256]{1,0:T(8,128)S(1)}, u32[]{:S(2)}, u32[]{:S(2)}) %collective-permute-start.21) | collective-permute-done | bytes 17440 | tf_op jit(solution)/shard_map/ppermute | solution.py:23
  127.7 1.4 collective-permute-start.23
  129.1 1.7 %collective-permute-start.22 = (f32[17,256]{1,0:T(8,128)S(1)}, f32[17,256]{1,0:T(8,128)S(1)}, u32[]{:S(2)}, u32[]{:S(2)}) collective-permute-start(f32[17,256]{1,0:T(8,128)S(1)} %add_add_fusion.1), channel_id=1, source_target_pairs={{0,2},{1,3},{2,4},{3,5},{4,6},{5,7},{6,0},{7,1},{8,10},{9,11},{10,... | collective-permute-start | bytes 52232 | tf_op jit(solution)/shard_map/ppermute | solution.py:23
  130.8 5.2 %collective-permute-done.24 = f32[17,256]{1,0:T(8,128)S(1)} collective-permute-done((f32[17,256]{1,0:T(8,128)S(1)}, f32[17,256]{1,0:T(8,128)S(1)}, u32[]{:S(2)}, u32[]{:S(2)}) %collective-permute-start.24) | collective-permute-done | bytes 17440 | tf_op jit(solution)/shard_map/ppermute | solution.py:23
  136.9 4.2 %all-to-all-start.2 = ((f32[8,16,256]{2,1,0:T(8,128)}), f32[8,16,256]{2,1,0:T(8,128)S(1)}, u32[]{:S(2)}, u32[]{:S(2)}) async-start(f32[8,16,256]{2,1,0:T(8,128)} %broadcast_in_dim.11), calls=%async_computation.2 | async-start | bytes 262144 | tf_op jit(solution)/shard_map/all_to_all | solution.py:312
  141.7 4.5 %all-to-all-done.2 = f32[8,16,256]{2,1,0:T(8,128)S(1)} async-done(((f32[8,16,256]{2,1,0:T(8,128)}), f32[8,16,256]{2,1,0:T(8,128)S(1)}, u32[]{:S(2)}, u32[]{:S(2)}) %all-to-all-start.2) | async-done | bytes 131104 | tf_op jit(solution)/shard_map/all_to_all | solution.py:312
  (52 shorter events, 7.7 us)
Async XLA Ops:
  0.6 6.7 %collective-permute-start.2 = (bf16[2048,512]{1,0:T(8,128)(2,1)}, bf16[2048,512]{1,0:T(8,128)(2,1)S(1)}, u32[]{:S(2)}, u32[]{:S(2)}) collective-permute-start(bf16[2048,512]{1,0:T(8,128)(2,1)} %own.1), channel_id=1, source_target_pairs={{0,1},{1,0},{2,3},{3,2},{4,5},{5,4},{6,7},{7,6},{8,9},{9,8},{10,11... | collective-permute-start | bytes 6291464 | tf_op jit(solution)/shard_map/ppermute | solution.py:23
  4.1 2.1 %collective-permute-start = (bf16[128,512]{1,0:T(8,128)(2,1)}, bf16[128,512]{1,0:T(8,128)(2,1)S(1)}, u32[]{:S(2)}, u32[]{:S(2)}) collective-permute-start(bf16[128,512]{1,0:T(8,128)(2,1)} %get-tuple-element.26), channel_id=1, source_target_pairs={{0,0},{1,1},{2,2},{3,3},{4,4},{5,5},{6,6},{7,7},{8,72},{9,73},{10,... | collective-permute-start | bytes 393224 | tf_op jit(solution)/shard_map/ppermute | solution.py:23
  5.7 1.7 %collective-permute-start.1 = (bf16[128,512]{1,0:T(8,128)(2,1)}, bf16[128,512]{1,0:T(8,128)(2,1)S(1)}, u32[]{:S(2)}, u32[]{:S(2)}) collective-permute-start(bf16[128,512]{1,0:T(8,128)(2,1)} %get-tuple-element.27), channel_id=1, source_target_pairs={{0,1},{1,0},{2,3},{3,2},{4,5},{5,4},{6,7},{7,6},{8,73},{9,72},{10,... | collective-permute-start | bytes 393224 | tf_op jit(solution)/shard_map/ppermute | solution.py:23
  7.4 70.4 %collective-permute-start.3 = (bf16[2048,512]{1,0:T(8,128)(2,1)}, bf16[2048,512]{1,0:T(8,128)(2,1)}, u32[]{:S(2)}, u32[]{:S(2)}) collective-permute-start(bf16[2048,512]{1,0:T(8,128)(2,1)} %own.1), channel_id=1, source_target_pairs={{0,32},{1,33},{2,34},{3,35},{4,36},{5,37},{6,38},{7,39},{8,40},{9,... | collective-permute-start | bytes 6291464 | tf_op jit(solution)/shard_map/ppermute | solution.py:23
  9.7 19.9 %collective-permute-start.7 = (bf16[1,2,128,512]{3,2,1,0:T(8,128)(2,1)S(1)}, bf16[1,2,128,512]{3,2,1,0:T(8,128)(2,1)S(1)}, u32[]{:S(2)}, u32[]{:S(2)}) collective-permute-start(bf16[1,2,128,512]{3,2,1,0:T(8,128)(2,1)S(1)} %bitcast.14), channel_id=1, source_target_pairs={{0,8},{1,25},{2,10},{3,27},{4,12},{5,29},{6,14},{7,31},{8,16},{9,1... | collective-permute-start | bytes 786440 | tf_op jit(solution)/shard_map/ppermute | solution.py:23
  19.5 10.7 %collective-permute-start.4 = (bf16[2,128,512]{2,1,0:T(8,128)(2,1)S(1)}, bf16[2,128,512]{2,1,0:T(8,128)(2,1)S(1)}, u32[]{:S(2)}, u32[]{:S(2)}) collective-permute-start(bf16[2,128,512]{2,1,0:T(8,128)(2,1)S(1)} %pad_maximum_fusion.1), channel_id=1, source_target_pairs={{0,2},{1,7},{2,4},{3,1},{4,6},{5,3},{6,0},{7,5},{8,10},{9,15},{10,... | collective-permute-start | bytes 786440 | tf_op jit(solution)/shard_map/ppermute | solution.py:23
  22.7 15.9 %collective-permute-start.5 = (bf16[2,128,512]{2,1,0:T(8,128)(2,1)S(1)}, bf16[2,128,512]{2,1,0:T(8,128)(2,1)S(1)}, u32[]{:S(2)}, u32[]{:S(2)}) collective-permute-start(bf16[2,128,512]{2,1,0:T(8,128)(2,1)S(1)} %pad_maximum_fusion.1), channel_id=1, source_target_pairs={{0,6},{1,3},{2,0},{3,5},{4,2},{5,7},{6,4},{7,1},{8,14},{9,11},{10,... | collective-permute-start | bytes 786440 | tf_op jit(solution)/shard_map/ppermute | solution.py:23
  25.8 13.0 %collective-permute-start.6 = (bf16[1,2,128,512]{3,2,1,0:T(8,128)(2,1)S(1)}, bf16[1,2,128,512]{3,2,1,0:T(8,128)(2,1)S(1)}, u32[]{:S(2)}, u32[]{:S(2)}) collective-permute-start(bf16[1,2,128,512]{3,2,1,0:T(8,128)(2,1)S(1)} %bitcast.15), channel_id=1, source_target_pairs={{0,24},{1,9},{2,26},{3,11},{4,28},{5,13},{6,30},{7,15},{8,0},{9,17... | collective-permute-start | bytes 786440 | tf_op jit(solution)/shard_map/ppermute | solution.py:23
  29.6 9.1 %collective-permute-start.8 = (bf16[1,2,128,512]{3,2,1,0:T(8,128)(2,1)S(1)}, bf16[1,2,128,512]{3,2,1,0:T(8,128)(2,1)S(1)}, u32[]{:S(2)}, u32[]{:S(2)}) collective-permute-start(bf16[1,2,128,512]{3,2,1,0:T(8,128)(2,1)S(1)} %collective-permute-done.7.refs_1_), channel_id=1, source_target_pairs={{0,8},{1,25},{2,10},{3,27},{4,12},{5,29},{6,14},{7,31},{8,16},{9,1... | collective-permute-start | bytes 786440 | tf_op jit(solution)/shard_map/ppermute | solution.py:23
  30.2 13.6 %collective-permute-start.11 = (bf16[2,128,512]{2,1,0:T(8,128)(2,1)S(1)}, bf16[2,128,512]{2,1,0:T(8,128)(2,1)S(1)}, u32[]{:S(2)}, u32[]{:S(2)}) collective-permute-start(bf16[2,128,512]{2,1,0:T(8,128)(2,1)S(1)} %collective-permute-done.4), channel_id=1, source_target_pairs={{0,2},{1,7},{2,4},{3,1},{4,6},{5,3},{6,0},{7,5},{8,10},{9,15},{10,... | collective-permute-start | bytes 786440 | tf_op jit(solution)/shard_map/ppermute | solution.py:23
  38.7 25.9 %collective-permute-start.10 = (bf16[2,2,128,512]{3,2,1,0:T(8,128)(2,1)S(1)}, bf16[2,2,128,512]{3,2,1,0:T(8,128)(2,1)S(1)}, u32[]{:S(2)}, u32[]{:S(2)}) collective-permute-start(bf16[2,2,128,512]{3,2,1,0:T(8,128)(2,1)S(1)} %pad_maximum_fusion.refs_4_), channel_id=1, source_target_pairs={{0,24},{1,9},{2,26},{3,11},{4,28},{5,13},{6,30},{7,15},{8,0},{9,17... | collective-permute-start | bytes 1572872 | tf_op jit(solution)/shard_map/ppermute | solution.py:23
  43.0 21.5 %collective-permute-start.9 = (bf16[2,2,128,512]{3,2,1,0:T(8,128)(2,1)S(1)}, bf16[2,2,128,512]{3,2,1,0:T(8,128)(2,1)S(1)}, u32[]{:S(2)}, u32[]{:S(2)}) collective-permute-start(bf16[2,2,128,512]{3,2,1,0:T(8,128)(2,1)S(1)} %pad_maximum_fusion.refs_4_), channel_id=1, source_target_pairs={{0,8},{1,25},{2,10},{3,27},{4,12},{5,29},{6,14},{7,31},{8,16},{9,1... | collective-permute-start | bytes 1572872 | tf_op jit(solution)/shard_map/ppermute | solution.py:23
  43.8 15.0 %collective-permute-start.13 = (bf16[1,2,128,512]{3,2,1,0:T(8,128)(2,1)S(1)}, bf16[1,2,128,512]{3,2,1,0:T(8,128)(2,1)S(1)}, u32[]{:S(2)}, u32[]{:S(2)}) collective-permute-start(bf16[1,2,128,512]{3,2,1,0:T(8,128)(2,1)S(1)} %bitcast.17), channel_id=1, source_target_pairs={{0,24},{1,9},{2,26},{3,11},{4,28},{5,13},{6,30},{7,15},{8,0},{9,17... | collective-permute-start | bytes 786440 | tf_op jit(solution)/shard_map/ppermute | solution.py:23
  52.0 12.6 %collective-permute-start.12 = (bf16[1,2,128,512]{3,2,1,0:T(8,128)(2,1)S(1)}, bf16[1,2,128,512]{3,2,1,0:T(8,128)(2,1)S(1)}, u32[]{:S(2)}, u32[]{:S(2)}) collective-permute-start(bf16[1,2,128,512]{3,2,1,0:T(8,128)(2,1)S(1)} %bitcast.18), channel_id=1, source_target_pairs={{0,8},{1,25},{2,10},{3,27},{4,12},{5,29},{6,14},{7,31},{8,16},{9,1... | collective-permute-start | bytes 786440 | tf_op jit(solution)/shard_map/ppermute | solution.py:23
  64.6 13.2 %collective-permute-start.14 = (bf16[2,2,128,512]{3,2,1,0:T(8,128)(2,1)S(1)}, bf16[2,2,128,512]{3,2,1,0:T(8,128)(2,1)S(1)}, u32[]{:S(2)}, u32[]{:S(2)}) collective-permute-start(bf16[2,2,128,512]{3,2,1,0:T(8,128)(2,1)S(1)} %collective-permute-done.9.refs_5_), channel_id=1, source_target_pairs={{0,8},{1,25},{2,10},{3,27},{4,12},{5,29},{6,14},{7,31},{8,16},{9,1... | collective-permute-start | bytes 1572872 | tf_op jit(solution)/shard_map/ppermute | solution.py:23
  64.6 13.2 %collective-permute-start.15 = (bf16[1,2,128,512]{3,2,1,0:T(8,128)(2,1)S(1)}, bf16[1,2,128,512]{3,2,1,0:T(8,128)(2,1)S(1)}, u32[]{:S(2)}, u32[]{:S(2)}) collective-permute-start(bf16[1,2,128,512]{3,2,1,0:T(8,128)(2,1)S(1)} %collective-permute-done.12.refs_9_), channel_id=1, source_target_pairs={{0,8},{1,25},{2,10},{3,27},{4,12},{5,29},{6,14},{7,31},{8,16},{9,1... | collective-permute-start | bytes 786440 | tf_op jit(solution)/shard_map/ppermute | solution.py:23
  77.8 11.8 %collective-permute-start.16 = (bf16[2048,512]{1,0:T(8,128)(2,1)}, bf16[2048,512]{1,0:T(8,128)(2,1)}, u32[]{:S(2)}, u32[]{:S(2)}) collective-permute-start(bf16[2048,512]{1,0:T(8,128)(2,1)} %collective-permute-done.3.far), channel_id=1, source_target_pairs={{0,1},{1,0},{2,3},{3,2},{4,5},{5,4},{6,7},{7,6},{8,9},{9,8},{10,11... | collective-permute-start | bytes 6291464 | tf_op jit(solution)/shard_map/ppermute | solution.py:23
  86.1 13.9 %all-to-all-start = ((bf16[4,128,512]{2,1,0:T(8,128)(2,1)}), bf16[4,128,512]{2,1,0:T(8,128)(2,1)S(1)}, u32[]{:S(2)}, u32[]{:S(2)}) async-start(bf16[4,128,512]{2,1,0:T(8,128)(2,1)} %get-tuple-element.40), calls=%async_computation | async-start | bytes 1048576 | tf_op jit(solution)/shard_map/all_to_all | solution.py:300
  89.6 2.2 %copy-start.1 = (bf16[512,4096]{1,0:T(8,128)(2,1)S(1)}, bf16[512,4096]{1,0:T(8,128)(2,1)}, u32[]{:S(2)}) copy-start(bf16[512,4096]{1,0:T(8,128)(2,1)} %copy-done) | copy-start | bytes 12582916
  95.6 19.2 %copy-start.3 = (s32[2,256,64]{1,2,0:T(8,128)S(1)}, s32[2,256,64]{1,2,0:T(8,128)}, u32[]{:S(2)}) copy-start(s32[2,256,64]{1,2,0:T(8,128)} %param.5) | copy-start | bytes 393220
  95.6 19.2 %copy-start.4 = (f32[256]{0:T(256)S(1)}, f32[256]{0:T(256)}, u32[]{:S(2)}) copy-start(f32[256]{0:T(256)} %param.7) | copy-start | bytes 3076
  95.6 19.2 %copy-start.5 = (f32[512,256]{1,0:T(8,128)S(1)}, f32[512,256]{1,0:T(8,128)}, u32[]{:S(2)}) copy-start(f32[512,256]{1,0:T(8,128)} %get-tuple-element.25.decoded) | copy-start | bytes 1572868
  100.0 13.1 %all-to-all-start.1 = ((bf16[4,128,512]{2,1,0:T(8,128)(2,1)}), bf16[4,128,512]{2,1,0:T(8,128)(2,1)S(1)}, u32[]{:S(2)}, u32[]{:S(2)}) async-start(bf16[4,128,512]{2,1,0:T(8,128)(2,1)} %second.1), calls=%async_computation.1 | async-start | bytes 1048576 | tf_op jit(solution)/shard_map/all_to_all | solution.py:300
  113.1 1.6 %collective-permute-start.17 = (f32[128,512]{1,0:T(8,128)S(1)}, f32[128,512]{1,0:T(8,128)S(1)}, u32[]{:S(2)}, u32[]{:S(2)}) collective-permute-start(f32[128,512]{1,0:T(8,128)S(1)} %convert_reduce_fusion), channel_id=1, source_target_pairs={{0,1},{1,0},{2,3},{3,2},{4,5},{5,4},{6,7},{7,6},{8,9},{9,8},{10,11... | collective-permute-start | bytes 786440 | tf_op jit(solution)/shard_map/ppermute | solution.py:23
  119.9 1.2 collective-permute-start.18
  121.1 5.4 %collective-permute-start.21 = (f32[17,256]{1,0:T(8,128)S(1)}, f32[17,256]{1,0:T(8,128)S(1)}, u32[]{:S(2)}, u32[]{:S(2)}) collective-permute-start(f32[17,256]{1,0:T(8,128)S(1)} %add.21), channel_id=1, source_target_pairs={{0,16},{1,17},{2,18},{3,19},{4,20},{5,21},{6,22},{7,23},{8,24},{9,... | collective-permute-start | bytes 52232 | tf_op jit(solution)/shard_map/ppermute | solution.py:23
  121.1 5.4 %collective-permute-start.20 = (f32[17,256]{1,0:T(8,128)S(1)}, f32[17,256]{1,0:T(8,128)S(1)}, u32[]{:S(2)}, u32[]{:S(2)}) collective-permute-start(f32[17,256]{1,0:T(8,128)S(1)} %add.21), channel_id=1, source_target_pairs={{0,24},{1,25},{2,26},{3,27},{4,28},{5,29},{6,30},{7,31},{8,0},{9,1... | collective-permute-start | bytes 52232 | tf_op jit(solution)/shard_map/ppermute | solution.py:23
  122.5 5.0 %collective-permute-start.19 = (f32[17,256]{1,0:T(8,128)S(1)}, f32[17,256]{1,0:T(8,128)S(1)}, u32[]{:S(2)}, u32[]{:S(2)}) collective-permute-start(f32[17,256]{1,0:T(8,128)S(1)} %add.21), channel_id=1, source_target_pairs={{0,8},{1,9},{2,10},{3,11},{4,12},{5,13},{6,14},{7,15},{8,16},{9,17... | collective-permute-start | bytes 52232 | tf_op jit(solution)/shard_map/ppermute | solution.py:23
  127.6 8.4 %collective-permute-start.24 = (f32[17,256]{1,0:T(8,128)S(1)}, f32[17,256]{1,0:T(8,128)S(1)}, u32[]{:S(2)}, u32[]{:S(2)}) collective-permute-start(f32[17,256]{1,0:T(8,128)S(1)} %add_add_fusion.1), channel_id=1, source_target_pairs={{0,4},{1,5},{2,6},{3,7},{4,0},{5,1},{6,2},{7,3},{8,12},{9,13},{10,... | collective-permute-start | bytes 52232 | tf_op jit(solution)/shard_map/ppermute | solution.py:23
  127.7 8.3 %collective-permute-start.23 = (f32[17,256]{1,0:T(8,128)S(1)}, f32[17,256]{1,0:T(8,128)S(1)}, u32[]{:S(2)}, u32[]{:S(2)}) collective-permute-start(f32[17,256]{1,0:T(8,128)S(1)} %add_add_fusion.1), channel_id=1, source_target_pairs={{0,6},{1,7},{2,0},{3,1},{4,2},{5,3},{6,4},{7,5},{8,14},{9,15},{10,... | collective-permute-start | bytes 52232 | tf_op jit(solution)/shard_map/ppermute | solution.py:23
  129.1 7.1 %collective-permute-start.22 = (f32[17,256]{1,0:T(8,128)S(1)}, f32[17,256]{1,0:T(8,128)S(1)}, u32[]{:S(2)}, u32[]{:S(2)}) collective-permute-start(f32[17,256]{1,0:T(8,128)S(1)} %add_add_fusion.1), channel_id=1, source_target_pairs={{0,2},{1,3},{2,4},{3,5},{4,6},{5,7},{6,0},{7,1},{8,10},{9,11},{10,... | collective-permute-start | bytes 52232 | tf_op jit(solution)/shard_map/ppermute | solution.py:23
  136.9 9.3 %all-to-all-start.2 = ((f32[8,16,256]{2,1,0:T(8,128)}), f32[8,16,256]{2,1,0:T(8,128)S(1)}, u32[]{:S(2)}, u32[]{:S(2)}) async-start(f32[8,16,256]{2,1,0:T(8,128)} %broadcast_in_dim.11), calls=%async_computation.2 | async-start | bytes 262144 | tf_op jit(solution)/shard_map/all_to_all | solution.py:312
  (2 other events, 3.6 us)

commit v8 on v7

--- a/solution.py
+++ b/solution.py
@@ -171,7 +171,7 @@
     return copies
 
 
-def multiply(held, hess, copies, out):
+def multiply(held, hess, copies, out, at=0):
     total = None
     for n, copy in enumerate(copies):
         copy.wait()
@@ -179,7 +179,7 @@
         term = jnp.dot(held[:, rows], hess[rows], preferred_element_type=jnp.float32)
         total = term if total is None else total + term
     for s in range(4):
-        out[s] = total[s * 128 : (s + 1) * 128].astype(out.dtype)
+        out[s, :, at : at + hess.shape[1]] = total[s * 128 : (s + 1) * 128].astype(out.dtype)
 
 
 def first_kernel(own, far, *refs):
@@ -217,11 +217,13 @@
     multiply(held, hess, fetched, out)
 
 
-def second_kernel(held, across, far_across, out, hess, sem):
+def second_kernel(kept, held, across, far_across, out, hess, sem):
     fetched = tile_copies((across, far_across), hess, sem)
     for copy in fetched:
         copy.start()
-    multiply(held, hess, fetched, out)
+    width = hess.shape[1]
+    out[:, :, :width] = kept[...]
+    multiply(held, hess, fetched, out, width)
 
 
 def body(codes, codebooks, row_scale, initial, hessian):
@@ -250,9 +252,7 @@
     near_back, near_on = turn(near, "x", 1), turn(near, "x", -1)
     last = turn(z_back, "z_hi", 1)[None]
     last_back, last_on = turn(last, "x", 1), turn(last, "x", -1)
-    near_back, near_on, last_back, last_on = lax.optimization_barrier(
-        (near_back, near_on, last_back, last_on)
-    )
+    near_on, last_back, last_on, own_two = lax.optimization_barrier((near_on, last_back, last_on, own_two))
     near_two, last_two = turn(near_back, "x", 1), turn(last_back, "x", 1)
     far, near_two, last_two = lax.optimization_barrier((far, near_two, last_two))
     far_across = shift(far, "core", 1)
@@ -283,10 +283,10 @@
         name="first",
         **settings,
     )(hessian, far, *blocks)
-    given = pl.pallas_call(
+    partial = pl.pallas_call(
         second_kernel,
-        out_shape=sums,
-        in_specs=[vmem, hbm, hbm],
+        out_shape=jax.ShapeDtypeStruct((4, half, 2 * width), jnp.bfloat16),
+        in_specs=[vmem, vmem, hbm, hbm],
         out_specs=vmem,
         scratch_shapes=[
             pltpu.VMEM((8 * width, width), jnp.bfloat16),
@@ -294,13 +294,11 @@
         ],
         name="second",
         **settings,
-    )(held, across, far_across)
-
-    def owned(partial):
-        parts = lax.all_to_all(partial, ("z_lo", "y_hi"), 0, 0, tiled=True)
-        return jnp.sum(parts.astype(jnp.float32), axis=0)
-
-    kept, given = lax.optimization_barrier((owned(kept), owned(given)))
+    )(kept, held, across, far_across)
+
+    parts = lax.all_to_all(partial, ("z_lo", "y_hi"), 0, 0, tiled=True)
+    summed = jnp.sum(parts.astype(jnp.float32), axis=0)
+    kept, given = summed[:, :width], summed[:, width:]
     got = shift(given, "core", 1)
     product, total = finish(codes, row_scale, decoded, kept, got)
 

time: 147 us -> 138 us (0.939)
  blocking collectives: 0 us -> 21.8 us
  waiting for transfers between devices: 59.1 us -> 45.6 us
  starting transfers between devices: 62.1 us -> 50.4 us
  local copies, waits for them, and re-layouts: 6.41 us -> 2.3 us
    all_to_all x0 -> x1, blocking collectives: none -> 21.8 us  [body(): parts = lax.all_to_all(partial, ('z_lo', 'y_hi'), 0, 0, tiled=True)]
    all_to_all x2 -> x0, waiting for transfers between devices: 13.9 us -> none  [owned(): parts = lax.all_to_all(partial, ('z_lo', 'y_hi'), 0, 0, tiled=True)]
    all_to_all x2 -> x0, starting transfers between devices: 6.94 us -> none  [owned(): parts = lax.all_to_all(partial, ('z_lo', 'y_hi'), 0, 0, tiled=True)]
    ppermute x25, starting transfers between devices: 51 us -> 45.8 us  [send(): return lax.ppermute(a, AXES, pairs)]
    unnamed x12 -> x8, local copies, waits for them, and re-layouts: 5.75 us -> 1.61 us
  transfers between devices with their start and end apart: 28 -> 26, of which waited for: 16 -> 15; matrix products, arithmetic and copies ran while one was open for 0% -> 0% of each run, Pallas kernels for 8% -> 5%
where the time goes in v8:
time: 138 us
  starting transfers between devices  50.4 us (37%)
  waiting for transfers between devices  45.6 us (33%)
  blocking collectives  21.8 us (16%)
  Pallas kernels  15.6 us (11%)
  local copies, waits for them, and re-layouts  2.3 us (2%)
  other arithmetic  1.47 us (1%)
    ppermute x25, starting transfers between devices, send(): return lax.ppermute(a, AXES, pairs)  45.8 us
    ppermute x25, waiting for transfers between devices, send(): return lax.ppermute(a, AXES, pairs)  41.1 us
    all_to_all x1, blocking collectives, body(): parts = lax.all_to_all(partial, ('z_lo', 'y_hi'), 0, 0, tiled=True)  21.8 us
    pallas_call x1, Pallas kernels, finish(): pl.pallas_call(finish_kernel, out_shape=(jax.ShapeDtypeStruct((rows, widt...  5.08 us
    all_to_all x1, starting transfers between devices, body(): books = jnp.sum(lax.all_to_all(copies, ROW, 0, 0, tiled=True), axis=0)  4.62 us
    all_to_all x1, waiting for transfers between devices, body(): books = jnp.sum(lax.all_to_all(copies, ROW, 0, 0, tiled=True), axis=0)  4.54 us
    pallas_call x1, Pallas kernels, body(): pl.pallas_call(first_kernel, out_shape=(sums, jax.ShapeDtypeStruct((4 * h...  4.01 us
    pallas_call x1, Pallas kernels, decode(): pl.pallas_call(decode_kernel, out_shape=(jax.ShapeDtypeStruct((width, row...  3.36 us
  transfers between devices with their start and end apart: 26, of which 15 were waited for; matrix products, arithmetic and copies ran while one was open for 0% of the time, Pallas kernels for 5%

profile of v8, /device:TPU:8, one launch (start us, length us, event | category | flops | bytes accessed | tf_op | source)
XLA Modules:
  0.0 138.0 jit_solution(8320598426906948110)
XLA Ops:
  0.7 3.4 %decode.1 = (f32[512,256]{1,0:T(8,128)}, bf16[128,512]{1,0:T(8,128)(2,1)}, bf16[128,512]{1,0:T(8,128)(2,1)}) custom-call(s32[2,64,256]{2,1,0:T(8,128)} %bitcast.20, bf16[2,8,256]{2,1,0:T(8,128)(2,1)} %bitcast.28, f32[1,256]{1,0:T(1,128)} %bitcast.22, bf16[256,512]{1,0:T(8,128)(2,1)} %initial_in.1), custom_call_target="tpu_custom_call" | custom-call | flops 2097152 | bytes 1048576 | tf_op jit(solution)/shard_map/decode/pallas_call | solution.py:81
  4.1 1.6 %collective-permute-start = (bf16[128,512]{1,0:T(8,128)(2,1)}, bf16[128,512]{1,0:T(8,128)(2,1)S(1)}, u32[]{:S(2)}, u32[]{:S(2)}) collective-permute-start(bf16[128,512]{1,0:T(8,128)(2,1)} %get-tuple-element.24), channel_id=1, source_target_pairs={{0,0},{1,1},{2,2},{3,3},{4,4},{5,5},{6,6},{7,7},{8,72},{9,73},{10,... | collective-permute-start | bytes 393224 | tf_op jit(solution)/shard_map/ppermute | solution.py:23
  6.2 1.2 collective-permute-done.1
  7.4 2.3 %collective-permute-start.3 = (bf16[2048,512]{1,0:T(8,128)(2,1)}, bf16[2048,512]{1,0:T(8,128)(2,1)S(1)}, u32[]{:S(2)}, u32[]{:S(2)}) collective-permute-start(bf16[2048,512]{1,0:T(8,128)(2,1)} %own.1), channel_id=1, source_target_pairs={{0,32},{1,33},{2,34},{3,35},{4,36},{5,37},{6,38},{7,39},{8,40},{9,... | collective-permute-start | bytes 6291464 | tf_op jit(solution)/shard_map/ppermute | solution.py:23
  9.7 9.8 %collective-permute-start.7 = (bf16[1,2,128,512]{3,2,1,0:T(8,128)(2,1)S(1)}, bf16[1,2,128,512]{3,2,1,0:T(8,128)(2,1)S(1)}, u32[]{:S(2)}, u32[]{:S(2)}) collective-permute-start(bf16[1,2,128,512]{3,2,1,0:T(8,128)(2,1)S(1)} %bitcast.14), channel_id=1, source_target_pairs={{0,8},{1,25},{2,10},{3,27},{4,12},{5,29},{6,14},{7,31},{8,16},{9,1... | collective-permute-start | bytes 786440 | tf_op jit(solution)/shard_map/ppermute | solution.py:23
  19.5 6.3 %collective-permute-start.5 = (bf16[2,128,512]{2,1,0:T(8,128)(2,1)S(1)}, bf16[2,128,512]{2,1,0:T(8,128)(2,1)S(1)}, u32[]{:S(2)}, u32[]{:S(2)}) collective-permute-start(bf16[2,128,512]{2,1,0:T(8,128)(2,1)S(1)} %pad_maximum_fusion.1), channel_id=1, source_target_pairs={{0,6},{1,3},{2,0},{3,5},{4,2},{5,7},{6,4},{7,1},{8,14},{9,11},{10,... | collective-permute-start | bytes 786440 | tf_op jit(solution)/shard_map/ppermute | solution.py:23
  25.8 3.8 %collective-permute-start.6 = (bf16[1,2,128,512]{3,2,1,0:T(8,128)(2,1)S(1)}, bf16[1,2,128,512]{3,2,1,0:T(8,128)(2,1)S(1)}, u32[]{:S(2)}, u32[]{:S(2)}) collective-permute-start(bf16[1,2,128,512]{3,2,1,0:T(8,128)(2,1)S(1)} %bitcast.15), channel_id=1, source_target_pairs={{0,24},{1,9},{2,26},{3,11},{4,28},{5,13},{6,30},{7,15},{8,0},{9,17... | collective-permute-start | bytes 786440 | tf_op jit(solution)/shard_map/ppermute | solution.py:23
  29.6 5.8 %collective-permute-done.5 = bf16[2,128,512]{2,1,0:T(8,128)(2,1)S(1)} collective-permute-done((bf16[2,128,512]{2,1,0:T(8,128)(2,1)S(1)}, bf16[2,128,512]{2,1,0:T(8,128)(2,1)S(1)}, u32[]{:S(2)}, u32[]{:S(2)}) %collective-permute-start.5) | collective-permute-done | bytes 262176 | tf_op jit(solution)/shard_map/ppermute | solution.py:23
  35.4 2.1 %collective-permute-done.4 = bf16[2,128,512]{2,1,0:T(8,128)(2,1)S(1)} collective-permute-done((bf16[2,128,512]{2,1,0:T(8,128)(2,1)S(1)}, bf16[2,128,512]{2,1,0:T(8,128)(2,1)S(1)}, u32[]{:S(2)}, u32[]{:S(2)}) %collective-permute-start.4) | collective-permute-done | bytes 262176 | tf_op jit(solution)/shard_map/ppermute | solution.py:23
  38.3 1.8 %collective-permute-start.9 = (bf16[2,2,128,512]{3,2,1,0:T(8,128)(2,1)S(1)}, bf16[2,2,128,512]{3,2,1,0:T(8,128)(2,1)S(1)}, u32[]{:S(2)}, u32[]{:S(2)}) collective-permute-start(bf16[2,2,128,512]{3,2,1,0:T(8,128)(2,1)S(1)} %pad_maximum_fusion.refs_4_), channel_id=1, source_target_pairs={{0,8},{1,25},{2,10},{3,27},{4,12},{5,29},{6,14},{7,31},{8,16},{9,1... | collective-permute-start | bytes 1572872 | tf_op jit(solution)/shard_map/ppermute | solution.py:23
  40.1 4.0 %collective-permute-start.11 = (bf16[2,2,128,512]{3,2,1,0:T(8,128)(2,1)S(1)}, bf16[2,2,128,512]{3,2,1,0:T(8,128)(2,1)S(1)}, u32[]{:S(2)}, u32[]{:S(2)}) collective-permute-start(bf16[2,2,128,512]{3,2,1,0:T(8,128)(2,1)S(1)} %pad_maximum_fusion.refs_4_), channel_id=1, source_target_pairs={{0,24},{1,9},{2,26},{3,11},{4,28},{5,13},{6,30},{7,15},{8,0},{9,17... | collective-permute-start | bytes 1572872 | tf_op jit(solution)/shard_map/ppermute | solution.py:23
  44.2 4.5 %collective-permute-done.12 = bf16[2,128,512]{2,1,0:T(8,128)(2,1)S(1)} collective-permute-done((bf16[2,128,512]{2,1,0:T(8,128)(2,1)S(1)}, bf16[2,128,512]{2,1,0:T(8,128)(2,1)S(1)}, u32[]{:S(2)}, u32[]{:S(2)}) %collective-permute-start.12) | collective-permute-done | bytes 262176 | tf_op jit(solution)/shard_map/ppermute | solution.py:23
  48.7 1.6 %collective-permute-start.14 = (bf16[1,2,128,512]{3,2,1,0:T(8,128)(2,1)S(1)}, bf16[1,2,128,512]{3,2,1,0:T(8,128)(2,1)S(1)}, u32[]{:S(2)}, u32[]{:S(2)}) collective-permute-start(bf16[1,2,128,512]{3,2,1,0:T(8,128)(2,1)S(1)} %bitcast.17), channel_id=1, source_target_pairs={{0,24},{1,9},{2,26},{3,11},{4,28},{5,13},{6,30},{7,15},{8,0},{9,17... | collective-permute-start | bytes 786440 | tf_op jit(solution)/shard_map/ppermute | solution.py:23
  50.7 1.9 %collective-permute-start.10 = (bf16[2,2,128,512]{3,2,1,0:T(8,128)(2,1)S(1)}, bf16[2,2,128,512]{3,2,1,0:T(8,128)(2,1)S(1)}, u32[]{:S(2)}, u32[]{:S(2)}) collective-permute-start(bf16[2,2,128,512]{3,2,1,0:T(8,128)(2,1)S(1)} %collective-permute-done.9.refs_5_), channel_id=1, source_target_pairs={{0,8},{1,25},{2,10},{3,27},{4,12},{5,29},{6,14},{7,31},{8,16},{9,1... | collective-permute-start | bytes 1572872 | tf_op jit(solution)/shard_map/ppermute | solution.py:23
  52.6 4.9 %collective-permute-done.14.refs_10_ = bf16[1,2,128,512]{3,2,1,0:T(8,128)(2,1)S(1)} collective-permute-done((bf16[1,2,128,512]{3,2,1,0:T(8,128)(2,1)S(1)}, bf16[1,2,128,512]{3,2,1,0:T(8,128)(2,1)S(1)}, u32[]{:S(2)}, u32[]{:S(2)}) %collective-permute-start.14) | collective-permute-done | bytes 262176 | tf_op jit(solution)/shard_map/ppermute | solution.py:23
  57.5 2.6 %collective-permute-done.13.refs_9_ = bf16[1,2,128,512]{3,2,1,0:T(8,128)(2,1)S(1)} collective-permute-done((bf16[1,2,128,512]{3,2,1,0:T(8,128)(2,1)S(1)}, bf16[1,2,128,512]{3,2,1,0:T(8,128)(2,1)S(1)}, u32[]{:S(2)}, u32[]{:S(2)}) %collective-permute-start.13) | collective-permute-done | bytes 262176 | tf_op jit(solution)/shard_map/ppermute | solution.py:23
  60.1 8.4 %collective-permute-done.15.refs_11_ = bf16[1,2,128,512]{3,2,1,0:T(8,128)(2,1)S(1)} collective-permute-done((bf16[1,2,128,512]{3,2,1,0:T(8,128)(2,1)S(1)}, bf16[1,2,128,512]{3,2,1,0:T(8,128)(2,1)S(1)}, u32[]{:S(2)}, u32[]{:S(2)}) %collective-permute-start.15) | collective-permute-done | bytes 262176 | tf_op jit(solution)/shard_map/ppermute | solution.py:23
  68.5 1.6 %copy-done = bf16[2048,512]{1,0:T(8,128)(2,1)S(1)} copy-done((bf16[2048,512]{1,0:T(8,128)(2,1)S(1)}, bf16[2048,512]{1,0:T(8,128)(2,1)}, u32[]{:S(2)}) %copy-start) | copy-done | bytes 2097176
  70.1 4.0 %first.1 = (bf16[4,128,512]{2,1,0:T(8,128)(2,1)S(1)}, bf16[512,4096]{1,0:T(8,128)(2,1)S(1)}) custom-call(bf16[2048,512]{1,0:T(8,128)(2,1)S(1)} %copy-done, bf16[2048,512]{1,0:T(8,128)(2,1)S(1)} %collective-permute-done.3.far, bf16[1,2,128,512]{3,2,1,0:T(8,128)(2,1)S(1)} %bitcast.16, bf16[1,2,128,512]{3,2,1,0:T(8,128)(2,1)S(1)} %collective-permute-done.7.refs_1_, ...), custom_call_target="tpu_custom_call" | custom-call | flops 2147483648 | bytes 8388608 | tf_op jit(solution)/shard_map/first/pallas_call | solution.py:274
  74.1 3.1 %second.1 = bf16[4,128,1024]{2,1,0:T(8,128)(2,1)S(1)} custom-call(bf16[4,128,512]{2,1,0:T(8,128)(2,1)S(1)} %get-tuple-element.38.kept, bf16[512,4096]{1,0:T(8,128)(2,1)S(1)} %get-tuple-element.39.held, bf16[2048,512]{1,0:T(8,128)(2,1)S(1)} %collective-permute-done.2.across, bf16[2048,512]{1,0:T(8,128)(2,1)S(1)} %collective-permute-done.16.far_across), custom_call_target="tpu_custom_call" | custom-call | flops 2147483648 | bytes 8388608 | tf_op jit(solution)/shard_map/second/pallas_call | solution.py:286
  77.3 21.8 %all_to_all.10 = bf16[4,128,1024]{2,1,0:T(8,128)(2,1)S(1)} all-to-all(bf16[4,128,1024]{2,1,0:T(8,128)(2,1)S(1)} %second.1), channel_id=1, replica_groups=mesh['z_lo'=2,'y_hi'=2,'y_lo'=2,'x'=4,'z_hi'=4,'core'=2] {'z_lo','y_hi'}, dimensions={0} | all-to-all | bytes 2097152 | tf_op jit(solution)/shard_map/all_to_all | solution.py:299
  99.4 1.5 %collective-permute-done.17.got = f32[128,512]{1,0:T(8,128)S(1)} collective-permute-done((f32[128,512]{1,0:T(8,128)S(1)}, f32[128,512]{1,0:T(8,128)S(1)}, u32[]{:S(2)}, u32[]{:S(2)}) %collective-permute-start.17) | collective-permute-done | bytes 262176 | tf_op jit(solution)/shard_map/ppermute | solution.py:23
  100.9 5.1 %finish.1 = (f32[256,512]{1,0:T(8,128)}, f32[17,256]{1,0:T(8,128)S(1)}) custom-call(s32[2,64,256]{2,1,0:T(8,128)S(1)} %bitcast.21, f32[1,256]{1,0:T(1,128)S(1)} %bitcast.23, f32[512,256]{1,0:T(8,128)S(1)} %copy-done.3, f32[128,512]{1,0:T(8,128)S(1)} %get-tuple-element.44.kept, f32[128,512]{1,0:T(8,128)S(1)} %collective-permute-done.17.got), custom_call_target="tpu_custom_call" | custom-call | flops 4294967296 | bytes 2097152 | tf_op jit(solution)/shard_map/finish/pallas_call | solution.py:148
  107.2 1.5 %collective-permute-start.20 = (f32[17,256]{1,0:T(8,128)S(1)}, f32[17,256]{1,0:T(8,128)S(1)}, u32[]{:S(2)}, u32[]{:S(2)}) collective-permute-start(f32[17,256]{1,0:T(8,128)S(1)} %add.21), channel_id=1, source_target_pairs={{0,24},{1,25},{2,26},{3,27},{4,28},{5,29},{6,30},{7,31},{8,0},{9,1... | collective-permute-start | bytes 52232 | tf_op jit(solution)/shard_map/ppermute | solution.py:23
  109.3 3.3 %collective-permute-done.21 = f32[17,256]{1,0:T(8,128)S(1)} collective-permute-done((f32[17,256]{1,0:T(8,128)S(1)}, f32[17,256]{1,0:T(8,128)S(1)}, u32[]{:S(2)}, u32[]{:S(2)}) %collective-permute-start.21) | collective-permute-done | bytes 17440 | tf_op jit(solution)/shard_map/ppermute | solution.py:23
  112.7 1.1 collective-permute-done.19
  113.8 6.4 %collective-permute-start.24 = (f32[17,256]{1,0:T(8,128)S(1)}, f32[17,256]{1,0:T(8,128)S(1)}, u32[]{:S(2)}, u32[]{:S(2)}) collective-permute-start(f32[17,256]{1,0:T(8,128)S(1)} %add_add_fusion.1), channel_id=1, source_target_pairs={{0,4},{1,5},{2,6},{3,7},{4,0},{5,1},{6,2},{7,3},{8,12},{9,13},{10,... | collective-permute-start | bytes 52232 | tf_op jit(solution)/shard_map/ppermute | solution.py:23
  120.7 2.4 %collective-permute-start.22 = (f32[17,256]{1,0:T(8,128)S(1)}, f32[17,256]{1,0:T(8,128)S(1)}, u32[]{:S(2)}, u32[]{:S(2)}) collective-permute-start(f32[17,256]{1,0:T(8,128)S(1)} %add_add_fusion.1), channel_id=1, source_target_pairs={{0,2},{1,3},{2,4},{3,5},{4,6},{5,7},{6,0},{7,1},{8,10},{9,11},{10,... | collective-permute-start | bytes 52232 | tf_op jit(solution)/shard_map/ppermute | solution.py:23
  123.1 1.8 %collective-permute-done.23 = f32[17,256]{1,0:T(8,128)S(1)} collective-permute-done((f32[17,256]{1,0:T(8,128)S(1)}, f32[17,256]{1,0:T(8,128)S(1)}, u32[]{:S(2)}, u32[]{:S(2)}) %collective-permute-start.23) | collective-permute-done | bytes 17440 | tf_op jit(solution)/shard_map/ppermute | solution.py:23
  124.9 2.0 %collective-permute-done.22 = f32[17,256]{1,0:T(8,128)S(1)} collective-permute-done((f32[17,256]{1,0:T(8,128)S(1)}, f32[17,256]{1,0:T(8,128)S(1)}, u32[]{:S(2)}, u32[]{:S(2)}) %collective-permute-start.22) | collective-permute-done | bytes 17440 | tf_op jit(solution)/shard_map/ppermute | solution.py:23
  127.6 4.6 %all-to-all-start.1 = ((f32[8,16,256]{2,1,0:T(8,128)}), f32[8,16,256]{2,1,0:T(8,128)S(1)}, u32[]{:S(2)}, u32[]{:S(2)}) async-start(f32[8,16,256]{2,1,0:T(8,128)} %broadcast_in_dim.11), calls=%async_computation.1 | async-start | bytes 262144 | tf_op jit(solution)/shard_map/all_to_all | solution.py:310
  132.8 4.5 %all-to-all-done.1 = f32[8,16,256]{2,1,0:T(8,128)S(1)} async-done(((f32[8,16,256]{2,1,0:T(8,128)}), f32[8,16,256]{2,1,0:T(8,128)S(1)}, u32[]{:S(2)}, u32[]{:S(2)}) %all-to-all-start.1) | async-done | bytes 131104 | tf_op jit(solution)/shard_map/all_to_all | solution.py:310
  (45 shorter events, 6.4 us)
Async XLA Ops:
  0.6 6.7 %collective-permute-start.2 = (bf16[2048,512]{1,0:T(8,128)(2,1)}, bf16[2048,512]{1,0:T(8,128)(2,1)S(1)}, u32[]{:S(2)}, u32[]{:S(2)}) collective-permute-start(bf16[2048,512]{1,0:T(8,128)(2,1)} %own.1), channel_id=1, source_target_pairs={{0,1},{1,0},{2,3},{3,2},{4,5},{5,4},{6,7},{7,6},{8,9},{9,8},{10,11... | collective-permute-start | bytes 6291464 | tf_op jit(solution)/shard_map/ppermute | solution.py:23
  4.1 2.1 %collective-permute-start = (bf16[128,512]{1,0:T(8,128)(2,1)}, bf16[128,512]{1,0:T(8,128)(2,1)S(1)}, u32[]{:S(2)}, u32[]{:S(2)}) collective-permute-start(bf16[128,512]{1,0:T(8,128)(2,1)} %get-tuple-element.24), channel_id=1, source_target_pairs={{0,0},{1,1},{2,2},{3,3},{4,4},{5,5},{6,6},{7,7},{8,72},{9,73},{10,... | collective-permute-start | bytes 393224 | tf_op jit(solution)/shard_map/ppermute | solution.py:23
  5.7 1.7 %collective-permute-start.1 = (bf16[128,512]{1,0:T(8,128)(2,1)}, bf16[128,512]{1,0:T(8,128)(2,1)S(1)}, u32[]{:S(2)}, u32[]{:S(2)}) collective-permute-start(bf16[128,512]{1,0:T(8,128)(2,1)} %get-tuple-element.25), channel_id=1, source_target_pairs={{0,1},{1,0},{2,3},{3,2},{4,5},{5,4},{6,7},{7,6},{8,73},{9,72},{10,... | collective-permute-start | bytes 393224 | tf_op jit(solution)/shard_map/ppermute | solution.py:23
  7.4 61.1 %collective-permute-start.3 = (bf16[2048,512]{1,0:T(8,128)(2,1)}, bf16[2048,512]{1,0:T(8,128)(2,1)S(1)}, u32[]{:S(2)}, u32[]{:S(2)}) collective-permute-start(bf16[2048,512]{1,0:T(8,128)(2,1)} %own.1), channel_id=1, source_target_pairs={{0,32},{1,33},{2,34},{3,35},{4,36},{5,37},{6,38},{7,39},{8,40},{9,... | collective-permute-start | bytes 6291464 | tf_op jit(solution)/shard_map/ppermute | solution.py:23
  9.7 19.9 %collective-permute-start.7 = (bf16[1,2,128,512]{3,2,1,0:T(8,128)(2,1)S(1)}, bf16[1,2,128,512]{3,2,1,0:T(8,128)(2,1)S(1)}, u32[]{:S(2)}, u32[]{:S(2)}) collective-permute-start(bf16[1,2,128,512]{3,2,1,0:T(8,128)(2,1)S(1)} %bitcast.14), channel_id=1, source_target_pairs={{0,8},{1,25},{2,10},{3,27},{4,12},{5,29},{6,14},{7,31},{8,16},{9,1... | collective-permute-start | bytes 786440 | tf_op jit(solution)/shard_map/ppermute | solution.py:23
  19.5 16.0 %collective-permute-start.5 = (bf16[2,128,512]{2,1,0:T(8,128)(2,1)S(1)}, bf16[2,128,512]{2,1,0:T(8,128)(2,1)S(1)}, u32[]{:S(2)}, u32[]{:S(2)}) collective-permute-start(bf16[2,128,512]{2,1,0:T(8,128)(2,1)S(1)} %pad_maximum_fusion.1), channel_id=1, source_target_pairs={{0,6},{1,3},{2,0},{3,5},{4,2},{5,7},{6,4},{7,1},{8,14},{9,11},{10,... | collective-permute-start | bytes 786440 | tf_op jit(solution)/shard_map/ppermute | solution.py:23
  25.8 11.7 %collective-permute-start.4 = (bf16[2,128,512]{2,1,0:T(8,128)(2,1)S(1)}, bf16[2,128,512]{2,1,0:T(8,128)(2,1)S(1)}, u32[]{:S(2)}, u32[]{:S(2)}) collective-permute-start(bf16[2,128,512]{2,1,0:T(8,128)(2,1)S(1)} %pad_maximum_fusion.1), channel_id=1, source_target_pairs={{0,2},{1,7},{2,4},{3,1},{4,6},{5,3},{6,0},{7,5},{8,10},{9,15},{10,... | collective-permute-start | bytes 786440 | tf_op jit(solution)/shard_map/ppermute | solution.py:23
  25.8 11.8 %collective-permute-start.6 = (bf16[1,2,128,512]{3,2,1,0:T(8,128)(2,1)S(1)}, bf16[1,2,128,512]{3,2,1,0:T(8,128)(2,1)S(1)}, u32[]{:S(2)}, u32[]{:S(2)}) collective-permute-start(bf16[1,2,128,512]{3,2,1,0:T(8,128)(2,1)S(1)} %bitcast.15), channel_id=1, source_target_pairs={{0,24},{1,9},{2,26},{3,11},{4,28},{5,13},{6,30},{7,15},{8,0},{9,17... | collective-permute-start | bytes 786440 | tf_op jit(solution)/shard_map/ppermute | solution.py:23
  29.6 8.7 %collective-permute-start.8 = (bf16[1,2,128,512]{3,2,1,0:T(8,128)(2,1)S(1)}, bf16[1,2,128,512]{3,2,1,0:T(8,128)(2,1)S(1)}, u32[]{:S(2)}, u32[]{:S(2)}) collective-permute-start(bf16[1,2,128,512]{3,2,1,0:T(8,128)(2,1)S(1)} %collective-permute-done.7.refs_1_), channel_id=1, source_target_pairs={{0,8},{1,25},{2,10},{3,27},{4,12},{5,29},{6,14},{7,31},{8,16},{9,1... | collective-permute-start | bytes 786440 | tf_op jit(solution)/shard_map/ppermute | solution.py:23
  38.3 12.4 %collective-permute-start.9 = (bf16[2,2,128,512]{3,2,1,0:T(8,128)(2,1)S(1)}, bf16[2,2,128,512]{3,2,1,0:T(8,128)(2,1)S(1)}, u32[]{:S(2)}, u32[]{:S(2)}) collective-permute-start(bf16[2,2,128,512]{3,2,1,0:T(8,128)(2,1)S(1)} %pad_maximum_fusion.refs_4_), channel_id=1, source_target_pairs={{0,8},{1,25},{2,10},{3,27},{4,12},{5,29},{6,14},{7,31},{8,16},{9,1... | collective-permute-start | bytes 1572872 | tf_op jit(solution)/shard_map/ppermute | solution.py:23
  40.1 8.6 %collective-permute-start.12 = (bf16[2,128,512]{2,1,0:T(8,128)(2,1)S(1)}, bf16[2,128,512]{2,1,0:T(8,128)(2,1)S(1)}, u32[]{:S(2)}, u32[]{:S(2)}) collective-permute-start(bf16[2,128,512]{2,1,0:T(8,128)(2,1)S(1)} %collective-permute-done.4), channel_id=1, source_target_pairs={{0,2},{1,7},{2,4},{3,1},{4,6},{5,3},{6,0},{7,5},{8,10},{9,15},{10,... | collective-permute-start | bytes 786440 | tf_op jit(solution)/shard_map/ppermute | solution.py:23
  40.1 20.0 %collective-permute-start.11 = (bf16[2,2,128,512]{3,2,1,0:T(8,128)(2,1)S(1)}, bf16[2,2,128,512]{3,2,1,0:T(8,128)(2,1)S(1)}, u32[]{:S(2)}, u32[]{:S(2)}) collective-permute-start(bf16[2,2,128,512]{3,2,1,0:T(8,128)(2,1)S(1)} %pad_maximum_fusion.refs_4_), channel_id=1, source_target_pairs={{0,24},{1,9},{2,26},{3,11},{4,28},{5,13},{6,30},{7,15},{8,0},{9,17... | collective-permute-start | bytes 1572872 | tf_op jit(solution)/shard_map/ppermute | solution.py:23
  48.7 8.8 %collective-permute-start.14 = (bf16[1,2,128,512]{3,2,1,0:T(8,128)(2,1)S(1)}, bf16[1,2,128,512]{3,2,1,0:T(8,128)(2,1)S(1)}, u32[]{:S(2)}, u32[]{:S(2)}) collective-permute-start(bf16[1,2,128,512]{3,2,1,0:T(8,128)(2,1)S(1)} %bitcast.17), channel_id=1, source_target_pairs={{0,24},{1,9},{2,26},{3,11},{4,28},{5,13},{6,30},{7,15},{8,0},{9,17... | collective-permute-start | bytes 786440 | tf_op jit(solution)/shard_map/ppermute | solution.py:23
  50.3 9.7 %collective-permute-start.13 = (bf16[1,2,128,512]{3,2,1,0:T(8,128)(2,1)S(1)}, bf16[1,2,128,512]{3,2,1,0:T(8,128)(2,1)S(1)}, u32[]{:S(2)}, u32[]{:S(2)}) collective-permute-start(bf16[1,2,128,512]{3,2,1,0:T(8,128)(2,1)S(1)} %bitcast.18), channel_id=1, source_target_pairs={{0,8},{1,25},{2,10},{3,27},{4,12},{5,29},{6,14},{7,31},{8,16},{9,1... | collective-permute-start | bytes 786440 | tf_op jit(solution)/shard_map/ppermute | solution.py:23
  50.7 17.8 %collective-permute-start.10 = (bf16[2,2,128,512]{3,2,1,0:T(8,128)(2,1)S(1)}, bf16[2,2,128,512]{3,2,1,0:T(8,128)(2,1)S(1)}, u32[]{:S(2)}, u32[]{:S(2)}) collective-permute-start(bf16[2,2,128,512]{3,2,1,0:T(8,128)(2,1)S(1)} %collective-permute-done.9.refs_5_), channel_id=1, source_target_pairs={{0,8},{1,25},{2,10},{3,27},{4,12},{5,29},{6,14},{7,31},{8,16},{9,1... | collective-permute-start | bytes 1572872 | tf_op jit(solution)/shard_map/ppermute | solution.py:23
  60.1 8.4 %collective-permute-start.15 = (bf16[1,2,128,512]{3,2,1,0:T(8,128)(2,1)S(1)}, bf16[1,2,128,512]{3,2,1,0:T(8,128)(2,1)S(1)}, u32[]{:S(2)}, u32[]{:S(2)}) collective-permute-start(bf16[1,2,128,512]{3,2,1,0:T(8,128)(2,1)S(1)} %collective-permute-done.13.refs_9_), channel_id=1, source_target_pairs={{0,8},{1,25},{2,10},{3,27},{4,12},{5,29},{6,14},{7,31},{8,16},{9,1... | collective-permute-start | bytes 786440 | tf_op jit(solution)/shard_map/ppermute | solution.py:23
  68.5 5.6 %collective-permute-start.16 = (bf16[2048,512]{1,0:T(8,128)(2,1)S(1)}, bf16[2048,512]{1,0:T(8,128)(2,1)S(1)}, u32[]{:S(2)}, u32[]{:S(2)}) collective-permute-start(bf16[2048,512]{1,0:T(8,128)(2,1)S(1)} %collective-permute-done.3.far), channel_id=1, source_target_pairs={{0,1},{1,0},{2,3},{3,2},{4,5},{5,4},{6,7},{7,6},{8,9},{9,8},{10,11... | collective-permute-start | bytes 6291464 | tf_op jit(solution)/shard_map/ppermute | solution.py:23
  68.5 1.6 %copy-start = (bf16[2048,512]{1,0:T(8,128)(2,1)S(1)}, bf16[2048,512]{1,0:T(8,128)(2,1)}, u32[]{:S(2)}) copy-start(bf16[2048,512]{1,0:T(8,128)(2,1)} %own.1) | copy-start | bytes 6291460
  77.3 23.7 %copy-start.1 = (s32[2,256,64]{1,2,0:T(8,128)S(1)}, s32[2,256,64]{1,2,0:T(8,128)}, u32[]{:S(2)}) copy-start(s32[2,256,64]{1,2,0:T(8,128)} %param.5) | copy-start | bytes 393220
  77.3 23.7 %copy-start.2 = (f32[256]{0:T(256)S(1)}, f32[256]{0:T(256)}, u32[]{:S(2)}) copy-start(f32[256]{0:T(256)} %param.7) | copy-start | bytes 3076
  77.3 23.7 %copy-start.3 = (f32[512,256]{1,0:T(8,128)S(1)}, f32[512,256]{1,0:T(8,128)}, u32[]{:S(2)}) copy-start(f32[512,256]{1,0:T(8,128)} %get-tuple-element.23.decoded) | copy-start | bytes 1572868
  99.3 1.6 %collective-permute-start.17 = (f32[128,512]{1,0:T(8,128)S(1)}, f32[128,512]{1,0:T(8,128)S(1)}, u32[]{:S(2)}, u32[]{:S(2)}) collective-permute-start(f32[128,512]{1,0:T(8,128)S(1)} %get-tuple-element.43), channel_id=1, source_target_pairs={{0,1},{1,0},{2,3},{3,2},{4,5},{5,4},{6,7},{7,6},{8,9},{9,8},{10,11... | collective-permute-start | bytes 786440 | tf_op jit(solution)/shard_map/ppermute | solution.py:23
  106.0 1.2 collective-permute-start.18
  107.2 5.4 %collective-permute-start.21 = (f32[17,256]{1,0:T(8,128)S(1)}, f32[17,256]{1,0:T(8,128)S(1)}, u32[]{:S(2)}, u32[]{:S(2)}) collective-permute-start(f32[17,256]{1,0:T(8,128)S(1)} %add.21), channel_id=1, source_target_pairs={{0,16},{1,17},{2,18},{3,19},{4,20},{5,21},{6,22},{7,23},{8,24},{9,... | collective-permute-start | bytes 52232 | tf_op jit(solution)/shard_map/ppermute | solution.py:23
  107.2 5.4 %collective-permute-start.20 = (f32[17,256]{1,0:T(8,128)S(1)}, f32[17,256]{1,0:T(8,128)S(1)}, u32[]{:S(2)}, u32[]{:S(2)}) collective-permute-start(f32[17,256]{1,0:T(8,128)S(1)} %add.21), channel_id=1, source_target_pairs={{0,24},{1,25},{2,26},{3,27},{4,28},{5,29},{6,30},{7,31},{8,0},{9,1... | collective-permute-start | bytes 52232 | tf_op jit(solution)/shard_map/ppermute | solution.py:23
  108.8 5.0 %collective-permute-start.19 = (f32[17,256]{1,0:T(8,128)S(1)}, f32[17,256]{1,0:T(8,128)S(1)}, u32[]{:S(2)}, u32[]{:S(2)}) collective-permute-start(f32[17,256]{1,0:T(8,128)S(1)} %add.21), channel_id=1, source_target_pairs={{0,8},{1,9},{2,10},{3,11},{4,12},{5,13},{6,14},{7,15},{8,16},{9,17... | collective-permute-start | bytes 52232 | tf_op jit(solution)/shard_map/ppermute | solution.py:23
  113.8 9.3 %collective-permute-start.24 = (f32[17,256]{1,0:T(8,128)S(1)}, f32[17,256]{1,0:T(8,128)S(1)}, u32[]{:S(2)}, u32[]{:S(2)}) collective-permute-start(f32[17,256]{1,0:T(8,128)S(1)} %add_add_fusion.1), channel_id=1, source_target_pairs={{0,4},{1,5},{2,6},{3,7},{4,0},{5,1},{6,2},{7,3},{8,12},{9,13},{10,... | collective-permute-start | bytes 52232 | tf_op jit(solution)/shard_map/ppermute | solution.py:23
  120.2 4.7 %collective-permute-start.23 = (f32[17,256]{1,0:T(8,128)S(1)}, f32[17,256]{1,0:T(8,128)S(1)}, u32[]{:S(2)}, u32[]{:S(2)}) collective-permute-start(f32[17,256]{1,0:T(8,128)S(1)} %add_add_fusion.1), channel_id=1, source_target_pairs={{0,6},{1,7},{2,0},{3,1},{4,2},{5,3},{6,4},{7,5},{8,14},{9,15},{10,... | collective-permute-start | bytes 52232 | tf_op jit(solution)/shard_map/ppermute | solution.py:23
  120.7 6.2 %collective-permute-start.22 = (f32[17,256]{1,0:T(8,128)S(1)}, f32[17,256]{1,0:T(8,128)S(1)}, u32[]{:S(2)}, u32[]{:S(2)}) collective-permute-start(f32[17,256]{1,0:T(8,128)S(1)} %add_add_fusion.1), channel_id=1, source_target_pairs={{0,2},{1,3},{2,4},{3,5},{4,6},{5,7},{6,0},{7,1},{8,10},{9,11},{10,... | collective-permute-start | bytes 52232 | tf_op jit(solution)/shard_map/ppermute | solution.py:23
  127.6 9.7 %all-to-all-start.1 = ((f32[8,16,256]{2,1,0:T(8,128)}), f32[8,16,256]{2,1,0:T(8,128)S(1)}, u32[]{:S(2)}, u32[]{:S(2)}) async-start(f32[8,16,256]{2,1,0:T(8,128)} %broadcast_in_dim.11), calls=%async_computation.1 | async-start | bytes 262144 | tf_op jit(solution)/shard_map/all_to_all | solution.py:310

commit v9 on v8

--- a/solution.py
+++ b/solution.py
@@ -34,7 +34,8 @@
 
 
 def to_plane(z_lo, y_hi, y_lo, x, z_hi, core):
-    return (x // 2, x % 2, y_lo, x + 2 * z_lo + y_hi, z_hi, core)
+    move = {(0, 0): 2, (1, 0): 1, (0, 1): -1, (1, 1): 0}[z_lo ^ (x // 2), y_hi ^ (x % 2)]
+    return (x // 2, x % 2, y_lo, x + move, z_hi, core)
 
 
 def decode_kernel(
@@ -105,11 +106,14 @@
     )(codes, codebooks, row_scale.reshape(1, rows), initial)
 
 
-def finish_kernel(codes, scale, decoded, kept, got, product, totals):
-    half = kept.shape[0]
+def finish_kernel(codes, scale, decoded, own, to_both, to_y, to_z, got, product, totals):
+    half, width = got.shape
+    kept = own[:, :width]
+    for part in (to_both, to_y, to_z):
+        kept = kept + part[:, :width].astype(jnp.float32)
     first = lax.axis_index("core") == 0
-    product[:half] = 2.0 * jnp.where(first, kept[...], got[...])
-    product[half:] = 2.0 * jnp.where(first, got[...], kept[...])
+    product[:half] = 2.0 * jnp.where(first, kept, got[...])
+    product[half:] = 2.0 * jnp.where(first, got[...], kept)
     rows, width = product.shape
     turned = product[...].T
     totals[16:17, :] = jnp.sum(turned * decoded[...], axis=0, keepdims=True)
@@ -142,18 +146,18 @@
     totals[8:16, :] = sums[:, 256:]
 
 
-def finish(codes, row_scale, decoded, kept, got):
-    half, width = kept.shape
+def finish(codes, row_scale, decoded, parts, got):
+    half, width = got.shape
     rows = 2 * half
     return pl.pallas_call(
         finish_kernel,
         out_shape=(jax.ShapeDtypeStruct((rows, width), jnp.float32), jax.ShapeDtypeStruct((17, 256), jnp.float32)),
-        in_specs=[pl.BlockSpec(memory_space=pltpu.VMEM)] * 5,
+        in_specs=[pl.BlockSpec(memory_space=pltpu.VMEM)] * (4 + len(parts)),
         out_specs=(pl.BlockSpec(memory_space=pltpu.VMEM),) * 2,
         compiler_params=pltpu.CompilerParams(vmem_limit_bytes=16 * 2**20),
         cost_estimate=pl.CostEstimate(flops=2**32, bytes_accessed=2**21, transcendentals=0),
         name="finish",
-    )(codes, row_scale.reshape(1, rows), decoded, kept, got)
+    )(codes, row_scale.reshape(1, rows), decoded, *parts, got)
 
 DEPTH = 512
 
@@ -171,15 +175,14 @@
     return copies
 
 
-def multiply(held, hess, copies, out, at=0):
+def multiply(held, hess, copies):
     total = None
     for n, copy in enumerate(copies):
         copy.wait()
         rows = slice(n * DEPTH, (n + 1) * DEPTH)
         term = jnp.dot(held[:, rows], hess[rows], preferred_element_type=jnp.float32)
         total = term if total is None else total + term
-    for s in range(4):
-        out[s, :, at : at + hess.shape[1]] = total[s * 128 : (s + 1) * 128].astype(out.dtype)
+    return total.reshape(4, -1, hess.shape[1])
 
 
 def first_kernel(own, far, *refs):
@@ -195,7 +198,9 @@
         for place, dz in enumerate(dzs):
             from_x = (x + 8 - step * dx) % 4
             from_z = (z_hi + 8 - step * dz) % 4
-            s = (from_x + 8 - 2 * z_lo - y_hi) % 4
+            move = (from_x + 8 - 2 * z_lo - y_hi) % 4
+            cross_z, cross_y = 1 - move // 2, 1 - (move + 1) % 4 // 2
+            s = (z_lo + cross_z) % 2 * 2 + (y_hi + cross_y) % 2
             tile = (from_z // 2 + y_lo) % 2
             for side in range(2):
                 n = len(copies)
@@ -214,16 +219,24 @@
         copy.start()
     for copy in copies:
         copy.wait()
-    multiply(held, hess, fetched, out)
-
-
-def second_kernel(kept, held, across, far_across, out, hess, sem):
+    out[...] = multiply(held, hess, fetched)
+
+
+def second_kernel(kept, held, across, far_across, own, to_y, to_z, to_both, given, hess, sem):
     fetched = tile_copies((across, far_across), hess, sem)
     for copy in fetched:
         copy.start()
+    given[...] = multiply(held, hess, fetched)
     width = hess.shape[1]
-    out[:, :, :width] = kept[...]
-    multiply(held, hess, fetched, out, width)
+    z_lo, y_hi = lax.axis_index("z_lo"), lax.axis_index("y_hi")
+    for out, s in (
+        (own, z_lo * 2 + y_hi),
+        (to_y, z_lo * 2 + 1 - y_hi),
+        (to_z, (1 - z_lo) * 2 + y_hi),
+        (to_both, (1 - z_lo) * 2 + 1 - y_hi),
+    ):
+        out[:, :width] = kept[s].astype(out.dtype)
+        out[:, width:] = given[s].astype(out.dtype)
 
 
 def body(codes, codebooks, row_scale, initial, hessian):
@@ -270,10 +283,12 @@
             flops=2 * 512 * 4096 * 512, bytes_accessed=8 * 2**20, transcendentals=0
         ),
     )
-    sums = jax.ShapeDtypeStruct((4, half, width), jnp.bfloat16)
     kept, held = pl.pallas_call(
         first_kernel,
-        out_shape=(sums, jax.ShapeDtypeStruct((4 * half, 8 * width), jnp.bfloat16)),
+        out_shape=(
+            jax.ShapeDtypeStruct((4, half, width), jnp.float32),
+            jax.ShapeDtypeStruct((4 * half, 8 * width), jnp.bfloat16),
+        ),
         in_specs=[hbm] * (2 + len(blocks)),
         out_specs=(vmem, vmem),
         scratch_shapes=[
@@ -283,12 +298,14 @@
         name="first",
         **settings,
     )(hessian, far, *blocks)
-    partial = pl.pallas_call(
+    sent = jax.ShapeDtypeStruct((half, 2 * width), jnp.bfloat16)
+    own, to_y, to_z, to_both = pl.pallas_call(
         second_kernel,
-        out_shape=jax.ShapeDtypeStruct((4, half, 2 * width), jnp.bfloat16),
+        out_shape=(jax.ShapeDtypeStruct(sent.shape, jnp.float32), sent, sent, sent),
         in_specs=[vmem, vmem, hbm, hbm],
-        out_specs=vmem,
+        out_specs=(vmem,) * 4,
         scratch_shapes=[
+            pltpu.VMEM((4, half, width), jnp.float32),
             pltpu.VMEM((8 * width, width), jnp.bfloat16),
             pltpu.SemaphoreType.DMA((8,)),
         ],
@@ -296,11 +313,15 @@
         **settings,
     )(kept, held, across, far_across)
 
-    parts = lax.all_to_all(partial, ("z_lo", "y_hi"), 0, 0, tiled=True)
-    summed = jnp.sum(parts.astype(jnp.float32), axis=0)
-    kept, given = summed[:, :width], summed[:, width:]
+    parts = [
+        own,
+        send(to_both, lambda zl, yh, yl, x, zh, c: (1 - zl, 1 - yh, yl, x, zh, c)),
+        shift(to_y, "y_hi", 1),
+        shift(to_z, "z_lo", 1),
+    ]
+    given = sum(part[:, width:].astype(jnp.float32) for part in parts)
     got = shift(given, "core", 1)
-    product, total = finish(codes, row_scale, decoded, kept, got)
+    product, total = finish(codes, row_scale, decoded, parts, got)
 
     total = total + shift(total, "core", 1)
     for axis in ("x", "z_hi"):

time: 138 us -> 136 us (0.986)
  blocking collectives: 21.8 us -> 0 us
  waiting for transfers between devices: 45.6 us -> 64.7 us
    all_to_all x1 -> x0, blocking collectives: 21.8 us -> none  [body(): parts = lax.all_to_all(partial, ('z_lo', 'y_hi'), 0, 0, tiled=True)]
    ppermute x25 -> x28, waiting for transfers between devices: 41.1 us -> 60.2 us  [send(): return lax.ppermute(a, AXES, pairs)]
    ppermute x25 -> x28, starting transfers between devices: 45.8 us -> 45.7 us  [send(): return lax.ppermute(a, AXES, pairs)]
  transfers between devices with their start and end apart: 26 -> 29, of which waited for: 15 -> 18; matrix products, arithmetic and copies ran while one was open for 0% -> 0% of each run, Pallas kernels for 5% -> 5%
where the time goes in v9:
time: 136 us
  waiting for transfers between devices  64.7 us (48%)
  starting transfers between devices  50.7 us (37%)
  Pallas kernels  15.7 us (12%)
  local copies, waits for them, and re-layouts  2.26 us (2%)
    ppermute x28, waiting for transfers between devices, send(): return lax.ppermute(a, AXES, pairs)  60.2 us
    ppermute x28, starting transfers between devices, send(): return lax.ppermute(a, AXES, pairs)  45.7 us
    pallas_call x1, Pallas kernels, finish(): pl.pallas_call(finish_kernel, out_shape=(jax.ShapeDtypeStruct((rows, widt...  5.13 us
    all_to_all x1, starting transfers between devices, body(): books = jnp.sum(lax.all_to_all(copies, ROW, 0, 0, tiled=True), axis=0)  5 us
    all_to_all x1, waiting for transfers between devices, body(): books = jnp.sum(lax.all_to_all(copies, ROW, 0, 0, tiled=True), axis=0)  4.5 us
    pallas_call x1, Pallas kernels, body(): pl.pallas_call(first_kernel, out_shape=(jax.ShapeDtypeStruct((4, half, wi...  4.1 us
    pallas_call x1, Pallas kernels, decode(): pl.pallas_call(decode_kernel, out_shape=(jax.ShapeDtypeStruct((width, row...  3.35 us
    pallas_call x1, Pallas kernels, body(): pl.pallas_call(second_kernel, out_shape=(jax.ShapeDtypeStruct(sent.shape,...  3.16 us
  transfers between devices with their start and end apart: 29, of which 18 were waited for; matrix products, arithmetic and copies ran while one was open for 0% of the time, Pallas kernels for 5%

profile of v9, /device:TPU:8, one launch (start us, length us, event | category | flops | bytes accessed | tf_op | source)
XLA Modules:
  0.0 135.6 jit_solution(4622358592521597359)
XLA Ops:
  0.7 3.4 %decode.1 = (f32[512,256]{1,0:T(8,128)}, bf16[128,512]{1,0:T(8,128)(2,1)}, bf16[128,512]{1,0:T(8,128)(2,1)}) custom-call(s32[2,64,256]{2,1,0:T(8,128)} %bitcast.20, bf16[2,8,256]{2,1,0:T(8,128)(2,1)} %bitcast.28, f32[1,256]{1,0:T(1,128)} %bitcast.22, bf16[256,512]{1,0:T(8,128)(2,1)} %initial_in.1), custom_call_target="tpu_custom_call" | custom-call | flops 2097152 | bytes 1048576 | tf_op jit(solution)/shard_map/decode/pallas_call | solution.py:82
  4.1 3.1 %collective-permute-start = (bf16[128,512]{1,0:T(8,128)(2,1)}, bf16[128,512]{1,0:T(8,128)(2,1)S(1)}, u32[]{:S(2)}, u32[]{:S(2)}) collective-permute-start(bf16[128,512]{1,0:T(8,128)(2,1)} %get-tuple-element.28), channel_id=1, source_target_pairs={{0,16},{1,17},{2,18},{3,19},{4,20},{5,21},{6,22},{7,23},{8,64},{9,... | collective-permute-start | bytes 393224 | tf_op jit(solution)/shard_map/ppermute | solution.py:23
  7.2 2.4 %collective-permute-start.1 = (bf16[128,512]{1,0:T(8,128)(2,1)}, bf16[128,512]{1,0:T(8,128)(2,1)S(1)}, u32[]{:S(2)}, u32[]{:S(2)}) collective-permute-start(bf16[128,512]{1,0:T(8,128)(2,1)} %get-tuple-element.29), channel_id=1, source_target_pairs={{0,17},{1,16},{2,19},{3,18},{4,21},{5,20},{6,23},{7,22},{8,65},{9,... | collective-permute-start | bytes 393224 | tf_op jit(solution)/shard_map/ppermute | solution.py:23
  9.6 6.4 %collective-permute-done = bf16[128,512]{1,0:T(8,128)(2,1)S(1)} collective-permute-done((bf16[128,512]{1,0:T(8,128)(2,1)}, bf16[128,512]{1,0:T(8,128)(2,1)S(1)}, u32[]{:S(2)}, u32[]{:S(2)}) %collective-permute-start) | collective-permute-done | bytes 131104 | tf_op jit(solution)/shard_map/ppermute | solution.py:23
  15.9 2.8 %collective-permute-done.1 = bf16[128,512]{1,0:T(8,128)(2,1)S(1)} collective-permute-done((bf16[128,512]{1,0:T(8,128)(2,1)}, bf16[128,512]{1,0:T(8,128)(2,1)S(1)}, u32[]{:S(2)}, u32[]{:S(2)}) %collective-permute-start.1) | collective-permute-done | bytes 131104 | tf_op jit(solution)/shard_map/ppermute | solution.py:23
  19.3 6.3 %collective-permute-start.5 = (bf16[2,128,512]{2,1,0:T(8,128)(2,1)S(1)}, bf16[2,128,512]{2,1,0:T(8,128)(2,1)S(1)}, u32[]{:S(2)}, u32[]{:S(2)}) collective-permute-start(bf16[2,128,512]{2,1,0:T(8,128)(2,1)S(1)} %pad_maximum_fusion.1), channel_id=1, source_target_pairs={{0,6},{1,3},{2,0},{3,5},{4,2},{5,7},{6,4},{7,1},{8,14},{9,11},{10,... | collective-permute-start | bytes 786440 | tf_op jit(solution)/shard_map/ppermute | solution.py:23
  25.6 6.1 %collective-permute-start.6 = (bf16[1,2,128,512]{3,2,1,0:T(8,128)(2,1)S(1)}, bf16[1,2,128,512]{3,2,1,0:T(8,128)(2,1)S(1)}, u32[]{:S(2)}, u32[]{:S(2)}) collective-permute-start(bf16[1,2,128,512]{3,2,1,0:T(8,128)(2,1)S(1)} %bitcast.15), channel_id=1, source_target_pairs={{0,24},{1,9},{2,26},{3,11},{4,28},{5,13},{6,30},{7,15},{8,0},{9,17... | collective-permute-start | bytes 786440 | tf_op jit(solution)/shard_map/ppermute | solution.py:23
  31.7 5.0 %collective-permute-done.5 = bf16[2,128,512]{2,1,0:T(8,128)(2,1)S(1)} collective-permute-done((bf16[2,128,512]{2,1,0:T(8,128)(2,1)S(1)}, bf16[2,128,512]{2,1,0:T(8,128)(2,1)S(1)}, u32[]{:S(2)}, u32[]{:S(2)}) %collective-permute-start.5) | collective-permute-done | bytes 262176 | tf_op jit(solution)/shard_map/ppermute | solution.py:23
  36.6 1.6 %collective-permute-done.4 = bf16[2,128,512]{2,1,0:T(8,128)(2,1)S(1)} collective-permute-done((bf16[2,128,512]{2,1,0:T(8,128)(2,1)S(1)}, bf16[2,128,512]{2,1,0:T(8,128)(2,1)S(1)}, u32[]{:S(2)}, u32[]{:S(2)}) %collective-permute-start.4) | collective-permute-done | bytes 262176 | tf_op jit(solution)/shard_map/ppermute | solution.py:23
  38.3 2.1 %collective-permute-done.8.refs_3_ = bf16[1,2,128,512]{3,2,1,0:T(8,128)(2,1)S(1)} collective-permute-done((bf16[1,2,128,512]{3,2,1,0:T(8,128)(2,1)S(1)}, bf16[1,2,128,512]{3,2,1,0:T(8,128)(2,1)S(1)}, u32[]{:S(2)}, u32[]{:S(2)}) %collective-permute-start.8) | collective-permute-done | bytes 262176 | tf_op jit(solution)/shard_map/ppermute | solution.py:23
  41.9 3.2 %collective-permute-start.11 = (bf16[2,2,128,512]{3,2,1,0:T(8,128)(2,1)S(1)}, bf16[2,2,128,512]{3,2,1,0:T(8,128)(2,1)S(1)}, u32[]{:S(2)}, u32[]{:S(2)}) collective-permute-start(bf16[2,2,128,512]{3,2,1,0:T(8,128)(2,1)S(1)} %pad_maximum_fusion.refs_4_), channel_id=1, source_target_pairs={{0,24},{1,9},{2,26},{3,11},{4,28},{5,13},{6,30},{7,15},{8,0},{9,17... | collective-permute-start | bytes 1572872 | tf_op jit(solution)/shard_map/ppermute | solution.py:23
  45.2 5.0 %collective-permute-done.12 = bf16[2,128,512]{2,1,0:T(8,128)(2,1)S(1)} collective-permute-done((bf16[2,128,512]{2,1,0:T(8,128)(2,1)S(1)}, bf16[2,128,512]{2,1,0:T(8,128)(2,1)S(1)}, u32[]{:S(2)}, u32[]{:S(2)}) %collective-permute-start.12) | collective-permute-done | bytes 262176 | tf_op jit(solution)/shard_map/ppermute | solution.py:23
  50.1 4.8 %collective-permute-start.14 = (bf16[1,2,128,512]{3,2,1,0:T(8,128)(2,1)S(1)}, bf16[1,2,128,512]{3,2,1,0:T(8,128)(2,1)S(1)}, u32[]{:S(2)}, u32[]{:S(2)}) collective-permute-start(bf16[1,2,128,512]{3,2,1,0:T(8,128)(2,1)S(1)} %bitcast.17), channel_id=1, source_target_pairs={{0,24},{1,9},{2,26},{3,11},{4,28},{5,13},{6,30},{7,15},{8,0},{9,17... | collective-permute-start | bytes 786440 | tf_op jit(solution)/shard_map/ppermute | solution.py:23
  55.3 6.5 %collective-permute-done.14.refs_10_ = bf16[1,2,128,512]{3,2,1,0:T(8,128)(2,1)S(1)} collective-permute-done((bf16[1,2,128,512]{3,2,1,0:T(8,128)(2,1)S(1)}, bf16[1,2,128,512]{3,2,1,0:T(8,128)(2,1)S(1)}, u32[]{:S(2)}, u32[]{:S(2)}) %collective-permute-start.14) | collective-permute-done | bytes 262176 | tf_op jit(solution)/shard_map/ppermute | solution.py:23
  62.6 8.4 %collective-permute-done.15.refs_11_ = bf16[1,2,128,512]{3,2,1,0:T(8,128)(2,1)S(1)} collective-permute-done((bf16[1,2,128,512]{3,2,1,0:T(8,128)(2,1)S(1)}, bf16[1,2,128,512]{3,2,1,0:T(8,128)(2,1)S(1)}, u32[]{:S(2)}, u32[]{:S(2)}) %collective-permute-start.15) | collective-permute-done | bytes 262176 | tf_op jit(solution)/shard_map/ppermute | solution.py:23
  71.0 1.6 %copy-done = bf16[2048,512]{1,0:T(8,128)(2,1)S(1)} copy-done((bf16[2048,512]{1,0:T(8,128)(2,1)S(1)}, bf16[2048,512]{1,0:T(8,128)(2,1)}, u32[]{:S(2)}) %copy-start) | copy-done | bytes 2097176
  72.6 4.1 %first.1 = (f32[4,128,512]{2,1,0:T(8,128)S(1)}, bf16[512,4096]{1,0:T(8,128)(2,1)S(1)}) custom-call(bf16[2048,512]{1,0:T(8,128)(2,1)S(1)} %copy-done, bf16[2048,512]{1,0:T(8,128)(2,1)S(1)} %collective-permute-done.3.far, bf16[1,2,128,512]{3,2,1,0:T(8,128)(2,1)S(1)} %bitcast.16, bf16[1,2,128,512]{3,2,1,0:T(8,128)(2,1)S(1)} %collective-permute-done.7.refs_1_, ...), custom_call_target="tpu_custom_call" | custom-call | flops 2147483648 | bytes 8388608 | tf_op jit(solution)/shard_map/first/pallas_call | solution.py:286
  76.8 3.2 %second.1 = (f32[128,1024]{1,0:T(8,128)S(1)}, bf16[128,1024]{1,0:T(8,128)(2,1)S(1)}, bf16[128,1024]{1,0:T(8,128)(2,1)S(1)}, bf16[128,1024]{1,0:T(8,128)(2,1)S(1)}) custom-call(f32[4,128,512]{2,1,0:T(8,128)S(1)} %get-tuple-element.42.kept, bf16[512,4096]{1,0:T(8,128)(2,1)S(1)} %get-tuple-element.43.held, bf16[2048,512]{1,0:T(8,128)(2,1)S(1)} %collective-permute-done.2.across, ...), custom_call_target="tpu_custom_call" | custom-call | flops 2147483648 | bytes 8388608 | tf_op jit(solution)/shard_map/second/pallas_call | solution.py:302
  80.0 3.4 %collective-permute-start.18 = (bf16[128,1024]{1,0:T(8,128)(2,1)S(1)}, bf16[128,1024]{1,0:T(8,128)(2,1)S(1)}, u32[]{:S(2)}, u32[]{:S(2)}) collective-permute-start(bf16[128,1024]{1,0:T(8,128)(2,1)S(1)} %get-tuple-element.47), channel_id=1, source_target_pairs={{0,64},{1,65},{2,66},{3,67},{4,68},{5,69},{6,70},{7,71},{8,72},{9,... | collective-permute-start | bytes 786440 | tf_op jit(solution)/shard_map/ppermute | solution.py:23
  83.5 1.5 %collective-permute-start.19 = (bf16[128,1024]{1,0:T(8,128)(2,1)S(1)}, bf16[128,1024]{1,0:T(8,128)(2,1)S(1)}, u32[]{:S(2)}, u32[]{:S(2)}) collective-permute-start(bf16[128,1024]{1,0:T(8,128)(2,1)S(1)} %get-tuple-element.48), channel_id=1, source_target_pairs={{0,128},{1,129},{2,130},{3,131},{4,132},{5,133},{6,134},{7,135},{8... | collective-permute-start | bytes 786440 | tf_op jit(solution)/shard_map/ppermute | solution.py:23
  85.0 6.6 %collective-permute-done.17.to_both = bf16[128,1024]{1,0:T(8,128)(2,1)S(1)} collective-permute-done((bf16[128,1024]{1,0:T(8,128)(2,1)S(1)}, bf16[128,1024]{1,0:T(8,128)(2,1)S(1)}, u32[]{:S(2)}, u32[]{:S(2)}) %collective-permute-start.17) | collective-permute-done | bytes 262176 | tf_op jit(solution)/shard_map/ppermute | solution.py:23
  91.6 4.4 %collective-permute-done.18.to_y = bf16[128,1024]{1,0:T(8,128)(2,1)S(1)} collective-permute-done((bf16[128,1024]{1,0:T(8,128)(2,1)S(1)}, bf16[128,1024]{1,0:T(8,128)(2,1)S(1)}, u32[]{:S(2)}, u32[]{:S(2)}) %collective-permute-start.18) | collective-permute-done | bytes 262176 | tf_op jit(solution)/shard_map/ppermute | solution.py:23
  96.1 1.5 %collective-permute-done.20.got = f32[128,512]{1,0:T(8,128)S(1)} collective-permute-done((f32[128,512]{1,0:T(8,128)S(1)}, f32[128,512]{1,0:T(8,128)S(1)}, u32[]{:S(2)}, u32[]{:S(2)}) %collective-permute-start.20) | collective-permute-done | bytes 262176 | tf_op jit(solution)/shard_map/ppermute | solution.py:23
  97.7 5.1 %finish.1 = (f32[256,512]{1,0:T(8,128)}, f32[17,256]{1,0:T(8,128)S(1)}) custom-call(s32[2,64,256]{2,1,0:T(8,128)S(1)} %bitcast.21, f32[1,256]{1,0:T(1,128)S(1)} %bitcast.23, f32[512,256]{1,0:T(8,128)S(1)} %copy-done.3, f32[128,1024]{1,0:T(8,128)S(1)} %get-tuple-element.45.own, bf16[128,1024]{1,0:T(8,128)(2,1)S(1)} %collective-permute-done.17.to_both, ...), custom_call_target="tpu_custom_call" | custom-call | flops 4294967296 | bytes 2097152 | tf_op jit(solution)/shard_map/finish/pallas_call | solution.py:152
  104.4 2.3 %collective-permute-start.23 = (f32[17,256]{1,0:T(8,128)S(1)}, f32[17,256]{1,0:T(8,128)S(1)}, u32[]{:S(2)}, u32[]{:S(2)}) collective-permute-start(f32[17,256]{1,0:T(8,128)S(1)} %add.33), channel_id=1, source_target_pairs={{0,24},{1,25},{2,26},{3,27},{4,28},{5,29},{6,30},{7,31},{8,0},{9,1... | collective-permute-start | bytes 52232 | tf_op jit(solution)/shard_map/ppermute | solution.py:23
  106.8 2.5 %collective-permute-done.24 = f32[17,256]{1,0:T(8,128)S(1)} collective-permute-done((f32[17,256]{1,0:T(8,128)S(1)}, f32[17,256]{1,0:T(8,128)S(1)}, u32[]{:S(2)}, u32[]{:S(2)}) %collective-permute-start.24) | collective-permute-done | bytes 17440 | tf_op jit(solution)/shard_map/ppermute | solution.py:23
  109.3 2.5 %collective-permute-done.22 = f32[17,256]{1,0:T(8,128)S(1)} collective-permute-done((f32[17,256]{1,0:T(8,128)S(1)}, f32[17,256]{1,0:T(8,128)S(1)}, u32[]{:S(2)}, u32[]{:S(2)}) %collective-permute-start.22) | collective-permute-done | bytes 17440 | tf_op jit(solution)/shard_map/ppermute | solution.py:23
  111.8 6.5 %collective-permute-start.27 = (f32[17,256]{1,0:T(8,128)S(1)}, f32[17,256]{1,0:T(8,128)S(1)}, u32[]{:S(2)}, u32[]{:S(2)}) collective-permute-start(f32[17,256]{1,0:T(8,128)S(1)} %add_add_fusion.1), channel_id=1, source_target_pairs={{0,4},{1,5},{2,6},{3,7},{4,0},{5,1},{6,2},{7,3},{8,12},{9,13},{10,... | collective-permute-start | bytes 52232 | tf_op jit(solution)/shard_map/ppermute | solution.py:23
  118.3 2.9 %collective-permute-start.25 = (f32[17,256]{1,0:T(8,128)S(1)}, f32[17,256]{1,0:T(8,128)S(1)}, u32[]{:S(2)}, u32[]{:S(2)}) collective-permute-start(f32[17,256]{1,0:T(8,128)S(1)} %add_add_fusion.1), channel_id=1, source_target_pairs={{0,2},{1,3},{2,4},{3,5},{4,6},{5,7},{6,0},{7,1},{8,10},{9,11},{10,... | collective-permute-start | bytes 52232 | tf_op jit(solution)/shard_map/ppermute | solution.py:23
  121.2 1.8 %collective-permute-done.26 = f32[17,256]{1,0:T(8,128)S(1)} collective-permute-done((f32[17,256]{1,0:T(8,128)S(1)}, f32[17,256]{1,0:T(8,128)S(1)}, u32[]{:S(2)}, u32[]{:S(2)}) %collective-permute-start.26) | collective-permute-done | bytes 17440 | tf_op jit(solution)/shard_map/ppermute | solution.py:23
  124.9 5.0 %all-to-all-start = ((f32[8,16,256]{2,1,0:T(8,128)}), f32[8,16,256]{2,1,0:T(8,128)S(1)}, u32[]{:S(2)}, u32[]{:S(2)}) async-start(f32[8,16,256]{2,1,0:T(8,128)} %broadcast_in_dim.11), calls=%async_computation | async-start | bytes 262144 | tf_op jit(solution)/shard_map/all_to_all | solution.py:331
  130.5 4.5 %all-to-all-done = f32[8,16,256]{2,1,0:T(8,128)S(1)} async-done(((f32[8,16,256]{2,1,0:T(8,128)}), f32[8,16,256]{2,1,0:T(8,128)S(1)}, u32[]{:S(2)}, u32[]{:S(2)}) %all-to-all-start) | async-done | bytes 131104 | tf_op jit(solution)/shard_map/all_to_all | solution.py:331
  (49 shorter events, 8.3 us)
Async XLA Ops:
  0.6 18.1 %collective-permute-start.2 = (bf16[2048,512]{1,0:T(8,128)(2,1)}, bf16[2048,512]{1,0:T(8,128)(2,1)S(1)}, u32[]{:S(2)}, u32[]{:S(2)}) collective-permute-start(bf16[2048,512]{1,0:T(8,128)(2,1)} %own.1), channel_id=1, source_target_pairs={{0,1},{1,0},{2,3},{3,2},{4,5},{5,4},{6,7},{7,6},{8,9},{9,8},{10,11... | collective-permute-start | bytes 6291464 | tf_op jit(solution)/shard_map/ppermute | solution.py:23
  4.1 11.8 %collective-permute-start = (bf16[128,512]{1,0:T(8,128)(2,1)}, bf16[128,512]{1,0:T(8,128)(2,1)S(1)}, u32[]{:S(2)}, u32[]{:S(2)}) collective-permute-start(bf16[128,512]{1,0:T(8,128)(2,1)} %get-tuple-element.28), channel_id=1, source_target_pairs={{0,16},{1,17},{2,18},{3,19},{4,20},{5,21},{6,22},{7,23},{8,64},{9,... | collective-permute-start | bytes 393224 | tf_op jit(solution)/shard_map/ppermute | solution.py:23
  7.2 11.5 %collective-permute-start.1 = (bf16[128,512]{1,0:T(8,128)(2,1)}, bf16[128,512]{1,0:T(8,128)(2,1)S(1)}, u32[]{:S(2)}, u32[]{:S(2)}) collective-permute-start(bf16[128,512]{1,0:T(8,128)(2,1)} %get-tuple-element.29), channel_id=1, source_target_pairs={{0,17},{1,16},{2,19},{3,18},{4,21},{5,20},{6,23},{7,22},{8,65},{9,... | collective-permute-start | bytes 393224 | tf_op jit(solution)/shard_map/ppermute | solution.py:23
  18.8 52.3 %collective-permute-start.3 = (bf16[2048,512]{1,0:T(8,128)(2,1)}, bf16[2048,512]{1,0:T(8,128)(2,1)S(1)}, u32[]{:S(2)}, u32[]{:S(2)}) collective-permute-start(bf16[2048,512]{1,0:T(8,128)(2,1)} %own.1), channel_id=1, source_target_pairs={{0,32},{1,33},{2,34},{3,35},{4,36},{5,37},{6,38},{7,39},{8,40},{9,... | collective-permute-start | bytes 6291464 | tf_op jit(solution)/shard_map/ppermute | solution.py:23
  19.3 12.4 %collective-permute-start.7 = (bf16[1,2,128,512]{3,2,1,0:T(8,128)(2,1)S(1)}, bf16[1,2,128,512]{3,2,1,0:T(8,128)(2,1)S(1)}, u32[]{:S(2)}, u32[]{:S(2)}) collective-permute-start(bf16[1,2,128,512]{3,2,1,0:T(8,128)(2,1)S(1)} %bitcast.14), channel_id=1, source_target_pairs={{0,8},{1,25},{2,10},{3,27},{4,12},{5,29},{6,14},{7,31},{8,16},{9,1... | collective-permute-start | bytes 786440 | tf_op jit(solution)/shard_map/ppermute | solution.py:23
  19.3 17.3 %collective-permute-start.5 = (bf16[2,128,512]{2,1,0:T(8,128)(2,1)S(1)}, bf16[2,128,512]{2,1,0:T(8,128)(2,1)S(1)}, u32[]{:S(2)}, u32[]{:S(2)}) collective-permute-start(bf16[2,128,512]{2,1,0:T(8,128)(2,1)S(1)} %pad_maximum_fusion.1), channel_id=1, source_target_pairs={{0,6},{1,3},{2,0},{3,5},{4,2},{5,7},{6,4},{7,1},{8,14},{9,11},{10,... | collective-permute-start | bytes 786440 | tf_op jit(solution)/shard_map/ppermute | solution.py:23
  25.6 12.7 %collective-permute-start.4 = (bf16[2,128,512]{2,1,0:T(8,128)(2,1)S(1)}, bf16[2,128,512]{2,1,0:T(8,128)(2,1)S(1)}, u32[]{:S(2)}, u32[]{:S(2)}) collective-permute-start(bf16[2,128,512]{2,1,0:T(8,128)(2,1)S(1)} %pad_maximum_fusion.1), channel_id=1, source_target_pairs={{0,2},{1,7},{2,4},{3,1},{4,6},{5,3},{6,0},{7,5},{8,10},{9,15},{10,... | collective-permute-start | bytes 786440 | tf_op jit(solution)/shard_map/ppermute | solution.py:23
  25.6 12.7 %collective-permute-start.6 = (bf16[1,2,128,512]{3,2,1,0:T(8,128)(2,1)S(1)}, bf16[1,2,128,512]{3,2,1,0:T(8,128)(2,1)S(1)}, u32[]{:S(2)}, u32[]{:S(2)}) collective-permute-start(bf16[1,2,128,512]{3,2,1,0:T(8,128)(2,1)S(1)} %bitcast.15), channel_id=1, source_target_pairs={{0,24},{1,9},{2,26},{3,11},{4,28},{5,13},{6,30},{7,15},{8,0},{9,17... | collective-permute-start | bytes 786440 | tf_op jit(solution)/shard_map/ppermute | solution.py:23
  31.7 8.8 %collective-permute-start.8 = (bf16[1,2,128,512]{3,2,1,0:T(8,128)(2,1)S(1)}, bf16[1,2,128,512]{3,2,1,0:T(8,128)(2,1)S(1)}, u32[]{:S(2)}, u32[]{:S(2)}) collective-permute-start(bf16[1,2,128,512]{3,2,1,0:T(8,128)(2,1)S(1)} %collective-permute-done.7.refs_1_), channel_id=1, source_target_pairs={{0,8},{1,25},{2,10},{3,27},{4,12},{5,29},{6,14},{7,31},{8,16},{9,1... | collective-permute-start | bytes 786440 | tf_op jit(solution)/shard_map/ppermute | solution.py:23
  40.5 14.5 %collective-permute-start.9 = (bf16[2,2,128,512]{3,2,1,0:T(8,128)(2,1)S(1)}, bf16[2,2,128,512]{3,2,1,0:T(8,128)(2,1)S(1)}, u32[]{:S(2)}, u32[]{:S(2)}) collective-permute-start(bf16[2,2,128,512]{3,2,1,0:T(8,128)(2,1)S(1)} %pad_maximum_fusion.refs_4_), channel_id=1, source_target_pairs={{0,8},{1,25},{2,10},{3,27},{4,12},{5,29},{6,14},{7,31},{8,16},{9,1... | collective-permute-start | bytes 1572872 | tf_op jit(solution)/shard_map/ppermute | solution.py:23
  41.5 8.7 %collective-permute-start.12 = (bf16[2,128,512]{2,1,0:T(8,128)(2,1)S(1)}, bf16[2,128,512]{2,1,0:T(8,128)(2,1)S(1)}, u32[]{:S(2)}, u32[]{:S(2)}) collective-permute-start(bf16[2,128,512]{2,1,0:T(8,128)(2,1)S(1)} %collective-permute-done.4), channel_id=1, source_target_pairs={{0,2},{1,7},{2,4},{3,1},{4,6},{5,3},{6,0},{7,5},{8,10},{9,15},{10,... | collective-permute-start | bytes 786440 | tf_op jit(solution)/shard_map/ppermute | solution.py:23
  41.9 20.7 %collective-permute-start.11 = (bf16[2,2,128,512]{3,2,1,0:T(8,128)(2,1)S(1)}, bf16[2,2,128,512]{3,2,1,0:T(8,128)(2,1)S(1)}, u32[]{:S(2)}, u32[]{:S(2)}) collective-permute-start(bf16[2,2,128,512]{3,2,1,0:T(8,128)(2,1)S(1)} %pad_maximum_fusion.refs_4_), channel_id=1, source_target_pairs={{0,24},{1,9},{2,26},{3,11},{4,28},{5,13},{6,30},{7,15},{8,0},{9,17... | collective-permute-start | bytes 1572872 | tf_op jit(solution)/shard_map/ppermute | solution.py:23
  50.1 11.6 %collective-permute-start.14 = (bf16[1,2,128,512]{3,2,1,0:T(8,128)(2,1)S(1)}, bf16[1,2,128,512]{3,2,1,0:T(8,128)(2,1)S(1)}, u32[]{:S(2)}, u32[]{:S(2)}) collective-permute-start(bf16[1,2,128,512]{3,2,1,0:T(8,128)(2,1)S(1)} %bitcast.17), channel_id=1, source_target_pairs={{0,24},{1,9},{2,26},{3,11},{4,28},{5,13},{6,30},{7,15},{8,0},{9,17... | collective-permute-start | bytes 786440 | tf_op jit(solution)/shard_map/ppermute | solution.py:23
  55.0 7.6 %collective-permute-start.13 = (bf16[1,2,128,512]{3,2,1,0:T(8,128)(2,1)S(1)}, bf16[1,2,128,512]{3,2,1,0:T(8,128)(2,1)S(1)}, u32[]{:S(2)}, u32[]{:S(2)}) collective-permute-start(bf16[1,2,128,512]{3,2,1,0:T(8,128)(2,1)S(1)} %bitcast.18), channel_id=1, source_target_pairs={{0,8},{1,25},{2,10},{3,27},{4,12},{5,29},{6,14},{7,31},{8,16},{9,1... | collective-permute-start | bytes 786440 | tf_op jit(solution)/shard_map/ppermute | solution.py:23
  55.0 16.0 %collective-permute-start.10 = (bf16[2,2,128,512]{3,2,1,0:T(8,128)(2,1)S(1)}, bf16[2,2,128,512]{3,2,1,0:T(8,128)(2,1)S(1)}, u32[]{:S(2)}, u32[]{:S(2)}) collective-permute-start(bf16[2,2,128,512]{3,2,1,0:T(8,128)(2,1)S(1)} %collective-permute-done.9.refs_5_), channel_id=1, source_target_pairs={{0,8},{1,25},{2,10},{3,27},{4,12},{5,29},{6,14},{7,31},{8,16},{9,1... | collective-permute-start | bytes 1572872 | tf_op jit(solution)/shard_map/ppermute | solution.py:23
  62.6 8.4 %collective-permute-start.15 = (bf16[1,2,128,512]{3,2,1,0:T(8,128)(2,1)S(1)}, bf16[1,2,128,512]{3,2,1,0:T(8,128)(2,1)S(1)}, u32[]{:S(2)}, u32[]{:S(2)}) collective-permute-start(bf16[1,2,128,512]{3,2,1,0:T(8,128)(2,1)S(1)} %collective-permute-done.13.refs_9_), channel_id=1, source_target_pairs={{0,8},{1,25},{2,10},{3,27},{4,12},{5,29},{6,14},{7,31},{8,16},{9,1... | collective-permute-start | bytes 786440 | tf_op jit(solution)/shard_map/ppermute | solution.py:23
  71.0 5.7 %collective-permute-start.16 = (bf16[2048,512]{1,0:T(8,128)(2,1)S(1)}, bf16[2048,512]{1,0:T(8,128)(2,1)S(1)}, u32[]{:S(2)}, u32[]{:S(2)}) collective-permute-start(bf16[2048,512]{1,0:T(8,128)(2,1)S(1)} %collective-permute-done.3.far), channel_id=1, source_target_pairs={{0,1},{1,0},{2,3},{3,2},{4,5},{5,4},{6,7},{7,6},{8,9},{9,8},{10,11... | collective-permute-start | bytes 6291464 | tf_op jit(solution)/shard_map/ppermute | solution.py:23
  76.7 20.9 %copy-start.1 = (s32[2,256,64]{1,2,0:T(8,128)S(1)}, s32[2,256,64]{1,2,0:T(8,128)}, u32[]{:S(2)}) copy-start(s32[2,256,64]{1,2,0:T(8,128)} %param.5) | copy-start | bytes 393220
  76.7 20.9 %copy-start.2 = (f32[256]{0:T(256)S(1)}, f32[256]{0:T(256)}, u32[]{:S(2)}) copy-start(f32[256]{0:T(256)} %param.7) | copy-start | bytes 3076
  76.8 20.9 %copy-start.3 = (f32[512,256]{1,0:T(8,128)S(1)}, f32[512,256]{1,0:T(8,128)}, u32[]{:S(2)}) copy-start(f32[512,256]{1,0:T(8,128)} %get-tuple-element.27.decoded) | copy-start | bytes 1572868
  79.9 11.6 %collective-permute-start.17 = (bf16[128,1024]{1,0:T(8,128)(2,1)S(1)}, bf16[128,1024]{1,0:T(8,128)(2,1)S(1)}, u32[]{:S(2)}, u32[]{:S(2)}) collective-permute-start(bf16[128,1024]{1,0:T(8,128)(2,1)S(1)} %get-tuple-element.46), channel_id=1, source_target_pairs={{0,192},{1,193},{2,194},{3,195},{4,196},{5,197},{6,198},{7,199},{8... | collective-permute-start | bytes 786440 | tf_op jit(solution)/shard_map/ppermute | solution.py:23
  80.0 15.9 %collective-permute-start.18 = (bf16[128,1024]{1,0:T(8,128)(2,1)S(1)}, bf16[128,1024]{1,0:T(8,128)(2,1)S(1)}, u32[]{:S(2)}, u32[]{:S(2)}) collective-permute-start(bf16[128,1024]{1,0:T(8,128)(2,1)S(1)} %get-tuple-element.47), channel_id=1, source_target_pairs={{0,64},{1,65},{2,66},{3,67},{4,68},{5,69},{6,70},{7,71},{8,72},{9,... | collective-permute-start | bytes 786440 | tf_op jit(solution)/shard_map/ppermute | solution.py:23
  83.5 12.5 %collective-permute-start.19 = (bf16[128,1024]{1,0:T(8,128)(2,1)S(1)}, bf16[128,1024]{1,0:T(8,128)(2,1)S(1)}, u32[]{:S(2)}, u32[]{:S(2)}) collective-permute-start(bf16[128,1024]{1,0:T(8,128)(2,1)S(1)} %get-tuple-element.48), channel_id=1, source_target_pairs={{0,128},{1,129},{2,130},{3,131},{4,132},{5,133},{6,134},{7,135},{8... | collective-permute-start | bytes 786440 | tf_op jit(solution)/shard_map/ppermute | solution.py:23
  96.0 1.6 %collective-permute-start.20 = (f32[128,512]{1,0:T(8,128)S(1)}, f32[128,512]{1,0:T(8,128)S(1)}, u32[]{:S(2)}, u32[]{:S(2)}) collective-permute-start(f32[128,512]{1,0:T(8,128)S(1)} %convert_add_fusion), channel_id=1, source_target_pairs={{0,1},{1,0},{2,3},{3,2},{4,5},{5,4},{6,7},{7,6},{8,9},{9,8},{10,11... | collective-permute-start | bytes 786440 | tf_op jit(solution)/shard_map/ppermute | solution.py:23
  102.8 1.2 collective-permute-start.21
  104.0 5.3 %collective-permute-start.24 = (f32[17,256]{1,0:T(8,128)S(1)}, f32[17,256]{1,0:T(8,128)S(1)}, u32[]{:S(2)}, u32[]{:S(2)}) collective-permute-start(f32[17,256]{1,0:T(8,128)S(1)} %add.33), channel_id=1, source_target_pairs={{0,16},{1,17},{2,18},{3,19},{4,20},{5,21},{6,22},{7,23},{8,24},{9,... | collective-permute-start | bytes 52232 | tf_op jit(solution)/shard_map/ppermute | solution.py:23
  104.4 4.9 %collective-permute-start.23 = (f32[17,256]{1,0:T(8,128)S(1)}, f32[17,256]{1,0:T(8,128)S(1)}, u32[]{:S(2)}, u32[]{:S(2)}) collective-permute-start(f32[17,256]{1,0:T(8,128)S(1)} %add.33), channel_id=1, source_target_pairs={{0,24},{1,25},{2,26},{3,27},{4,28},{5,29},{6,30},{7,31},{8,0},{9,1... | collective-permute-start | bytes 52232 | tf_op jit(solution)/shard_map/ppermute | solution.py:23
  106.8 5.0 %collective-permute-start.22 = (f32[17,256]{1,0:T(8,128)S(1)}, f32[17,256]{1,0:T(8,128)S(1)}, u32[]{:S(2)}, u32[]{:S(2)}) collective-permute-start(f32[17,256]{1,0:T(8,128)S(1)} %add.33), channel_id=1, source_target_pairs={{0,8},{1,9},{2,10},{3,11},{4,12},{5,13},{6,14},{7,15},{8,16},{9,17... | collective-permute-start | bytes 52232 | tf_op jit(solution)/shard_map/ppermute | solution.py:23
  111.8 9.4 %collective-permute-start.27 = (f32[17,256]{1,0:T(8,128)S(1)}, f32[17,256]{1,0:T(8,128)S(1)}, u32[]{:S(2)}, u32[]{:S(2)}) collective-permute-start(f32[17,256]{1,0:T(8,128)S(1)} %add_add_fusion.1), channel_id=1, source_target_pairs={{0,4},{1,5},{2,6},{3,7},{4,0},{5,1},{6,2},{7,3},{8,12},{9,13},{10,... | collective-permute-start | bytes 52232 | tf_op jit(solution)/shard_map/ppermute | solution.py:23
  118.3 4.7 %collective-permute-start.26 = (f32[17,256]{1,0:T(8,128)S(1)}, f32[17,256]{1,0:T(8,128)S(1)}, u32[]{:S(2)}, u32[]{:S(2)}) collective-permute-start(f32[17,256]{1,0:T(8,128)S(1)} %add_add_fusion.1), channel_id=1, source_target_pairs={{0,6},{1,7},{2,0},{3,1},{4,2},{5,3},{6,4},{7,5},{8,14},{9,15},{10,... | collective-permute-start | bytes 52232 | tf_op jit(solution)/shard_map/ppermute | solution.py:23
  118.3 5.9 %collective-permute-start.25 = (f32[17,256]{1,0:T(8,128)S(1)}, f32[17,256]{1,0:T(8,128)S(1)}, u32[]{:S(2)}, u32[]{:S(2)}) collective-permute-start(f32[17,256]{1,0:T(8,128)S(1)} %add_add_fusion.1), channel_id=1, source_target_pairs={{0,2},{1,3},{2,4},{3,5},{4,6},{5,7},{6,0},{7,1},{8,10},{9,11},{10,... | collective-permute-start | bytes 52232 | tf_op jit(solution)/shard_map/ppermute | solution.py:23
  124.9 10.1 %all-to-all-start = ((f32[8,16,256]{2,1,0:T(8,128)}), f32[8,16,256]{2,1,0:T(8,128)S(1)}, u32[]{:S(2)}, u32[]{:S(2)}) async-start(f32[8,16,256]{2,1,0:T(8,128)} %broadcast_in_dim.11), calls=%async_computation | async-start | bytes 262144 | tf_op jit(solution)/shard_map/all_to_all | solution.py:331
  (1 other events, 1.6 us)

commit v10 on v9

--- a/solution.py
+++ b/solution.py
@@ -34,8 +34,7 @@
 
 
 def to_plane(z_lo, y_hi, y_lo, x, z_hi, core):
-    move = {(0, 0): 2, (1, 0): 1, (0, 1): -1, (1, 1): 0}[z_lo ^ (x // 2), y_hi ^ (x % 2)]
-    return (x // 2, x % 2, y_lo, x + move, z_hi, core)
+    return (x // 2, x % 2, y_lo, x + 2 * z_lo + y_hi, z_hi, core)
 
 
 def decode_kernel(
@@ -198,9 +197,7 @@
         for place, dz in enumerate(dzs):
             from_x = (x + 8 - step * dx) % 4
             from_z = (z_hi + 8 - step * dz) % 4
-            move = (from_x + 8 - 2 * z_lo - y_hi) % 4
-            cross_z, cross_y = 1 - move // 2, 1 - (move + 1) % 4 // 2
-            s = (z_lo + cross_z) % 2 * 2 + (y_hi + cross_y) % 2
+            s = (from_x + 8 - 2 * z_lo - y_hi) % 4
             tile = (from_z // 2 + y_lo) % 2
             for side in range(2):
                 n = len(copies)
@@ -297,7 +294,7 @@
         ],
         name="first",
         **settings,
-    )(hessian, far, *blocks)
+    )(pltpu.with_memory_space_constraint(hessian, pltpu.HBM), far, *blocks)
     sent = jax.ShapeDtypeStruct((half, 2 * width), jnp.bfloat16)
     own, to_y, to_z, to_both = pl.pallas_call(
         second_kernel,
@@ -324,11 +321,15 @@
     product, total = finish(codes, row_scale, decoded, parts, got)
 
     total = total + shift(total, "core", 1)
-    for axis in ("x", "z_hi"):
-        total = total + shift(total, axis, 1) + shift(total, axis, -1) + shift(total, axis, 2)
-    scale_total, books = total[16], total[:16]
-    copies = jnp.broadcast_to(books, (8, *books.shape))
-    books = jnp.sum(lax.all_to_all(copies, ROW, 0, 0, tiled=True), axis=0)
+    total = total + shift(total, "x", 1) + shift(total, "x", -1) + shift(total, "x", 2)
+    copies = jnp.broadcast_to(total, (8, *total.shape))
+    copies = lax.all_to_all(copies, ("z_hi", "z_lo"), 0, 0, tiled=True)
+    scales = copies[:, 16].reshape(4, 2, rows)
+    scale_total = jnp.sum(jnp.where(lax.axis_index("z_lo") == 0, scales[:, 0], scales[:, 1]), axis=0)
+    books = jnp.sum(copies[:, :16], axis=0)
+    beside, across_y = shift(books, "y_lo", 1), shift(books, "y_hi", 1)
+    both = send(books, lambda zl, yh, yl, x, zh, c: (zl, 1 - yh, 1 - yl, x, zh, c))
+    books = books + beside + across_y + both
     full_width = width * 32
     all_groups = rows * 8 * (full_width // 8)
     scale_grad = scale_total / full_width

time: 136 us -> 134 us (0.985)
  waiting for transfers between devices: 64.7 us -> 62.2 us
  local copies, waits for them, and re-layouts: 2.26 us -> 0.76 us
  starting transfers between devices: 50.7 us -> 52.1 us
    ppermute x28, waiting for transfers between devices: 60.2 us -> 52.4 us  [send(): return lax.ppermute(a, AXES, pairs)]
    all_to_all x1, waiting for transfers between devices: 4.5 us -> 9.78 us  [body(): copies = lax.all_to_all(copies, ('z_hi', 'z_lo'), 0, 0, tiled=True)]
    unnamed x8 -> x6, local copies, waits for them, and re-layouts: 1.61 us -> 0.02 us
  transfers between devices with their start and end apart: 29 -> 29, of which waited for: 18 -> 14; matrix products, arithmetic and copies ran while one was open for 0% -> 1% of each run, Pallas kernels for 5% -> 6%
where the time goes in v10:
time: 134 us
  waiting for transfers between devices  62.2 us (46%)
  starting transfers between devices  52.1 us (39%)
  Pallas kernels  16.3 us (12%)
  other arithmetic  1.38 us (1%)
    ppermute x28, waiting for transfers between devices, send(): return lax.ppermute(a, AXES, pairs)  52.4 us
    ppermute x28, starting transfers between devices, send(): return lax.ppermute(a, AXES, pairs)  46.4 us
    all_to_all x1, waiting for transfers between devices, body(): copies = lax.all_to_all(copies, ('z_hi', 'z_lo'), 0, 0, tiled=True)  9.78 us
    all_to_all x1, starting transfers between devices, body(): copies = lax.all_to_all(copies, ('z_hi', 'z_lo'), 0, 0, tiled=True)  5.68 us
    pallas_call x1, Pallas kernels, finish(): pl.pallas_call(finish_kernel, out_shape=(jax.ShapeDtypeStruct((rows, widt...  5.12 us
    pallas_call x1, Pallas kernels, body(): pl.pallas_call(first_kernel, out_shape=(jax.ShapeDtypeStruct((4, half, wi...  4.69 us
    pallas_call x1, Pallas kernels, decode(): pl.pallas_call(decode_kernel, out_shape=(jax.ShapeDtypeStruct((width, row...  3.36 us
    pallas_call x1, Pallas kernels, body(): pl.pallas_call(second_kernel, out_shape=(jax.ShapeDtypeStruct(sent.shape,...  3.16 us
  transfers between devices with their start and end apart: 29, of which 14 were waited for; matrix products, arithmetic and copies ran while one was open for 1% of the time, Pallas kernels for 6%

profile of v10, /device:TPU:8, one launch (start us, length us, event | category | flops | bytes accessed | tf_op | source)
XLA Modules:
  0.0 133.5 jit_solution(13979847257794734877)
XLA Ops:
  0.7 3.4 %decode.1 = (f32[512,256]{1,0:T(8,128)}, bf16[128,512]{1,0:T(8,128)(2,1)}, bf16[128,512]{1,0:T(8,128)(2,1)}) custom-call(s32[2,64,256]{2,1,0:T(8,128)} %bitcast.19, bf16[2,8,256]{2,1,0:T(8,128)(2,1)} %bitcast.27, f32[1,256]{1,0:T(1,128)} %bitcast.21, bf16[256,512]{1,0:T(8,128)(2,1)} %initial_in.1), custom_call_target="tpu_custom_call" | custom-call | flops 2097152 | bytes 1048576 | tf_op jit(solution)/shard_map/decode/pallas_call | solution.py:81
  4.7 1.6 %collective-permute-start = (bf16[128,512]{1,0:T(8,128)(2,1)}, bf16[128,512]{1,0:T(8,128)(2,1)S(1)}, u32[]{:S(2)}, u32[]{:S(2)}) collective-permute-start(bf16[128,512]{1,0:T(8,128)(2,1)} %get-tuple-element.28), channel_id=1, source_target_pairs={{0,0},{1,1},{2,2},{3,3},{4,4},{5,5},{6,6},{7,7},{8,72},{9,73},{10,... | collective-permute-start | bytes 393224 | tf_op jit(solution)/shard_map/ppermute | solution.py:23
  6.3 2.3 %collective-permute-start.3 = (bf16[2048,512]{1,0:T(8,128)(2,1)}, bf16[2048,512]{1,0:T(8,128)(2,1)S(1)}, u32[]{:S(2)}, u32[]{:S(2)}) collective-permute-start(bf16[2048,512]{1,0:T(8,128)(2,1)} %own.1), channel_id=1, source_target_pairs={{0,32},{1,33},{2,34},{3,35},{4,36},{5,37},{6,38},{7,39},{8,40},{9,... | collective-permute-start | bytes 6291464 | tf_op jit(solution)/shard_map/ppermute | solution.py:23
  8.5 10.9 %collective-permute-start.7 = (bf16[1,2,128,512]{3,2,1,0:T(8,128)(2,1)S(1)}, bf16[1,2,128,512]{3,2,1,0:T(8,128)(2,1)S(1)}, u32[]{:S(2)}, u32[]{:S(2)}) collective-permute-start(bf16[1,2,128,512]{3,2,1,0:T(8,128)(2,1)S(1)} %bitcast.13), channel_id=1, source_target_pairs={{0,8},{1,25},{2,10},{3,27},{4,12},{5,29},{6,14},{7,31},{8,16},{9,1... | collective-permute-start | bytes 786440 | tf_op jit(solution)/shard_map/ppermute | solution.py:23
  19.5 6.3 %collective-permute-start.5 = (bf16[2,128,512]{2,1,0:T(8,128)(2,1)S(1)}, bf16[2,128,512]{2,1,0:T(8,128)(2,1)S(1)}, u32[]{:S(2)}, u32[]{:S(2)}) collective-permute-start(bf16[2,128,512]{2,1,0:T(8,128)(2,1)S(1)} %pad_maximum_fusion.1), channel_id=1, source_target_pairs={{0,6},{1,3},{2,0},{3,5},{4,2},{5,7},{6,4},{7,1},{8,14},{9,11},{10,... | collective-permute-start | bytes 786440 | tf_op jit(solution)/shard_map/ppermute | solution.py:23
  25.8 3.8 %collective-permute-start.6 = (bf16[1,2,128,512]{3,2,1,0:T(8,128)(2,1)S(1)}, bf16[1,2,128,512]{3,2,1,0:T(8,128)(2,1)S(1)}, u32[]{:S(2)}, u32[]{:S(2)}) collective-permute-start(bf16[1,2,128,512]{3,2,1,0:T(8,128)(2,1)S(1)} %bitcast.14), channel_id=1, source_target_pairs={{0,24},{1,9},{2,26},{3,11},{4,28},{5,13},{6,30},{7,15},{8,0},{9,17... | collective-permute-start | bytes 786440 | tf_op jit(solution)/shard_map/ppermute | solution.py:23
  29.6 7.1 %collective-permute-done.5 = bf16[2,128,512]{2,1,0:T(8,128)(2,1)S(1)} collective-permute-done((bf16[2,128,512]{2,1,0:T(8,128)(2,1)S(1)}, bf16[2,128,512]{2,1,0:T(8,128)(2,1)S(1)}, u32[]{:S(2)}, u32[]{:S(2)}) %collective-permute-start.5) | collective-permute-done | bytes 262176 | tf_op jit(solution)/shard_map/ppermute | solution.py:23
  36.7 3.6 %collective-permute-done.4 = bf16[2,128,512]{2,1,0:T(8,128)(2,1)S(1)} collective-permute-done((bf16[2,128,512]{2,1,0:T(8,128)(2,1)S(1)}, bf16[2,128,512]{2,1,0:T(8,128)(2,1)S(1)}, u32[]{:S(2)}, u32[]{:S(2)}) %collective-permute-start.4) | collective-permute-done | bytes 262176 | tf_op jit(solution)/shard_map/ppermute | solution.py:23
  40.9 3.2 %collective-permute-start.11 = (bf16[2,2,128,512]{3,2,1,0:T(8,128)(2,1)S(1)}, bf16[2,2,128,512]{3,2,1,0:T(8,128)(2,1)S(1)}, u32[]{:S(2)}, u32[]{:S(2)}) collective-permute-start(bf16[2,2,128,512]{3,2,1,0:T(8,128)(2,1)S(1)} %pad_maximum_fusion.refs_4_), channel_id=1, source_target_pairs={{0,24},{1,9},{2,26},{3,11},{4,28},{5,13},{6,30},{7,15},{8,0},{9,17... | collective-permute-start | bytes 1572872 | tf_op jit(solution)/shard_map/ppermute | solution.py:23
  44.1 7.0 %collective-permute-done.12 = bf16[2,128,512]{2,1,0:T(8,128)(2,1)S(1)} collective-permute-done((bf16[2,128,512]{2,1,0:T(8,128)(2,1)S(1)}, bf16[2,128,512]{2,1,0:T(8,128)(2,1)S(1)}, u32[]{:S(2)}, u32[]{:S(2)}) %collective-permute-start.12) | collective-permute-done | bytes 262176 | tf_op jit(solution)/shard_map/ppermute | solution.py:23
  51.2 1.0 collective-permute-start.13
  52.2 2.2 %collective-permute-start.14 = (bf16[1,2,128,512]{3,2,1,0:T(8,128)(2,1)S(1)}, bf16[1,2,128,512]{3,2,1,0:T(8,128)(2,1)S(1)}, u32[]{:S(2)}, u32[]{:S(2)}) collective-permute-start(bf16[1,2,128,512]{3,2,1,0:T(8,128)(2,1)S(1)} %bitcast.17), channel_id=1, source_target_pairs={{0,24},{1,9},{2,26},{3,11},{4,28},{5,13},{6,30},{7,15},{8,0},{9,17... | collective-permute-start | bytes 786440 | tf_op jit(solution)/shard_map/ppermute | solution.py:23
  54.4 7.2 %collective-permute-done.13.refs_9_ = bf16[1,2,128,512]{3,2,1,0:T(8,128)(2,1)S(1)} collective-permute-done((bf16[1,2,128,512]{3,2,1,0:T(8,128)(2,1)S(1)}, bf16[1,2,128,512]{3,2,1,0:T(8,128)(2,1)S(1)}, u32[]{:S(2)}, u32[]{:S(2)}) %collective-permute-start.13) | collective-permute-done | bytes 262176 | tf_op jit(solution)/shard_map/ppermute | solution.py:23
  61.7 1.3 %collective-permute-start.15 = (bf16[1,2,128,512]{3,2,1,0:T(8,128)(2,1)S(1)}, bf16[1,2,128,512]{3,2,1,0:T(8,128)(2,1)S(1)}, u32[]{:S(2)}, u32[]{:S(2)}) collective-permute-start(bf16[1,2,128,512]{3,2,1,0:T(8,128)(2,1)S(1)} %collective-permute-done.13.refs_9_), channel_id=1, source_target_pairs={{0,8},{1,25},{2,10},{3,27},{4,12},{5,29},{6,14},{7,31},{8,16},{9,1... | collective-permute-start | bytes 786440 | tf_op jit(solution)/shard_map/ppermute | solution.py:23
  63.0 7.4 %collective-permute-done.15.refs_11_ = bf16[1,2,128,512]{3,2,1,0:T(8,128)(2,1)S(1)} collective-permute-done((bf16[1,2,128,512]{3,2,1,0:T(8,128)(2,1)S(1)}, bf16[1,2,128,512]{3,2,1,0:T(8,128)(2,1)S(1)}, u32[]{:S(2)}, u32[]{:S(2)}) %collective-permute-start.15) | collective-permute-done | bytes 262176 | tf_op jit(solution)/shard_map/ppermute | solution.py:23
  70.4 4.7 %first.1 = (f32[4,128,512]{2,1,0:T(8,128)S(1)}, bf16[512,4096]{1,0:T(8,128)(2,1)S(1)}) custom-call(bf16[2048,512]{1,0:T(8,128)(2,1)} %own.1, bf16[2048,512]{1,0:T(8,128)(2,1)S(1)} %collective-permute-done.3.far, bf16[1,2,128,512]{3,2,1,0:T(8,128)(2,1)S(1)} %bitcast.15, bf16[1,2,128,512]{3,2,1,0:T(8,128)(2,1)S(1)} %collective-permute-done.7.refs_1_, ...), custom_call_target="tpu_custom_call" | custom-call | flops 2147483648 | bytes 8388608 | tf_op jit(solution)/shard_map/first/pallas_call | solution.py:283
  75.2 3.2 %second.1 = (f32[128,1024]{1,0:T(8,128)S(1)}, bf16[128,1024]{1,0:T(8,128)(2,1)S(1)}, bf16[128,1024]{1,0:T(8,128)(2,1)S(1)}, bf16[128,1024]{1,0:T(8,128)(2,1)S(1)}) custom-call(f32[4,128,512]{2,1,0:T(8,128)S(1)} %get-tuple-element.42.kept, bf16[512,4096]{1,0:T(8,128)(2,1)S(1)} %get-tuple-element.43.held, bf16[2048,512]{1,0:T(8,128)(2,1)S(1)} %collective-permute-done.2.across, ...), custom_call_target="tpu_custom_call" | custom-call | flops 2147483648 | bytes 8388608 | tf_op jit(solution)/shard_map/second/pallas_call | solution.py:299
  78.9 2.9 %collective-permute-start.18 = (bf16[128,1024]{1,0:T(8,128)(2,1)S(1)}, bf16[128,1024]{1,0:T(8,128)(2,1)S(1)}, u32[]{:S(2)}, u32[]{:S(2)}) collective-permute-start(bf16[128,1024]{1,0:T(8,128)(2,1)S(1)} %get-tuple-element.47), channel_id=1, source_target_pairs={{0,64},{1,65},{2,66},{3,67},{4,68},{5,69},{6,70},{7,71},{8,72},{9,... | collective-permute-start | bytes 786440 | tf_op jit(solution)/shard_map/ppermute | solution.py:23
  81.7 1.7 %collective-permute-start.19 = (bf16[128,1024]{1,0:T(8,128)(2,1)S(1)}, bf16[128,1024]{1,0:T(8,128)(2,1)S(1)}, u32[]{:S(2)}, u32[]{:S(2)}) collective-permute-start(bf16[128,1024]{1,0:T(8,128)(2,1)S(1)} %get-tuple-element.48), channel_id=1, source_target_pairs={{0,128},{1,129},{2,130},{3,131},{4,132},{5,133},{6,134},{7,135},{8... | collective-permute-start | bytes 786440 | tf_op jit(solution)/shard_map/ppermute | solution.py:23
  83.4 6.6 %collective-permute-done.17.to_both = bf16[128,1024]{1,0:T(8,128)(2,1)S(1)} collective-permute-done((bf16[128,1024]{1,0:T(8,128)(2,1)S(1)}, bf16[128,1024]{1,0:T(8,128)(2,1)S(1)}, u32[]{:S(2)}, u32[]{:S(2)}) %collective-permute-start.17) | collective-permute-done | bytes 262176 | tf_op jit(solution)/shard_map/ppermute | solution.py:23
  90.0 4.4 %collective-permute-done.18.to_y = bf16[128,1024]{1,0:T(8,128)(2,1)S(1)} collective-permute-done((bf16[128,1024]{1,0:T(8,128)(2,1)S(1)}, bf16[128,1024]{1,0:T(8,128)(2,1)S(1)}, u32[]{:S(2)}, u32[]{:S(2)}) %collective-permute-start.18) | collective-permute-done | bytes 262176 | tf_op jit(solution)/shard_map/ppermute | solution.py:23
  94.6 1.5 %collective-permute-done.20.got = f32[128,512]{1,0:T(8,128)S(1)} collective-permute-done((f32[128,512]{1,0:T(8,128)S(1)}, f32[128,512]{1,0:T(8,128)S(1)}, u32[]{:S(2)}, u32[]{:S(2)}) %collective-permute-start.20) | collective-permute-done | bytes 262176 | tf_op jit(solution)/shard_map/ppermute | solution.py:23
  96.1 5.1 %finish.1 = (f32[256,512]{1,0:T(8,128)}, f32[17,256]{1,0:T(8,128)S(1)}) custom-call(s32[2,64,256]{2,1,0:T(8,128)S(1)} %bitcast.20, f32[1,256]{1,0:T(1,128)S(1)} %bitcast.22, f32[512,256]{1,0:T(8,128)S(1)} %copy-done.2, f32[128,1024]{1,0:T(8,128)S(1)} %get-tuple-element.45.own, bf16[128,1024]{1,0:T(8,128)(2,1)S(1)} %collective-permute-done.17.to_both, ...), custom_call_target="tpu_custom_call" | custom-call | flops 4294967296 | bytes 2097152 | tf_op jit(solution)/shard_map/finish/pallas_call | solution.py:151
  101.4 1.1 collective-permute-done.21
  104.0 1.4 %collective-permute-start.22 = (f32[17,256]{1,0:T(8,128)S(1)}, f32[17,256]{1,0:T(8,128)S(1)}, u32[]{:S(2)}, u32[]{:S(2)}) collective-permute-start(f32[17,256]{1,0:T(8,128)S(1)} %add.33), channel_id=1, source_target_pairs={{0,8},{1,9},{2,10},{3,11},{4,12},{5,13},{6,14},{7,15},{8,16},{9,17... | collective-permute-start | bytes 52232 | tf_op jit(solution)/shard_map/ppermute | solution.py:23
  105.4 2.5 %collective-permute-done.24 = f32[17,256]{1,0:T(8,128)S(1)} collective-permute-done((f32[17,256]{1,0:T(8,128)S(1)}, f32[17,256]{1,0:T(8,128)S(1)}, u32[]{:S(2)}, u32[]{:S(2)}) %collective-permute-start.24) | collective-permute-done | bytes 17440 | tf_op jit(solution)/shard_map/ppermute | solution.py:23
  107.9 1.1 collective-permute-done.22
  109.7 5.7 %all-to-all-start = ((f32[8,17,256]{2,1,0:T(8,128)}), f32[8,17,256]{2,1,0:T(8,128)S(1)}, u32[]{:S(2)}, u32[]{:S(2)}) async-start(f32[8,17,256]{2,1,0:T(8,128)} %broadcast_in_dim.11), calls=%async_computation | async-start | bytes 393216 | tf_op jit(solution)/shard_map/all_to_all | solution.py:326
  115.4 9.8 %all-to-all-done = f32[8,17,256]{2,1,0:T(8,128)S(1)} async-done(((f32[8,17,256]{2,1,0:T(8,128)}), f32[8,17,256]{2,1,0:T(8,128)S(1)}, u32[]{:S(2)}, u32[]{:S(2)}) %all-to-all-start) | async-done | bytes 139296 | tf_op jit(solution)/shard_map/all_to_all | solution.py:326
  125.2 1.6 %collective-permute-start.27 = (f32[16,256]{1,0:T(8,128)S(1)}, f32[16,256]{1,0:T(8,128)S(1)}, u32[]{:S(2)}, u32[]{:S(2)}) collective-permute-start(f32[16,256]{1,0:T(8,128)S(1)} %slice_reduce_fusion), channel_id=1, source_target_pairs={{0,96},{1,97},{2,98},{3,99},{4,100},{5,101},{6,102},{7,103},{8,104... | collective-permute-start | bytes 49160 | tf_op jit(solution)/shard_map/ppermute | solution.py:23
  126.8 2.4 %collective-permute-start.26 = (f32[16,256]{1,0:T(8,128)S(1)}, f32[16,256]{1,0:T(8,128)S(1)}, u32[]{:S(2)}, u32[]{:S(2)}) collective-permute-start(f32[16,256]{1,0:T(8,128)S(1)} %slice_reduce_fusion), channel_id=1, source_target_pairs={{0,64},{1,65},{2,66},{3,67},{4,68},{5,69},{6,70},{7,71},{8,72},{9,... | collective-permute-start | bytes 49160 | tf_op jit(solution)/shard_map/ppermute | solution.py:23
  130.0 2.0 %collective-permute-done.26 = f32[16,256]{1,0:T(8,128)S(1)} collective-permute-done((f32[16,256]{1,0:T(8,128)S(1)}, f32[16,256]{1,0:T(8,128)S(1)}, u32[]{:S(2)}, u32[]{:S(2)}) %collective-permute-start.26) | collective-permute-done | bytes 16416 | tf_op jit(solution)/shard_map/ppermute | solution.py:23
  (48 shorter events, 6.9 us)
Async XLA Ops:
  0.6 5.6 %collective-permute-start.2 = (bf16[2048,512]{1,0:T(8,128)(2,1)}, bf16[2048,512]{1,0:T(8,128)(2,1)S(1)}, u32[]{:S(2)}, u32[]{:S(2)}) collective-permute-start(bf16[2048,512]{1,0:T(8,128)(2,1)} %own.1), channel_id=1, source_target_pairs={{0,1},{1,0},{2,3},{3,2},{4,5},{5,4},{6,7},{7,6},{8,9},{9,8},{10,11... | collective-permute-start | bytes 6291464 | tf_op jit(solution)/shard_map/ppermute | solution.py:23
  4.1 2.1 %collective-permute-start.1 = (bf16[128,512]{1,0:T(8,128)(2,1)}, bf16[128,512]{1,0:T(8,128)(2,1)S(1)}, u32[]{:S(2)}, u32[]{:S(2)}) collective-permute-start(bf16[128,512]{1,0:T(8,128)(2,1)} %get-tuple-element.29), channel_id=1, source_target_pairs={{0,1},{1,0},{2,3},{3,2},{4,5},{5,4},{6,7},{7,6},{8,73},{9,72},{10,... | collective-permute-start | bytes 393224 | tf_op jit(solution)/shard_map/ppermute | solution.py:23
  4.7 1.6 %collective-permute-start = (bf16[128,512]{1,0:T(8,128)(2,1)}, bf16[128,512]{1,0:T(8,128)(2,1)S(1)}, u32[]{:S(2)}, u32[]{:S(2)}) collective-permute-start(bf16[128,512]{1,0:T(8,128)(2,1)} %get-tuple-element.28), channel_id=1, source_target_pairs={{0,0},{1,1},{2,2},{3,3},{4,4},{5,5},{6,6},{7,7},{8,72},{9,73},{10,... | collective-permute-start | bytes 393224 | tf_op jit(solution)/shard_map/ppermute | solution.py:23
  6.3 64.2 %collective-permute-start.3 = (bf16[2048,512]{1,0:T(8,128)(2,1)}, bf16[2048,512]{1,0:T(8,128)(2,1)S(1)}, u32[]{:S(2)}, u32[]{:S(2)}) collective-permute-start(bf16[2048,512]{1,0:T(8,128)(2,1)} %own.1), channel_id=1, source_target_pairs={{0,32},{1,33},{2,34},{3,35},{4,36},{5,37},{6,38},{7,39},{8,40},{9,... | collective-permute-start | bytes 6291464 | tf_op jit(solution)/shard_map/ppermute | solution.py:23
  8.5 21.1 %collective-permute-start.7 = (bf16[1,2,128,512]{3,2,1,0:T(8,128)(2,1)S(1)}, bf16[1,2,128,512]{3,2,1,0:T(8,128)(2,1)S(1)}, u32[]{:S(2)}, u32[]{:S(2)}) collective-permute-start(bf16[1,2,128,512]{3,2,1,0:T(8,128)(2,1)S(1)} %bitcast.13), channel_id=1, source_target_pairs={{0,8},{1,25},{2,10},{3,27},{4,12},{5,29},{6,14},{7,31},{8,16},{9,1... | collective-permute-start | bytes 786440 | tf_op jit(solution)/shard_map/ppermute | solution.py:23
  19.5 17.2 %collective-permute-start.5 = (bf16[2,128,512]{2,1,0:T(8,128)(2,1)S(1)}, bf16[2,128,512]{2,1,0:T(8,128)(2,1)S(1)}, u32[]{:S(2)}, u32[]{:S(2)}) collective-permute-start(bf16[2,128,512]{2,1,0:T(8,128)(2,1)S(1)} %pad_maximum_fusion.1), channel_id=1, source_target_pairs={{0,6},{1,3},{2,0},{3,5},{4,2},{5,7},{6,4},{7,1},{8,14},{9,11},{10,... | collective-permute-start | bytes 786440 | tf_op jit(solution)/shard_map/ppermute | solution.py:23
  25.8 14.5 %collective-permute-start.4 = (bf16[2,128,512]{2,1,0:T(8,128)(2,1)S(1)}, bf16[2,128,512]{2,1,0:T(8,128)(2,1)S(1)}, u32[]{:S(2)}, u32[]{:S(2)}) collective-permute-start(bf16[2,128,512]{2,1,0:T(8,128)(2,1)S(1)} %pad_maximum_fusion.1), channel_id=1, source_target_pairs={{0,2},{1,7},{2,4},{3,1},{4,6},{5,3},{6,0},{7,5},{8,10},{9,15},{10,... | collective-permute-start | bytes 786440 | tf_op jit(solution)/shard_map/ppermute | solution.py:23
  25.8 14.5 %collective-permute-start.6 = (bf16[1,2,128,512]{3,2,1,0:T(8,128)(2,1)S(1)}, bf16[1,2,128,512]{3,2,1,0:T(8,128)(2,1)S(1)}, u32[]{:S(2)}, u32[]{:S(2)}) collective-permute-start(bf16[1,2,128,512]{3,2,1,0:T(8,128)(2,1)S(1)} %bitcast.14), channel_id=1, source_target_pairs={{0,24},{1,9},{2,26},{3,11},{4,28},{5,13},{6,30},{7,15},{8,0},{9,17... | collective-permute-start | bytes 786440 | tf_op jit(solution)/shard_map/ppermute | solution.py:23
  29.6 10.7 %collective-permute-start.8 = (bf16[1,2,128,512]{3,2,1,0:T(8,128)(2,1)S(1)}, bf16[1,2,128,512]{3,2,1,0:T(8,128)(2,1)S(1)}, u32[]{:S(2)}, u32[]{:S(2)}) collective-permute-start(bf16[1,2,128,512]{3,2,1,0:T(8,128)(2,1)S(1)} %collective-permute-done.7.refs_1_), channel_id=1, source_target_pairs={{0,8},{1,25},{2,10},{3,27},{4,12},{5,29},{6,14},{7,31},{8,16},{9,1... | collective-permute-start | bytes 786440 | tf_op jit(solution)/shard_map/ppermute | solution.py:23
  40.3 14.1 %collective-permute-start.9 = (bf16[2,2,128,512]{3,2,1,0:T(8,128)(2,1)S(1)}, bf16[2,2,128,512]{3,2,1,0:T(8,128)(2,1)S(1)}, u32[]{:S(2)}, u32[]{:S(2)}) collective-permute-start(bf16[2,2,128,512]{3,2,1,0:T(8,128)(2,1)S(1)} %pad_maximum_fusion.refs_4_), channel_id=1, source_target_pairs={{0,8},{1,25},{2,10},{3,27},{4,12},{5,29},{6,14},{7,31},{8,16},{9,1... | collective-permute-start | bytes 1572872 | tf_op jit(solution)/shard_map/ppermute | solution.py:23
  40.4 10.8 %collective-permute-start.12 = (bf16[2,128,512]{2,1,0:T(8,128)(2,1)S(1)}, bf16[2,128,512]{2,1,0:T(8,128)(2,1)S(1)}, u32[]{:S(2)}, u32[]{:S(2)}) collective-permute-start(bf16[2,128,512]{2,1,0:T(8,128)(2,1)S(1)} %collective-permute-done.4), channel_id=1, source_target_pairs={{0,2},{1,7},{2,4},{3,1},{4,6},{5,3},{6,0},{7,5},{8,10},{9,15},{10,... | collective-permute-start | bytes 786440 | tf_op jit(solution)/shard_map/ppermute | solution.py:23
  40.9 20.7 %collective-permute-start.11 = (bf16[2,2,128,512]{3,2,1,0:T(8,128)(2,1)S(1)}, bf16[2,2,128,512]{3,2,1,0:T(8,128)(2,1)S(1)}, u32[]{:S(2)}, u32[]{:S(2)}) collective-permute-start(bf16[2,2,128,512]{3,2,1,0:T(8,128)(2,1)S(1)} %pad_maximum_fusion.refs_4_), channel_id=1, source_target_pairs={{0,24},{1,9},{2,26},{3,11},{4,28},{5,13},{6,30},{7,15},{8,0},{9,17... | collective-permute-start | bytes 1572872 | tf_op jit(solution)/shard_map/ppermute | solution.py:23
  51.2 10.5 %collective-permute-start.13 = (bf16[1,2,128,512]{3,2,1,0:T(8,128)(2,1)S(1)}, bf16[1,2,128,512]{3,2,1,0:T(8,128)(2,1)S(1)}, u32[]{:S(2)}, u32[]{:S(2)}) collective-permute-start(bf16[1,2,128,512]{3,2,1,0:T(8,128)(2,1)S(1)} %bitcast.16), channel_id=1, source_target_pairs={{0,8},{1,25},{2,10},{3,27},{4,12},{5,29},{6,14},{7,31},{8,16},{9,1... | collective-permute-start | bytes 786440 | tf_op jit(solution)/shard_map/ppermute | solution.py:23
  52.2 9.4 %collective-permute-start.14 = (bf16[1,2,128,512]{3,2,1,0:T(8,128)(2,1)S(1)}, bf16[1,2,128,512]{3,2,1,0:T(8,128)(2,1)S(1)}, u32[]{:S(2)}, u32[]{:S(2)}) collective-permute-start(bf16[1,2,128,512]{3,2,1,0:T(8,128)(2,1)S(1)} %bitcast.17), channel_id=1, source_target_pairs={{0,24},{1,9},{2,26},{3,11},{4,28},{5,13},{6,30},{7,15},{8,0},{9,17... | collective-permute-start | bytes 786440 | tf_op jit(solution)/shard_map/ppermute | solution.py:23
  54.4 16.0 %collective-permute-start.10 = (bf16[2,2,128,512]{3,2,1,0:T(8,128)(2,1)S(1)}, bf16[2,2,128,512]{3,2,1,0:T(8,128)(2,1)S(1)}, u32[]{:S(2)}, u32[]{:S(2)}) collective-permute-start(bf16[2,2,128,512]{3,2,1,0:T(8,128)(2,1)S(1)} %collective-permute-done.9.refs_5_), channel_id=1, source_target_pairs={{0,8},{1,25},{2,10},{3,27},{4,12},{5,29},{6,14},{7,31},{8,16},{9,1... | collective-permute-start | bytes 1572872 | tf_op jit(solution)/shard_map/ppermute | solution.py:23
  61.7 8.8 %collective-permute-start.15 = (bf16[1,2,128,512]{3,2,1,0:T(8,128)(2,1)S(1)}, bf16[1,2,128,512]{3,2,1,0:T(8,128)(2,1)S(1)}, u32[]{:S(2)}, u32[]{:S(2)}) collective-permute-start(bf16[1,2,128,512]{3,2,1,0:T(8,128)(2,1)S(1)} %collective-permute-done.13.refs_9_), channel_id=1, source_target_pairs={{0,8},{1,25},{2,10},{3,27},{4,12},{5,29},{6,14},{7,31},{8,16},{9,1... | collective-permute-start | bytes 786440 | tf_op jit(solution)/shard_map/ppermute | solution.py:23
  70.4 4.7 %collective-permute-start.16 = (bf16[2048,512]{1,0:T(8,128)(2,1)S(1)}, bf16[2048,512]{1,0:T(8,128)(2,1)S(1)}, u32[]{:S(2)}, u32[]{:S(2)}) collective-permute-start(bf16[2048,512]{1,0:T(8,128)(2,1)S(1)} %collective-permute-done.3.far), channel_id=1, source_target_pairs={{0,1},{1,0},{2,3},{3,2},{4,5},{5,4},{6,7},{7,6},{8,9},{9,8},{10,11... | collective-permute-start | bytes 6291464 | tf_op jit(solution)/shard_map/ppermute | solution.py:23
  75.1 20.9 %copy-start = (s32[2,256,64]{1,2,0:T(8,128)S(1)}, s32[2,256,64]{1,2,0:T(8,128)}, u32[]{:S(2)}) copy-start(s32[2,256,64]{1,2,0:T(8,128)} %param.5) | copy-start | bytes 393220
  75.2 20.9 %copy-start.1 = (f32[256]{0:T(256)S(1)}, f32[256]{0:T(256)}, u32[]{:S(2)}) copy-start(f32[256]{0:T(256)} %param.7) | copy-start | bytes 3076
  75.2 20.9 %copy-start.2 = (f32[512,256]{1,0:T(8,128)S(1)}, f32[512,256]{1,0:T(8,128)}, u32[]{:S(2)}) copy-start(f32[512,256]{1,0:T(8,128)} %get-tuple-element.27.decoded) | copy-start | bytes 1572868
  78.3 11.6 %collective-permute-start.17 = (bf16[128,1024]{1,0:T(8,128)(2,1)S(1)}, bf16[128,1024]{1,0:T(8,128)(2,1)S(1)}, u32[]{:S(2)}, u32[]{:S(2)}) collective-permute-start(bf16[128,1024]{1,0:T(8,128)(2,1)S(1)} %get-tuple-element.46), channel_id=1, source_target_pairs={{0,192},{1,193},{2,194},{3,195},{4,196},{5,197},{6,198},{7,199},{8... | collective-permute-start | bytes 786440 | tf_op jit(solution)/shard_map/ppermute | solution.py:23
  78.9 15.5 %collective-permute-start.18 = (bf16[128,1024]{1,0:T(8,128)(2,1)S(1)}, bf16[128,1024]{1,0:T(8,128)(2,1)S(1)}, u32[]{:S(2)}, u32[]{:S(2)}) collective-permute-start(bf16[128,1024]{1,0:T(8,128)(2,1)S(1)} %get-tuple-element.47), channel_id=1, source_target_pairs={{0,64},{1,65},{2,66},{3,67},{4,68},{5,69},{6,70},{7,71},{8,72},{9,... | collective-permute-start | bytes 786440 | tf_op jit(solution)/shard_map/ppermute | solution.py:23
  81.7 12.6 %collective-permute-start.19 = (bf16[128,1024]{1,0:T(8,128)(2,1)S(1)}, bf16[128,1024]{1,0:T(8,128)(2,1)S(1)}, u32[]{:S(2)}, u32[]{:S(2)}) collective-permute-start(bf16[128,1024]{1,0:T(8,128)(2,1)S(1)} %get-tuple-element.48), channel_id=1, source_target_pairs={{0,128},{1,129},{2,130},{3,131},{4,132},{5,133},{6,134},{7,135},{8... | collective-permute-start | bytes 786440 | tf_op jit(solution)/shard_map/ppermute | solution.py:23
  94.5 1.6 %collective-permute-start.20 = (f32[128,512]{1,0:T(8,128)S(1)}, f32[128,512]{1,0:T(8,128)S(1)}, u32[]{:S(2)}, u32[]{:S(2)}) collective-permute-start(f32[128,512]{1,0:T(8,128)S(1)} %convert_add_fusion), channel_id=1, source_target_pairs={{0,1},{1,0},{2,3},{3,2},{4,5},{5,4},{6,7},{7,6},{8,9},{9,8},{10,11... | collective-permute-start | bytes 786440 | tf_op jit(solution)/shard_map/ppermute | solution.py:23
  101.2 1.2 collective-permute-start.21
  102.4 5.4 %collective-permute-start.24 = (f32[17,256]{1,0:T(8,128)S(1)}, f32[17,256]{1,0:T(8,128)S(1)}, u32[]{:S(2)}, u32[]{:S(2)}) collective-permute-start(f32[17,256]{1,0:T(8,128)S(1)} %add.33), channel_id=1, source_target_pairs={{0,16},{1,17},{2,18},{3,19},{4,20},{5,21},{6,22},{7,23},{8,24},{9,... | collective-permute-start | bytes 52232 | tf_op jit(solution)/shard_map/ppermute | solution.py:23
  103.4 4.5 %collective-permute-start.23 = (f32[17,256]{1,0:T(8,128)S(1)}, f32[17,256]{1,0:T(8,128)S(1)}, u32[]{:S(2)}, u32[]{:S(2)}) collective-permute-start(f32[17,256]{1,0:T(8,128)S(1)} %add.33), channel_id=1, source_target_pairs={{0,24},{1,25},{2,26},{3,27},{4,28},{5,29},{6,30},{7,31},{8,0},{9,1... | collective-permute-start | bytes 52232 | tf_op jit(solution)/shard_map/ppermute | solution.py:23
  104.0 5.0 %collective-permute-start.22 = (f32[17,256]{1,0:T(8,128)S(1)}, f32[17,256]{1,0:T(8,128)S(1)}, u32[]{:S(2)}, u32[]{:S(2)}) collective-permute-start(f32[17,256]{1,0:T(8,128)S(1)} %add.33), channel_id=1, source_target_pairs={{0,8},{1,9},{2,10},{3,11},{4,12},{5,13},{6,14},{7,15},{8,16},{9,17... | collective-permute-start | bytes 52232 | tf_op jit(solution)/shard_map/ppermute | solution.py:23
  109.7 15.5 %all-to-all-start = ((f32[8,17,256]{2,1,0:T(8,128)}), f32[8,17,256]{2,1,0:T(8,128)S(1)}, u32[]{:S(2)}, u32[]{:S(2)}) async-start(f32[8,17,256]{2,1,0:T(8,128)} %broadcast_in_dim.11), calls=%async_computation | async-start | bytes 393216 | tf_op jit(solution)/shard_map/all_to_all | solution.py:326
  125.2 4.8 %collective-permute-start.27 = (f32[16,256]{1,0:T(8,128)S(1)}, f32[16,256]{1,0:T(8,128)S(1)}, u32[]{:S(2)}, u32[]{:S(2)}) collective-permute-start(f32[16,256]{1,0:T(8,128)S(1)} %slice_reduce_fusion), channel_id=1, source_target_pairs={{0,96},{1,97},{2,98},{3,99},{4,100},{5,101},{6,102},{7,103},{8,104... | collective-permute-start | bytes 49160 | tf_op jit(solution)/shard_map/ppermute | solution.py:23
  126.8 5.2 %collective-permute-start.26 = (f32[16,256]{1,0:T(8,128)S(1)}, f32[16,256]{1,0:T(8,128)S(1)}, u32[]{:S(2)}, u32[]{:S(2)}) collective-permute-start(f32[16,256]{1,0:T(8,128)S(1)} %slice_reduce_fusion), channel_id=1, source_target_pairs={{0,64},{1,65},{2,66},{3,67},{4,68},{5,69},{6,70},{7,71},{8,72},{9,... | collective-permute-start | bytes 49160 | tf_op jit(solution)/shard_map/ppermute | solution.py:23
  129.2 3.7 %collective-permute-start.25 = (f32[16,256]{1,0:T(8,128)S(1)}, f32[16,256]{1,0:T(8,128)S(1)}, u32[]{:S(2)}, u32[]{:S(2)}) collective-permute-start(f32[16,256]{1,0:T(8,128)S(1)} %slice_reduce_fusion), channel_id=1, source_target_pairs={{0,32},{1,33},{2,34},{3,35},{4,36},{5,37},{6,38},{7,39},{8,40},{9,... | collective-permute-start | bytes 49160 | tf_op jit(solution)/shard_map/ppermute | solution.py:23

commit v11 on v10

--- a/solution.py
+++ b/solution.py
@@ -193,7 +193,7 @@
     z_lo, y_hi, y_lo, x, z_hi, core = (lax.axis_index(a) for a in AXES)
     step = 1 - 2 * core
     copies = []
-    for at, (dx, dzs) in enumerate((dx, dzs) for dzs in ((0,), (1, 3), (2,)) for dx in (0, 1, 3, 2)):
+    for at, (dx, dzs) in enumerate((dx, dzs) for dzs in ((0,), (1,), (3,), (2,)) for dx in (0, 1, 3, 2)):
         for place, dz in enumerate(dzs):
             from_x = (x + 8 - step * dx) % 4
             from_z = (z_hi + 8 - step * dz) % 4
@@ -253,22 +253,26 @@
     far = shift(tile, "y_lo", 1)
 
     own = block[None]
-    z_back, z_on = turn(block, "z_hi", 1), turn(block, "z_hi", -1)
+    back, on = turn(own, "z_hi", 1), turn(own, "z_hi", -1)
+    last = turn(back, "z_hi", 1)
     own_back, own_on = turn(own, "x", 1), turn(own, "x", -1)
     own_two = turn(own_back, "x", 1)
-    near, own_on, own_two = lax.optimization_barrier(
-        (jnp.stack([z_back, z_on]), own_on, own_two)
-    )
-    near_back, near_on = turn(near, "x", 1), turn(near, "x", -1)
-    last = turn(z_back, "z_hi", 1)[None]
+    back, own_back, own_on = lax.optimization_barrier((back, own_back, own_on))
+    back_back, back_on = turn(back, "x", 1), turn(back, "x", -1)
+    on, own_two = lax.optimization_barrier((on, own_two))
+    on_back, on_on = turn(on, "x", 1), turn(on, "x", -1)
+    back_back, back_on = lax.optimization_barrier((back_back, back_on))
+    back_two = turn(back_back, "x", 1)
     last_back, last_on = turn(last, "x", 1), turn(last, "x", -1)
-    near_on, last_back, last_on, own_two = lax.optimization_barrier((near_on, last_back, last_on, own_two))
-    near_two, last_two = turn(near_back, "x", 1), turn(last_back, "x", 1)
-    far, near_two, last_two = lax.optimization_barrier((far, near_two, last_two))
+    on_back, on_on, last_on, last_back, back_two = lax.optimization_barrier((on_back, on_on, last_on, last_back, back_two))
+    on_two = turn(on_back, "x", 1)
+    last_two = turn(last_back, "x", 1)
+    far, *_ = lax.optimization_barrier((far, back_two, on_two, last_two))
     far_across = shift(far, "core", 1)
     wide = (
         (own, own_back, own_on, own_two),
-        (near, near_back, near_on, near_two),
+        (back, back_back, back_on, back_two),
+        (on, on_back, on_on, on_two),
         (last, last_back, last_on, last_two),
     )
 

time: 134 us -> 138 us (1.030)
  starting transfers between devices: 52.1 us -> 68.6 us
  waiting for transfers between devices: 62.2 us -> 49.6 us
    ppermute x28 -> x31, starting transfers between devices: 46.4 us -> 62.1 us  [send(): return lax.ppermute(a, AXES, pairs)]
    ppermute x28 -> x31, waiting for transfers between devices: 52.4 us -> 39.8 us  [send(): return lax.ppermute(a, AXES, pairs)]
  transfers between devices with their start and end apart: 29 -> 32, of which waited for: 14 -> 17; matrix products, arithmetic and copies ran while one was open for 1% -> 0% of each run, Pallas kernels for 6% -> 6%
where the time goes in v11:
time: 138 us; the launch traced here: 137 us
  starting transfers between devices  68.6 us (50%)
  waiting for transfers between devices  49.6 us (36%)
  Pallas kernels  16.3 us (12%)
    ppermute x31, starting transfers between devices, send(): return lax.ppermute(a, AXES, pairs)  62.1 us
    ppermute x31, waiting for transfers between devices, send(): return lax.ppermute(a, AXES, pairs)  39.8 us
    all_to_all x1, waiting for transfers between devices, body(): copies = lax.all_to_all(copies, ('z_hi', 'z_lo'), 0, 0, tiled=True)  9.78 us
    all_to_all x1, starting transfers between devices, body(): copies = lax.all_to_all(copies, ('z_hi', 'z_lo'), 0, 0, tiled=True)  6.4 us
    pallas_call x1, Pallas kernels, finish(): pl.pallas_call(finish_kernel, out_shape=(jax.ShapeDtypeStruct((rows, widt...  5.12 us
    pallas_call x1, Pallas kernels, body(): pl.pallas_call(first_kernel, out_shape=(jax.ShapeDtypeStruct((4, half, wi...  4.64 us
    pallas_call x1, Pallas kernels, decode(): pl.pallas_call(decode_kernel, out_shape=(jax.ShapeDtypeStruct((width, row...  3.35 us
    pallas_call x1, Pallas kernels, body(): pl.pallas_call(second_kernel, out_shape=(jax.ShapeDtypeStruct(sent.shape,...  3.16 us
  transfers between devices with their start and end apart: 32, of which 17 were waited for; matrix products, arithmetic and copies ran while one was open for 0% of the time, Pallas kernels for 6%

profile of v11, /device:TPU:8, one launch (start us, length us, event | category | flops | bytes accessed | tf_op | source)
XLA Modules:
  0.0 137.2 jit_solution(13683500406415743450)
XLA Ops:
  0.7 3.3 %decode.1 = (f32[512,256]{1,0:T(8,128)}, bf16[128,512]{1,0:T(8,128)(2,1)}, bf16[128,512]{1,0:T(8,128)(2,1)}) custom-call(s32[2,64,256]{2,1,0:T(8,128)} %bitcast.15, bf16[2,8,256]{2,1,0:T(8,128)(2,1)} %bitcast.21, f32[1,256]{1,0:T(1,128)} %bitcast.17, bf16[256,512]{1,0:T(8,128)(2,1)} %initial_in.1), custom_call_target="tpu_custom_call" | custom-call | flops 2097152 | bytes 1048576 | tf_op jit(solution)/shard_map/decode/pallas_call | solution.py:81
  4.7 1.6 %collective-permute-start = (bf16[128,512]{1,0:T(8,128)(2,1)}, bf16[128,512]{1,0:T(8,128)(2,1)S(1)}, u32[]{:S(2)}, u32[]{:S(2)}) collective-permute-start(bf16[128,512]{1,0:T(8,128)(2,1)} %get-tuple-element.31), channel_id=1, source_target_pairs={{0,0},{1,1},{2,2},{3,3},{4,4},{5,5},{6,6},{7,7},{8,72},{9,73},{10,... | collective-permute-start | bytes 393224 | tf_op jit(solution)/shard_map/ppermute | solution.py:23
  6.3 2.3 %collective-permute-start.3 = (bf16[2048,512]{1,0:T(8,128)(2,1)}, bf16[2048,512]{1,0:T(8,128)(2,1)S(1)}, u32[]{:S(2)}, u32[]{:S(2)}) collective-permute-start(bf16[2048,512]{1,0:T(8,128)(2,1)} %own.1), channel_id=1, source_target_pairs={{0,32},{1,33},{2,34},{3,35},{4,36},{5,37},{6,38},{7,39},{8,40},{9,... | collective-permute-start | bytes 6291464 | tf_op jit(solution)/shard_map/ppermute | solution.py:23
  8.5 10.9 %collective-permute-start.5 = (bf16[1,2,128,512]{3,2,1,0:T(8,128)(2,1)S(1)}, bf16[1,2,128,512]{3,2,1,0:T(8,128)(2,1)S(1)}, u32[]{:S(2)}, u32[]{:S(2)}) collective-permute-start(bf16[1,2,128,512]{3,2,1,0:T(8,128)(2,1)S(1)} %bitcast.10), channel_id=1, source_target_pairs={{0,8},{1,25},{2,10},{3,27},{4,12},{5,29},{6,14},{7,31},{8,16},{9,1... | collective-permute-start | bytes 786440 | tf_op jit(solution)/shard_map/ppermute | solution.py:23
  19.4 3.3 %collective-permute-start.9 = (bf16[1,2,128,512]{3,2,1,0:T(8,128)(2,1)S(1)}, bf16[1,2,128,512]{3,2,1,0:T(8,128)(2,1)S(1)}, u32[]{:S(2)}, u32[]{:S(2)}) collective-permute-start(bf16[1,2,128,512]{3,2,1,0:T(8,128)(2,1)S(1)} %bitcast.11), channel_id=1, source_target_pairs={{0,2},{1,7},{2,4},{3,1},{4,6},{5,3},{6,0},{7,5},{8,10},{9,15},{10,... | collective-permute-start | bytes 786440 | tf_op jit(solution)/shard_map/ppermute | solution.py:23
  22.7 4.7 %collective-permute-start.13 = (bf16[1,2,128,512]{3,2,1,0:T(8,128)(2,1)S(1)}, bf16[1,2,128,512]{3,2,1,0:T(8,128)(2,1)S(1)}, u32[]{:S(2)}, u32[]{:S(2)}) collective-permute-start(bf16[1,2,128,512]{3,2,1,0:T(8,128)(2,1)S(1)} %bitcast.12), channel_id=1, source_target_pairs={{0,24},{1,9},{2,26},{3,11},{4,28},{5,13},{6,30},{7,15},{8,0},{9,17... | collective-permute-start | bytes 786440 | tf_op jit(solution)/shard_map/ppermute | solution.py:23
  27.4 2.1 %collective-permute-start.4 = (bf16[1,2,128,512]{3,2,1,0:T(8,128)(2,1)S(1)}, bf16[1,2,128,512]{3,2,1,0:T(8,128)(2,1)S(1)}, u32[]{:S(2)}, u32[]{:S(2)}) collective-permute-start(bf16[1,2,128,512]{3,2,1,0:T(8,128)(2,1)S(1)} %bitcast.13), channel_id=1, source_target_pairs={{0,6},{1,3},{2,0},{3,5},{4,2},{5,7},{6,4},{7,1},{8,14},{9,11},{10,... | collective-permute-start | bytes 786440 | tf_op jit(solution)/shard_map/ppermute | solution.py:23
  31.6 4.2 %collective-permute-start.14 = (bf16[1,2,128,512]{3,2,1,0:T(8,128)(2,1)S(1)}, bf16[1,2,128,512]{3,2,1,0:T(8,128)(2,1)S(1)}, u32[]{:S(2)}, u32[]{:S(2)}) collective-permute-start(bf16[1,2,128,512]{3,2,1,0:T(8,128)(2,1)S(1)} %collective-permute-done.9.refs_4_), channel_id=1, source_target_pairs={{0,8},{1,25},{2,10},{3,27},{4,12},{5,29},{6,14},{7,31},{8,16},{9,1... | collective-permute-start | bytes 786440 | tf_op jit(solution)/shard_map/ppermute | solution.py:23
  35.8 3.6 %collective-permute-start.15 = (bf16[1,2,128,512]{3,2,1,0:T(8,128)(2,1)S(1)}, bf16[1,2,128,512]{3,2,1,0:T(8,128)(2,1)S(1)}, u32[]{:S(2)}, u32[]{:S(2)}) collective-permute-start(bf16[1,2,128,512]{3,2,1,0:T(8,128)(2,1)S(1)} %collective-permute-done.9.refs_4_), channel_id=1, source_target_pairs={{0,24},{1,9},{2,26},{3,11},{4,28},{5,13},{6,30},{7,15},{8,0},{9,17... | collective-permute-start | bytes 786440 | tf_op jit(solution)/shard_map/ppermute | solution.py:23
  39.4 2.5 %collective-permute-start.10 = (bf16[1,2,128,512]{3,2,1,0:T(8,128)(2,1)S(1)}, bf16[1,2,128,512]{3,2,1,0:T(8,128)(2,1)S(1)}, u32[]{:S(2)}, u32[]{:S(2)}) collective-permute-start(bf16[1,2,128,512]{3,2,1,0:T(8,128)(2,1)S(1)} %collective-permute-done.9.refs_4_), channel_id=1, source_target_pairs={{0,2},{1,7},{2,4},{3,1},{4,6},{5,3},{6,0},{7,5},{8,10},{9,15},{10,... | collective-permute-start | bytes 786440 | tf_op jit(solution)/shard_map/ppermute | solution.py:23
  41.8 2.5 %collective-permute-start.7 = (bf16[1,2,128,512]{3,2,1,0:T(8,128)(2,1)S(1)}, bf16[1,2,128,512]{3,2,1,0:T(8,128)(2,1)S(1)}, u32[]{:S(2)}, u32[]{:S(2)}) collective-permute-start(bf16[1,2,128,512]{3,2,1,0:T(8,128)(2,1)S(1)} %collective-permute-done.4.refs_8_), channel_id=1, source_target_pairs={{0,8},{1,25},{2,10},{3,27},{4,12},{5,29},{6,14},{7,31},{8,16},{9,1... | collective-permute-start | bytes 786440 | tf_op jit(solution)/shard_map/ppermute | solution.py:23
  44.4 4.5 %collective-permute-start.8 = (bf16[1,2,128,512]{3,2,1,0:T(8,128)(2,1)S(1)}, bf16[1,2,128,512]{3,2,1,0:T(8,128)(2,1)S(1)}, u32[]{:S(2)}, u32[]{:S(2)}) collective-permute-start(bf16[1,2,128,512]{3,2,1,0:T(8,128)(2,1)S(1)} %collective-permute-done.4.refs_8_), channel_id=1, source_target_pairs={{0,24},{1,9},{2,26},{3,11},{4,28},{5,13},{6,30},{7,15},{8,0},{9,17... | collective-permute-start | bytes 786440 | tf_op jit(solution)/shard_map/ppermute | solution.py:23
  49.5 4.2 %collective-permute-start.11 = (bf16[1,2,128,512]{3,2,1,0:T(8,128)(2,1)S(1)}, bf16[1,2,128,512]{3,2,1,0:T(8,128)(2,1)S(1)}, u32[]{:S(2)}, u32[]{:S(2)}) collective-permute-start(bf16[1,2,128,512]{3,2,1,0:T(8,128)(2,1)S(1)} %collective-permute-done.10.refs_12_), channel_id=1, source_target_pairs={{0,24},{1,9},{2,26},{3,11},{4,28},{5,13},{6,30},{7,15},{8,0},{9,17... | collective-permute-start | bytes 786440 | tf_op jit(solution)/shard_map/ppermute | solution.py:23
  53.7 1.5 %collective-permute-start.16 = (bf16[1,2,128,512]{3,2,1,0:T(8,128)(2,1)S(1)}, bf16[1,2,128,512]{3,2,1,0:T(8,128)(2,1)S(1)}, u32[]{:S(2)}, u32[]{:S(2)}) collective-permute-start(bf16[1,2,128,512]{3,2,1,0:T(8,128)(2,1)S(1)} %collective-permute-done.14.refs_5_), channel_id=1, source_target_pairs={{0,8},{1,25},{2,10},{3,27},{4,12},{5,29},{6,14},{7,31},{8,16},{9,1... | collective-permute-start | bytes 786440 | tf_op jit(solution)/shard_map/ppermute | solution.py:23
  56.7 5.6 %collective-permute-done.11.refs_14_ = bf16[1,2,128,512]{3,2,1,0:T(8,128)(2,1)S(1)} collective-permute-done((bf16[1,2,128,512]{3,2,1,0:T(8,128)(2,1)S(1)}, bf16[1,2,128,512]{3,2,1,0:T(8,128)(2,1)S(1)}, u32[]{:S(2)}, u32[]{:S(2)}) %collective-permute-start.11) | collective-permute-done | bytes 262176 | tf_op jit(solution)/shard_map/ppermute | solution.py:23
  62.3 1.8 %collective-permute-done.16.refs_7_ = bf16[1,2,128,512]{3,2,1,0:T(8,128)(2,1)S(1)} collective-permute-done((bf16[1,2,128,512]{3,2,1,0:T(8,128)(2,1)S(1)}, bf16[1,2,128,512]{3,2,1,0:T(8,128)(2,1)S(1)}, u32[]{:S(2)}, u32[]{:S(2)}) %collective-permute-start.16) | collective-permute-done | bytes 262176 | tf_op jit(solution)/shard_map/ppermute | solution.py:23
  64.1 1.6 %collective-permute-start.18 = (bf16[1,2,128,512]{3,2,1,0:T(8,128)(2,1)S(1)}, bf16[1,2,128,512]{3,2,1,0:T(8,128)(2,1)S(1)}, u32[]{:S(2)}, u32[]{:S(2)}) collective-permute-start(bf16[1,2,128,512]{3,2,1,0:T(8,128)(2,1)S(1)} %collective-permute-done.12.refs_13_), channel_id=1, source_target_pairs={{0,8},{1,25},{2,10},{3,27},{4,12},{5,29},{6,14},{7,31},{8,16},{9,1... | collective-permute-start | bytes 786440 | tf_op jit(solution)/shard_map/ppermute | solution.py:23
  65.7 6.0 %collective-permute-done.17.refs_11_ = bf16[1,2,128,512]{3,2,1,0:T(8,128)(2,1)S(1)} collective-permute-done((bf16[1,2,128,512]{3,2,1,0:T(8,128)(2,1)S(1)}, bf16[1,2,128,512]{3,2,1,0:T(8,128)(2,1)S(1)}, u32[]{:S(2)}, u32[]{:S(2)}) %collective-permute-start.17) | collective-permute-done | bytes 262176 | tf_op jit(solution)/shard_map/ppermute | solution.py:23
  71.7 2.8 %collective-permute-done.18.refs_15_ = bf16[1,2,128,512]{3,2,1,0:T(8,128)(2,1)S(1)} collective-permute-done((bf16[1,2,128,512]{3,2,1,0:T(8,128)(2,1)S(1)}, bf16[1,2,128,512]{3,2,1,0:T(8,128)(2,1)S(1)}, u32[]{:S(2)}, u32[]{:S(2)}) %collective-permute-start.18) | collective-permute-done | bytes 262176 | tf_op jit(solution)/shard_map/ppermute | solution.py:23
  74.5 4.6 %first.1 = (f32[4,128,512]{2,1,0:T(8,128)S(1)}, bf16[512,4096]{1,0:T(8,128)(2,1)S(1)}) custom-call(bf16[2048,512]{1,0:T(8,128)(2,1)} %own.1, bf16[2048,512]{1,0:T(8,128)(2,1)S(1)} %collective-permute-done.3.far, bf16[1,2,128,512]{3,2,1,0:T(8,128)(2,1)S(1)} %bitcast.14, bf16[1,2,128,512]{3,2,1,0:T(8,128)(2,1)S(1)} %collective-permute-done.5.refs_1_, ...), custom_call_target="tpu_custom_call" | custom-call | flops 2147483648 | bytes 8388608 | tf_op jit(solution)/shard_map/first/pallas_call | solution.py:287
  79.2 3.2 %second.1 = (f32[128,1024]{1,0:T(8,128)S(1)}, bf16[128,1024]{1,0:T(8,128)(2,1)S(1)}, bf16[128,1024]{1,0:T(8,128)(2,1)S(1)}, bf16[128,1024]{1,0:T(8,128)(2,1)S(1)}) custom-call(f32[4,128,512]{2,1,0:T(8,128)S(1)} %get-tuple-element.48.kept, bf16[512,4096]{1,0:T(8,128)(2,1)S(1)} %get-tuple-element.49.held, bf16[2048,512]{1,0:T(8,128)(2,1)S(1)} %collective-permute-done.2.across, ...), custom_call_target="tpu_custom_call" | custom-call | flops 2147483648 | bytes 8388608 | tf_op jit(solution)/shard_map/second/pallas_call | solution.py:303
  82.5 2.3 %collective-permute-start.21 = (bf16[128,1024]{1,0:T(8,128)(2,1)S(1)}, bf16[128,1024]{1,0:T(8,128)(2,1)S(1)}, u32[]{:S(2)}, u32[]{:S(2)}) collective-permute-start(bf16[128,1024]{1,0:T(8,128)(2,1)S(1)} %get-tuple-element.53), channel_id=1, source_target_pairs={{0,64},{1,65},{2,66},{3,67},{4,68},{5,69},{6,70},{7,71},{8,72},{9,... | collective-permute-start | bytes 786440 | tf_op jit(solution)/shard_map/ppermute | solution.py:23
  84.8 2.7 %collective-permute-start.22 = (bf16[128,1024]{1,0:T(8,128)(2,1)S(1)}, bf16[128,1024]{1,0:T(8,128)(2,1)S(1)}, u32[]{:S(2)}, u32[]{:S(2)}) collective-permute-start(bf16[128,1024]{1,0:T(8,128)(2,1)S(1)} %get-tuple-element.54), channel_id=1, source_target_pairs={{0,128},{1,129},{2,130},{3,131},{4,132},{5,133},{6,134},{7,135},{8... | collective-permute-start | bytes 786440 | tf_op jit(solution)/shard_map/ppermute | solution.py:23
  87.4 6.6 %collective-permute-done.20.to_both = bf16[128,1024]{1,0:T(8,128)(2,1)S(1)} collective-permute-done((bf16[128,1024]{1,0:T(8,128)(2,1)S(1)}, bf16[128,1024]{1,0:T(8,128)(2,1)S(1)}, u32[]{:S(2)}, u32[]{:S(2)}) %collective-permute-start.20) | collective-permute-done | bytes 262176 | tf_op jit(solution)/shard_map/ppermute | solution.py:23
  94.0 4.4 %collective-permute-done.21.to_y = bf16[128,1024]{1,0:T(8,128)(2,1)S(1)} collective-permute-done((bf16[128,1024]{1,0:T(8,128)(2,1)S(1)}, bf16[128,1024]{1,0:T(8,128)(2,1)S(1)}, u32[]{:S(2)}, u32[]{:S(2)}) %collective-permute-start.21) | collective-permute-done | bytes 262176 | tf_op jit(solution)/shard_map/ppermute | solution.py:23
  98.6 1.5 %collective-permute-done.23.got = f32[128,512]{1,0:T(8,128)S(1)} collective-permute-done((f32[128,512]{1,0:T(8,128)S(1)}, f32[128,512]{1,0:T(8,128)S(1)}, u32[]{:S(2)}, u32[]{:S(2)}) %collective-permute-start.23) | collective-permute-done | bytes 262176 | tf_op jit(solution)/shard_map/ppermute | solution.py:23
  100.1 5.1 %finish.1 = (f32[256,512]{1,0:T(8,128)}, f32[17,256]{1,0:T(8,128)S(1)}) custom-call(s32[2,64,256]{2,1,0:T(8,128)S(1)} %bitcast.16, f32[1,256]{1,0:T(1,128)S(1)} %bitcast.18, f32[512,256]{1,0:T(8,128)S(1)} %copy-done.2, f32[128,1024]{1,0:T(8,128)S(1)} %get-tuple-element.51.own, bf16[128,1024]{1,0:T(8,128)(2,1)S(1)} %collective-permute-done.20.to_both, ...), custom_call_target="tpu_custom_call" | custom-call | flops 4294967296 | bytes 2097152 | tf_op jit(solution)/shard_map/finish/pallas_call | solution.py:151
  108.9 2.9 %collective-permute-done.27 = f32[17,256]{1,0:T(8,128)S(1)} collective-permute-done((f32[17,256]{1,0:T(8,128)S(1)}, f32[17,256]{1,0:T(8,128)S(1)}, u32[]{:S(2)}, u32[]{:S(2)}) %collective-permute-start.27) | collective-permute-done | bytes 17440 | tf_op jit(solution)/shard_map/ppermute | solution.py:23
  113.6 6.4 %all-to-all-start = ((f32[8,17,256]{2,1,0:T(8,128)}), f32[8,17,256]{2,1,0:T(8,128)S(1)}, u32[]{:S(2)}, u32[]{:S(2)}) async-start(f32[8,17,256]{2,1,0:T(8,128)} %broadcast_in_dim.7), calls=%async_computation | async-start | bytes 393216 | tf_op jit(solution)/shard_map/all_to_all | solution.py:330
  120.0 9.8 %all-to-all-done = f32[8,17,256]{2,1,0:T(8,128)S(1)} async-done(((f32[8,17,256]{2,1,0:T(8,128)}), f32[8,17,256]{2,1,0:T(8,128)S(1)}, u32[]{:S(2)}, u32[]{:S(2)}) %all-to-all-start) | async-done | bytes 139296 | tf_op jit(solution)/shard_map/all_to_all | solution.py:330
  131.3 1.6 %collective-permute-start.29 = (f32[16,256]{1,0:T(8,128)S(1)}, f32[16,256]{1,0:T(8,128)S(1)}, u32[]{:S(2)}, u32[]{:S(2)}) collective-permute-start(f32[16,256]{1,0:T(8,128)S(1)} %slice_reduce_fusion), channel_id=1, source_target_pairs={{0,64},{1,65},{2,66},{3,67},{4,68},{5,69},{6,70},{7,71},{8,72},{9,... | collective-permute-start | bytes 49160 | tf_op jit(solution)/shard_map/ppermute | solution.py:23
  134.6 1.8 %collective-permute-done.29 = f32[16,256]{1,0:T(8,128)S(1)} collective-permute-done((f32[16,256]{1,0:T(8,128)S(1)}, f32[16,256]{1,0:T(8,128)S(1)}, u32[]{:S(2)}, u32[]{:S(2)}) %collective-permute-start.29) | collective-permute-done | bytes 16416 | tf_op jit(solution)/shard_map/ppermute | solution.py:23
  (53 shorter events, 14.4 us)
Async XLA Ops:
  0.6 5.6 %collective-permute-start.2 = (bf16[2048,512]{1,0:T(8,128)(2,1)}, bf16[2048,512]{1,0:T(8,128)(2,1)S(1)}, u32[]{:S(2)}, u32[]{:S(2)}) collective-permute-start(bf16[2048,512]{1,0:T(8,128)(2,1)} %own.1), channel_id=1, source_target_pairs={{0,1},{1,0},{2,3},{3,2},{4,5},{5,4},{6,7},{7,6},{8,9},{9,8},{10,11... | collective-permute-start | bytes 6291464 | tf_op jit(solution)/shard_map/ppermute | solution.py:23
  4.1 2.1 %collective-permute-start.1 = (bf16[128,512]{1,0:T(8,128)(2,1)}, bf16[128,512]{1,0:T(8,128)(2,1)S(1)}, u32[]{:S(2)}, u32[]{:S(2)}) collective-permute-start(bf16[128,512]{1,0:T(8,128)(2,1)} %get-tuple-element.32), channel_id=1, source_target_pairs={{0,1},{1,0},{2,3},{3,2},{4,5},{5,4},{6,7},{7,6},{8,73},{9,72},{10,... | collective-permute-start | bytes 393224 | tf_op jit(solution)/shard_map/ppermute | solution.py:23
  4.7 1.6 %collective-permute-start = (bf16[128,512]{1,0:T(8,128)(2,1)}, bf16[128,512]{1,0:T(8,128)(2,1)S(1)}, u32[]{:S(2)}, u32[]{:S(2)}) collective-permute-start(bf16[128,512]{1,0:T(8,128)(2,1)} %get-tuple-element.31), channel_id=1, source_target_pairs={{0,0},{1,1},{2,2},{3,3},{4,4},{5,5},{6,6},{7,7},{8,72},{9,73},{10,... | collective-permute-start | bytes 393224 | tf_op jit(solution)/shard_map/ppermute | solution.py:23
  6.3 68.2 %collective-permute-start.3 = (bf16[2048,512]{1,0:T(8,128)(2,1)}, bf16[2048,512]{1,0:T(8,128)(2,1)S(1)}, u32[]{:S(2)}, u32[]{:S(2)}) collective-permute-start(bf16[2048,512]{1,0:T(8,128)(2,1)} %own.1), channel_id=1, source_target_pairs={{0,32},{1,33},{2,34},{3,35},{4,36},{5,37},{6,38},{7,39},{8,40},{9,... | collective-permute-start | bytes 6291464 | tf_op jit(solution)/shard_map/ppermute | solution.py:23
  8.5 21.1 %collective-permute-start.5 = (bf16[1,2,128,512]{3,2,1,0:T(8,128)(2,1)S(1)}, bf16[1,2,128,512]{3,2,1,0:T(8,128)(2,1)S(1)}, u32[]{:S(2)}, u32[]{:S(2)}) collective-permute-start(bf16[1,2,128,512]{3,2,1,0:T(8,128)(2,1)S(1)} %bitcast.10), channel_id=1, source_target_pairs={{0,8},{1,25},{2,10},{3,27},{4,12},{5,29},{6,14},{7,31},{8,16},{9,1... | collective-permute-start | bytes 786440 | tf_op jit(solution)/shard_map/ppermute | solution.py:23
  19.4 10.7 %collective-permute-start.9 = (bf16[1,2,128,512]{3,2,1,0:T(8,128)(2,1)S(1)}, bf16[1,2,128,512]{3,2,1,0:T(8,128)(2,1)S(1)}, u32[]{:S(2)}, u32[]{:S(2)}) collective-permute-start(bf16[1,2,128,512]{3,2,1,0:T(8,128)(2,1)S(1)} %bitcast.11), channel_id=1, source_target_pairs={{0,2},{1,7},{2,4},{3,1},{4,6},{5,3},{6,0},{7,5},{8,10},{9,15},{10,... | collective-permute-start | bytes 786440 | tf_op jit(solution)/shard_map/ppermute | solution.py:23
  22.7 8.9 %collective-permute-start.13 = (bf16[1,2,128,512]{3,2,1,0:T(8,128)(2,1)S(1)}, bf16[1,2,128,512]{3,2,1,0:T(8,128)(2,1)S(1)}, u32[]{:S(2)}, u32[]{:S(2)}) collective-permute-start(bf16[1,2,128,512]{3,2,1,0:T(8,128)(2,1)S(1)} %bitcast.12), channel_id=1, source_target_pairs={{0,24},{1,9},{2,26},{3,11},{4,28},{5,13},{6,30},{7,15},{8,0},{9,17... | collective-permute-start | bytes 786440 | tf_op jit(solution)/shard_map/ppermute | solution.py:23
  27.4 11.9 %collective-permute-start.4 = (bf16[1,2,128,512]{3,2,1,0:T(8,128)(2,1)S(1)}, bf16[1,2,128,512]{3,2,1,0:T(8,128)(2,1)S(1)}, u32[]{:S(2)}, u32[]{:S(2)}) collective-permute-start(bf16[1,2,128,512]{3,2,1,0:T(8,128)(2,1)S(1)} %bitcast.13), channel_id=1, source_target_pairs={{0,6},{1,3},{2,0},{3,5},{4,2},{5,7},{6,4},{7,1},{8,14},{9,11},{10,... | collective-permute-start | bytes 786440 | tf_op jit(solution)/shard_map/ppermute | solution.py:23
  29.6 12.3 %collective-permute-start.6 = (bf16[1,2,128,512]{3,2,1,0:T(8,128)(2,1)S(1)}, bf16[1,2,128,512]{3,2,1,0:T(8,128)(2,1)S(1)}, u32[]{:S(2)}, u32[]{:S(2)}) collective-permute-start(bf16[1,2,128,512]{3,2,1,0:T(8,128)(2,1)S(1)} %collective-permute-done.5.refs_1_), channel_id=1, source_target_pairs={{0,8},{1,25},{2,10},{3,27},{4,12},{5,29},{6,14},{7,31},{8,16},{9,1... | collective-permute-start | bytes 786440 | tf_op jit(solution)/shard_map/ppermute | solution.py:23
  31.6 12.7 %collective-permute-start.14 = (bf16[1,2,128,512]{3,2,1,0:T(8,128)(2,1)S(1)}, bf16[1,2,128,512]{3,2,1,0:T(8,128)(2,1)S(1)}, u32[]{:S(2)}, u32[]{:S(2)}) collective-permute-start(bf16[1,2,128,512]{3,2,1,0:T(8,128)(2,1)S(1)} %collective-permute-done.9.refs_4_), channel_id=1, source_target_pairs={{0,8},{1,25},{2,10},{3,27},{4,12},{5,29},{6,14},{7,31},{8,16},{9,1... | collective-permute-start | bytes 786440 | tf_op jit(solution)/shard_map/ppermute | solution.py:23
  35.8 13.6 %collective-permute-start.15 = (bf16[1,2,128,512]{3,2,1,0:T(8,128)(2,1)S(1)}, bf16[1,2,128,512]{3,2,1,0:T(8,128)(2,1)S(1)}, u32[]{:S(2)}, u32[]{:S(2)}) collective-permute-start(bf16[1,2,128,512]{3,2,1,0:T(8,128)(2,1)S(1)} %collective-permute-done.9.refs_4_), channel_id=1, source_target_pairs={{0,24},{1,9},{2,26},{3,11},{4,28},{5,13},{6,30},{7,15},{8,0},{9,17... | collective-permute-start | bytes 786440 | tf_op jit(solution)/shard_map/ppermute | solution.py:23
  39.4 10.1 %collective-permute-start.10 = (bf16[1,2,128,512]{3,2,1,0:T(8,128)(2,1)S(1)}, bf16[1,2,128,512]{3,2,1,0:T(8,128)(2,1)S(1)}, u32[]{:S(2)}, u32[]{:S(2)}) collective-permute-start(bf16[1,2,128,512]{3,2,1,0:T(8,128)(2,1)S(1)} %collective-permute-done.9.refs_4_), channel_id=1, source_target_pairs={{0,2},{1,7},{2,4},{3,1},{4,6},{5,3},{6,0},{7,5},{8,10},{9,15},{10,... | collective-permute-start | bytes 786440 | tf_op jit(solution)/shard_map/ppermute | solution.py:23
  41.8 11.9 %collective-permute-start.7 = (bf16[1,2,128,512]{3,2,1,0:T(8,128)(2,1)S(1)}, bf16[1,2,128,512]{3,2,1,0:T(8,128)(2,1)S(1)}, u32[]{:S(2)}, u32[]{:S(2)}) collective-permute-start(bf16[1,2,128,512]{3,2,1,0:T(8,128)(2,1)S(1)} %collective-permute-done.4.refs_8_), channel_id=1, source_target_pairs={{0,8},{1,25},{2,10},{3,27},{4,12},{5,29},{6,14},{7,31},{8,16},{9,1... | collective-permute-start | bytes 786440 | tf_op jit(solution)/shard_map/ppermute | solution.py:23
  44.4 12.3 %collective-permute-start.8 = (bf16[1,2,128,512]{3,2,1,0:T(8,128)(2,1)S(1)}, bf16[1,2,128,512]{3,2,1,0:T(8,128)(2,1)S(1)}, u32[]{:S(2)}, u32[]{:S(2)}) collective-permute-start(bf16[1,2,128,512]{3,2,1,0:T(8,128)(2,1)S(1)} %collective-permute-done.4.refs_8_), channel_id=1, source_target_pairs={{0,24},{1,9},{2,26},{3,11},{4,28},{5,13},{6,30},{7,15},{8,0},{9,17... | collective-permute-start | bytes 786440 | tf_op jit(solution)/shard_map/ppermute | solution.py:23
  49.5 12.8 %collective-permute-start.11 = (bf16[1,2,128,512]{3,2,1,0:T(8,128)(2,1)S(1)}, bf16[1,2,128,512]{3,2,1,0:T(8,128)(2,1)S(1)}, u32[]{:S(2)}, u32[]{:S(2)}) collective-permute-start(bf16[1,2,128,512]{3,2,1,0:T(8,128)(2,1)S(1)} %collective-permute-done.10.refs_12_), channel_id=1, source_target_pairs={{0,24},{1,9},{2,26},{3,11},{4,28},{5,13},{6,30},{7,15},{8,0},{9,17... | collective-permute-start | bytes 786440 | tf_op jit(solution)/shard_map/ppermute | solution.py:23
  53.7 8.6 %collective-permute-start.12 = (bf16[1,2,128,512]{3,2,1,0:T(8,128)(2,1)S(1)}, bf16[1,2,128,512]{3,2,1,0:T(8,128)(2,1)S(1)}, u32[]{:S(2)}, u32[]{:S(2)}) collective-permute-start(bf16[1,2,128,512]{3,2,1,0:T(8,128)(2,1)S(1)} %collective-permute-done.10.refs_12_), channel_id=1, source_target_pairs={{0,8},{1,25},{2,10},{3,27},{4,12},{5,29},{6,14},{7,31},{8,16},{9,1... | collective-permute-start | bytes 786440 | tf_op jit(solution)/shard_map/ppermute | solution.py:23
  53.7 10.4 %collective-permute-start.16 = (bf16[1,2,128,512]{3,2,1,0:T(8,128)(2,1)S(1)}, bf16[1,2,128,512]{3,2,1,0:T(8,128)(2,1)S(1)}, u32[]{:S(2)}, u32[]{:S(2)}) collective-permute-start(bf16[1,2,128,512]{3,2,1,0:T(8,128)(2,1)S(1)} %collective-permute-done.14.refs_5_), channel_id=1, source_target_pairs={{0,8},{1,25},{2,10},{3,27},{4,12},{5,29},{6,14},{7,31},{8,16},{9,1... | collective-permute-start | bytes 786440 | tf_op jit(solution)/shard_map/ppermute | solution.py:23
  64.1 7.6 %collective-permute-start.17 = (bf16[1,2,128,512]{3,2,1,0:T(8,128)(2,1)S(1)}, bf16[1,2,128,512]{3,2,1,0:T(8,128)(2,1)S(1)}, u32[]{:S(2)}, u32[]{:S(2)}) collective-permute-start(bf16[1,2,128,512]{3,2,1,0:T(8,128)(2,1)S(1)} %collective-permute-done.7.refs_9_), channel_id=1, source_target_pairs={{0,8},{1,25},{2,10},{3,27},{4,12},{5,29},{6,14},{7,31},{8,16},{9,1... | collective-permute-start | bytes 786440 | tf_op jit(solution)/shard_map/ppermute | solution.py:23
  64.1 10.4 %collective-permute-start.18 = (bf16[1,2,128,512]{3,2,1,0:T(8,128)(2,1)S(1)}, bf16[1,2,128,512]{3,2,1,0:T(8,128)(2,1)S(1)}, u32[]{:S(2)}, u32[]{:S(2)}) collective-permute-start(bf16[1,2,128,512]{3,2,1,0:T(8,128)(2,1)S(1)} %collective-permute-done.12.refs_13_), channel_id=1, source_target_pairs={{0,8},{1,25},{2,10},{3,27},{4,12},{5,29},{6,14},{7,31},{8,16},{9,1... | collective-permute-start | bytes 786440 | tf_op jit(solution)/shard_map/ppermute | solution.py:23
  74.5 4.7 %collective-permute-start.19 = (bf16[2048,512]{1,0:T(8,128)(2,1)S(1)}, bf16[2048,512]{1,0:T(8,128)(2,1)S(1)}, u32[]{:S(2)}, u32[]{:S(2)}) collective-permute-start(bf16[2048,512]{1,0:T(8,128)(2,1)S(1)} %collective-permute-done.3.far), channel_id=1, source_target_pairs={{0,1},{1,0},{2,3},{3,2},{4,5},{5,4},{6,7},{7,6},{8,9},{9,8},{10,11... | collective-permute-start | bytes 6291464 | tf_op jit(solution)/shard_map/ppermute | solution.py:23
  82.4 11.6 %collective-permute-start.20 = (bf16[128,1024]{1,0:T(8,128)(2,1)S(1)}, bf16[128,1024]{1,0:T(8,128)(2,1)S(1)}, u32[]{:S(2)}, u32[]{:S(2)}) collective-permute-start(bf16[128,1024]{1,0:T(8,128)(2,1)S(1)} %get-tuple-element.52), channel_id=1, source_target_pairs={{0,192},{1,193},{2,194},{3,195},{4,196},{5,197},{6,198},{7,199},{8... | collective-permute-start | bytes 786440 | tf_op jit(solution)/shard_map/ppermute | solution.py:23
  82.5 15.9 %collective-permute-start.21 = (bf16[128,1024]{1,0:T(8,128)(2,1)S(1)}, bf16[128,1024]{1,0:T(8,128)(2,1)S(1)}, u32[]{:S(2)}, u32[]{:S(2)}) collective-permute-start(bf16[128,1024]{1,0:T(8,128)(2,1)S(1)} %get-tuple-element.53), channel_id=1, source_target_pairs={{0,64},{1,65},{2,66},{3,67},{4,68},{5,69},{6,70},{7,71},{8,72},{9,... | collective-permute-start | bytes 786440 | tf_op jit(solution)/shard_map/ppermute | solution.py:23
  84.8 13.6 %collective-permute-start.22 = (bf16[128,1024]{1,0:T(8,128)(2,1)S(1)}, bf16[128,1024]{1,0:T(8,128)(2,1)S(1)}, u32[]{:S(2)}, u32[]{:S(2)}) collective-permute-start(bf16[128,1024]{1,0:T(8,128)(2,1)S(1)} %get-tuple-element.54), channel_id=1, source_target_pairs={{0,128},{1,129},{2,130},{3,131},{4,132},{5,133},{6,134},{7,135},{8... | collective-permute-start | bytes 786440 | tf_op jit(solution)/shard_map/ppermute | solution.py:23
  98.5 1.6 %collective-permute-start.23 = (f32[128,512]{1,0:T(8,128)S(1)}, f32[128,512]{1,0:T(8,128)S(1)}, u32[]{:S(2)}, u32[]{:S(2)}) collective-permute-start(f32[128,512]{1,0:T(8,128)S(1)} %convert_add_fusion), channel_id=1, source_target_pairs={{0,1},{1,0},{2,3},{3,2},{4,5},{5,4},{6,7},{7,6},{8,9},{9,8},{10,11... | collective-permute-start | bytes 786440 | tf_op jit(solution)/shard_map/ppermute | solution.py:23
  105.2 1.2 collective-permute-start.24
  106.4 5.4 %collective-permute-start.27 = (f32[17,256]{1,0:T(8,128)S(1)}, f32[17,256]{1,0:T(8,128)S(1)}, u32[]{:S(2)}, u32[]{:S(2)}) collective-permute-start(f32[17,256]{1,0:T(8,128)S(1)} %add.33), channel_id=1, source_target_pairs={{0,16},{1,17},{2,18},{3,19},{4,20},{5,21},{6,22},{7,23},{8,24},{9,... | collective-permute-start | bytes 52232 | tf_op jit(solution)/shard_map/ppermute | solution.py:23
  106.8 5.0 %collective-permute-start.26 = (f32[17,256]{1,0:T(8,128)S(1)}, f32[17,256]{1,0:T(8,128)S(1)}, u32[]{:S(2)}, u32[]{:S(2)}) collective-permute-start(f32[17,256]{1,0:T(8,128)S(1)} %add.33), channel_id=1, source_target_pairs={{0,24},{1,25},{2,26},{3,27},{4,28},{5,29},{6,30},{7,31},{8,0},{9,1... | collective-permute-start | bytes 52232 | tf_op jit(solution)/shard_map/ppermute | solution.py:23
  107.9 5.0 %collective-permute-start.25 = (f32[17,256]{1,0:T(8,128)S(1)}, f32[17,256]{1,0:T(8,128)S(1)}, u32[]{:S(2)}, u32[]{:S(2)}) collective-permute-start(f32[17,256]{1,0:T(8,128)S(1)} %add.33), channel_id=1, source_target_pairs={{0,8},{1,9},{2,10},{3,11},{4,12},{5,13},{6,14},{7,15},{8,16},{9,17... | collective-permute-start | bytes 52232 | tf_op jit(solution)/shard_map/ppermute | solution.py:23
  113.6 16.2 %all-to-all-start = ((f32[8,17,256]{2,1,0:T(8,128)}), f32[8,17,256]{2,1,0:T(8,128)S(1)}, u32[]{:S(2)}, u32[]{:S(2)}) async-start(f32[8,17,256]{2,1,0:T(8,128)} %broadcast_in_dim.7), calls=%async_computation | async-start | bytes 393216 | tf_op jit(solution)/shard_map/all_to_all | solution.py:330
  129.8 4.8 %collective-permute-start.30 = (f32[16,256]{1,0:T(8,128)S(1)}, f32[16,256]{1,0:T(8,128)S(1)}, u32[]{:S(2)}, u32[]{:S(2)}) collective-permute-start(f32[16,256]{1,0:T(8,128)S(1)} %slice_reduce_fusion), channel_id=1, source_target_pairs={{0,96},{1,97},{2,98},{3,99},{4,100},{5,101},{6,102},{7,103},{8,104... | collective-permute-start | bytes 49160 | tf_op jit(solution)/shard_map/ppermute | solution.py:23
  131.3 5.2 %collective-permute-start.29 = (f32[16,256]{1,0:T(8,128)S(1)}, f32[16,256]{1,0:T(8,128)S(1)}, u32[]{:S(2)}, u32[]{:S(2)}) collective-permute-start(f32[16,256]{1,0:T(8,128)S(1)} %slice_reduce_fusion), channel_id=1, source_target_pairs={{0,64},{1,65},{2,66},{3,67},{4,68},{5,69},{6,70},{7,71},{8,72},{9,... | collective-permute-start | bytes 49160 | tf_op jit(solution)/shard_map/ppermute | solution.py:23
  132.9 3.7 %collective-permute-start.28 = (f32[16,256]{1,0:T(8,128)S(1)}, f32[16,256]{1,0:T(8,128)S(1)}, u32[]{:S(2)}, u32[]{:S(2)}) collective-permute-start(f32[16,256]{1,0:T(8,128)S(1)} %slice_reduce_fusion), channel_id=1, source_target_pairs={{0,32},{1,33},{2,34},{3,35},{4,36},{5,37},{6,38},{7,39},{8,40},{9,... | collective-permute-start | bytes 49160 | tf_op jit(solution)/shard_map/ppermute | solution.py:23
  (3 other events, 62.7 us)

commit v12 on v10

--- a/solution.py
+++ b/solution.py
@@ -236,6 +236,20 @@
         out[:, width:] = given[s].astype(out.dtype)
 
 
+def gather_sum(total, axes, kept):
+    sizes = [lax.axis_size(a) for a in axes]
+    copies = jnp.broadcast_to(total, (int(np.prod(sizes)), *total.shape))
+    copies = lax.all_to_all(copies, axes, 0, 0, tiled=True)
+    own = 0
+    for a in kept:
+        own = own * lax.axis_size(a) + lax.axis_index(a)
+    behind = int(np.prod(sizes[len(kept) :]))
+    source = lax.broadcasted_iota(jnp.int32, copies.shape, 0) // behind
+    row = lax.broadcasted_iota(jnp.int32, copies.shape, 1)
+    counts = (row < total.shape[0] - 1) | (source == own)
+    return jnp.sum(jnp.where(counts, copies, 0.0), axis=0)
+
+
 def body(codes, codebooks, row_scale, initial, hessian):
     rows, width = initial.shape
     words = codebooks.shape[1]
@@ -321,15 +335,9 @@
     product, total = finish(codes, row_scale, decoded, parts, got)
 
     total = total + shift(total, "core", 1)
-    total = total + shift(total, "x", 1) + shift(total, "x", -1) + shift(total, "x", 2)
-    copies = jnp.broadcast_to(total, (8, *total.shape))
-    copies = lax.all_to_all(copies, ("z_hi", "z_lo"), 0, 0, tiled=True)
-    scales = copies[:, 16].reshape(4, 2, rows)
-    scale_total = jnp.sum(jnp.where(lax.axis_index("z_lo") == 0, scales[:, 0], scales[:, 1]), axis=0)
-    books = jnp.sum(copies[:, :16], axis=0)
-    beside, across_y = shift(books, "y_lo", 1), shift(books, "y_hi", 1)
-    both = send(books, lambda zl, yh, yl, x, zh, c: (zl, 1 - yh, 1 - yl, x, zh, c))
-    books = books + beside + across_y + both
+    total = gather_sum(total, ("y_hi", "y_lo", "x"), ("y_hi", "y_lo"))
+    total = gather_sum(total, ("z_lo", "z_hi"), ("z_lo",))
+    scale_total, books = total[16], total[:16]
     full_width = width * 32
     all_groups = rows * 8 * (full_width // 8)
     scale_grad = scale_total / full_width

time: 134 us -> 136 us (1.015); the launches traced: 134 us -> 133 us
  starting transfers between devices: 52.1 us -> 50.4 us
    ppermute x28 -> x22, starting transfers between devices: 46.4 us -> 39.3 us  [send(): return lax.ppermute(a, AXES, pairs)]
    all_to_all x1 -> x2, waiting for transfers between devices: 9.78 us -> 16.4 us  [gather_sum(): copies = lax.all_to_all(copies, axes, 0, 0, tiled=True)]
    ppermute x28 -> x22, waiting for transfers between devices: 52.4 us -> 45.9 us  [send(): return lax.ppermute(a, AXES, pairs)]
    all_to_all x1 -> x2, starting transfers between devices: 5.68 us -> 11.1 us  [gather_sum(): copies = lax.all_to_all(copies, axes, 0, 0, tiled=True)]
  transfers between devices with their start and end apart: 29 -> 24, of which waited for: 14 -> 11; matrix products, arithmetic and copies ran while one was open for 1% -> 0% of each run, Pallas kernels for 6% -> 6%
where the time goes in v12:
time: 136 us; the launch traced here: 133 us
  waiting for transfers between devices  62.3 us (46%)
  starting transfers between devices  50.4 us (37%)
  Pallas kernels  16.3 us (12%)
  other arithmetic  1.58 us (1%)
  local copies, waits for them, and re-layouts  1.5 us (1%)
    ppermute x22, waiting for transfers between devices, send(): return lax.ppermute(a, AXES, pairs)  45.9 us
    ppermute x22, starting transfers between devices, send(): return lax.ppermute(a, AXES, pairs)  39.3 us
    all_to_all x2, waiting for transfers between devices, gather_sum(): copies = lax.all_to_all(copies, axes, 0, 0, tiled=True)  16.4 us
    all_to_all x2, starting transfers between devices, gather_sum(): copies = lax.all_to_all(copies, axes, 0, 0, tiled=True)  11.1 us
    pallas_call x1, Pallas kernels, finish(): pl.pallas_call(finish_kernel, out_shape=(jax.ShapeDtypeStruct((rows, widt...  5.12 us
    pallas_call x1, Pallas kernels, body(): pl.pallas_call(first_kernel, out_shape=(jax.ShapeDtypeStruct((4, half, wi...  4.68 us
    pallas_call x1, Pallas kernels, decode(): pl.pallas_call(decode_kernel, out_shape=(jax.ShapeDtypeStruct((width, row...  3.36 us
    pallas_call x1, Pallas kernels, body(): pl.pallas_call(second_kernel, out_shape=(jax.ShapeDtypeStruct(sent.shape,...  3.15 us
  transfers between devices with their start and end apart: 24, of which 11 were waited for; matrix products, arithmetic and copies ran while one was open for 0% of the time, Pallas kernels for 6%

profile of v12, /device:TPU:8, one launch (start us, length us, event | category | flops | bytes accessed | tf_op | source)
XLA Modules:
  0.0 133.0 jit_solution(15379815399122893424)
XLA Ops:
  0.7 3.4 %decode.1 = (f32[512,256]{1,0:T(8,128)}, bf16[128,512]{1,0:T(8,128)(2,1)}, bf16[128,512]{1,0:T(8,128)(2,1)}) custom-call(s32[2,64,256]{2,1,0:T(8,128)} %bitcast.20, bf16[2,8,256]{2,1,0:T(8,128)(2,1)} %bitcast.28, f32[1,256]{1,0:T(1,128)} %bitcast.22, bf16[256,512]{1,0:T(8,128)(2,1)} %initial_in.1), custom_call_target="tpu_custom_call" | custom-call | flops 2097152 | bytes 1048576 | tf_op jit(solution)/shard_map/decode/pallas_call | solution.py:81
  4.7 1.6 %collective-permute-start = (bf16[128,512]{1,0:T(8,128)(2,1)}, bf16[128,512]{1,0:T(8,128)(2,1)S(1)}, u32[]{:S(2)}, u32[]{:S(2)}) collective-permute-start(bf16[128,512]{1,0:T(8,128)(2,1)} %get-tuple-element.28), channel_id=1, source_target_pairs={{0,0},{1,1},{2,2},{3,3},{4,4},{5,5},{6,6},{7,7},{8,72},{9,73},{10,... | collective-permute-start | bytes 393224 | tf_op jit(solution)/shard_map/ppermute | solution.py:23
  6.3 2.3 %collective-permute-start.3 = (bf16[2048,512]{1,0:T(8,128)(2,1)}, bf16[2048,512]{1,0:T(8,128)(2,1)S(1)}, u32[]{:S(2)}, u32[]{:S(2)}) collective-permute-start(bf16[2048,512]{1,0:T(8,128)(2,1)} %own.1), channel_id=1, source_target_pairs={{0,32},{1,33},{2,34},{3,35},{4,36},{5,37},{6,38},{7,39},{8,40},{9,... | collective-permute-start | bytes 6291464 | tf_op jit(solution)/shard_map/ppermute | solution.py:23
  8.5 10.9 %collective-permute-start.7 = (bf16[1,2,128,512]{3,2,1,0:T(8,128)(2,1)S(1)}, bf16[1,2,128,512]{3,2,1,0:T(8,128)(2,1)S(1)}, u32[]{:S(2)}, u32[]{:S(2)}) collective-permute-start(bf16[1,2,128,512]{3,2,1,0:T(8,128)(2,1)S(1)} %bitcast.14), channel_id=1, source_target_pairs={{0,8},{1,25},{2,10},{3,27},{4,12},{5,29},{6,14},{7,31},{8,16},{9,1... | collective-permute-start | bytes 786440 | tf_op jit(solution)/shard_map/ppermute | solution.py:23
  19.4 6.3 %collective-permute-start.5 = (bf16[2,128,512]{2,1,0:T(8,128)(2,1)S(1)}, bf16[2,128,512]{2,1,0:T(8,128)(2,1)S(1)}, u32[]{:S(2)}, u32[]{:S(2)}) collective-permute-start(bf16[2,128,512]{2,1,0:T(8,128)(2,1)S(1)} %pad_maximum_fusion.1), channel_id=1, source_target_pairs={{0,6},{1,3},{2,0},{3,5},{4,2},{5,7},{6,4},{7,1},{8,14},{9,11},{10,... | collective-permute-start | bytes 786440 | tf_op jit(solution)/shard_map/ppermute | solution.py:23
  25.8 3.8 %collective-permute-start.6 = (bf16[1,2,128,512]{3,2,1,0:T(8,128)(2,1)S(1)}, bf16[1,2,128,512]{3,2,1,0:T(8,128)(2,1)S(1)}, u32[]{:S(2)}, u32[]{:S(2)}) collective-permute-start(bf16[1,2,128,512]{3,2,1,0:T(8,128)(2,1)S(1)} %bitcast.15), channel_id=1, source_target_pairs={{0,24},{1,9},{2,26},{3,11},{4,28},{5,13},{6,30},{7,15},{8,0},{9,17... | collective-permute-start | bytes 786440 | tf_op jit(solution)/shard_map/ppermute | solution.py:23
  29.6 7.1 %collective-permute-done.5 = bf16[2,128,512]{2,1,0:T(8,128)(2,1)S(1)} collective-permute-done((bf16[2,128,512]{2,1,0:T(8,128)(2,1)S(1)}, bf16[2,128,512]{2,1,0:T(8,128)(2,1)S(1)}, u32[]{:S(2)}, u32[]{:S(2)}) %collective-permute-start.5) | collective-permute-done | bytes 262176 | tf_op jit(solution)/shard_map/ppermute | solution.py:23
  36.6 3.6 %collective-permute-done.4 = bf16[2,128,512]{2,1,0:T(8,128)(2,1)S(1)} collective-permute-done((bf16[2,128,512]{2,1,0:T(8,128)(2,1)S(1)}, bf16[2,128,512]{2,1,0:T(8,128)(2,1)S(1)}, u32[]{:S(2)}, u32[]{:S(2)}) %collective-permute-start.4) | collective-permute-done | bytes 262176 | tf_op jit(solution)/shard_map/ppermute | solution.py:23
  40.9 3.2 %collective-permute-start.11 = (bf16[2,2,128,512]{3,2,1,0:T(8,128)(2,1)S(1)}, bf16[2,2,128,512]{3,2,1,0:T(8,128)(2,1)S(1)}, u32[]{:S(2)}, u32[]{:S(2)}) collective-permute-start(bf16[2,2,128,512]{3,2,1,0:T(8,128)(2,1)S(1)} %pad_maximum_fusion.refs_4_), channel_id=1, source_target_pairs={{0,24},{1,9},{2,26},{3,11},{4,28},{5,13},{6,30},{7,15},{8,0},{9,17... | collective-permute-start | bytes 1572872 | tf_op jit(solution)/shard_map/ppermute | solution.py:23
  44.1 7.0 %collective-permute-done.12 = bf16[2,128,512]{2,1,0:T(8,128)(2,1)S(1)} collective-permute-done((bf16[2,128,512]{2,1,0:T(8,128)(2,1)S(1)}, bf16[2,128,512]{2,1,0:T(8,128)(2,1)S(1)}, u32[]{:S(2)}, u32[]{:S(2)}) %collective-permute-start.12) | collective-permute-done | bytes 262176 | tf_op jit(solution)/shard_map/ppermute | solution.py:23
  51.2 1.0 collective-permute-start.13
  52.2 2.2 %collective-permute-start.14 = (bf16[1,2,128,512]{3,2,1,0:T(8,128)(2,1)S(1)}, bf16[1,2,128,512]{3,2,1,0:T(8,128)(2,1)S(1)}, u32[]{:S(2)}, u32[]{:S(2)}) collective-permute-start(bf16[1,2,128,512]{3,2,1,0:T(8,128)(2,1)S(1)} %bitcast.18), channel_id=1, source_target_pairs={{0,24},{1,9},{2,26},{3,11},{4,28},{5,13},{6,30},{7,15},{8,0},{9,17... | collective-permute-start | bytes 786440 | tf_op jit(solution)/shard_map/ppermute | solution.py:23
  54.4 7.2 %collective-permute-done.13.refs_9_ = bf16[1,2,128,512]{3,2,1,0:T(8,128)(2,1)S(1)} collective-permute-done((bf16[1,2,128,512]{3,2,1,0:T(8,128)(2,1)S(1)}, bf16[1,2,128,512]{3,2,1,0:T(8,128)(2,1)S(1)}, u32[]{:S(2)}, u32[]{:S(2)}) %collective-permute-start.13) | collective-permute-done | bytes 262176 | tf_op jit(solution)/shard_map/ppermute | solution.py:23
  61.7 1.3 %collective-permute-start.15 = (bf16[1,2,128,512]{3,2,1,0:T(8,128)(2,1)S(1)}, bf16[1,2,128,512]{3,2,1,0:T(8,128)(2,1)S(1)}, u32[]{:S(2)}, u32[]{:S(2)}) collective-permute-start(bf16[1,2,128,512]{3,2,1,0:T(8,128)(2,1)S(1)} %collective-permute-done.13.refs_9_), channel_id=1, source_target_pairs={{0,8},{1,25},{2,10},{3,27},{4,12},{5,29},{6,14},{7,31},{8,16},{9,1... | collective-permute-start | bytes 786440 | tf_op jit(solution)/shard_map/ppermute | solution.py:23
  63.0 7.4 %collective-permute-done.15.refs_11_ = bf16[1,2,128,512]{3,2,1,0:T(8,128)(2,1)S(1)} collective-permute-done((bf16[1,2,128,512]{3,2,1,0:T(8,128)(2,1)S(1)}, bf16[1,2,128,512]{3,2,1,0:T(8,128)(2,1)S(1)}, u32[]{:S(2)}, u32[]{:S(2)}) %collective-permute-start.15) | collective-permute-done | bytes 262176 | tf_op jit(solution)/shard_map/ppermute | solution.py:23
  70.4 4.7 %first.1 = (f32[4,128,512]{2,1,0:T(8,128)S(1)}, bf16[512,4096]{1,0:T(8,128)(2,1)S(1)}) custom-call(bf16[2048,512]{1,0:T(8,128)(2,1)} %own.1, bf16[2048,512]{1,0:T(8,128)(2,1)S(1)} %collective-permute-done.3.far, bf16[1,2,128,512]{3,2,1,0:T(8,128)(2,1)S(1)} %bitcast.16, bf16[1,2,128,512]{3,2,1,0:T(8,128)(2,1)S(1)} %collective-permute-done.7.refs_1_, ...), custom_call_target="tpu_custom_call" | custom-call | flops 2147483648 | bytes 8388608 | tf_op jit(solution)/shard_map/first/pallas_call | solution.py:297
  75.2 3.2 %second.1 = (f32[128,1024]{1,0:T(8,128)S(1)}, bf16[128,1024]{1,0:T(8,128)(2,1)S(1)}, bf16[128,1024]{1,0:T(8,128)(2,1)S(1)}, bf16[128,1024]{1,0:T(8,128)(2,1)S(1)}) custom-call(f32[4,128,512]{2,1,0:T(8,128)S(1)} %get-tuple-element.42.kept, bf16[512,4096]{1,0:T(8,128)(2,1)S(1)} %get-tuple-element.43.held, bf16[2048,512]{1,0:T(8,128)(2,1)S(1)} %collective-permute-done.2.across, ...), custom_call_target="tpu_custom_call" | custom-call | flops 2147483648 | bytes 8388608 | tf_op jit(solution)/shard_map/second/pallas_call | solution.py:313
  78.9 2.9 %collective-permute-start.18 = (bf16[128,1024]{1,0:T(8,128)(2,1)S(1)}, bf16[128,1024]{1,0:T(8,128)(2,1)S(1)}, u32[]{:S(2)}, u32[]{:S(2)}) collective-permute-start(bf16[128,1024]{1,0:T(8,128)(2,1)S(1)} %get-tuple-element.47), channel_id=1, source_target_pairs={{0,64},{1,65},{2,66},{3,67},{4,68},{5,69},{6,70},{7,71},{8,72},{9,... | collective-permute-start | bytes 786440 | tf_op jit(solution)/shard_map/ppermute | solution.py:23
  81.7 1.7 %collective-permute-start.19 = (bf16[128,1024]{1,0:T(8,128)(2,1)S(1)}, bf16[128,1024]{1,0:T(8,128)(2,1)S(1)}, u32[]{:S(2)}, u32[]{:S(2)}) collective-permute-start(bf16[128,1024]{1,0:T(8,128)(2,1)S(1)} %get-tuple-element.48), channel_id=1, source_target_pairs={{0,128},{1,129},{2,130},{3,131},{4,132},{5,133},{6,134},{7,135},{8... | collective-permute-start | bytes 786440 | tf_op jit(solution)/shard_map/ppermute | solution.py:23
  83.4 6.6 %collective-permute-done.17.to_both = bf16[128,1024]{1,0:T(8,128)(2,1)S(1)} collective-permute-done((bf16[128,1024]{1,0:T(8,128)(2,1)S(1)}, bf16[128,1024]{1,0:T(8,128)(2,1)S(1)}, u32[]{:S(2)}, u32[]{:S(2)}) %collective-permute-start.17) | collective-permute-done | bytes 262176 | tf_op jit(solution)/shard_map/ppermute | solution.py:23
  90.0 4.4 %collective-permute-done.18.to_y = bf16[128,1024]{1,0:T(8,128)(2,1)S(1)} collective-permute-done((bf16[128,1024]{1,0:T(8,128)(2,1)S(1)}, bf16[128,1024]{1,0:T(8,128)(2,1)S(1)}, u32[]{:S(2)}, u32[]{:S(2)}) %collective-permute-start.18) | collective-permute-done | bytes 262176 | tf_op jit(solution)/shard_map/ppermute | solution.py:23
  94.6 1.5 %collective-permute-done.20.got = f32[128,512]{1,0:T(8,128)S(1)} collective-permute-done((f32[128,512]{1,0:T(8,128)S(1)}, f32[128,512]{1,0:T(8,128)S(1)}, u32[]{:S(2)}, u32[]{:S(2)}) %collective-permute-start.20) | collective-permute-done | bytes 262176 | tf_op jit(solution)/shard_map/ppermute | solution.py:23
  96.1 5.1 %finish.1 = (f32[256,512]{1,0:T(8,128)}, f32[17,256]{1,0:T(8,128)S(1)}) custom-call(s32[2,64,256]{2,1,0:T(8,128)S(1)} %bitcast.21, f32[1,256]{1,0:T(1,128)S(1)} %bitcast.23, f32[512,256]{1,0:T(8,128)S(1)} %copy-done.2, f32[128,1024]{1,0:T(8,128)S(1)} %get-tuple-element.45.own, bf16[128,1024]{1,0:T(8,128)(2,1)S(1)} %collective-permute-done.17.to_both, ...), custom_call_target="tpu_custom_call" | custom-call | flops 4294967296 | bytes 2097152 | tf_op jit(solution)/shard_map/finish/pallas_call | solution.py:151
  101.4 1.1 collective-permute-done.21
  102.4 0.8 broadcast_in_dim.22
  103.2 4.8 %all-to-all-start = ((f32[16,17,256]{2,1,0:T(8,128)}), f32[16,17,256]{2,1,0:T(8,128)S(1)}, u32[]{:S(2)}, u32[]{:S(2)}) async-start(f32[16,17,256]{2,1,0:T(8,128)} %broadcast_in_dim.22), calls=%async_computation | async-start | bytes 786432 | tf_op jit(solution)/shard_map/all_to_all | solution.py:242
  108.0 8.3 %all-to-all-done = f32[16,17,256]{2,1,0:T(8,128)S(1)} async-done(((f32[16,17,256]{2,1,0:T(8,128)}), f32[16,17,256]{2,1,0:T(8,128)S(1)}, u32[]{:S(2)}, u32[]{:S(2)}) %all-to-all-start) | async-done | bytes 278560 | tf_op jit(solution)/shard_map/all_to_all | solution.py:242
  116.5 0.7 broadcast_in_dim.24
  117.1 6.4 %all-to-all-start.1 = ((f32[8,17,256]{2,1,0:T(8,128)}), f32[8,17,256]{2,1,0:T(8,128)S(1)}, u32[]{:S(2)}, u32[]{:S(2)}) async-start(f32[8,17,256]{2,1,0:T(8,128)} %broadcast_in_dim.24), calls=%async_computation.1 | async-start | bytes 393216 | tf_op jit(solution)/shard_map/all_to_all | solution.py:242
  123.5 8.1 %all-to-all-done.1 = f32[8,17,256]{2,1,0:T(8,128)S(1)} async-done(((f32[8,17,256]{2,1,0:T(8,128)}), f32[8,17,256]{2,1,0:T(8,128)S(1)}, u32[]{:S(2)}, u32[]{:S(2)}) %all-to-all-start.1) | async-done | bytes 139296 | tf_op jit(solution)/shard_map/all_to_all | solution.py:242
  131.8 0.6 slice_multiply_fusion.1
  132.3 0.6 fusion.2
  (41 shorter events, 2.5 us)
Async XLA Ops:
  0.6 5.6 %collective-permute-start.2 = (bf16[2048,512]{1,0:T(8,128)(2,1)}, bf16[2048,512]{1,0:T(8,128)(2,1)S(1)}, u32[]{:S(2)}, u32[]{:S(2)}) collective-permute-start(bf16[2048,512]{1,0:T(8,128)(2,1)} %own.1), channel_id=1, source_target_pairs={{0,1},{1,0},{2,3},{3,2},{4,5},{5,4},{6,7},{7,6},{8,9},{9,8},{10,11... | collective-permute-start | bytes 6291464 | tf_op jit(solution)/shard_map/ppermute | solution.py:23
  4.1 2.1 %collective-permute-start.1 = (bf16[128,512]{1,0:T(8,128)(2,1)}, bf16[128,512]{1,0:T(8,128)(2,1)S(1)}, u32[]{:S(2)}, u32[]{:S(2)}) collective-permute-start(bf16[128,512]{1,0:T(8,128)(2,1)} %get-tuple-element.29), channel_id=1, source_target_pairs={{0,1},{1,0},{2,3},{3,2},{4,5},{5,4},{6,7},{7,6},{8,73},{9,72},{10,... | collective-permute-start | bytes 393224 | tf_op jit(solution)/shard_map/ppermute | solution.py:23
  4.7 1.6 %collective-permute-start = (bf16[128,512]{1,0:T(8,128)(2,1)}, bf16[128,512]{1,0:T(8,128)(2,1)S(1)}, u32[]{:S(2)}, u32[]{:S(2)}) collective-permute-start(bf16[128,512]{1,0:T(8,128)(2,1)} %get-tuple-element.28), channel_id=1, source_target_pairs={{0,0},{1,1},{2,2},{3,3},{4,4},{5,5},{6,6},{7,7},{8,72},{9,73},{10,... | collective-permute-start | bytes 393224 | tf_op jit(solution)/shard_map/ppermute | solution.py:23
  6.3 64.2 %collective-permute-start.3 = (bf16[2048,512]{1,0:T(8,128)(2,1)}, bf16[2048,512]{1,0:T(8,128)(2,1)S(1)}, u32[]{:S(2)}, u32[]{:S(2)}) collective-permute-start(bf16[2048,512]{1,0:T(8,128)(2,1)} %own.1), channel_id=1, source_target_pairs={{0,32},{1,33},{2,34},{3,35},{4,36},{5,37},{6,38},{7,39},{8,40},{9,... | collective-permute-start | bytes 6291464 | tf_op jit(solution)/shard_map/ppermute | solution.py:23
  8.5 21.1 %collective-permute-start.7 = (bf16[1,2,128,512]{3,2,1,0:T(8,128)(2,1)S(1)}, bf16[1,2,128,512]{3,2,1,0:T(8,128)(2,1)S(1)}, u32[]{:S(2)}, u32[]{:S(2)}) collective-permute-start(bf16[1,2,128,512]{3,2,1,0:T(8,128)(2,1)S(1)} %bitcast.14), channel_id=1, source_target_pairs={{0,8},{1,25},{2,10},{3,27},{4,12},{5,29},{6,14},{7,31},{8,16},{9,1... | collective-permute-start | bytes 786440 | tf_op jit(solution)/shard_map/ppermute | solution.py:23
  19.4 17.2 %collective-permute-start.5 = (bf16[2,128,512]{2,1,0:T(8,128)(2,1)S(1)}, bf16[2,128,512]{2,1,0:T(8,128)(2,1)S(1)}, u32[]{:S(2)}, u32[]{:S(2)}) collective-permute-start(bf16[2,128,512]{2,1,0:T(8,128)(2,1)S(1)} %pad_maximum_fusion.1), channel_id=1, source_target_pairs={{0,6},{1,3},{2,0},{3,5},{4,2},{5,7},{6,4},{7,1},{8,14},{9,11},{10,... | collective-permute-start | bytes 786440 | tf_op jit(solution)/shard_map/ppermute | solution.py:23
  25.8 14.5 %collective-permute-start.4 = (bf16[2,128,512]{2,1,0:T(8,128)(2,1)S(1)}, bf16[2,128,512]{2,1,0:T(8,128)(2,1)S(1)}, u32[]{:S(2)}, u32[]{:S(2)}) collective-permute-start(bf16[2,128,512]{2,1,0:T(8,128)(2,1)S(1)} %pad_maximum_fusion.1), channel_id=1, source_target_pairs={{0,2},{1,7},{2,4},{3,1},{4,6},{5,3},{6,0},{7,5},{8,10},{9,15},{10,... | collective-permute-start | bytes 786440 | tf_op jit(solution)/shard_map/ppermute | solution.py:23
  25.8 14.5 %collective-permute-start.6 = (bf16[1,2,128,512]{3,2,1,0:T(8,128)(2,1)S(1)}, bf16[1,2,128,512]{3,2,1,0:T(8,128)(2,1)S(1)}, u32[]{:S(2)}, u32[]{:S(2)}) collective-permute-start(bf16[1,2,128,512]{3,2,1,0:T(8,128)(2,1)S(1)} %bitcast.15), channel_id=1, source_target_pairs={{0,24},{1,9},{2,26},{3,11},{4,28},{5,13},{6,30},{7,15},{8,0},{9,17... | collective-permute-start | bytes 786440 | tf_op jit(solution)/shard_map/ppermute | solution.py:23
  29.6 10.7 %collective-permute-start.8 = (bf16[1,2,128,512]{3,2,1,0:T(8,128)(2,1)S(1)}, bf16[1,2,128,512]{3,2,1,0:T(8,128)(2,1)S(1)}, u32[]{:S(2)}, u32[]{:S(2)}) collective-permute-start(bf16[1,2,128,512]{3,2,1,0:T(8,128)(2,1)S(1)} %collective-permute-done.7.refs_1_), channel_id=1, source_target_pairs={{0,8},{1,25},{2,10},{3,27},{4,12},{5,29},{6,14},{7,31},{8,16},{9,1... | collective-permute-start | bytes 786440 | tf_op jit(solution)/shard_map/ppermute | solution.py:23
  40.3 14.1 %collective-permute-start.9 = (bf16[2,2,128,512]{3,2,1,0:T(8,128)(2,1)S(1)}, bf16[2,2,128,512]{3,2,1,0:T(8,128)(2,1)S(1)}, u32[]{:S(2)}, u32[]{:S(2)}) collective-permute-start(bf16[2,2,128,512]{3,2,1,0:T(8,128)(2,1)S(1)} %pad_maximum_fusion.refs_4_), channel_id=1, source_target_pairs={{0,8},{1,25},{2,10},{3,27},{4,12},{5,29},{6,14},{7,31},{8,16},{9,1... | collective-permute-start | bytes 1572872 | tf_op jit(solution)/shard_map/ppermute | solution.py:23
  40.4 10.8 %collective-permute-start.12 = (bf16[2,128,512]{2,1,0:T(8,128)(2,1)S(1)}, bf16[2,128,512]{2,1,0:T(8,128)(2,1)S(1)}, u32[]{:S(2)}, u32[]{:S(2)}) collective-permute-start(bf16[2,128,512]{2,1,0:T(8,128)(2,1)S(1)} %collective-permute-done.4), channel_id=1, source_target_pairs={{0,2},{1,7},{2,4},{3,1},{4,6},{5,3},{6,0},{7,5},{8,10},{9,15},{10,... | collective-permute-start | bytes 786440 | tf_op jit(solution)/shard_map/ppermute | solution.py:23
  40.9 20.7 %collective-permute-start.11 = (bf16[2,2,128,512]{3,2,1,0:T(8,128)(2,1)S(1)}, bf16[2,2,128,512]{3,2,1,0:T(8,128)(2,1)S(1)}, u32[]{:S(2)}, u32[]{:S(2)}) collective-permute-start(bf16[2,2,128,512]{3,2,1,0:T(8,128)(2,1)S(1)} %pad_maximum_fusion.refs_4_), channel_id=1, source_target_pairs={{0,24},{1,9},{2,26},{3,11},{4,28},{5,13},{6,30},{7,15},{8,0},{9,17... | collective-permute-start | bytes 1572872 | tf_op jit(solution)/shard_map/ppermute | solution.py:23
  51.2 10.5 %collective-permute-start.13 = (bf16[1,2,128,512]{3,2,1,0:T(8,128)(2,1)S(1)}, bf16[1,2,128,512]{3,2,1,0:T(8,128)(2,1)S(1)}, u32[]{:S(2)}, u32[]{:S(2)}) collective-permute-start(bf16[1,2,128,512]{3,2,1,0:T(8,128)(2,1)S(1)} %bitcast.17), channel_id=1, source_target_pairs={{0,8},{1,25},{2,10},{3,27},{4,12},{5,29},{6,14},{7,31},{8,16},{9,1... | collective-permute-start | bytes 786440 | tf_op jit(solution)/shard_map/ppermute | solution.py:23
  52.2 9.4 %collective-permute-start.14 = (bf16[1,2,128,512]{3,2,1,0:T(8,128)(2,1)S(1)}, bf16[1,2,128,512]{3,2,1,0:T(8,128)(2,1)S(1)}, u32[]{:S(2)}, u32[]{:S(2)}) collective-permute-start(bf16[1,2,128,512]{3,2,1,0:T(8,128)(2,1)S(1)} %bitcast.18), channel_id=1, source_target_pairs={{0,24},{1,9},{2,26},{3,11},{4,28},{5,13},{6,30},{7,15},{8,0},{9,17... | collective-permute-start | bytes 786440 | tf_op jit(solution)/shard_map/ppermute | solution.py:23
  54.4 16.0 %collective-permute-start.10 = (bf16[2,2,128,512]{3,2,1,0:T(8,128)(2,1)S(1)}, bf16[2,2,128,512]{3,2,1,0:T(8,128)(2,1)S(1)}, u32[]{:S(2)}, u32[]{:S(2)}) collective-permute-start(bf16[2,2,128,512]{3,2,1,0:T(8,128)(2,1)S(1)} %collective-permute-done.9.refs_5_), channel_id=1, source_target_pairs={{0,8},{1,25},{2,10},{3,27},{4,12},{5,29},{6,14},{7,31},{8,16},{9,1... | collective-permute-start | bytes 1572872 | tf_op jit(solution)/shard_map/ppermute | solution.py:23
  61.7 8.8 %collective-permute-start.15 = (bf16[1,2,128,512]{3,2,1,0:T(8,128)(2,1)S(1)}, bf16[1,2,128,512]{3,2,1,0:T(8,128)(2,1)S(1)}, u32[]{:S(2)}, u32[]{:S(2)}) collective-permute-start(bf16[1,2,128,512]{3,2,1,0:T(8,128)(2,1)S(1)} %collective-permute-done.13.refs_9_), channel_id=1, source_target_pairs={{0,8},{1,25},{2,10},{3,27},{4,12},{5,29},{6,14},{7,31},{8,16},{9,1... | collective-permute-start | bytes 786440 | tf_op jit(solution)/shard_map/ppermute | solution.py:23
  70.4 4.7 %collective-permute-start.16 = (bf16[2048,512]{1,0:T(8,128)(2,1)S(1)}, bf16[2048,512]{1,0:T(8,128)(2,1)S(1)}, u32[]{:S(2)}, u32[]{:S(2)}) collective-permute-start(bf16[2048,512]{1,0:T(8,128)(2,1)S(1)} %collective-permute-done.3.far), channel_id=1, source_target_pairs={{0,1},{1,0},{2,3},{3,2},{4,5},{5,4},{6,7},{7,6},{8,9},{9,8},{10,11... | collective-permute-start | bytes 6291464 | tf_op jit(solution)/shard_map/ppermute | solution.py:23
  75.1 20.9 %copy-start = (s32[2,256,64]{1,2,0:T(8,128)S(1)}, s32[2,256,64]{1,2,0:T(8,128)}, u32[]{:S(2)}) copy-start(s32[2,256,64]{1,2,0:T(8,128)} %param.5) | copy-start | bytes 393220
  75.2 20.9 %copy-start.1 = (f32[256]{0:T(256)S(1)}, f32[256]{0:T(256)}, u32[]{:S(2)}) copy-start(f32[256]{0:T(256)} %param.7) | copy-start | bytes 3076
  75.2 20.9 %copy-start.2 = (f32[512,256]{1,0:T(8,128)S(1)}, f32[512,256]{1,0:T(8,128)}, u32[]{:S(2)}) copy-start(f32[512,256]{1,0:T(8,128)} %get-tuple-element.27.decoded) | copy-start | bytes 1572868
  78.3 11.6 %collective-permute-start.17 = (bf16[128,1024]{1,0:T(8,128)(2,1)S(1)}, bf16[128,1024]{1,0:T(8,128)(2,1)S(1)}, u32[]{:S(2)}, u32[]{:S(2)}) collective-permute-start(bf16[128,1024]{1,0:T(8,128)(2,1)S(1)} %get-tuple-element.46), channel_id=1, source_target_pairs={{0,192},{1,193},{2,194},{3,195},{4,196},{5,197},{6,198},{7,199},{8... | collective-permute-start | bytes 786440 | tf_op jit(solution)/shard_map/ppermute | solution.py:23
  78.9 15.5 %collective-permute-start.18 = (bf16[128,1024]{1,0:T(8,128)(2,1)S(1)}, bf16[128,1024]{1,0:T(8,128)(2,1)S(1)}, u32[]{:S(2)}, u32[]{:S(2)}) collective-permute-start(bf16[128,1024]{1,0:T(8,128)(2,1)S(1)} %get-tuple-element.47), channel_id=1, source_target_pairs={{0,64},{1,65},{2,66},{3,67},{4,68},{5,69},{6,70},{7,71},{8,72},{9,... | collective-permute-start | bytes 786440 | tf_op jit(solution)/shard_map/ppermute | solution.py:23
  81.7 12.6 %collective-permute-start.19 = (bf16[128,1024]{1,0:T(8,128)(2,1)S(1)}, bf16[128,1024]{1,0:T(8,128)(2,1)S(1)}, u32[]{:S(2)}, u32[]{:S(2)}) collective-permute-start(bf16[128,1024]{1,0:T(8,128)(2,1)S(1)} %get-tuple-element.48), channel_id=1, source_target_pairs={{0,128},{1,129},{2,130},{3,131},{4,132},{5,133},{6,134},{7,135},{8... | collective-permute-start | bytes 786440 | tf_op jit(solution)/shard_map/ppermute | solution.py:23
  94.5 1.6 %collective-permute-start.20 = (f32[128,512]{1,0:T(8,128)S(1)}, f32[128,512]{1,0:T(8,128)S(1)}, u32[]{:S(2)}, u32[]{:S(2)}) collective-permute-start(f32[128,512]{1,0:T(8,128)S(1)} %convert_add_fusion), channel_id=1, source_target_pairs={{0,1},{1,0},{2,3},{3,2},{4,5},{5,4},{6,7},{7,6},{8,9},{9,8},{10,11... | collective-permute-start | bytes 786440 | tf_op jit(solution)/shard_map/ppermute | solution.py:23
  101.2 1.2 collective-permute-start.21
  103.2 13.1 %all-to-all-start = ((f32[16,17,256]{2,1,0:T(8,128)}), f32[16,17,256]{2,1,0:T(8,128)S(1)}, u32[]{:S(2)}, u32[]{:S(2)}) async-start(f32[16,17,256]{2,1,0:T(8,128)} %broadcast_in_dim.22), calls=%async_computation | async-start | bytes 786432 | tf_op jit(solution)/shard_map/all_to_all | solution.py:242
  117.1 14.5 %all-to-all-start.1 = ((f32[8,17,256]{2,1,0:T(8,128)}), f32[8,17,256]{2,1,0:T(8,128)S(1)}, u32[]{:S(2)}, u32[]{:S(2)}) async-start(f32[8,17,256]{2,1,0:T(8,128)} %broadcast_in_dim.24), calls=%async_computation.1 | async-start | bytes 393216 | tf_op jit(solution)/shard_map/all_to_all | solution.py:242

commit v13 on v12

--- a/solution.py
+++ b/solution.py
@@ -335,9 +335,12 @@
     product, total = finish(codes, row_scale, decoded, parts, got)
 
     total = total + shift(total, "core", 1)
-    total = gather_sum(total, ("y_hi", "y_lo", "x"), ("y_hi", "y_lo"))
+    total = total + shift(total, "x", 1) + shift(total, "x", -1) + shift(total, "x", 2)
     total = gather_sum(total, ("z_lo", "z_hi"), ("z_lo",))
     scale_total, books = total[16], total[:16]
+    beside, across_y = shift(books, "y_lo", 1), shift(books, "y_hi", 1)
+    both = send(books, lambda zl, yh, yl, x, zh, c: (zl, 1 - yh, 1 - yl, x, zh, c))
+    books = books + beside + across_y + both
     full_width = width * 32
     all_groups = rows * 8 * (full_width // 8)
     scale_grad = scale_total / full_width

time: 136 us -> 132 us (0.971); the launches traced: 133 us -> 132 us
  waiting for transfers between devices: 62.3 us -> 60.5 us
  starting transfers between devices: 50.4 us -> 52.1 us
    all_to_all x2 -> x1, waiting for transfers between devices: 16.4 us -> 8.54 us  [gather_sum(): copies = lax.all_to_all(copies, axes, 0, 0, tiled=True)]
    ppermute x22 -> x28, starting transfers between devices: 39.3 us -> 46.4 us  [send(): return lax.ppermute(a, AXES, pairs)]
    ppermute x22 -> x28, waiting for transfers between devices: 45.9 us -> 52 us  [send(): return lax.ppermute(a, AXES, pairs)]
    all_to_all x2 -> x1, starting transfers between devices: 11.1 us -> 5.68 us  [gather_sum(): copies = lax.all_to_all(copies, axes, 0, 0, tiled=True)]
  transfers between devices with their start and end apart: 24 -> 29, of which waited for: 11 -> 14; matrix products, arithmetic and copies ran while one was open for 0% -> 0% of each run, Pallas kernels for 6% -> 6%
where the time goes in v13:
time: 132 us
  waiting for transfers between devices  60.5 us (46%)
  starting transfers between devices  52.1 us (39%)
  Pallas kernels  16.3 us (12%)
  other arithmetic  1.45 us (1%)
    ppermute x28, waiting for transfers between devices, send(): return lax.ppermute(a, AXES, pairs)  52 us
    ppermute x28, starting transfers between devices, send(): return lax.ppermute(a, AXES, pairs)  46.4 us
    all_to_all x1, waiting for transfers between devices, gather_sum(): copies = lax.all_to_all(copies, axes, 0, 0, tiled=True)  8.54 us
    all_to_all x1, starting transfers between devices, gather_sum(): copies = lax.all_to_all(copies, axes, 0, 0, tiled=True)  5.68 us
    pallas_call x1, Pallas kernels, finish(): pl.pallas_call(finish_kernel, out_shape=(jax.ShapeDtypeStruct((rows, widt...  5.12 us
    pallas_call x1, Pallas kernels, body(): pl.pallas_call(first_kernel, out_shape=(jax.ShapeDtypeStruct((4, half, wi...  4.68 us
    pallas_call x1, Pallas kernels, decode(): pl.pallas_call(decode_kernel, out_shape=(jax.ShapeDtypeStruct((width, row...  3.35 us
    pallas_call x1, Pallas kernels, body(): pl.pallas_call(second_kernel, out_shape=(jax.ShapeDtypeStruct(sent.shape,...  3.16 us
  transfers between devices with their start and end apart: 29, of which 14 were waited for; matrix products, arithmetic and copies ran while one was open for 0% of the time, Pallas kernels for 6%

profile of v13, /device:TPU:8, one launch (start us, length us, event | category | flops | bytes accessed | tf_op | source)
XLA Modules:
  0.0 131.9 jit_solution(2545076074666076358)
XLA Ops:
  0.7 3.4 %decode.1 = (f32[512,256]{1,0:T(8,128)}, bf16[128,512]{1,0:T(8,128)(2,1)}, bf16[128,512]{1,0:T(8,128)(2,1)}) custom-call(s32[2,64,256]{2,1,0:T(8,128)} %bitcast.20, bf16[2,8,256]{2,1,0:T(8,128)(2,1)} %bitcast.28, f32[1,256]{1,0:T(1,128)} %bitcast.22, bf16[256,512]{1,0:T(8,128)(2,1)} %initial_in.1), custom_call_target="tpu_custom_call" | custom-call | flops 2097152 | bytes 1048576 | tf_op jit(solution)/shard_map/decode/pallas_call | solution.py:81
  4.7 1.6 %collective-permute-start = (bf16[128,512]{1,0:T(8,128)(2,1)}, bf16[128,512]{1,0:T(8,128)(2,1)S(1)}, u32[]{:S(2)}, u32[]{:S(2)}) collective-permute-start(bf16[128,512]{1,0:T(8,128)(2,1)} %get-tuple-element.28), channel_id=1, source_target_pairs={{0,0},{1,1},{2,2},{3,3},{4,4},{5,5},{6,6},{7,7},{8,72},{9,73},{10,... | collective-permute-start | bytes 393224 | tf_op jit(solution)/shard_map/ppermute | solution.py:23
  6.3 2.3 %collective-permute-start.3 = (bf16[2048,512]{1,0:T(8,128)(2,1)}, bf16[2048,512]{1,0:T(8,128)(2,1)S(1)}, u32[]{:S(2)}, u32[]{:S(2)}) collective-permute-start(bf16[2048,512]{1,0:T(8,128)(2,1)} %own.1), channel_id=1, source_target_pairs={{0,32},{1,33},{2,34},{3,35},{4,36},{5,37},{6,38},{7,39},{8,40},{9,... | collective-permute-start | bytes 6291464 | tf_op jit(solution)/shard_map/ppermute | solution.py:23
  8.5 10.9 %collective-permute-start.7 = (bf16[1,2,128,512]{3,2,1,0:T(8,128)(2,1)S(1)}, bf16[1,2,128,512]{3,2,1,0:T(8,128)(2,1)S(1)}, u32[]{:S(2)}, u32[]{:S(2)}) collective-permute-start(bf16[1,2,128,512]{3,2,1,0:T(8,128)(2,1)S(1)} %bitcast.14), channel_id=1, source_target_pairs={{0,8},{1,25},{2,10},{3,27},{4,12},{5,29},{6,14},{7,31},{8,16},{9,1... | collective-permute-start | bytes 786440 | tf_op jit(solution)/shard_map/ppermute | solution.py:23
  19.4 6.3 %collective-permute-start.5 = (bf16[2,128,512]{2,1,0:T(8,128)(2,1)S(1)}, bf16[2,128,512]{2,1,0:T(8,128)(2,1)S(1)}, u32[]{:S(2)}, u32[]{:S(2)}) collective-permute-start(bf16[2,128,512]{2,1,0:T(8,128)(2,1)S(1)} %pad_maximum_fusion.1), channel_id=1, source_target_pairs={{0,6},{1,3},{2,0},{3,5},{4,2},{5,7},{6,4},{7,1},{8,14},{9,11},{10,... | collective-permute-start | bytes 786440 | tf_op jit(solution)/shard_map/ppermute | solution.py:23
  25.8 3.8 %collective-permute-start.6 = (bf16[1,2,128,512]{3,2,1,0:T(8,128)(2,1)S(1)}, bf16[1,2,128,512]{3,2,1,0:T(8,128)(2,1)S(1)}, u32[]{:S(2)}, u32[]{:S(2)}) collective-permute-start(bf16[1,2,128,512]{3,2,1,0:T(8,128)(2,1)S(1)} %bitcast.15), channel_id=1, source_target_pairs={{0,24},{1,9},{2,26},{3,11},{4,28},{5,13},{6,30},{7,15},{8,0},{9,17... | collective-permute-start | bytes 786440 | tf_op jit(solution)/shard_map/ppermute | solution.py:23
  29.6 7.1 %collective-permute-done.5 = bf16[2,128,512]{2,1,0:T(8,128)(2,1)S(1)} collective-permute-done((bf16[2,128,512]{2,1,0:T(8,128)(2,1)S(1)}, bf16[2,128,512]{2,1,0:T(8,128)(2,1)S(1)}, u32[]{:S(2)}, u32[]{:S(2)}) %collective-permute-start.5) | collective-permute-done | bytes 262176 | tf_op jit(solution)/shard_map/ppermute | solution.py:23
  36.6 3.6 %collective-permute-done.4 = bf16[2,128,512]{2,1,0:T(8,128)(2,1)S(1)} collective-permute-done((bf16[2,128,512]{2,1,0:T(8,128)(2,1)S(1)}, bf16[2,128,512]{2,1,0:T(8,128)(2,1)S(1)}, u32[]{:S(2)}, u32[]{:S(2)}) %collective-permute-start.4) | collective-permute-done | bytes 262176 | tf_op jit(solution)/shard_map/ppermute | solution.py:23
  40.9 3.2 %collective-permute-start.11 = (bf16[2,2,128,512]{3,2,1,0:T(8,128)(2,1)S(1)}, bf16[2,2,128,512]{3,2,1,0:T(8,128)(2,1)S(1)}, u32[]{:S(2)}, u32[]{:S(2)}) collective-permute-start(bf16[2,2,128,512]{3,2,1,0:T(8,128)(2,1)S(1)} %pad_maximum_fusion.refs_4_), channel_id=1, source_target_pairs={{0,24},{1,9},{2,26},{3,11},{4,28},{5,13},{6,30},{7,15},{8,0},{9,17... | collective-permute-start | bytes 1572872 | tf_op jit(solution)/shard_map/ppermute | solution.py:23
  44.1 7.0 %collective-permute-done.12 = bf16[2,128,512]{2,1,0:T(8,128)(2,1)S(1)} collective-permute-done((bf16[2,128,512]{2,1,0:T(8,128)(2,1)S(1)}, bf16[2,128,512]{2,1,0:T(8,128)(2,1)S(1)}, u32[]{:S(2)}, u32[]{:S(2)}) %collective-permute-start.12) | collective-permute-done | bytes 262176 | tf_op jit(solution)/shard_map/ppermute | solution.py:23
  51.2 1.0 collective-permute-start.13
  52.2 2.2 %collective-permute-start.14 = (bf16[1,2,128,512]{3,2,1,0:T(8,128)(2,1)S(1)}, bf16[1,2,128,512]{3,2,1,0:T(8,128)(2,1)S(1)}, u32[]{:S(2)}, u32[]{:S(2)}) collective-permute-start(bf16[1,2,128,512]{3,2,1,0:T(8,128)(2,1)S(1)} %bitcast.18), channel_id=1, source_target_pairs={{0,24},{1,9},{2,26},{3,11},{4,28},{5,13},{6,30},{7,15},{8,0},{9,17... | collective-permute-start | bytes 786440 | tf_op jit(solution)/shard_map/ppermute | solution.py:23
  54.4 7.2 %collective-permute-done.13.refs_9_ = bf16[1,2,128,512]{3,2,1,0:T(8,128)(2,1)S(1)} collective-permute-done((bf16[1,2,128,512]{3,2,1,0:T(8,128)(2,1)S(1)}, bf16[1,2,128,512]{3,2,1,0:T(8,128)(2,1)S(1)}, u32[]{:S(2)}, u32[]{:S(2)}) %collective-permute-start.13) | collective-permute-done | bytes 262176 | tf_op jit(solution)/shard_map/ppermute | solution.py:23
  61.6 1.3 %collective-permute-start.15 = (bf16[1,2,128,512]{3,2,1,0:T(8,128)(2,1)S(1)}, bf16[1,2,128,512]{3,2,1,0:T(8,128)(2,1)S(1)}, u32[]{:S(2)}, u32[]{:S(2)}) collective-permute-start(bf16[1,2,128,512]{3,2,1,0:T(8,128)(2,1)S(1)} %collective-permute-done.13.refs_9_), channel_id=1, source_target_pairs={{0,8},{1,25},{2,10},{3,27},{4,12},{5,29},{6,14},{7,31},{8,16},{9,1... | collective-permute-start | bytes 786440 | tf_op jit(solution)/shard_map/ppermute | solution.py:23
  63.0 7.4 %collective-permute-done.15.refs_11_ = bf16[1,2,128,512]{3,2,1,0:T(8,128)(2,1)S(1)} collective-permute-done((bf16[1,2,128,512]{3,2,1,0:T(8,128)(2,1)S(1)}, bf16[1,2,128,512]{3,2,1,0:T(8,128)(2,1)S(1)}, u32[]{:S(2)}, u32[]{:S(2)}) %collective-permute-start.15) | collective-permute-done | bytes 262176 | tf_op jit(solution)/shard_map/ppermute | solution.py:23
  70.4 4.7 %first.1 = (f32[4,128,512]{2,1,0:T(8,128)S(1)}, bf16[512,4096]{1,0:T(8,128)(2,1)S(1)}) custom-call(bf16[2048,512]{1,0:T(8,128)(2,1)} %own.1, bf16[2048,512]{1,0:T(8,128)(2,1)S(1)} %collective-permute-done.3.far, bf16[1,2,128,512]{3,2,1,0:T(8,128)(2,1)S(1)} %bitcast.16, bf16[1,2,128,512]{3,2,1,0:T(8,128)(2,1)S(1)} %collective-permute-done.7.refs_1_, ...), custom_call_target="tpu_custom_call" | custom-call | flops 2147483648 | bytes 8388608 | tf_op jit(solution)/shard_map/first/pallas_call | solution.py:297
  75.2 3.2 %second.1 = (f32[128,1024]{1,0:T(8,128)S(1)}, bf16[128,1024]{1,0:T(8,128)(2,1)S(1)}, bf16[128,1024]{1,0:T(8,128)(2,1)S(1)}, bf16[128,1024]{1,0:T(8,128)(2,1)S(1)}) custom-call(f32[4,128,512]{2,1,0:T(8,128)S(1)} %get-tuple-element.42.kept, bf16[512,4096]{1,0:T(8,128)(2,1)S(1)} %get-tuple-element.43.held, bf16[2048,512]{1,0:T(8,128)(2,1)S(1)} %collective-permute-done.2.across, ...), custom_call_target="tpu_custom_call" | custom-call | flops 2147483648 | bytes 8388608 | tf_op jit(solution)/shard_map/second/pallas_call | solution.py:313
  78.9 2.9 %collective-permute-start.18 = (bf16[128,1024]{1,0:T(8,128)(2,1)S(1)}, bf16[128,1024]{1,0:T(8,128)(2,1)S(1)}, u32[]{:S(2)}, u32[]{:S(2)}) collective-permute-start(bf16[128,1024]{1,0:T(8,128)(2,1)S(1)} %get-tuple-element.47), channel_id=1, source_target_pairs={{0,64},{1,65},{2,66},{3,67},{4,68},{5,69},{6,70},{7,71},{8,72},{9,... | collective-permute-start | bytes 786440 | tf_op jit(solution)/shard_map/ppermute | solution.py:23
  81.7 1.7 %collective-permute-start.19 = (bf16[128,1024]{1,0:T(8,128)(2,1)S(1)}, bf16[128,1024]{1,0:T(8,128)(2,1)S(1)}, u32[]{:S(2)}, u32[]{:S(2)}) collective-permute-start(bf16[128,1024]{1,0:T(8,128)(2,1)S(1)} %get-tuple-element.48), channel_id=1, source_target_pairs={{0,128},{1,129},{2,130},{3,131},{4,132},{5,133},{6,134},{7,135},{8... | collective-permute-start | bytes 786440 | tf_op jit(solution)/shard_map/ppermute | solution.py:23
  83.4 6.6 %collective-permute-done.17.to_both = bf16[128,1024]{1,0:T(8,128)(2,1)S(1)} collective-permute-done((bf16[128,1024]{1,0:T(8,128)(2,1)S(1)}, bf16[128,1024]{1,0:T(8,128)(2,1)S(1)}, u32[]{:S(2)}, u32[]{:S(2)}) %collective-permute-start.17) | collective-permute-done | bytes 262176 | tf_op jit(solution)/shard_map/ppermute | solution.py:23
  90.0 4.4 %collective-permute-done.18.to_y = bf16[128,1024]{1,0:T(8,128)(2,1)S(1)} collective-permute-done((bf16[128,1024]{1,0:T(8,128)(2,1)S(1)}, bf16[128,1024]{1,0:T(8,128)(2,1)S(1)}, u32[]{:S(2)}, u32[]{:S(2)}) %collective-permute-start.18) | collective-permute-done | bytes 262176 | tf_op jit(solution)/shard_map/ppermute | solution.py:23
  94.6 1.5 %collective-permute-done.20.got = f32[128,512]{1,0:T(8,128)S(1)} collective-permute-done((f32[128,512]{1,0:T(8,128)S(1)}, f32[128,512]{1,0:T(8,128)S(1)}, u32[]{:S(2)}, u32[]{:S(2)}) %collective-permute-start.20) | collective-permute-done | bytes 262176 | tf_op jit(solution)/shard_map/ppermute | solution.py:23
  96.1 5.1 %finish.1 = (f32[256,512]{1,0:T(8,128)}, f32[17,256]{1,0:T(8,128)S(1)}) custom-call(s32[2,64,256]{2,1,0:T(8,128)S(1)} %bitcast.21, f32[1,256]{1,0:T(1,128)S(1)} %bitcast.23, f32[512,256]{1,0:T(8,128)S(1)} %copy-done.2, f32[128,1024]{1,0:T(8,128)S(1)} %get-tuple-element.45.own, bf16[128,1024]{1,0:T(8,128)(2,1)S(1)} %collective-permute-done.17.to_both, ...), custom_call_target="tpu_custom_call" | custom-call | flops 4294967296 | bytes 2097152 | tf_op jit(solution)/shard_map/finish/pallas_call | solution.py:151
  101.4 1.1 collective-permute-done.21
  104.0 1.4 %collective-permute-start.22 = (f32[17,256]{1,0:T(8,128)S(1)}, f32[17,256]{1,0:T(8,128)S(1)}, u32[]{:S(2)}, u32[]{:S(2)}) collective-permute-start(f32[17,256]{1,0:T(8,128)S(1)} %add.35), channel_id=1, source_target_pairs={{0,8},{1,9},{2,10},{3,11},{4,12},{5,13},{6,14},{7,15},{8,16},{9,17... | collective-permute-start | bytes 52232 | tf_op jit(solution)/shard_map/ppermute | solution.py:23
  105.4 2.5 %collective-permute-done.24 = f32[17,256]{1,0:T(8,128)S(1)} collective-permute-done((f32[17,256]{1,0:T(8,128)S(1)}, f32[17,256]{1,0:T(8,128)S(1)}, u32[]{:S(2)}, u32[]{:S(2)}) %collective-permute-start.24) | collective-permute-done | bytes 17440 | tf_op jit(solution)/shard_map/ppermute | solution.py:23
  107.9 1.1 collective-permute-done.22
  109.7 5.7 %all-to-all-start = ((f32[8,17,256]{2,1,0:T(8,128)}), f32[8,17,256]{2,1,0:T(8,128)S(1)}, u32[]{:S(2)}, u32[]{:S(2)}) async-start(f32[8,17,256]{2,1,0:T(8,128)} %broadcast_in_dim.15), calls=%async_computation | async-start | bytes 393216 | tf_op jit(solution)/shard_map/all_to_all | solution.py:242
  115.4 8.5 %all-to-all-done = f32[8,17,256]{2,1,0:T(8,128)S(1)} async-done(((f32[8,17,256]{2,1,0:T(8,128)}), f32[8,17,256]{2,1,0:T(8,128)S(1)}, u32[]{:S(2)}, u32[]{:S(2)}) %all-to-all-start) | async-done | bytes 139296 | tf_op jit(solution)/shard_map/all_to_all | solution.py:242
  124.1 1.0 collective-permute-start.27
  125.1 2.4 %collective-permute-start.26 = (f32[16,256]{1,0:T(8,128)S(1)}, f32[16,256]{1,0:T(8,128)S(1)}, u32[]{:S(2)}, u32[]{:S(2)}) collective-permute-start(f32[16,256]{1,0:T(8,128)S(1)} %slice.28), channel_id=1, source_target_pairs={{0,64},{1,65},{2,66},{3,67},{4,68},{5,69},{6,70},{7,71},{8,72},{9,... | collective-permute-start | bytes 49160 | tf_op jit(solution)/shard_map/ppermute | solution.py:23
  128.8 1.5 %collective-permute-done.26 = f32[16,256]{1,0:T(8,128)S(1)} collective-permute-done((f32[16,256]{1,0:T(8,128)S(1)}, f32[16,256]{1,0:T(8,128)S(1)}, u32[]{:S(2)}, u32[]{:S(2)}) %collective-permute-start.26) | collective-permute-done | bytes 16416 | tf_op jit(solution)/shard_map/ppermute | solution.py:23
  (49 shorter events, 7.4 us)
Async XLA Ops:
  0.6 5.6 %collective-permute-start.2 = (bf16[2048,512]{1,0:T(8,128)(2,1)}, bf16[2048,512]{1,0:T(8,128)(2,1)S(1)}, u32[]{:S(2)}, u32[]{:S(2)}) collective-permute-start(bf16[2048,512]{1,0:T(8,128)(2,1)} %own.1), channel_id=1, source_target_pairs={{0,1},{1,0},{2,3},{3,2},{4,5},{5,4},{6,7},{7,6},{8,9},{9,8},{10,11... | collective-permute-start | bytes 6291464 | tf_op jit(solution)/shard_map/ppermute | solution.py:23
  4.1 2.1 %collective-permute-start.1 = (bf16[128,512]{1,0:T(8,128)(2,1)}, bf16[128,512]{1,0:T(8,128)(2,1)S(1)}, u32[]{:S(2)}, u32[]{:S(2)}) collective-permute-start(bf16[128,512]{1,0:T(8,128)(2,1)} %get-tuple-element.29), channel_id=1, source_target_pairs={{0,1},{1,0},{2,3},{3,2},{4,5},{5,4},{6,7},{7,6},{8,73},{9,72},{10,... | collective-permute-start | bytes 393224 | tf_op jit(solution)/shard_map/ppermute | solution.py:23
  4.7 1.6 %collective-permute-start = (bf16[128,512]{1,0:T(8,128)(2,1)}, bf16[128,512]{1,0:T(8,128)(2,1)S(1)}, u32[]{:S(2)}, u32[]{:S(2)}) collective-permute-start(bf16[128,512]{1,0:T(8,128)(2,1)} %get-tuple-element.28), channel_id=1, source_target_pairs={{0,0},{1,1},{2,2},{3,3},{4,4},{5,5},{6,6},{7,7},{8,72},{9,73},{10,... | collective-permute-start | bytes 393224 | tf_op jit(solution)/shard_map/ppermute | solution.py:23
  6.3 64.2 %collective-permute-start.3 = (bf16[2048,512]{1,0:T(8,128)(2,1)}, bf16[2048,512]{1,0:T(8,128)(2,1)S(1)}, u32[]{:S(2)}, u32[]{:S(2)}) collective-permute-start(bf16[2048,512]{1,0:T(8,128)(2,1)} %own.1), channel_id=1, source_target_pairs={{0,32},{1,33},{2,34},{3,35},{4,36},{5,37},{6,38},{7,39},{8,40},{9,... | collective-permute-start | bytes 6291464 | tf_op jit(solution)/shard_map/ppermute | solution.py:23
  8.5 21.1 %collective-permute-start.7 = (bf16[1,2,128,512]{3,2,1,0:T(8,128)(2,1)S(1)}, bf16[1,2,128,512]{3,2,1,0:T(8,128)(2,1)S(1)}, u32[]{:S(2)}, u32[]{:S(2)}) collective-permute-start(bf16[1,2,128,512]{3,2,1,0:T(8,128)(2,1)S(1)} %bitcast.14), channel_id=1, source_target_pairs={{0,8},{1,25},{2,10},{3,27},{4,12},{5,29},{6,14},{7,31},{8,16},{9,1... | collective-permute-start | bytes 786440 | tf_op jit(solution)/shard_map/ppermute | solution.py:23
  19.4 17.2 %collective-permute-start.5 = (bf16[2,128,512]{2,1,0:T(8,128)(2,1)S(1)}, bf16[2,128,512]{2,1,0:T(8,128)(2,1)S(1)}, u32[]{:S(2)}, u32[]{:S(2)}) collective-permute-start(bf16[2,128,512]{2,1,0:T(8,128)(2,1)S(1)} %pad_maximum_fusion.1), channel_id=1, source_target_pairs={{0,6},{1,3},{2,0},{3,5},{4,2},{5,7},{6,4},{7,1},{8,14},{9,11},{10,... | collective-permute-start | bytes 786440 | tf_op jit(solution)/shard_map/ppermute | solution.py:23
  25.7 14.5 %collective-permute-start.4 = (bf16[2,128,512]{2,1,0:T(8,128)(2,1)S(1)}, bf16[2,128,512]{2,1,0:T(8,128)(2,1)S(1)}, u32[]{:S(2)}, u32[]{:S(2)}) collective-permute-start(bf16[2,128,512]{2,1,0:T(8,128)(2,1)S(1)} %pad_maximum_fusion.1), channel_id=1, source_target_pairs={{0,2},{1,7},{2,4},{3,1},{4,6},{5,3},{6,0},{7,5},{8,10},{9,15},{10,... | collective-permute-start | bytes 786440 | tf_op jit(solution)/shard_map/ppermute | solution.py:23
  25.8 14.5 %collective-permute-start.6 = (bf16[1,2,128,512]{3,2,1,0:T(8,128)(2,1)S(1)}, bf16[1,2,128,512]{3,2,1,0:T(8,128)(2,1)S(1)}, u32[]{:S(2)}, u32[]{:S(2)}) collective-permute-start(bf16[1,2,128,512]{3,2,1,0:T(8,128)(2,1)S(1)} %bitcast.15), channel_id=1, source_target_pairs={{0,24},{1,9},{2,26},{3,11},{4,28},{5,13},{6,30},{7,15},{8,0},{9,17... | collective-permute-start | bytes 786440 | tf_op jit(solution)/shard_map/ppermute | solution.py:23
  29.6 10.7 %collective-permute-start.8 = (bf16[1,2,128,512]{3,2,1,0:T(8,128)(2,1)S(1)}, bf16[1,2,128,512]{3,2,1,0:T(8,128)(2,1)S(1)}, u32[]{:S(2)}, u32[]{:S(2)}) collective-permute-start(bf16[1,2,128,512]{3,2,1,0:T(8,128)(2,1)S(1)} %collective-permute-done.7.refs_1_), channel_id=1, source_target_pairs={{0,8},{1,25},{2,10},{3,27},{4,12},{5,29},{6,14},{7,31},{8,16},{9,1... | collective-permute-start | bytes 786440 | tf_op jit(solution)/shard_map/ppermute | solution.py:23
  40.3 14.1 %collective-permute-start.9 = (bf16[2,2,128,512]{3,2,1,0:T(8,128)(2,1)S(1)}, bf16[2,2,128,512]{3,2,1,0:T(8,128)(2,1)S(1)}, u32[]{:S(2)}, u32[]{:S(2)}) collective-permute-start(bf16[2,2,128,512]{3,2,1,0:T(8,128)(2,1)S(1)} %pad_maximum_fusion.refs_4_), channel_id=1, source_target_pairs={{0,8},{1,25},{2,10},{3,27},{4,12},{5,29},{6,14},{7,31},{8,16},{9,1... | collective-permute-start | bytes 1572872 | tf_op jit(solution)/shard_map/ppermute | solution.py:23
  40.4 10.8 %collective-permute-start.12 = (bf16[2,128,512]{2,1,0:T(8,128)(2,1)S(1)}, bf16[2,128,512]{2,1,0:T(8,128)(2,1)S(1)}, u32[]{:S(2)}, u32[]{:S(2)}) collective-permute-start(bf16[2,128,512]{2,1,0:T(8,128)(2,1)S(1)} %collective-permute-done.4), channel_id=1, source_target_pairs={{0,2},{1,7},{2,4},{3,1},{4,6},{5,3},{6,0},{7,5},{8,10},{9,15},{10,... | collective-permute-start | bytes 786440 | tf_op jit(solution)/shard_map/ppermute | solution.py:23
  40.9 20.7 %collective-permute-start.11 = (bf16[2,2,128,512]{3,2,1,0:T(8,128)(2,1)S(1)}, bf16[2,2,128,512]{3,2,1,0:T(8,128)(2,1)S(1)}, u32[]{:S(2)}, u32[]{:S(2)}) collective-permute-start(bf16[2,2,128,512]{3,2,1,0:T(8,128)(2,1)S(1)} %pad_maximum_fusion.refs_4_), channel_id=1, source_target_pairs={{0,24},{1,9},{2,26},{3,11},{4,28},{5,13},{6,30},{7,15},{8,0},{9,17... | collective-permute-start | bytes 1572872 | tf_op jit(solution)/shard_map/ppermute | solution.py:23
  51.2 10.5 %collective-permute-start.13 = (bf16[1,2,128,512]{3,2,1,0:T(8,128)(2,1)S(1)}, bf16[1,2,128,512]{3,2,1,0:T(8,128)(2,1)S(1)}, u32[]{:S(2)}, u32[]{:S(2)}) collective-permute-start(bf16[1,2,128,512]{3,2,1,0:T(8,128)(2,1)S(1)} %bitcast.17), channel_id=1, source_target_pairs={{0,8},{1,25},{2,10},{3,27},{4,12},{5,29},{6,14},{7,31},{8,16},{9,1... | collective-permute-start | bytes 786440 | tf_op jit(solution)/shard_map/ppermute | solution.py:23
  52.2 9.4 %collective-permute-start.14 = (bf16[1,2,128,512]{3,2,1,0:T(8,128)(2,1)S(1)}, bf16[1,2,128,512]{3,2,1,0:T(8,128)(2,1)S(1)}, u32[]{:S(2)}, u32[]{:S(2)}) collective-permute-start(bf16[1,2,128,512]{3,2,1,0:T(8,128)(2,1)S(1)} %bitcast.18), channel_id=1, source_target_pairs={{0,24},{1,9},{2,26},{3,11},{4,28},{5,13},{6,30},{7,15},{8,0},{9,17... | collective-permute-start | bytes 786440 | tf_op jit(solution)/shard_map/ppermute | solution.py:23
  54.4 16.0 %collective-permute-start.10 = (bf16[2,2,128,512]{3,2,1,0:T(8,128)(2,1)S(1)}, bf16[2,2,128,512]{3,2,1,0:T(8,128)(2,1)S(1)}, u32[]{:S(2)}, u32[]{:S(2)}) collective-permute-start(bf16[2,2,128,512]{3,2,1,0:T(8,128)(2,1)S(1)} %collective-permute-done.9.refs_5_), channel_id=1, source_target_pairs={{0,8},{1,25},{2,10},{3,27},{4,12},{5,29},{6,14},{7,31},{8,16},{9,1... | collective-permute-start | bytes 1572872 | tf_op jit(solution)/shard_map/ppermute | solution.py:23
  61.6 8.8 %collective-permute-start.15 = (bf16[1,2,128,512]{3,2,1,0:T(8,128)(2,1)S(1)}, bf16[1,2,128,512]{3,2,1,0:T(8,128)(2,1)S(1)}, u32[]{:S(2)}, u32[]{:S(2)}) collective-permute-start(bf16[1,2,128,512]{3,2,1,0:T(8,128)(2,1)S(1)} %collective-permute-done.13.refs_9_), channel_id=1, source_target_pairs={{0,8},{1,25},{2,10},{3,27},{4,12},{5,29},{6,14},{7,31},{8,16},{9,1... | collective-permute-start | bytes 786440 | tf_op jit(solution)/shard_map/ppermute | solution.py:23
  70.4 4.7 %collective-permute-start.16 = (bf16[2048,512]{1,0:T(8,128)(2,1)S(1)}, bf16[2048,512]{1,0:T(8,128)(2,1)S(1)}, u32[]{:S(2)}, u32[]{:S(2)}) collective-permute-start(bf16[2048,512]{1,0:T(8,128)(2,1)S(1)} %collective-permute-done.3.far), channel_id=1, source_target_pairs={{0,1},{1,0},{2,3},{3,2},{4,5},{5,4},{6,7},{7,6},{8,9},{9,8},{10,11... | collective-permute-start | bytes 6291464 | tf_op jit(solution)/shard_map/ppermute | solution.py:23
  75.1 21.0 %copy-start = (s32[2,256,64]{1,2,0:T(8,128)S(1)}, s32[2,256,64]{1,2,0:T(8,128)}, u32[]{:S(2)}) copy-start(s32[2,256,64]{1,2,0:T(8,128)} %param.5) | copy-start | bytes 393220
  75.1 20.9 %copy-start.1 = (f32[256]{0:T(256)S(1)}, f32[256]{0:T(256)}, u32[]{:S(2)}) copy-start(f32[256]{0:T(256)} %param.7) | copy-start | bytes 3076
  75.2 20.9 %copy-start.2 = (f32[512,256]{1,0:T(8,128)S(1)}, f32[512,256]{1,0:T(8,128)}, u32[]{:S(2)}) copy-start(f32[512,256]{1,0:T(8,128)} %get-tuple-element.27.decoded) | copy-start | bytes 1572868
  78.3 11.6 %collective-permute-start.17 = (bf16[128,1024]{1,0:T(8,128)(2,1)S(1)}, bf16[128,1024]{1,0:T(8,128)(2,1)S(1)}, u32[]{:S(2)}, u32[]{:S(2)}) collective-permute-start(bf16[128,1024]{1,0:T(8,128)(2,1)S(1)} %get-tuple-element.46), channel_id=1, source_target_pairs={{0,192},{1,193},{2,194},{3,195},{4,196},{5,197},{6,198},{7,199},{8... | collective-permute-start | bytes 786440 | tf_op jit(solution)/shard_map/ppermute | solution.py:23
  78.9 15.5 %collective-permute-start.18 = (bf16[128,1024]{1,0:T(8,128)(2,1)S(1)}, bf16[128,1024]{1,0:T(8,128)(2,1)S(1)}, u32[]{:S(2)}, u32[]{:S(2)}) collective-permute-start(bf16[128,1024]{1,0:T(8,128)(2,1)S(1)} %get-tuple-element.47), channel_id=1, source_target_pairs={{0,64},{1,65},{2,66},{3,67},{4,68},{5,69},{6,70},{7,71},{8,72},{9,... | collective-permute-start | bytes 786440 | tf_op jit(solution)/shard_map/ppermute | solution.py:23
  81.7 12.7 %collective-permute-start.19 = (bf16[128,1024]{1,0:T(8,128)(2,1)S(1)}, bf16[128,1024]{1,0:T(8,128)(2,1)S(1)}, u32[]{:S(2)}, u32[]{:S(2)}) collective-permute-start(bf16[128,1024]{1,0:T(8,128)(2,1)S(1)} %get-tuple-element.48), channel_id=1, source_target_pairs={{0,128},{1,129},{2,130},{3,131},{4,132},{5,133},{6,134},{7,135},{8... | collective-permute-start | bytes 786440 | tf_op jit(solution)/shard_map/ppermute | solution.py:23
  94.5 1.6 %collective-permute-start.20 = (f32[128,512]{1,0:T(8,128)S(1)}, f32[128,512]{1,0:T(8,128)S(1)}, u32[]{:S(2)}, u32[]{:S(2)}) collective-permute-start(f32[128,512]{1,0:T(8,128)S(1)} %convert_add_fusion), channel_id=1, source_target_pairs={{0,1},{1,0},{2,3},{3,2},{4,5},{5,4},{6,7},{7,6},{8,9},{9,8},{10,11... | collective-permute-start | bytes 786440 | tf_op jit(solution)/shard_map/ppermute | solution.py:23
  101.2 1.2 collective-permute-start.21
  102.4 5.4 %collective-permute-start.24 = (f32[17,256]{1,0:T(8,128)S(1)}, f32[17,256]{1,0:T(8,128)S(1)}, u32[]{:S(2)}, u32[]{:S(2)}) collective-permute-start(f32[17,256]{1,0:T(8,128)S(1)} %add.35), channel_id=1, source_target_pairs={{0,16},{1,17},{2,18},{3,19},{4,20},{5,21},{6,22},{7,23},{8,24},{9,... | collective-permute-start | bytes 52232 | tf_op jit(solution)/shard_map/ppermute | solution.py:23
  103.4 4.5 %collective-permute-start.23 = (f32[17,256]{1,0:T(8,128)S(1)}, f32[17,256]{1,0:T(8,128)S(1)}, u32[]{:S(2)}, u32[]{:S(2)}) collective-permute-start(f32[17,256]{1,0:T(8,128)S(1)} %add.35), channel_id=1, source_target_pairs={{0,24},{1,25},{2,26},{3,27},{4,28},{5,29},{6,30},{7,31},{8,0},{9,1... | collective-permute-start | bytes 52232 | tf_op jit(solution)/shard_map/ppermute | solution.py:23
  104.0 5.0 %collective-permute-start.22 = (f32[17,256]{1,0:T(8,128)S(1)}, f32[17,256]{1,0:T(8,128)S(1)}, u32[]{:S(2)}, u32[]{:S(2)}) collective-permute-start(f32[17,256]{1,0:T(8,128)S(1)} %add.35), channel_id=1, source_target_pairs={{0,8},{1,9},{2,10},{3,11},{4,12},{5,13},{6,14},{7,15},{8,16},{9,17... | collective-permute-start | bytes 52232 | tf_op jit(solution)/shard_map/ppermute | solution.py:23
  109.7 14.3 %all-to-all-start = ((f32[8,17,256]{2,1,0:T(8,128)}), f32[8,17,256]{2,1,0:T(8,128)S(1)}, u32[]{:S(2)}, u32[]{:S(2)}) async-start(f32[8,17,256]{2,1,0:T(8,128)} %broadcast_in_dim.15), calls=%async_computation | async-start | bytes 393216 | tf_op jit(solution)/shard_map/all_to_all | solution.py:242
  124.1 4.7 %collective-permute-start.27 = (f32[16,256]{1,0:T(8,128)S(1)}, f32[16,256]{1,0:T(8,128)S(1)}, u32[]{:S(2)}, u32[]{:S(2)}) collective-permute-start(f32[16,256]{1,0:T(8,128)S(1)} %slice.28), channel_id=1, source_target_pairs={{0,96},{1,97},{2,98},{3,99},{4,100},{5,101},{6,102},{7,103},{8,104... | collective-permute-start | bytes 49160 | tf_op jit(solution)/shard_map/ppermute | solution.py:23
  125.1 5.2 %collective-permute-start.26 = (f32[16,256]{1,0:T(8,128)S(1)}, f32[16,256]{1,0:T(8,128)S(1)}, u32[]{:S(2)}, u32[]{:S(2)}) collective-permute-start(f32[16,256]{1,0:T(8,128)S(1)} %slice.28), channel_id=1, source_target_pairs={{0,64},{1,65},{2,66},{3,67},{4,68},{5,69},{6,70},{7,71},{8,72},{9,... | collective-permute-start | bytes 49160 | tf_op jit(solution)/shard_map/ppermute | solution.py:23
  127.5 3.7 %collective-permute-start.25 = (f32[16,256]{1,0:T(8,128)S(1)}, f32[16,256]{1,0:T(8,128)S(1)}, u32[]{:S(2)}, u32[]{:S(2)}) collective-permute-start(f32[16,256]{1,0:T(8,128)S(1)} %slice.28), channel_id=1, source_target_pairs={{0,32},{1,33},{2,34},{3,35},{4,36},{5,37},{6,38},{7,39},{8,40},{9,... | collective-permute-start | bytes 49160 | tf_op jit(solution)/shard_map/ppermute | solution.py:23
